TPU v7x, 32 devices: a whole 2x2x4 slice. The times are simulated.
32 devices in a mesh: samp: 4 (over y, x), chrom: 8 (over z, core).
Axes of the slice: x: 2, y: 2, z: 4, core: 2. Of those that a mesh axis runs over, the one named last changes fastest.
Arguments:
- dosages: float32 [4096, 8192], P('samp', 'chrom'), may hold values from -12 to 12
- traits: float32 [4096, 128], P('samp'), may hold values from -14 to 14
- start_coef: float32 [8192, 128], P('chrom'), may hold values from -1 to 1
- groups: int32 [8192], P('chrom'), may hold values from 0 to 15, as said below
- tested: bfloat16 [4096, 8192], P('samp', 'chrom'), may hold values from -16 to 16
- owners: int32 [8192], P('chrom'), may hold values from 0 to 15, as said below
Outputs:
- scores: float32 [8192, 128], P('chrom')
- residual: float32 [4096, 128], P('samp')
Inputs may be any that keep to these rules, and one draw needn't show every extreme that they name: `groups`: training variant j belongs to group 2 * (j // 1024) + r with r from 0 to 1; every such group has a variant. `owners`: tested variant i belongs to group 2 * (i // 1024) + r with r from 0 to 1; every such group has a tested variant.
All inputs are finite; a program needn't handle non-finite values.
Results may differ from a plain program's by a relative error of at most 0.00045.
The roundings to bfloat16 on the way count: a program that leaves them out, or rounds other values in their place, can miss the bound.
Values sent between devices are 32-bit elements; how exact they have to be, the bound alone decides.
No kernel may reach another device: no remote copies, remote signals or barrier semaphores. Data moves between devices by JAX's collectives and lax.ppermute only.
A program may use at most 64 MiB of HBM per device.

v0:
```python
import math

import jax
import jax.numpy as jnp
from jax import lax
from jax.sharding import PartitionSpec as P

GPD = 2
ITERS = 2


def matmul(left, right):
    return jnp.dot(left, right, precision=lax.Precision.HIGHEST, preferred_element_type=jnp.float32)


def inner_rows(left, right):
    return lax.dot_general(
        left,
        right,
        (((0,), (0,)), ((), ())),
        precision=lax.Precision.HIGHEST,
        preferred_element_type=jnp.float32,
    )


def total_prediction(partial_value):
    return lax.psum(partial_value, "chrom")


def body(dosages, traits, start_coef, groups, tested, owners):
    rows_dev = dosages.shape[0]
    total_rows = rows_dev * lax.axis_size("samp")
    penalty = 1.5 * math.sqrt(traits.shape[1] / total_rows)
    group_base = lax.axis_index("chrom") * GPD
    local_group = groups - group_base
    group_masks = [(local_group == which).astype(jnp.float32)[:, None] for which in range(GPD)]
    coefficients = start_coef
    for iteration in range(ITERS):
        prediction = total_prediction(matmul(dosages, coefficients))
        residual_now = traits - prediction
        gradient = lax.psum(inner_rows(dosages, residual_now) / total_rows, "samp")
        grad_sq = jnp.sum(gradient * gradient) / lax.axis_size("samp")

        def image_rows(start, count, gradient=gradient):
            return matmul(dosages, gradient)

        image_part = lax.psum_scatter(
            image_rows(jnp.int32(0), rows_dev // lax.axis_size("chrom") * lax.axis_size("chrom")),
            "chrom",
            scatter_dimension=0,
            tiled=True,
        )
        image_sq = jnp.sum(image_part * image_part)
        grad_sq, image_sq = lax.psum((grad_sq, image_sq), ("samp", "chrom"))
        step_size = grad_sq / (image_sq / total_rows + 1e-06)
        moved_rows = coefficients + step_size * gradient
        length = jnp.sqrt(jnp.sum(moved_rows * moved_rows, axis=1, keepdims=True))
        coefficients = moved_rows * (
            jnp.maximum(length - step_size * penalty, 0.0)
            / jnp.maximum(length, step_size * penalty)
        )
    prediction = total_prediction(matmul(dosages, coefficients))
    own_parts = [matmul(dosages, coefficients * mask) for mask in group_masks]
    residual = traits - prediction
    tested_sq = jnp.sum(jnp.square(tested.astype(jnp.float32)), axis=0)
    picked = jnp.zeros((tested.shape[1], traits.shape[1]), jnp.float32)
    loco_list = []
    chosen_list = []
    for which in range(GPD):
        loco_resid = residual + own_parts[which]
        loco_list.append(jnp.sum(loco_resid * loco_resid, axis=0))
        products = lax.dot_general(
            tested,
            loco_resid.astype(jnp.bfloat16),
            (((0,), (0,)), ((), ())),
            preferred_element_type=jnp.float32,
        )
        chosen = (owners - group_base == which).astype(jnp.float32)[:, None]
        chosen_list.append(chosen)
        picked = picked + chosen * products
    picked, tested_sq, loco_all = lax.psum((picked, tested_sq, jnp.stack(loco_list)), "samp")
    loco_pick = jnp.zeros_like(picked)
    for which in range(GPD):
        loco_pick = loco_pick + chosen_list[which] * loco_all[which][None, :]
    denom = math.sqrt(total_rows) * jnp.sqrt(
        (tested_sq[:, None] / total_rows + 1e-06) * (loco_pick / total_rows + 1e-06)
    )
    return (picked / denom, residual)


def solution(mesh):
    placed = (
        P("samp", "chrom"),
        P("samp", None),
        P("chrom", None),
        P("chrom"),
        P("samp", "chrom"),
        P("chrom"),
    )
    return jax.shard_map(
        body,
        mesh=mesh,
        in_specs=placed,
        out_specs=(P("chrom", None), P("samp", None)),
        check_vma=False,
    )
```

profile of v0, /device:TPU:0, one launch (start us, length us, event | category | flops | bytes accessed | tf_op | source)
XLA Modules:
  0.0 530.6 jit_solution(15229958044899135012)
XLA Ops:
  7.2 6.6 %fusion.22 = f32[1024,128]{1,0:T(8,128)} fusion(f32[1024,1024]{1,0:T(8,128)} %param.6, f32[1024,128]{1,0:T(8,128)} %param.8), kind=kOutput, calls=%fused_computation.54 | convolution fusion | flops 1610612736 | bytes 5242880 | tf_op jit(solution)/shard_map/dot_general | solution.py:13
  13.9 58.9 %all-reduce.10.cloned.1.call-done = f32[1024,128]{1,0:T(8,128)} async-done(((f32[1024,128]{1,0:T(8,128)}), f32[1024,128]{1,0:T(8,128)}) %all-reduce.10.cloned.1.call-update) | async-done | bytes 524304 | tf_op jit(solution)/shard_map/psum | solution.py:27
  72.8 5.6 %fusion = f32[1024,128]{0,1:T(8,128)} fusion(f32[1024,1024]{1,0:T(8,128)} %param.6, f32[1024,128]{1,0:T(8,128)S(1)} %copy-done.4, f32[1024,128]{1,0:T(8,128)} %all-reduce.10.cloned.1.call-done), kind=kOutput, calls=%fused_computation.3 | convolution fusion | flops 1610874880 | bytes 5767168 | tf_op jit(solution)/shard_map/dot_general | solution.py:17
  78.4 44.4 %all-reduce.12.cloned.1.call-done = f32[1024,128]{0,1:T(8,128)} async-done(((f32[1024,128]{0,1:T(8,128)}), f32[1024,128]{0,1:T(8,128)}) %all-reduce.12.cloned.1.call-update) | async-done | bytes 524304 | tf_op jit(solution)/shard_map/psum | solution.py:41
  122.9 7.6 %convolution_bitcast_fusion.5 = f32[1024,128]{0,1:T(8,128)} fusion(f32[1024,128]{0,1:T(8,128)} %all-reduce.12.cloned.1.call-done, f32[1024,1024]{1,0:T(8,128)} %param.6), kind=kOutput, calls=%fused_computation.16 | convolution fusion | flops 1610612736 | bytes 5242880 | tf_op jit(solution)/shard_map/dot_general | solution.py:13
  130.5 0.7 multiply_reduce_fusion.6
  131.9 29.7 %reduce-scatter.3.cloned.1.call-done = f32[128,128]{0,1:T(8,128)} async-done(((f32[1024,128]{0,1:T(8,128)}), f32[128,128]{0,1:T(8,128)}) %reduce-scatter.3.cloned.1.call-update) | async-done | bytes 65552 | tf_op jit(solution)/shard_map/reduce_scatter | solution.py:47
  161.6 1.5 multiply_reduce_fusion.8
  163.2 38.2 %all-reduce.1 = (f32[]{:T(128)}, f32[]{:T(128)}) all-reduce(f32[]{:T(128)S(6)} %div.58, f32[]{:T(128)} %multiply_reduce_fusion.8), channel_id=1, replica_groups=mesh['samp'=4,'chrom'=8] {'samp','chrom'}, use_global_device_ids=true, to_apply=%region_3.0 | all-reduce | flops 2 | bytes 16 | tf_op jit(solution)/shard_map/psum | solution.py:54
  202.9 6.4 %convolution_bitcast_fusion.4 = f32[1024,128]{1,0:T(8,128)} fusion(f32[1024,1024]{1,0:T(8,128)} %param.6, f32[1024,128]{0,1:T(8,128)S(1)} %get-tuple-element.13, f32[1024]{0:T(1024)S(1)} %maximum_divide_fusion.1), kind=kOutput, calls=%fused_computation.15 | convolution fusion | flops 1610743808 | bytes 5246976 | tf_op jit(solution)/shard_map/dot_general | solution.py:13
  209.4 57.0 %all-reduce.14.cloned.1.call-done = f32[1024,128]{1,0:T(8,128)} async-done(((f32[1024,128]{1,0:T(8,128)}), f32[1024,128]{1,0:T(8,128)}) %all-reduce.14.cloned.1.call-update) | async-done | bytes 524304 | tf_op jit(solution)/shard_map/psum | solution.py:27
  266.3 5.6 %fusion.1 = f32[1024,128]{0,1:T(8,128)} fusion(f32[1024,1024]{1,0:T(8,128)} %param.6, f32[1024,128]{1,0:T(8,128)S(1)} %copy-done.4, f32[1024,128]{1,0:T(8,128)} %all-reduce.14.cloned.1.call-done), kind=kOutput, calls=%fused_computation.4 | convolution fusion | flops 1610874880 | bytes 5767168 | tf_op jit(solution)/shard_map/dot_general | solution.py:17
  272.0 44.4 %all-reduce.16.cloned.1.call-done = f32[1024,128]{0,1:T(8,128)} async-done(((f32[1024,128]{0,1:T(8,128)}), f32[1024,128]{0,1:T(8,128)}) %all-reduce.16.cloned.1.call-update) | async-done | bytes 524304 | tf_op jit(solution)/shard_map/psum | solution.py:41
  316.4 7.6 %convolution_bitcast_fusion.3 = f32[1024,128]{0,1:T(8,128)} fusion(f32[1024,128]{0,1:T(8,128)} %all-reduce.16.cloned.1.call-done, f32[1024,1024]{1,0:T(8,128)} %param.6), kind=kOutput, calls=%fused_computation.14 | convolution fusion | flops 1610612736 | bytes 5242880 | tf_op jit(solution)/shard_map/dot_general | solution.py:13
  324.1 0.7 multiply_reduce_fusion.4
  325.5 29.7 %reduce-scatter.5.cloned.1.call-done = f32[128,128]{0,1:T(8,128)} async-done(((f32[1024,128]{0,1:T(8,128)}), f32[128,128]{0,1:T(8,128)}) %reduce-scatter.5.cloned.1.call-update) | async-done | bytes 65552 | tf_op jit(solution)/shard_map/reduce_scatter | solution.py:47
  355.1 1.5 multiply_reduce_fusion.7
  356.6 38.2 %all-reduce = (f32[]{:T(128)}, f32[]{:T(128)}) all-reduce(f32[]{:T(128)S(6)} %div.64, f32[]{:T(128)} %multiply_reduce_fusion.7), channel_id=1, replica_groups=mesh['samp'=4,'chrom'=8] {'samp','chrom'}, use_global_device_ids=true, to_apply=%region_11.0 | all-reduce | flops 2 | bytes 16 | tf_op jit(solution)/shard_map/psum | solution.py:54
  396.2 1.3 multiply_reduce_fusion.3
  397.5 7.3 %convolution_bitcast_fusion.2 = f32[1024,128]{0,1:T(8,128)} fusion(f32[1024,1024]{1,0:T(8,128)} %param.6, f32[1024,128]{0,1:T(8,128)S(1)} %get-tuple-element.11, f32[1024]{0:T(1024)S(1)} %maximum_divide_fusion), kind=kOutput, calls=%fused_computation.13 | convolution fusion | flops 1610743808 | bytes 5246976 | tf_op jit(solution)/shard_map/dot_general | solution.py:13
  404.9 2.0 copy.9
  406.9 0.5 multiply_reduce_fusion
  407.4 54.3 %all-reduce.18.cloned.1.call-done = f32[1024,128]{0,1:T(8,128)} async-done(((f32[1024,128]{0,1:T(8,128)}), f32[1024,128]{0,1:T(8,128)}) %all-reduce.18.cloned.1.call-update) | async-done | bytes 524304 | tf_op jit(solution)/shard_map/psum | solution.py:27
  461.7 1.3 sub.51
  463.0 1.0 copy.11
  464.0 6.7 %multiply_reduce_fusion.1 = (f32[128]{0:T(128)S(1)}, bf16[1024,128]{0,1:T(8,128)(2,1)S(1)}) fusion(f32[1024,128]{0,1:T(8,128)S(1)} %sub.51, f32[1024,1024]{1,0:T(8,128)} %param.6, f32[1024,128]{0,1:T(8,128)S(1)} %get-tuple-element.11, f32[1024]{0:T(1024)S(1)} %get-tuple-element.16, f32[1024]{0:T(1024)S(1)} %maximum_divide_fusion), kind=kOutput, calls=%fused_computation.18 | convolution fusion | flops 1611399040 | bytes 5513728 | tf_op jit(solution)/shard_map/dot_general | solution.py:13
  470.7 4.4 multiply_reduce_fusion.2
  475.6 1.3 fusion.3
  476.9 10.2 %all-reduce.2 = (f32[2,128]{1,0:T(2,128)S(1)}, f32[1024]{0:T(1024)S(1)}) all-reduce(f32[2,128]{1,0:T(2,128)S(1)} %pad_maximum_fusion, f32[1024]{0:T(1024)S(1)} %multiply_reduce_fusion), channel_id=1, replica_groups=mesh['samp'=4,'chrom'=8] {'samp'}, use_global_device_ids=true, to_apply=%region_22.0 | all-reduce | flops 1280 | bytes 10240 | tf_op jit(solution)/shard_map/psum | solution.py:81
  487.1 34.3 %all-reduce.20.cloned.1.call-done = f32[1024,128]{0,1:T(8,128)} async-done(((f32[1024,128]{0,1:T(8,128)}), f32[1024,128]{0,1:T(8,128)}) %all-reduce.20.cloned.1.call-update) | async-done | bytes 524304 | tf_op jit(solution)/shard_map/psum | solution.py:81
  521.4 1.4 multiply_divide_fusion
  522.8 1.0 copy.10
  (42 shorter events, 1.3 us)
Async XLA Ops:
  7.2 65.6 %copy-start.4 = (f32[1024,128]{1,0:T(8,128)S(1)}, f32[1024,128]{1,0:T(8,128)}, u32[]{:S(2)}) copy-start(f32[1024,128]{1,0:T(8,128)} %param.7) | copy-start | bytes 1572868
  7.2 65.6 %all-reduce.10.cloned.1.call-start = ((), (), s32[]{:S(2)}) async-start(), calls=%async_computation.2 | async-start | bytes 1048576 | tf_op jit(solution)/shard_map/psum | solution.py:27
  13.8 109.1 %all-reduce.12.cloned.1.call-start = ((), (), s32[]{:S(2)}) async-start(), calls=%async_computation.3 | async-start | bytes 1048576 | tf_op jit(solution)/shard_map/psum | solution.py:41
  78.4 84.7 %copy-start.5 = (f32[1024,128]{1,0:T(8,128)S(1)}, f32[1024,128]{1,0:T(8,128)}, u32[]{:S(2)}) copy-start(f32[1024,128]{1,0:T(8,128)} %param.8) | copy-start | bytes 1572868
  78.4 83.2 %reduce-scatter.3.cloned.1.call-start = ((), (), s32[]{:S(2)}) async-start(), calls=%async_computation.4 | async-start | bytes 589824 | tf_op jit(solution)/shard_map/reduce_scatter | solution.py:47
  122.9 7.7 %copy-start.3 = (f32[1024,128]{0,1:T(8,128)S(1)}, f32[1024,128]{0,1:T(8,128)}, u32[]{:S(2)}) copy-start(f32[1024,128]{0,1:T(8,128)} %all-reduce.12.cloned.1.call-done) | copy-start | bytes 1572868
  130.5 135.9 %all-reduce.14.cloned.1.call-start = ((), (), s32[]{:S(2)}) async-start(), calls=%async_computation.5 | async-start | bytes 1048576 | tf_op jit(solution)/shard_map/psum | solution.py:27
  209.3 107.1 %all-reduce.16.cloned.1.call-start = ((), (), s32[]{:S(2)}) async-start(), calls=%async_computation.6 | async-start | bytes 1048576 | tf_op jit(solution)/shard_map/psum | solution.py:41
  271.9 84.7 %copy-start.6 = (s32[1024]{0:T(1024)S(1)}, s32[1024]{0:T(1024)}, u32[]{:S(2)}) copy-start(s32[1024]{0:T(1024)} %param.9) | copy-start | bytes 12292
  271.9 83.2 %reduce-scatter.5.cloned.1.call-start = ((), (), s32[]{:S(2)}) async-start(), calls=%async_computation.7 | async-start | bytes 589824 | tf_op jit(solution)/shard_map/reduce_scatter | solution.py:47
  316.4 7.7 %copy-start.2 = (f32[1024,128]{0,1:T(8,128)S(1)}, f32[1024,128]{0,1:T(8,128)}, u32[]{:S(2)}) copy-start(f32[1024,128]{0,1:T(8,128)} %all-reduce.16.cloned.1.call-done) | copy-start | bytes 1572868
  324.0 80.9 %copy-start.7 = (s32[1024]{0:T(1024)S(1)}, s32[1024]{0:T(1024)}, u32[]{:S(2)}) copy-start(s32[1024]{0:T(1024)} %param.11) | copy-start | bytes 12292
  324.0 137.7 %all-reduce.18.cloned.1.call-start = ((), (), s32[]{:S(2)}) async-start(), calls=%async_computation.8 | async-start | bytes 1048576 | tf_op jit(solution)/shard_map/psum | solution.py:27
  396.1 10.8 %copy-start.1 = (bf16[1024,1024]{1,0:T(8,128)(2,1)S(1)}, bf16[1024,1024]{1,0:T(8,128)(2,1)}, u32[]{:S(2)}) copy-start(bf16[1024,1024]{1,0:T(8,128)(2,1)} %param.10) | copy-start | bytes 6291460
  404.8 116.6 %all-reduce.20.cloned.1.call-start = ((), (), s32[]{:S(2)}) async-start(), calls=%async_computation.9 | async-start | bytes 1048576 | tf_op jit(solution)/shard_map/psum | solution.py:81
  464.0 6.7 %copy-start = (f32[1024,1024]{1,0:T(8,128)S(1)}, f32[1024,1024]{1,0:T(8,128)}, u32[]{:S(2)}) copy-start(f32[1024,1024]{1,0:T(8,128)} %param.6) | copy-start | bytes 12582916
Sparse Core Ops, SparseCore 0:
  13.9 58.8 all-reduce.9
  78.5 44.3 all-reduce.11
  130.6 30.9 reduce-scatter.2
  209.4 56.8 all-reduce.13
  272.1 44.3 all-reduce.15
  324.1 30.9 reduce-scatter.4
  404.9 56.7 all-reduce.17
  477.0 44.3 all-reduce.19
where the time goes:
time: 531 us
  waiting for transfers between devices  353 us (66%)
  blocking collectives  86.6 us (16%)
  matrix products  59.3 us (11%)
  between operations  18.2 us (3%)
  other arithmetic  8.97 us (2%)
    psum x3, waiting for transfers between devices, total_prediction(): return lax.psum(partial_value, 'chrom')  170 us
    psum x2, waiting for transfers between devices, body(): gradient = lax.psum(inner_rows(dosages, residual_now) / total_rows, 'samp')  88.8 us
    psum x2, blocking collectives, body(): grad_sq, image_sq = lax.psum((grad_sq, image_sq), ('samp', 'chrom'))  76.4 us
    reduce_scatter x2, waiting for transfers between devices, body(): lax.psum_scatter(image_rows(jnp.int32(0), rows_dev // lax.axis_size('chro...  59.3 us
    dot_general x7, matrix products, matmul(): jnp.dot(left, right, precision=lax.Precision.HIGHEST, preferred_element_t...  46.5 us
    psum x1, waiting for transfers between devices, body(): lax.psum((picked, tested_sq, jnp.stack(loco_list)), 'samp')  34.3 us
    dot_general x2, matrix products, inner_rows(): lax.dot_general(left, right, (((0,), (0,)), ((), ())), precision=lax.Prec...  11.1 us
  transfers between devices with their start and end apart: 8, of which 8 were waited for; matrix products, arithmetic and copies ran while one was open for 1% of the time, Pallas kernels for 0%

commit v1 on v0

v1 whole, which is shorter than its diff:
```python
import functools
import math

import jax
import jax.numpy as jnp
from jax import lax
from jax.experimental import pallas as pl
from jax.experimental.pallas import tpu as pltpu
from jax.sharding import PartitionSpec as P

GPD = 2
ITERS = 2
STATS = 16
VMEM_LIMIT = 24 * 1024 * 1024


def swap(value, axis, bits):
    size = lax.axis_size(axis)
    return lax.ppermute(value, axis, [(i, i ^ bits) for i in range(size)])


def split(value):
    high = value.astype(jnp.bfloat16)
    low = (value - high.astype(jnp.float32)).astype(jnp.bfloat16)
    return high, low


def pack(value):
    return jnp.concatenate(split(value), axis=1)


def wide_dot(high, low, packed):
    total = jnp.dot(high, packed, preferred_element_type=jnp.float32)
    total = total + jnp.dot(low, packed, preferred_element_type=jnp.float32)
    traits = packed.shape[1] // 2
    return total[:, :traits] + total[:, traits:]


def whole():
    return pl.BlockSpec(memory_space=pltpu.VMEM)


def shape(dims, dtype=jnp.float32):
    return jax.ShapeDtypeStruct(dims, dtype)


def call(kernel, outs, scratch=(), flops=0, moved=0):
    def run(*operands):
        return pl.pallas_call(
            kernel,
            out_shape=outs,
            in_specs=[whole()] * len(operands),
            out_specs=jax.tree.map(lambda _: whole(), outs),
            scratch_shapes=list(scratch),
            compiler_params=pltpu.CompilerParams(vmem_limit_bytes=VMEM_LIMIT),
            cost_estimate=pl.CostEstimate(flops=flops, bytes_accessed=moved, transcendentals=0),
        )(*operands)

    return run


def halves(parts, bits):
    me = lax.axis_index("chrom")
    place, core = me // 2, me % 2
    half = parts.shape[0]
    return [parts.at[place ^ k, core ^ bits] for k in range(half)]


def store_prediction(high_ref, low_ref, packed, give_ref, keep_ref):
    for bits, out in ((1, give_ref), (0, keep_ref)):
        high = jnp.concatenate([block[...] for block in halves(high_ref, bits)])
        low = jnp.concatenate([block[...] for block in halves(low_ref, bits)])
        out[...] = wide_dot(high, low, packed).reshape(out.shape)


def first_kernel(dosage_ref, coef_ref, high_ref, low_ref, give_ref, keep_ref, packed_ref):
    step = pl.program_id(0)
    place = lax.axis_index("chrom") // 2

    @pl.when(step == 0)
    def _():
        packed_ref[...] = pack(coef_ref[...])

    highs, lows = [], []
    for k in range(dosage_ref.shape[0]):
        high, low = split(dosage_ref[place ^ k, 0])
        high_ref[place ^ k, 0] = high
        low_ref[place ^ k, 0] = low
        highs.append(high)
        lows.append(low)
    total = wide_dot(jnp.concatenate(highs), jnp.concatenate(lows), packed_ref[...])

    @pl.when(step == 0)
    def _():
        give_ref[...] = total.reshape(give_ref.shape)

    @pl.when(step == 1)
    def _():
        keep_ref[...] = total.reshape(keep_ref.shape)


def first_prediction(dosages, coefficients):
    half, _, block, cols = dosages.shape
    traits = coefficients.shape[1]

    def rows(step, core_ref):
        return (0, 1 - step + core_ref[0] * (2 * step - 1), 0, 0)

    core = (lax.axis_index("chrom") % 2).astype(jnp.int32).reshape(1)
    part = pl.BlockSpec((half, 1, block, cols), rows)
    fixed = pl.BlockSpec((half, block, traits), lambda step, core_ref: (0, 0, 0))

    def kernel(core_ref, *refs):
        first_kernel(*refs)

    return pl.pallas_call(
        kernel,
        grid_spec=pltpu.PrefetchScalarGridSpec(
            num_scalar_prefetch=1,
            grid=(2,),
            in_specs=[part, pl.BlockSpec(coefficients.shape, lambda step, core_ref: (0, 0))],
            out_specs=[part, part, fixed, fixed],
            scratch_shapes=[pltpu.VMEM((cols, 2 * traits), jnp.bfloat16)],
        ),
        out_shape=[
            shape(dosages.shape, jnp.bfloat16),
            shape(dosages.shape, jnp.bfloat16),
            shape((half, block, traits)),
            shape((half, block, traits)),
        ],
        compiler_params=pltpu.CompilerParams(vmem_limit_bytes=VMEM_LIMIT),
    )(core, dosages, coefficients)


def turn_kernel(high_ref, low_ref, high_out, low_out):
    high_out[...] = high_ref[...].T
    low_out[...] = low_ref[...].T


def turned(high, low, blocks):
    rows, cols = high.shape
    width = cols // blocks
    return pl.pallas_call(
        turn_kernel,
        grid=(blocks,),
        in_specs=[pl.BlockSpec((rows, width), lambda step: (0, step))] * 2,
        out_specs=[pl.BlockSpec((width, rows), lambda step: (step, 0))] * 2,
        out_shape=[shape((cols, rows), jnp.bfloat16)] * 2,
        compiler_params=pltpu.CompilerParams(vmem_limit_bytes=VMEM_LIMIT),
        cost_estimate=pl.CostEstimate(flops=0, bytes_accessed=16 * rows * cols, transcendentals=0),
    )(high, low)


def tested_kernel(tested_ref, turned_ref, square_ref):
    value = tested_ref[...]
    turned_ref[...] = value.T
    wide = value.astype(jnp.float32)
    square_ref[0] = jnp.sum(wide * wide, axis=0).reshape(square_ref.shape[1:])


def tested_parts(tested, blocks):
    rows, cols = tested.shape
    width = cols // blocks
    return pl.pallas_call(
        tested_kernel,
        grid=(blocks,),
        in_specs=[pl.BlockSpec((rows, width), lambda step: (0, step))],
        out_specs=[
            pl.BlockSpec((width, rows), lambda step: (step, 0)),
            pl.BlockSpec((1, width // 128, 128), lambda step: (step, 0, 0)),
        ],
        out_shape=[shape((cols, rows), jnp.bfloat16), shape((blocks, width // 128, 128))],
        compiler_params=pltpu.CompilerParams(vmem_limit_bytes=VMEM_LIMIT),
        cost_estimate=pl.CostEstimate(flops=0, bytes_accessed=8 * rows * cols, transcendentals=0),
    )(tested)


def place_rows(pieces, store):
    me = lax.axis_index("chrom")
    for bits, piece in pieces.items():
        store((me ^ bits) * piece.shape[0], piece)


def residual_order(size):
    return list(range(size))


def grad_kernel(count, *refs):
    pieces, (high_ref, low_ref), outs, packed_ref = (
        refs[:count],
        refs[count : count + 2],
        refs[count + 2 : -1],
        refs[-1],
    )
    me, samp = lax.axis_index("chrom"), lax.axis_index("samp")
    block = pieces[0].shape[0]
    for bits, piece in enumerate(pieces):
        start = pl.multiple_of((me ^ bits) * block, block)
        packed_ref[pl.ds(start, block)] = pack(piece[...])
    packed = packed_ref[...]
    for bits in reversed(range(len(outs))):
        outs[bits][...] = wide_dot(high_ref[samp ^ bits], low_ref[samp ^ bits], packed)


def image_kernel(count, *refs):
    pieces = refs[:count]
    high_ref, low_ref, grad_ref, give_ref, keep_ref, packed_ref = refs[count:]
    samp = lax.axis_index("samp")
    block = pieces[0].shape[0]
    for bits, piece in enumerate(pieces):
        start = pl.multiple_of((samp ^ bits) * block, block)
        value = piece[...]
        grad_ref[pl.ds(start, block)] = value
        packed_ref[pl.ds(start, block)] = pack(value)
    store_prediction(high_ref, low_ref, packed_ref[...], give_ref, keep_ref)


def prox_kernel(total_rows, coef_ref, grad_ref, sums_ref, high_ref, low_ref, new_ref, give_ref, keep_ref):
    sums = jnp.sum(sums_ref[...], axis=0)
    grad_sq = jnp.sum(sums[0:1], axis=1, keepdims=True)
    image_sq = jnp.sum(sums[1:2], axis=1, keepdims=True)
    step_size = grad_sq / (image_sq / total_rows + 1e-06)
    penalty = 1.5 * math.sqrt(coef_ref.shape[1] / total_rows)
    moved = coef_ref[...] + step_size * grad_ref[...]
    length = jnp.sqrt(jnp.sum(moved * moved, axis=1, keepdims=True))
    cut = step_size * penalty
    new = moved * (jnp.maximum(length - cut, 0.0) / jnp.maximum(length, cut))
    new_ref[...] = new
    store_prediction(high_ref, low_ref, pack(new), give_ref, keep_ref)


def own_kernel(coef_ref, mask_ref, high_ref, low_ref, *outs):
    high, low = high_ref[...], low_ref[...]
    coef = coef_ref[...]
    mask = mask_ref[...]
    for which, out in enumerate(outs):
        out[...] = wide_dot(high, low, pack(jnp.where(mask == which, coef, 0.0)))


def loco_kernel(count, *refs):
    pieces = refs[:count]
    own_refs = refs[count : count + GPD]
    tested_ref, square_ref, pick_ref, residual_ref = refs[count + GPD : count + GPD + 4]
    outs, loco_ref = refs[count + GPD + 4 : -1], refs[-1]
    me, samp = lax.axis_index("chrom"), lax.axis_index("samp")
    block, traits = pieces[0].shape
    squares = [jnp.zeros((1, traits), jnp.float32)] * GPD
    for bits, piece in enumerate(pieces):
        rows = pl.ds(pl.multiple_of((me ^ bits) * block, block), block)
        value = piece[...]
        residual_ref[rows] = value
        for which in range(GPD):
            loco = value + own_refs[which][rows]
            squares[which] = squares[which] + jnp.sum(loco * loco, axis=0, keepdims=True)
            loco_ref[rows, which * traits : (which + 1) * traits] = loco.astype(jnp.bfloat16)
    loco = loco_ref[...]
    for bits in reversed(range(len(outs))):
        other, out = samp ^ bits, outs[bits]
        cols = tested_ref.shape[1]
        products = jnp.dot(tested_ref[other], loco, preferred_element_type=jnp.float32)
        pick = pick_ref[other]
        chosen = products[:, :traits]
        for which in range(1, GPD):
            chosen = jnp.where(pick == which, products[:, which * traits : (which + 1) * traits], chosen)
        out[0:cols] = chosen
        out[cols : cols + STATS] = jnp.zeros((STATS, traits), jnp.float32)
        for which in range(GPD):
            out[cols + which : cols + which + 1] = squares[which]
        out[cols + 8 : cols + 8 + square_ref.shape[1]] = square_ref[other]


def score_kernel(total_rows, pick_ref, *refs):
    pieces, out = refs[:-1], refs[-1]
    total = pieces[0][...]
    for piece in pieces[1:]:
        total = total + piece[...]
    cols, traits = out.shape
    pick = pick_ref[lax.axis_index("samp")]
    loco_sq = jnp.broadcast_to(total[cols : cols + 1], (cols, traits))
    for which in range(1, GPD):
        loco_sq = jnp.where(pick == which, total[cols + which : cols + which + 1], loco_sq)
    diagonal = lax.broadcasted_iota(jnp.int32, (128, 128), 0) == lax.broadcasted_iota(jnp.int32, (128, 128), 1)
    columns = []
    for row in range(cols // 128):
        squares = total[cols + 8 + row : cols + 9 + row, :128]
        columns.append(jnp.sum(jnp.where(diagonal, squares, 0.0), axis=1, keepdims=True))
    tested_sq = jnp.concatenate(columns)
    denom = math.sqrt(total_rows) * jnp.sqrt((tested_sq / total_rows + 1e-06) * (loco_sq / total_rows + 1e-06))
    out[...] = total[:cols] / denom


def place_kernel(*refs):
    pieces, out = refs[:-1], refs[-1]
    samp = lax.axis_index("samp")
    block = pieces[0].shape[0]
    for bits, piece in enumerate(pieces):
        out[pl.ds(pl.multiple_of((samp ^ bits) * block, block), block)] = piece[...]


def chrom_scatter(give, keep):
    got = swap(give, "chrom", 1)
    count = keep.shape[0]
    sums = [keep[k] + got[k] for k in range(count)]
    total = sums[0]
    for block in [swap(sums[k], "chrom", 2 * k) for k in reversed(range(1, count))]:
        total = total + block
    return total


def chrom_gather(own):
    size = lax.axis_size("chrom")
    mine = [own] + [swap(own, "chrom", 2 * k) for k in range(1, size // 2)]
    other = [swap(block, "chrom", 1) for block in mine]
    return [block for pair in zip(mine, other) for block in pair]


def samp_swaps(pieces):
    return [swap(pieces[k], "samp", k) for k in reversed(range(1, len(pieces)))]


def body(dosages, traits, start_coef, groups, tested, owners):
    n_samp, n_chrom = lax.axis_size("samp"), lax.axis_size("chrom")
    rows, cols = dosages.shape
    tests, n_traits = tested.shape[1], traits.shape[1]
    total_rows = rows * n_samp
    me, samp = lax.axis_index("chrom"), lax.axis_index("samp")
    half, block, width, test_width = n_chrom // 2, rows // n_chrom, cols // n_samp, tests // n_samp
    flops = 2 * rows * cols * 4 * n_traits
    moved = 4 * rows * cols
    half_shape = shape((half, block, n_traits))
    packed = pltpu.VMEM((cols, 2 * n_traits), jnp.bfloat16)

    mask = jnp.broadcast_to((groups - me * GPD)[:, None], (cols, n_traits))
    pick = jnp.broadcast_to((owners - me * GPD)[:, None], (tests, n_traits)).reshape(n_samp, test_width, n_traits)
    own_traits = lax.dynamic_slice_in_dim(traits, me * block, block, 0)

    coefficients = start_coef
    high4, low4, give, keep = first_prediction(dosages.reshape(half, 2, block, cols), coefficients)
    high, low = high4.reshape(rows, cols), low4.reshape(rows, cols)
    turn_high, turn_low = turned(high, low, n_samp)
    turn_high, turn_low = (part.reshape(n_samp, width, rows) for part in (turn_high, turn_low))
    turn_tested, tested_sq = tested_parts(tested, n_samp)
    turn_tested = turn_tested.reshape(n_samp, test_width, rows)

    grad_call = call(
        functools.partial(grad_kernel, n_chrom),
        [shape((width, n_traits))] * n_samp,
        [pltpu.VMEM((rows, 2 * n_traits), jnp.bfloat16)],
        flops,
        moved,
    )
    image_call = call(
        functools.partial(image_kernel, n_samp),
        [shape((cols, n_traits)), half_shape, half_shape],
        [packed],
        flops,
        moved,
    )
    prox_call = call(
        functools.partial(prox_kernel, total_rows),
        [shape((cols, n_traits)), half_shape, half_shape],
        (),
        flops,
        moved,
    )
    for iteration in range(ITERS):
        pieces = chrom_gather(own_traits - chrom_scatter(give, keep))
        pieces = grad_call(*pieces, turn_high, turn_low)
        own_grad = pieces[0]
        for piece in samp_swaps(pieces):
            own_grad = own_grad + piece
        own_grad = own_grad / total_rows
        pieces = [own_grad] + [swap(own_grad, "samp", k) for k in range(1, n_samp)]
        gradient, give, keep = image_call(*pieces, high4, low4)
        image = chrom_scatter(give, keep)
        sums = jnp.stack([jnp.sum(own_grad * own_grad, axis=0), jnp.sum(image * image, axis=0)])
        size = n_samp * n_chrom
        sums = lax.all_to_all(jnp.broadcast_to(sums, (size,) + sums.shape), ("samp", "chrom"), 0, 0)
        coefficients, give, keep = prox_call(coefficients, gradient, sums, high4, low4)
    own_parts = call(own_kernel, [shape((rows, n_traits))] * GPD, (), GPD * flops, moved)(
        coefficients, mask, high, low
    )
    pieces = chrom_gather(own_traits - chrom_scatter(give, keep))
    residual, *pieces = call(
        functools.partial(loco_kernel, n_chrom),
        [shape((rows, n_traits))] + [shape((test_width + STATS, n_traits))] * n_samp,
        [pltpu.VMEM((rows, GPD * n_traits), jnp.bfloat16)],
        flops,
        moved,
    )(*pieces, *own_parts, turn_tested, tested_sq, pick)
    own_scores = call(functools.partial(score_kernel, total_rows), shape((test_width, n_traits)))(
        pick, pieces[0], *samp_swaps(pieces)
    )
    scores = call(place_kernel, shape((tests, n_traits)))(
        own_scores, *[swap(own_scores, "samp", k) for k in range(1, n_samp)]
    )
    return (scores, residual)


def solution(mesh):
    placed = (
        P("samp", "chrom"),
        P("samp", None),
        P("chrom", None),
        P("chrom"),
        P("samp", "chrom"),
        P("chrom"),
    )
    return jax.shard_map(
        body,
        mesh=mesh,
        in_specs=placed,
        out_specs=(P("chrom", None), P("samp", None)),
        check_vma=False,
    )
```

time: 531 us -> 185 us (0.35)
  waiting for transfers between devices: 353 us -> 73 us
  blocking collectives: 86.6 us -> 20.4 us
  starting transfers between devices: 0.33 us -> 60.3 us
  matrix products: 59.3 us -> 0 us
  Pallas kernels: 0 us -> 19.3 us
  between operations: 18.2 us -> 0.97 us
  other arithmetic: 8.97 us -> 2.93 us
    psum x6 -> x0, waiting for transfers between devices: 293 us -> none  [the longest x3 170 us: total_prediction(): return lax.psum(partial_value, 'chrom')]
    psum x3 -> x0, blocking collectives: 86.6 us -> none  [the longest x2 76.4 us: body(): grad_sq, image_sq = lax.psum((grad_sq, image_sq), ('samp', 'chrom'))]
    ppermute x0 -> x59, waiting for transfers between devices: none -> 73 us  [swap(): return lax.ppermute(value, axis, [(i, i ^ bits) for i in range(size)])]
    ppermute x0 -> x59, starting transfers between devices: none -> 60.3 us  [swap(): return lax.ppermute(value, axis, [(i, i ^ bits) for i in range(size)])]
    dot_general x11 -> x0, matrix products: 59.3 us -> none  [the longest x7 46.5 us: matmul(): jnp.dot(left, right, precision=lax.Precision.HIGHEST, preferred_element_t...]
    reduce_scatter x2 -> x0, waiting for transfers between devices: 59.3 us -> none  [body(): lax.psum_scatter(image_rows(jnp.int32(0), rows_dev // lax.axis_size('chro...]
    all_to_all x0 -> x2, blocking collectives: none -> 20.4 us  [body(): lax.all_to_all(jnp.broadcast_to(sums, (size,) + sums.shape), ('samp', 'ch...]
    pallas_call x0 -> x13, Pallas kernels: none -> 19.3 us  [the longest x10 13.7 us: run(): pl.pallas_call(kernel, out_shape=outs, in_specs=[whole()] * len(operands)...]
  transfers between devices with their start and end apart: 8 -> 59, of which waited for: 8 -> 37; matrix products, arithmetic and copies ran while one was open for 1% -> 0% of each run, Pallas kernels for 0% -> 3%
where the time goes in v1:
time: 185 us
  waiting for transfers between devices  73 us (39%)
  starting transfers between devices  60.3 us (33%)
  blocking collectives  20.4 us (11%)
  Pallas kernels  19.3 us (10%)
  local copies, waits for them, and re-layouts  8.14 us (4%)
  other arithmetic  2.93 us (2%)
    ppermute x59, waiting for transfers between devices, swap(): return lax.ppermute(value, axis, [(i, i ^ bits) for i in range(size)])  73 us
    ppermute x59, starting transfers between devices, swap(): return lax.ppermute(value, axis, [(i, i ^ bits) for i in range(size)])  60.3 us
    all_to_all x2, blocking collectives, body(): lax.all_to_all(jnp.broadcast_to(sums, (size,) + sums.shape), ('samp', 'ch...  20.4 us
    pallas_call x10, Pallas kernels, run(): pl.pallas_call(kernel, out_shape=outs, in_specs=[whole()] * len(operands)...  13.7 us
    unnamed x20, local copies, waits for them, and re-layouts  7.72 us
  transfers between devices with their start and end apart: 59, of which 37 were waited for; matrix products, arithmetic and copies ran while one was open for 0% of the time, Pallas kernels for 3%

profile of v1, /device:TPU:0, one launch (start us, length us, event | category | flops | bytes accessed | tf_op | source)
XLA Modules:
  0.0 185.0 jit_solution(304027377047960806)
XLA Ops:
  0.6 2.2 %copy-done.4 = f32[1024,1024]{1,0:T(8,128)S(1)} copy-done((f32[1024,1024]{1,0:T(8,128)S(1)}, f32[1024,1024]{1,0:T(8,128)}, u32[]{:S(2)}) %copy-start.4) | copy-done | bytes 4194328
  3.9 2.5 %shard_map.77 = (bf16[4,2,128,1024]{3,2,1,0:T(8,128)(2,1)S(1)}, bf16[4,2,128,1024]{3,2,1,0:T(8,128)(2,1)S(1)}, f32[4,128,128]{2,1,0:T(8,128)S(1)}, f32[4,128,128]{2,1,0:T(8,128)S(1)}) custom-call(s32[1]{0:T(128)} %bitcast.core_ref, f32[4,2,128,1024]{3,2,1,0:T(8,128)S(1)} %bitcast.103, f32[1024,128]{1,0:T(8,128)S(1)} %copy-done.5), custom_call_target="tpu_custom_call" | custom-call | tf_op jit(solution)/shard_map/pallas_call | solution.py:116
  9.3 5.0 %collective-permute-start.1 = (f32[128,128]{1,0:T(8,128)S(1)}, f32[128,128]{1,0:T(8,128)S(1)}, u32[]{:S(2)}, u32[]{:S(2)}) collective-permute-start(f32[128,128]{1,0:T(8,128)S(1)} %get-tuple-element.88), channel_id=1, source_target_pairs={{0,6},{1,7},{2,4},{3,5},{4,2},{5,3},{6,0},{7,1},{8,14},{9,15},{10,... | collective-permute-start | bytes 196616 | tf_op jit(solution)/shard_map/ppermute | solution.py:19
  15.0 2.0 %collective-permute-done.1 = f32[128,128]{1,0:T(8,128)S(1)} collective-permute-done((f32[128,128]{1,0:T(8,128)S(1)}, f32[128,128]{1,0:T(8,128)S(1)}, u32[]{:S(2)}, u32[]{:S(2)}) %collective-permute-start.1) | collective-permute-done | bytes 65568 | tf_op jit(solution)/shard_map/ppermute | solution.py:19
  17.0 3.3 %collective-permute-done.2 = f32[128,128]{1,0:T(8,128)S(1)} collective-permute-done((f32[128,128]{1,0:T(8,128)S(1)}, f32[128,128]{1,0:T(8,128)S(1)}, u32[]{:S(2)}, u32[]{:S(2)}) %collective-permute-start.2) | collective-permute-done | bytes 65568 | tf_op jit(solution)/shard_map/ppermute | solution.py:19
  21.1 2.5 %collective-permute-start.9 = (f32[128,128]{1,0:T(8,128)S(1)}, f32[128,128]{1,0:T(8,128)S(1)}, u32[]{:S(2)}, u32[]{:S(2)}) collective-permute-start(f32[128,128]{1,0:T(8,128)S(1)} %fusion.41.refs_0_), channel_id=1, source_target_pairs={{0,6},{1,7},{2,4},{3,5},{4,2},{5,3},{6,0},{7,1},{8,14},{9,15},{10,... | collective-permute-start | bytes 196616 | tf_op jit(solution)/shard_map/ppermute | solution.py:19
  25.6 1.9 %collective-permute-done.9.refs_6_ = f32[128,128]{1,0:T(8,128)S(1)} collective-permute-done((f32[128,128]{1,0:T(8,128)S(1)}, f32[128,128]{1,0:T(8,128)S(1)}, u32[]{:S(2)}, u32[]{:S(2)}) %collective-permute-start.9) | collective-permute-done | bytes 65568 | tf_op jit(solution)/shard_map/ppermute | solution.py:19
  31.1 2.0 %shard_map.78 = (bf16[1024,1024]{1,0:T(8,128)(2,1)S(1)}, bf16[1024,1024]{1,0:T(8,128)(2,1)S(1)}) custom-call(bf16[1024,1024]{1,0:T(8,128)(2,1)S(1)} %bitcast.95, bf16[1024,1024]{1,0:T(8,128)(2,1)S(1)} %bitcast.97), custom_call_target="tpu_custom_call" | custom-call | bytes 16777216 | tf_op jit(solution)/shard_map/pallas_call | solution.py:143
  34.4 2.5 %collective-permute-start.11 = (f32[256,128]{1,0:T(8,128)S(1)}, f32[256,128]{1,0:T(8,128)S(1)}, u32[]{:S(2)}, u32[]{:S(2)}) collective-permute-start(f32[256,128]{1,0:T(8,128)S(1)} %get-tuple-element.44), channel_id=1, source_target_pairs={{0,24},{8,16},{16,8},{24,0},{1,25},{9,17},{17,9},{25,1},{2,26},{10... | collective-permute-start | bytes 393224 | tf_op jit(solution)/shard_map/ppermute | solution.py:19
  38.0 3.6 %collective-permute-done.11 = f32[256,128]{1,0:T(8,128)S(1)} collective-permute-done((f32[256,128]{1,0:T(8,128)S(1)}, f32[256,128]{1,0:T(8,128)S(1)}, u32[]{:S(2)}, u32[]{:S(2)}) %collective-permute-start.11) | collective-permute-done | bytes 131104 | tf_op jit(solution)/shard_map/ppermute | solution.py:19
  41.6 2.5 %collective-permute-done.12 = f32[256,128]{1,0:T(8,128)S(1)} collective-permute-done((f32[256,128]{1,0:T(8,128)S(1)}, f32[256,128]{1,0:T(8,128)S(1)}, u32[]{:S(2)}, u32[]{:S(2)}) %collective-permute-start.12) | collective-permute-done | bytes 131104 | tf_op jit(solution)/shard_map/ppermute | solution.py:19
  47.8 2.2 %collective-permute-done.14.refs_1_ = f32[256,128]{1,0:T(8,128)S(1)} collective-permute-done((f32[256,128]{1,0:T(8,128)S(1)}, f32[256,128]{1,0:T(8,128)S(1)}, u32[]{:S(2)}, u32[]{:S(2)}) %collective-permute-start.14) | collective-permute-done | bytes 131104 | tf_op jit(solution)/shard_map/ppermute | solution.py:19
  50.0 3.6 %collective-permute-done.15.refs_2_ = f32[256,128]{1,0:T(8,128)S(1)} collective-permute-done((f32[256,128]{1,0:T(8,128)S(1)}, f32[256,128]{1,0:T(8,128)S(1)}, u32[]{:S(2)}, u32[]{:S(2)}) %collective-permute-start.15) | collective-permute-done | bytes 131104 | tf_op jit(solution)/shard_map/ppermute | solution.py:19
  61.2 2.4 %collective-permute-done.18 = f32[128,128]{1,0:T(8,128)S(1)} collective-permute-done((f32[128,128]{1,0:T(8,128)S(1)}, f32[128,128]{1,0:T(8,128)S(1)}, u32[]{:S(2)}, u32[]{:S(2)}) %collective-permute-start.18) | collective-permute-done | bytes 65568 | tf_op jit(solution)/shard_map/ppermute | solution.py:19
  63.6 2.5 %collective-permute-done.19 = f32[128,128]{1,0:T(8,128)S(1)} collective-permute-done((f32[128,128]{1,0:T(8,128)S(1)}, f32[128,128]{1,0:T(8,128)S(1)}, u32[]{:S(2)}, u32[]{:S(2)}) %collective-permute-start.19) | collective-permute-done | bytes 65568 | tf_op jit(solution)/shard_map/ppermute | solution.py:19
  66.1 9.9 %all_to_all.10.sums_ref = f32[32,2,128]{2,1,0:T(2,128)S(1)} all-to-all(f32[32,2,128]{2,1,0:T(2,128)S(1)} %broadcast_in_dim.22), channel_id=1, replica_groups=mesh['samp'=4,'chrom'=8] {'samp','chrom'}, dimensions={0} | all-to-all | bytes 65536 | tf_op jit(solution)/shard_map/all_to_all | solution.py:378
  81.5 2.4 %collective-permute-start.24 = (f32[128,128]{1,0:T(8,128)S(1)}, f32[128,128]{1,0:T(8,128)S(1)}, u32[]{:S(2)}, u32[]{:S(2)}) collective-permute-start(f32[128,128]{1,0:T(8,128)S(1)} %get-tuple-element.83), channel_id=1, source_target_pairs={{0,2},{1,3},{2,0},{3,1},{4,6},{5,7},{6,4},{7,5},{8,10},{9,11},{10,... | collective-permute-start | bytes 196616 | tf_op jit(solution)/shard_map/ppermute | solution.py:19
  83.9 2.4 %collective-permute-done.22 = f32[128,128]{1,0:T(8,128)S(1)} collective-permute-done((f32[128,128]{1,0:T(8,128)S(1)}, f32[128,128]{1,0:T(8,128)S(1)}, u32[]{:S(2)}, u32[]{:S(2)}) %collective-permute-start.22) | collective-permute-done | bytes 65568 | tf_op jit(solution)/shard_map/ppermute | solution.py:19
  90.8 2.4 %collective-permute-start.30 = (f32[128,128]{1,0:T(8,128)S(1)}, f32[128,128]{1,0:T(8,128)S(1)}, u32[]{:S(2)}, u32[]{:S(2)}) collective-permute-start(f32[128,128]{1,0:T(8,128)S(1)} %fusion.24.refs_0_), channel_id=1, source_target_pairs={{0,6},{1,7},{2,4},{3,5},{4,2},{5,3},{6,0},{7,1},{8,14},{9,15},{10,... | collective-permute-start | bytes 196616 | tf_op jit(solution)/shard_map/ppermute | solution.py:19
  93.8 2.4 %collective-permute-done.28.refs_4_ = f32[128,128]{1,0:T(8,128)S(1)} collective-permute-done((f32[128,128]{1,0:T(8,128)S(1)}, f32[128,128]{1,0:T(8,128)S(1)}, u32[]{:S(2)}, u32[]{:S(2)}) %collective-permute-start.28) | collective-permute-done | bytes 65568 | tf_op jit(solution)/shard_map/ppermute | solution.py:19
  103.1 3.8 %collective-permute-done.32 = f32[256,128]{1,0:T(8,128)S(1)} collective-permute-done((f32[256,128]{1,0:T(8,128)S(1)}, f32[256,128]{1,0:T(8,128)S(1)}, u32[]{:S(2)}, u32[]{:S(2)}) %collective-permute-start.32) | collective-permute-done | bytes 131104 | tf_op jit(solution)/shard_map/ppermute | solution.py:19
  113.7 3.8 %collective-permute-done.36.refs_2_ = f32[256,128]{1,0:T(8,128)S(1)} collective-permute-done((f32[256,128]{1,0:T(8,128)S(1)}, f32[256,128]{1,0:T(8,128)S(1)}, u32[]{:S(2)}, u32[]{:S(2)}) %collective-permute-start.36) | collective-permute-done | bytes 131104 | tf_op jit(solution)/shard_map/ppermute | solution.py:19
  120.5 2.5 %collective-permute-start.39 = (f32[128,128]{1,0:T(8,128)S(1)}, f32[128,128]{1,0:T(8,128)S(1)}, u32[]{:S(2)}, u32[]{:S(2)}) collective-permute-start(f32[128,128]{1,0:T(8,128)S(1)} %get-tuple-element.79), channel_id=1, source_target_pairs={{0,6},{1,7},{2,4},{3,5},{4,2},{5,3},{6,0},{7,1},{8,14},{9,15},{10,... | collective-permute-start | bytes 196616 | tf_op jit(solution)/shard_map/ppermute | solution.py:19
  125.0 2.4 %collective-permute-done.39 = f32[128,128]{1,0:T(8,128)S(1)} collective-permute-done((f32[128,128]{1,0:T(8,128)S(1)}, f32[128,128]{1,0:T(8,128)S(1)}, u32[]{:S(2)}, u32[]{:S(2)}) %collective-permute-start.39) | collective-permute-done | bytes 65568 | tf_op jit(solution)/shard_map/ppermute | solution.py:19
  127.3 2.3 %collective-permute-done.40 = f32[128,128]{1,0:T(8,128)S(1)} collective-permute-done((f32[128,128]{1,0:T(8,128)S(1)}, f32[128,128]{1,0:T(8,128)S(1)}, u32[]{:S(2)}, u32[]{:S(2)}) %collective-permute-start.40) | collective-permute-done | bytes 65568 | tf_op jit(solution)/shard_map/ppermute | solution.py:19
  129.7 10.5 %all_to_all.11.sums_ref = f32[32,2,128]{2,1,0:T(2,128)S(1)} all-to-all(f32[32,2,128]{2,1,0:T(2,128)S(1)} %broadcast_in_dim.23), channel_id=1, replica_groups=mesh['samp'=4,'chrom'=8] {'samp','chrom'}, dimensions={0} | all-to-all | bytes 65536 | tf_op jit(solution)/shard_map/all_to_all | solution.py:378
  145.6 2.4 %collective-permute-start.45 = (f32[128,128]{1,0:T(8,128)S(1)}, f32[128,128]{1,0:T(8,128)S(1)}, u32[]{:S(2)}, u32[]{:S(2)}) collective-permute-start(f32[128,128]{1,0:T(8,128)S(1)} %get-tuple-element.77), channel_id=1, source_target_pairs={{0,2},{1,3},{2,0},{3,1},{4,6},{5,7},{6,4},{7,5},{8,10},{9,11},{10,... | collective-permute-start | bytes 196616 | tf_op jit(solution)/shard_map/ppermute | solution.py:19
  148.0 2.4 %collective-permute-done.43 = f32[128,128]{1,0:T(8,128)S(1)} collective-permute-done((f32[128,128]{1,0:T(8,128)S(1)}, f32[128,128]{1,0:T(8,128)S(1)}, u32[]{:S(2)}, u32[]{:S(2)}) %collective-permute-start.43) | collective-permute-done | bytes 65568 | tf_op jit(solution)/shard_map/ppermute | solution.py:19
  154.9 2.4 %collective-permute-start.51 = (f32[128,128]{1,0:T(8,128)S(1)}, f32[128,128]{1,0:T(8,128)S(1)}, u32[]{:S(2)}, u32[]{:S(2)}) collective-permute-start(f32[128,128]{1,0:T(8,128)S(1)} %fusion.7.refs_0_), channel_id=1, source_target_pairs={{0,6},{1,7},{2,4},{3,5},{4,2},{5,3},{6,0},{7,1},{8,14},{9,15},{10,... | collective-permute-start | bytes 196616 | tf_op jit(solution)/shard_map/ppermute | solution.py:19
  161.4 2.4 %shard_map.85 = (f32[1024,128]{1,0:T(8,128)S(1)}, f32[1024,128]{1,0:T(8,128)S(1)}) custom-call(f32[1024,128]{1,0:T(8,128)S(1)} %get-tuple-element.62.coef_ref, s32[1024,128]{1,0:T(8,128)S(1)} %broadcast_in_dim.24.mask_ref, bf16[1024,1024]{1,0:T(8,128)(2,1)S(1)} %bitcast.96, bf16[1024,1024]{1,0:T(8,128)(2,1)S(1)} %bitcast.98), custom_call_target="tpu_custom_call" | custom-call | flops 2147483648 | bytes 4194304 | tf_op jit(solution)/shard_map/pallas_call | solution.py:49
  169.0 3.9 %collective-permute-done.53.refs_1_ = f32[272,128]{1,0:T(8,128)S(1)} collective-permute-done((f32[272,128]{1,0:T(8,128)S(1)}, f32[272,128]{1,0:T(8,128)S(1)}, u32[]{:S(2)}, u32[]{:S(2)}) %collective-permute-start.53) | collective-permute-done | bytes 139296 | tf_op jit(solution)/shard_map/ppermute | solution.py:19
  180.3 3.8 %collective-permute-done.57.refs_2_ = f32[256,128]{1,0:T(8,128)S(1)} collective-permute-done((f32[256,128]{1,0:T(8,128)S(1)}, f32[256,128]{1,0:T(8,128)S(1)}, u32[]{:S(2)}, u32[]{:S(2)}) %collective-permute-start.57) | collective-permute-done | bytes 131104 | tf_op jit(solution)/shard_map/ppermute | solution.py:19
  (142 shorter events, 81.0 us)
Async XLA Ops:
  9.3 7.7 %collective-permute-start.1 = (f32[128,128]{1,0:T(8,128)S(1)}, f32[128,128]{1,0:T(8,128)S(1)}, u32[]{:S(2)}, u32[]{:S(2)}) collective-permute-start(f32[128,128]{1,0:T(8,128)S(1)} %get-tuple-element.88), channel_id=1, source_target_pairs={{0,6},{1,7},{2,4},{3,5},{4,2},{5,3},{6,0},{7,1},{8,14},{9,15},{10,... | collective-permute-start | bytes 196616 | tf_op jit(solution)/shard_map/ppermute | solution.py:19
  25.6 7.5 %collective-permute-start.4 = (f32[128,128]{1,0:T(8,128)S(1)}, f32[128,128]{1,0:T(8,128)S(1)}, u32[]{:S(2)}, u32[]{:S(2)}) collective-permute-start(f32[128,128]{1,0:T(8,128)S(1)} %fusion.41.refs_0_), channel_id=1, source_target_pairs={{0,1},{1,0},{2,3},{3,2},{4,5},{5,4},{6,7},{7,6},{8,9},{9,8},{10,11... | collective-permute-start | bytes 196616 | tf_op jit(solution)/shard_map/ppermute | solution.py:19
  34.4 7.2 %collective-permute-start.11 = (f32[256,128]{1,0:T(8,128)S(1)}, f32[256,128]{1,0:T(8,128)S(1)}, u32[]{:S(2)}, u32[]{:S(2)}) collective-permute-start(f32[256,128]{1,0:T(8,128)S(1)} %get-tuple-element.44), channel_id=1, source_target_pairs={{0,24},{8,16},{16,8},{24,0},{1,25},{9,17},{17,9},{25,1},{2,26},{10... | collective-permute-start | bytes 393224 | tf_op jit(solution)/shard_map/ppermute | solution.py:19
  36.9 7.2 %collective-permute-start.12 = (f32[256,128]{1,0:T(8,128)S(1)}, f32[256,128]{1,0:T(8,128)S(1)}, u32[]{:S(2)}, u32[]{:S(2)}) collective-permute-start(f32[256,128]{1,0:T(8,128)S(1)} %get-tuple-element.45), channel_id=1, source_target_pairs={{0,16},{8,24},{16,0},{24,8},{1,17},{9,25},{17,1},{25,9},{2,18},{10... | collective-permute-start | bytes 393224 | tf_op jit(solution)/shard_map/ppermute | solution.py:19
  37.4 6.8 %collective-permute-start.13 = (f32[256,128]{1,0:T(8,128)S(1)}, f32[256,128]{1,0:T(8,128)S(1)}, u32[]{:S(2)}, u32[]{:S(2)}) collective-permute-start(f32[256,128]{1,0:T(8,128)S(1)} %get-tuple-element.46), channel_id=1, source_target_pairs={{0,8},{8,0},{16,24},{24,16},{1,9},{9,1},{17,25},{25,17},{2,10},{10... | collective-permute-start | bytes 393224 | tf_op jit(solution)/shard_map/ppermute | solution.py:19
  45.8 7.9 %collective-permute-start.15 = (f32[256,128]{1,0:T(8,128)S(1)}, f32[256,128]{1,0:T(8,128)S(1)}, u32[]{:S(2)}, u32[]{:S(2)}) collective-permute-start(f32[256,128]{1,0:T(8,128)S(1)} %get-tuple-element.75.refs_0_), channel_id=1, source_target_pairs={{0,16},{8,24},{16,0},{24,8},{1,17},{9,25},{17,1},{25,9},{2,18},{10... | collective-permute-start | bytes 393224 | tf_op jit(solution)/shard_map/ppermute | solution.py:19
  46.5 7.2 %collective-permute-start.16 = (f32[256,128]{1,0:T(8,128)S(1)}, f32[256,128]{1,0:T(8,128)S(1)}, u32[]{:S(2)}, u32[]{:S(2)}) collective-permute-start(f32[256,128]{1,0:T(8,128)S(1)} %get-tuple-element.75.refs_0_), channel_id=1, source_target_pairs={{0,24},{8,16},{16,8},{24,0},{1,25},{9,17},{17,9},{25,1},{2,26},{10... | collective-permute-start | bytes 393224 | tf_op jit(solution)/shard_map/ppermute | solution.py:19
  56.7 6.8 %collective-permute-start.18 = (f32[128,128]{1,0:T(8,128)S(1)}, f32[128,128]{1,0:T(8,128)S(1)}, u32[]{:S(2)}, u32[]{:S(2)}) collective-permute-start(f32[128,128]{1,0:T(8,128)S(1)} %get-tuple-element.85), channel_id=1, source_target_pairs={{0,6},{1,7},{2,4},{3,5},{4,2},{5,3},{6,0},{7,1},{8,14},{9,15},{10,... | collective-permute-start | bytes 196616 | tf_op jit(solution)/shard_map/ppermute | solution.py:19
  58.5 7.6 %collective-permute-start.19 = (f32[128,128]{1,0:T(8,128)S(1)}, f32[128,128]{1,0:T(8,128)S(1)}, u32[]{:S(2)}, u32[]{:S(2)}) collective-permute-start(f32[128,128]{1,0:T(8,128)S(1)} %get-tuple-element.87), channel_id=1, source_target_pairs={{0,4},{1,5},{2,6},{3,7},{4,0},{5,1},{6,2},{7,3},{8,12},{9,13},{10,... | collective-permute-start | bytes 196616 | tf_op jit(solution)/shard_map/ppermute | solution.py:19
  59.6 6.5 %collective-permute-start.20 = (f32[128,128]{1,0:T(8,128)S(1)}, f32[128,128]{1,0:T(8,128)S(1)}, u32[]{:S(2)}, u32[]{:S(2)}) collective-permute-start(f32[128,128]{1,0:T(8,128)S(1)} %get-tuple-element.86), channel_id=1, source_target_pairs={{0,2},{1,3},{2,0},{3,1},{4,6},{5,7},{6,4},{7,5},{8,10},{9,11},{10,... | collective-permute-start | bytes 196616 | tf_op jit(solution)/shard_map/ppermute | solution.py:19
  79.4 6.9 %collective-permute-start.22 = (f32[128,128]{1,0:T(8,128)S(1)}, f32[128,128]{1,0:T(8,128)S(1)}, u32[]{:S(2)}, u32[]{:S(2)}) collective-permute-start(f32[128,128]{1,0:T(8,128)S(1)} %get-tuple-element.82), channel_id=1, source_target_pairs={{0,6},{1,7},{2,4},{3,5},{4,2},{5,3},{6,0},{7,1},{8,14},{9,15},{10,... | collective-permute-start | bytes 196616 | tf_op jit(solution)/shard_map/ppermute | solution.py:19
  80.0 7.9 %collective-permute-start.23 = (f32[128,128]{1,0:T(8,128)S(1)}, f32[128,128]{1,0:T(8,128)S(1)}, u32[]{:S(2)}, u32[]{:S(2)}) collective-permute-start(f32[128,128]{1,0:T(8,128)S(1)} %get-tuple-element.84), channel_id=1, source_target_pairs={{0,4},{1,5},{2,6},{3,7},{4,0},{5,1},{6,2},{7,3},{8,12},{9,13},{10,... | collective-permute-start | bytes 196616 | tf_op jit(solution)/shard_map/ppermute | solution.py:19
  81.5 6.5 %collective-permute-start.24 = (f32[128,128]{1,0:T(8,128)S(1)}, f32[128,128]{1,0:T(8,128)S(1)}, u32[]{:S(2)}, u32[]{:S(2)}) collective-permute-start(f32[128,128]{1,0:T(8,128)S(1)} %get-tuple-element.83), channel_id=1, source_target_pairs={{0,2},{1,3},{2,0},{3,1},{4,6},{5,7},{6,4},{7,5},{8,10},{9,11},{10,... | collective-permute-start | bytes 196616 | tf_op jit(solution)/shard_map/ppermute | solution.py:19
  89.1 7.1 %collective-permute-start.28 = (f32[128,128]{1,0:T(8,128)S(1)}, f32[128,128]{1,0:T(8,128)S(1)}, u32[]{:S(2)}, u32[]{:S(2)}) collective-permute-start(f32[128,128]{1,0:T(8,128)S(1)} %fusion.24.refs_0_), channel_id=1, source_target_pairs={{0,4},{1,5},{2,6},{3,7},{4,0},{5,1},{6,2},{7,3},{8,12},{9,13},{10,... | collective-permute-start | bytes 196616 | tf_op jit(solution)/shard_map/ppermute | solution.py:19
  99.5 7.4 %collective-permute-start.32 = (f32[256,128]{1,0:T(8,128)S(1)}, f32[256,128]{1,0:T(8,128)S(1)}, u32[]{:S(2)}, u32[]{:S(2)}) collective-permute-start(f32[256,128]{1,0:T(8,128)S(1)} %get-tuple-element.54), channel_id=1, source_target_pairs={{0,24},{8,16},{16,8},{24,0},{1,25},{9,17},{17,9},{25,1},{2,26},{10... | collective-permute-start | bytes 393224 | tf_op jit(solution)/shard_map/ppermute | solution.py:19
  100.2 8.1 %collective-permute-start.33 = (f32[256,128]{1,0:T(8,128)S(1)}, f32[256,128]{1,0:T(8,128)S(1)}, u32[]{:S(2)}, u32[]{:S(2)}) collective-permute-start(f32[256,128]{1,0:T(8,128)S(1)} %get-tuple-element.55), channel_id=1, source_target_pairs={{0,16},{8,24},{16,0},{24,8},{1,17},{9,25},{17,1},{25,9},{2,18},{10... | collective-permute-start | bytes 393224 | tf_op jit(solution)/shard_map/ppermute | solution.py:19
  101.6 6.7 %collective-permute-start.34 = (f32[256,128]{1,0:T(8,128)S(1)}, f32[256,128]{1,0:T(8,128)S(1)}, u32[]{:S(2)}, u32[]{:S(2)}) collective-permute-start(f32[256,128]{1,0:T(8,128)S(1)} %get-tuple-element.56), channel_id=1, source_target_pairs={{0,8},{8,0},{16,24},{24,16},{1,9},{9,1},{17,25},{25,17},{2,10},{10... | collective-permute-start | bytes 393224 | tf_op jit(solution)/shard_map/ppermute | solution.py:19
  109.6 7.9 %collective-permute-start.36 = (f32[256,128]{1,0:T(8,128)S(1)}, f32[256,128]{1,0:T(8,128)S(1)}, u32[]{:S(2)}, u32[]{:S(2)}) collective-permute-start(f32[256,128]{1,0:T(8,128)S(1)} %get-tuple-element.73.refs_0_), channel_id=1, source_target_pairs={{0,16},{8,24},{16,0},{24,8},{1,17},{9,25},{17,1},{25,9},{2,18},{10... | collective-permute-start | bytes 393224 | tf_op jit(solution)/shard_map/ppermute | solution.py:19
  110.2 7.4 %collective-permute-start.37 = (f32[256,128]{1,0:T(8,128)S(1)}, f32[256,128]{1,0:T(8,128)S(1)}, u32[]{:S(2)}, u32[]{:S(2)}) collective-permute-start(f32[256,128]{1,0:T(8,128)S(1)} %get-tuple-element.73.refs_0_), channel_id=1, source_target_pairs={{0,24},{8,16},{16,8},{24,0},{1,25},{9,17},{17,9},{25,1},{2,26},{10... | collective-permute-start | bytes 393224 | tf_op jit(solution)/shard_map/ppermute | solution.py:19
  120.5 6.8 %collective-permute-start.39 = (f32[128,128]{1,0:T(8,128)S(1)}, f32[128,128]{1,0:T(8,128)S(1)}, u32[]{:S(2)}, u32[]{:S(2)}) collective-permute-start(f32[128,128]{1,0:T(8,128)S(1)} %get-tuple-element.79), channel_id=1, source_target_pairs={{0,6},{1,7},{2,4},{3,5},{4,2},{5,3},{6,0},{7,1},{8,14},{9,15},{10,... | collective-permute-start | bytes 196616 | tf_op jit(solution)/shard_map/ppermute | solution.py:19
  123.1 6.6 %collective-permute-start.40 = (f32[128,128]{1,0:T(8,128)S(1)}, f32[128,128]{1,0:T(8,128)S(1)}, u32[]{:S(2)}, u32[]{:S(2)}) collective-permute-start(f32[128,128]{1,0:T(8,128)S(1)} %get-tuple-element.81), channel_id=1, source_target_pairs={{0,4},{1,5},{2,6},{3,7},{4,0},{5,1},{6,2},{7,3},{8,12},{9,13},{10,... | collective-permute-start | bytes 196616 | tf_op jit(solution)/shard_map/ppermute | solution.py:19
  123.2 6.5 %collective-permute-start.41 = (f32[128,128]{1,0:T(8,128)S(1)}, f32[128,128]{1,0:T(8,128)S(1)}, u32[]{:S(2)}, u32[]{:S(2)}) collective-permute-start(f32[128,128]{1,0:T(8,128)S(1)} %get-tuple-element.80), channel_id=1, source_target_pairs={{0,2},{1,3},{2,0},{3,1},{4,6},{5,7},{6,4},{7,5},{8,10},{9,11},{10,... | collective-permute-start | bytes 196616 | tf_op jit(solution)/shard_map/ppermute | solution.py:19
  143.5 6.9 %collective-permute-start.43 = (f32[128,128]{1,0:T(8,128)S(1)}, f32[128,128]{1,0:T(8,128)S(1)}, u32[]{:S(2)}, u32[]{:S(2)}) collective-permute-start(f32[128,128]{1,0:T(8,128)S(1)} %get-tuple-element.76), channel_id=1, source_target_pairs={{0,6},{1,7},{2,4},{3,5},{4,2},{5,3},{6,0},{7,1},{8,14},{9,15},{10,... | collective-permute-start | bytes 196616 | tf_op jit(solution)/shard_map/ppermute | solution.py:19
  144.2 7.9 %collective-permute-start.44 = (f32[128,128]{1,0:T(8,128)S(1)}, f32[128,128]{1,0:T(8,128)S(1)}, u32[]{:S(2)}, u32[]{:S(2)}) collective-permute-start(f32[128,128]{1,0:T(8,128)S(1)} %get-tuple-element.78), channel_id=1, source_target_pairs={{0,4},{1,5},{2,6},{3,7},{4,0},{5,1},{6,2},{7,3},{8,12},{9,13},{10,... | collective-permute-start | bytes 196616 | tf_op jit(solution)/shard_map/ppermute | solution.py:19
  145.6 6.5 %collective-permute-start.45 = (f32[128,128]{1,0:T(8,128)S(1)}, f32[128,128]{1,0:T(8,128)S(1)}, u32[]{:S(2)}, u32[]{:S(2)}) collective-permute-start(f32[128,128]{1,0:T(8,128)S(1)} %get-tuple-element.77), channel_id=1, source_target_pairs={{0,2},{1,3},{2,0},{3,1},{4,6},{5,7},{6,4},{7,5},{8,10},{9,11},{10,... | collective-permute-start | bytes 196616 | tf_op jit(solution)/shard_map/ppermute | solution.py:19
  152.9 7.3 %collective-permute-start.47 = (f32[128,128]{1,0:T(8,128)S(1)}, f32[128,128]{1,0:T(8,128)S(1)}, u32[]{:S(2)}, u32[]{:S(2)}) collective-permute-start(f32[128,128]{1,0:T(8,128)S(1)} %fusion.7.refs_0_), channel_id=1, source_target_pairs={{0,2},{1,3},{2,0},{3,1},{4,6},{5,7},{6,4},{7,5},{8,10},{9,11},{10,... | collective-permute-start | bytes 196616 | tf_op jit(solution)/shard_map/ppermute | solution.py:19
  153.2 7.5 %collective-permute-start.49 = (f32[128,128]{1,0:T(8,128)S(1)}, f32[128,128]{1,0:T(8,128)S(1)}, u32[]{:S(2)}, u32[]{:S(2)}) collective-permute-start(f32[128,128]{1,0:T(8,128)S(1)} %fusion.7.refs_0_), channel_id=1, source_target_pairs={{0,4},{1,5},{2,6},{3,7},{4,0},{5,1},{6,2},{7,3},{8,12},{9,13},{10,... | collective-permute-start | bytes 196616 | tf_op jit(solution)/shard_map/ppermute | solution.py:19
  165.5 7.5 %collective-permute-start.53 = (f32[272,128]{1,0:T(8,128)S(1)}, f32[272,128]{1,0:T(8,128)S(1)}, u32[]{:S(2)}, u32[]{:S(2)}) collective-permute-start(f32[272,128]{1,0:T(8,128)S(1)} %get-tuple-element.68), channel_id=1, source_target_pairs={{0,24},{8,16},{16,8},{24,0},{1,25},{9,17},{17,9},{25,1},{2,26},{10... | collective-permute-start | bytes 417800 | tf_op jit(solution)/shard_map/ppermute | solution.py:19
  166.1 8.6 %collective-permute-start.54 = (f32[272,128]{1,0:T(8,128)S(1)}, f32[272,128]{1,0:T(8,128)S(1)}, u32[]{:S(2)}, u32[]{:S(2)}) collective-permute-start(f32[272,128]{1,0:T(8,128)S(1)} %get-tuple-element.69), channel_id=1, source_target_pairs={{0,16},{8,24},{16,0},{24,8},{1,17},{9,25},{17,1},{25,9},{2,18},{10... | collective-permute-start | bytes 417800 | tf_op jit(solution)/shard_map/ppermute | solution.py:19
  167.5 7.2 %collective-permute-start.55 = (f32[272,128]{1,0:T(8,128)S(1)}, f32[272,128]{1,0:T(8,128)S(1)}, u32[]{:S(2)}, u32[]{:S(2)}) collective-permute-start(f32[272,128]{1,0:T(8,128)S(1)} %get-tuple-element.70), channel_id=1, source_target_pairs={{0,8},{8,0},{16,24},{24,16},{1,9},{9,1},{17,25},{25,17},{2,10},{10... | collective-permute-start | bytes 417800 | tf_op jit(solution)/shard_map/ppermute | solution.py:19
  176.2 8.0 %collective-permute-start.57 = (f32[256,128]{1,0:T(8,128)S(1)}, f32[256,128]{1,0:T(8,128)S(1)}, u32[]{:S(2)}, u32[]{:S(2)}) collective-permute-start(f32[256,128]{1,0:T(8,128)S(1)} %shard_map.88.refs_0_), channel_id=1, source_target_pairs={{0,16},{8,24},{16,0},{24,8},{1,17},{9,25},{17,1},{25,9},{2,18},{10... | collective-permute-start | bytes 393224 | tf_op jit(solution)/shard_map/ppermute | solution.py:19
  176.8 7.4 %collective-permute-start.58 = (f32[256,128]{1,0:T(8,128)S(1)}, f32[256,128]{1,0:T(8,128)S(1)}, u32[]{:S(2)}, u32[]{:S(2)}) collective-permute-start(f32[256,128]{1,0:T(8,128)S(1)} %shard_map.88.refs_0_), channel_id=1, source_target_pairs={{0,24},{8,16},{16,8},{24,0},{1,25},{9,17},{17,9},{25,1},{2,26},{10... | collective-permute-start | bytes 393224 | tf_op jit(solution)/shard_map/ppermute | solution.py:19
  (37 other events, 194.3 us)

commit v2 on v0

v2 whole, which is shorter than its diff:
```python
import functools
import math

import jax
import jax.numpy as jnp
from jax import lax
from jax.experimental import pallas as pl
from jax.experimental.pallas import tpu as pltpu
from jax.sharding import PartitionSpec as P

GPD = 2
ITERS = 2
STATS = 16
VMEM_LIMIT = 14 * 1024 * 1024
FIRST_LIMIT = 60 * 1024 * 1024


def swap(value, axis, bits):
    size = lax.axis_size(axis)
    return lax.ppermute(value, axis, [(i, i ^ bits) for i in range(size)])


def split(value):
    high = value.astype(jnp.bfloat16)
    low = (value - high.astype(jnp.float32)).astype(jnp.bfloat16)
    return high, low


def pack(value):
    return jnp.concatenate(split(value), axis=1)


def wide_dot(high, low, packed):
    total = jnp.dot(high, packed, preferred_element_type=jnp.float32)
    total = total + jnp.dot(low, packed, preferred_element_type=jnp.float32)
    traits = packed.shape[1] // 2
    return total[:, :traits] + total[:, traits:]


def whole():
    return pl.BlockSpec(memory_space=pltpu.VMEM)


def anywhere():
    return pl.BlockSpec(memory_space=pl.ANY)


def shape(dims, dtype=jnp.float32):
    return jax.ShapeDtypeStruct(dims, dtype)


def call(kernel, outs, specs, scratch=(), flops=0, moved=0, limit=VMEM_LIMIT):
    return pl.pallas_call(
        kernel,
        out_shape=outs,
        in_specs=specs,
        out_specs=jax.tree.map(lambda _: whole(), outs),
        scratch_shapes=list(scratch),
        compiler_params=pltpu.CompilerParams(vmem_limit_bytes=limit),
        cost_estimate=pl.CostEstimate(flops=flops, bytes_accessed=moved, transcendentals=0),
    )


def first_kernel(bits, dosage_ref, coef_ref, high_ref, low_ref, out_ref, *rest):
    *packed_out, buffer_ref, sems = rest
    me = lax.axis_index("chrom")
    place, core = me // 2, me % 2
    half, block = buffer_ref.shape[0], buffer_ref.shape[1]
    copies = [
        pltpu.make_async_copy(dosage_ref.at[place ^ k, core ^ bits], buffer_ref.at[k], sems.at[k]) for k in range(half)
    ]
    for copy in copies:
        copy.start()
    if packed_out:
        packed_out[0][...] = pack(coef_ref[...])
        packed = packed_out[0][...]
    else:
        packed = coef_ref[...]
    for k, copy in enumerate(copies):
        copy.wait()
        high, low = split(buffer_ref[k])
        high_ref[k * block : (k + 1) * block] = high
        low_ref[k * block : (k + 1) * block] = low
    out_ref[...] = wide_dot(high_ref[...], low_ref[...], packed).reshape(out_ref.shape)


def turn_kernel(count, *refs):
    for source, target in zip(refs[:count], refs[-count:]):
        target[0] = source[...].T


def turned(parts, blocks, after):
    rows, cols = parts[0].shape
    width = cols // blocks
    return pl.pallas_call(
        functools.partial(turn_kernel, len(parts)),
        grid=(blocks,),
        in_specs=[pl.BlockSpec((rows, width), lambda step: (0, step))] * len(parts) + [anywhere()],
        out_specs=[pl.BlockSpec((1, width, rows), lambda step: (step, 0, 0))] * len(parts),
        out_shape=[shape((blocks, width, rows), jnp.bfloat16)] * len(parts),
        compiler_params=pltpu.CompilerParams(vmem_limit_bytes=VMEM_LIMIT),
        cost_estimate=pl.CostEstimate(flops=0, bytes_accessed=8 * rows * cols * len(parts), transcendentals=0),
    )(*parts, after)


def tested_kernel(tested_ref, turned_ref, square_ref):
    value = tested_ref[...]
    turned_ref[0] = value.T
    wide = value.astype(jnp.float32)
    square_ref[0] = jnp.sum(wide * wide, axis=0).reshape(square_ref.shape[1:])


def tested_parts(tested, blocks):
    rows, cols = tested.shape
    width = cols // blocks
    return pl.pallas_call(
        tested_kernel,
        grid=(blocks,),
        in_specs=[pl.BlockSpec((rows, width), lambda step: (0, step))],
        out_specs=[
            pl.BlockSpec((1, width, rows), lambda step: (step, 0, 0)),
            pl.BlockSpec((1, width // 128, 128), lambda step: (step, 0, 0)),
        ],
        out_shape=[shape((blocks, width, rows), jnp.bfloat16), shape((blocks, width // 128, 128))],
        compiler_params=pltpu.CompilerParams(vmem_limit_bytes=VMEM_LIMIT),
        cost_estimate=pl.CostEstimate(flops=0, bytes_accessed=8 * rows * cols, transcendentals=0),
    )(tested)


def rest_kernel(high_ref, low_ref, packed_ref, out_ref):
    out_ref[...] = wide_dot(high_ref[...], low_ref[...], packed_ref[...]).reshape(out_ref.shape)


def residual_kernel(count, traits_ref, *refs):
    total = refs[0][...]
    for piece in refs[1:count]:
        total = total + piece[...]
    refs[-1][...] = traits_ref[...] - total


def grad_dot(turn_refs, packed_ref, which):
    half = packed_ref.shape[0] // 2
    own = wide_dot(turn_refs[0][which], turn_refs[1][which], packed_ref[0:half])
    return own + wide_dot(turn_refs[2][which], turn_refs[3][which], packed_ref[half:])


def grad_far_kernel(count, partners, *refs):
    pieces, turn_refs, (packed_ref, *outs) = refs[:count], refs[count : count + 4], refs[count + 4 :]
    samp = lax.axis_index("samp")
    block = pieces[0].shape[0]
    for bits, piece in enumerate(pieces):
        start = ((bits % 2) * (count // 2) + bits // 2) * block
        packed_ref[start : start + block] = pack(piece[...])
    for partner, out in zip(partners, outs):
        out[...] = grad_dot(turn_refs, packed_ref, samp ^ partner)


def grad_near_kernel(partners, *refs):
    packed_ref, turn_refs, outs = refs[0], refs[1:5], refs[5:]
    samp = lax.axis_index("samp")
    for partner, out in zip(partners, outs):
        out[...] = grad_dot(turn_refs, packed_ref, samp ^ partner)


def image_kernel(count, *refs):
    pieces = refs[:count]
    high_ref, low_ref = refs[count : count + 2]
    grad_ref, packed_ref, give_ref = refs[-3:]
    samp = lax.axis_index("samp")
    block = pieces[0].shape[0]
    for bits, piece in enumerate(pieces):
        rows = pl.ds(pl.multiple_of((samp ^ bits) * block, block), block)
        value = piece[...]
        grad_ref[rows] = value
        packed_ref[rows] = pack(value)
    rest_kernel(high_ref, low_ref, packed_ref, give_ref)


def norm_kernel(count, *refs):
    grad_ref, pieces, out = refs[0], refs[1 : count + 1], refs[-1]
    total = pieces[0][...]
    for piece in pieces[1:]:
        total = total + piece[...]
    grad = grad_ref[...]
    grad_sq = jnp.sum(grad * grad, axis=0, keepdims=True)
    image_sq = jnp.sum(total * total, axis=0, keepdims=True)
    row = lax.broadcasted_iota(jnp.int32, out.shape[1:], 0)
    sums = jnp.where(row == 0, grad_sq, jnp.where(row == 1, image_sq, 0.0))
    for place in range(out.shape[0]):
        out[place] = sums


def prox_kernel(total_rows, coef_ref, grad_ref, sums_ref, high_ref, low_ref, new_ref, packed_ref, give_ref):
    sums = sums_ref[0]
    for place in range(1, sums_ref.shape[0]):
        sums = sums + sums_ref[place]
    grad_sq = jnp.sum(sums[0:1], axis=1, keepdims=True)
    image_sq = jnp.sum(sums[1:2], axis=1, keepdims=True)
    step_size = grad_sq / (image_sq / total_rows + 1e-06)
    penalty = 1.5 * math.sqrt(coef_ref.shape[1] / total_rows)
    moved = coef_ref[...] + step_size * grad_ref[...]
    length = jnp.sqrt(jnp.sum(moved * moved, axis=1, keepdims=True))
    cut = step_size * penalty
    new = moved * (jnp.maximum(length - cut, 0.0) / jnp.maximum(length, cut))
    new_ref[...] = new
    packed_ref[...] = pack(new)
    rest_kernel(high_ref, low_ref, packed_ref, give_ref)


def own_kernel(coef_ref, mask_ref, *refs):
    parts, outs = refs[:4], refs[4:]
    coef = coef_ref[...]
    mask = mask_ref[...]
    half = parts[0].shape[0]
    for which, out in enumerate(outs):
        packed = pack(jnp.where(mask == which, coef, 0.0))
        out[0:half] = wide_dot(parts[0][...], parts[1][...], packed)
        out[half:] = wide_dot(parts[2][...], parts[3][...], packed)


def score_products(partner, out, tested_ref, square_ref, pick_ref, loco_ref, sums_ref):
    cols, traits = tested_ref.shape[1], out.shape[1]
    products = jnp.dot(tested_ref[partner], loco_ref[...], preferred_element_type=jnp.float32)
    pick = pick_ref[partner]
    chosen = products[:, :traits]
    for which in range(1, GPD):
        chosen = jnp.where(pick == which, products[:, which * traits : (which + 1) * traits], chosen)
    out[0:cols] = chosen
    out[cols : cols + 8] = sums_ref[...]
    out[cols + 8 : cols + STATS] = jnp.zeros((STATS - 8, traits), jnp.float32)
    out[cols + 8 : cols + 8 + square_ref.shape[1]] = square_ref[partner]


def loco_kernel(count, partners, *refs):
    pieces, own_refs = refs[:count], refs[count : count + GPD]
    tested_ref, square_ref, pick_ref, residual_ref, loco_ref, sums_ref = refs[count + GPD : count + GPD + 6]
    outs = refs[count + GPD + 6 :]
    me, samp = lax.axis_index("chrom"), lax.axis_index("samp")
    block, traits = pieces[0].shape
    sums_ref[...] = jnp.zeros_like(sums_ref)
    for bits, piece in enumerate(pieces):
        rows = pl.ds(pl.multiple_of((me ^ bits) * block, block), block)
        start = ((bits % 2) * (count // 2) + bits // 2) * block
        value = piece[...]
        residual_ref[rows] = value
        for which in range(GPD):
            loco = value + own_refs[which][start : start + block]
            sums_ref[which : which + 1] += jnp.sum(loco * loco, axis=0, keepdims=True)
            loco_ref[rows, which * traits : (which + 1) * traits] = loco.astype(jnp.bfloat16)
    for partner, out in zip(partners, outs):
        score_products(samp ^ partner, out, tested_ref, square_ref, pick_ref, loco_ref, sums_ref)


def loco_near_kernel(partners, *refs):
    samp = lax.axis_index("samp")
    for partner, out in zip(partners, refs[5:]):
        score_products(samp ^ partner, out, *refs[:5])


def score_kernel(total_rows, pick_ref, *refs):
    pieces, out = refs[:-1], refs[-1]
    total = pieces[0][...]
    for piece in pieces[1:]:
        total = total + piece[...]
    cols, traits = out.shape
    pick = pick_ref[lax.axis_index("samp")]
    loco_sq = jnp.broadcast_to(total[cols : cols + 1], (cols, traits))
    for which in range(1, GPD):
        loco_sq = jnp.where(pick == which, total[cols + which : cols + which + 1], loco_sq)
    diagonal = lax.broadcasted_iota(jnp.int32, (128, 128), 0) == lax.broadcasted_iota(jnp.int32, (128, 128), 1)
    columns = []
    for row in range(cols // 128):
        squares = total[cols + 8 + row : cols + 9 + row, :128]
        columns.append(jnp.sum(jnp.where(diagonal, squares, 0.0), axis=1, keepdims=True))
    tested_sq = jnp.concatenate(columns)
    denom = math.sqrt(total_rows) * jnp.sqrt((tested_sq / total_rows + 1e-06) * (loco_sq / total_rows + 1e-06))
    out[...] = total[:cols] / denom


def place_kernel(*refs):
    pieces, out = refs[:-1], refs[-1]
    samp = lax.axis_index("samp")
    block = pieces[0].shape[0]
    for bits, piece in enumerate(pieces):
        out[pl.ds(pl.multiple_of((samp ^ bits) * block, block), block)] = piece[...]


def chrom_scatter(give, keep):
    got = swap(give, "chrom", 1)
    count = keep.shape[0]
    sums = [keep[k] + got[k] for k in range(count)]
    return [sums[0]] + [swap(sums[k], "chrom", 2 * k) for k in reversed(range(1, count))]


def chrom_gather(own):
    count = lax.axis_size("chrom") // 2
    far = [swap(own, "chrom", 2 * k) for k in reversed(range(1, count))]
    mine = [own] + far[::-1]
    other = [swap(block, "chrom", 1) for block in mine]
    return [block for pair in zip(mine, other) for block in pair]


def samp_order(size):
    return list(reversed(range(size)))


def samp_gather(own):
    size = lax.axis_size("samp")
    return [own] + [swap(own, "samp", k) for k in samp_order(size)[:-1]][::-1]


def body(dosages, traits, start_coef, groups, tested, owners):
    n_samp, n_chrom = lax.axis_size("samp"), lax.axis_size("chrom")
    rows, cols = dosages.shape
    tests, n_traits = tested.shape[1], traits.shape[1]
    total_rows = rows * n_samp
    me = lax.axis_index("chrom")
    half, block, width, test_width = n_chrom // 2, rows // n_chrom, cols // n_samp, tests // n_samp
    flops = 4 * rows * cols * n_traits
    moved = 2 * rows * cols
    order = samp_order(n_samp)
    far, near = order[: n_samp // 2], order[n_samp // 2 :]

    part = shape((rows // 2, cols), jnp.bfloat16)
    half_out = shape((half, block, n_traits))
    packed_cols = shape((cols, 2 * n_traits), jnp.bfloat16)
    packed_rows = shape((rows, 2 * n_traits), jnp.bfloat16)
    grad_block = shape((width, n_traits))
    score_block = shape((test_width + STATS, n_traits))
    coef_out = shape((cols, n_traits))
    buffers = [pltpu.VMEM((half, block, cols), jnp.float32), pltpu.SemaphoreType.DMA((half,))]

    mask = jnp.broadcast_to((groups - me * GPD)[:, None], (cols, n_traits))
    pick = jnp.broadcast_to((owners - me * GPD)[:, None], (tests, n_traits)).reshape(n_samp, test_width, n_traits)
    own_traits = lax.dynamic_slice_in_dim(traits, me * block, block, 0)

    def rest(high, low, packed):
        return call(rest_kernel, half_out, [whole()] * 3, (), flops, moved)(high, low, packed)

    def own_residual(summands, after=()):
        return call(
            functools.partial(residual_kernel, len(summands)),
            shape((block, n_traits)),
            [whole()] * (1 + len(summands)) + [anywhere()] * len(after),
        )(own_traits, *summands, *after)

    def first(bits, coefficients, outs):
        return call(
            functools.partial(first_kernel, bits),
            [part, part, half_out] + outs,
            [pl.BlockSpec(memory_space=pltpu.HBM), whole()],
            buffers,
            flops,
            2 * moved,
            FIRST_LIMIT,
        )(dosages.reshape(half, 2, block, cols), coefficients)

    coefficients = start_coef
    high1, low1, give, packed = first(1, coefficients, [packed_cols])
    high0, low0, keep = first(0, packed, [])
    summands = chrom_scatter(give, keep)
    turns = turned([high0, low0, high1, low1], n_samp, summands[0])
    turn_tested, tested_sq = tested_parts(tested, n_samp)

    for iteration in range(ITERS):
        own = own_residual(summands, turns if iteration == 0 else ())
        pieces = chrom_gather(own)
        packed, *far_out = call(
            functools.partial(grad_far_kernel, n_chrom, far),
            [packed_rows] + [grad_block] * len(far),
            [whole()] * (n_chrom + 4),
            (),
            flops,
            moved,
        )(*pieces, *turns)
        near_out = call(
            functools.partial(grad_near_kernel, near), [grad_block] * len(near), [whole()] * 5, (), flops, moved
        )(packed, *turns)
        own_grad = near_out[-1]
        for partner, piece in zip(order, far_out + list(near_out[:-1])):
            own_grad = own_grad + swap(piece, "samp", partner)
        own_grad = own_grad / total_rows
        pieces = samp_gather(own_grad)
        after = (turn_tested, tested_sq, mask, pick) if iteration == 0 else ()
        gradient, packed, give = call(
            functools.partial(image_kernel, n_samp),
            [coef_out, packed_cols, half_out],
            [whole()] * (n_samp + 2) + [anywhere()] * len(after),
            (),
            flops,
            moved,
        )(*pieces, high1, low1, *after)
        summands = chrom_scatter(give, rest(high0, low0, packed))
        size = n_samp * n_chrom
        sums = call(
            functools.partial(norm_kernel, half), shape((size, 8, n_traits)), [whole()] * (half + 1)
        )(own_grad, *summands)
        sums = lax.all_to_all(sums, ("samp", "chrom"), 0, 0)
        coefficients, packed, give = call(
            functools.partial(prox_kernel, total_rows),
            [coef_out, packed_cols, half_out],
            [whole()] * 5,
            (),
            flops,
            moved,
        )(coefficients, gradient, sums, high1, low1)
        summands = chrom_scatter(give, rest(high0, low0, packed))

    own_parts = call(own_kernel, [shape((rows, n_traits))] * GPD, [whole()] * 6, (), 4 * flops, 4 * moved)(
        coefficients, mask, high0, low0, high1, low1
    )
    pieces = chrom_gather(own_residual(summands, own_parts))
    residual, loco, loco_sq, *far_out = call(
        functools.partial(loco_kernel, n_chrom, far),
        [shape((rows, n_traits)), shape((rows, GPD * n_traits), jnp.bfloat16), shape((8, n_traits))]
        + [score_block] * len(far),
        [whole()] * (n_chrom + GPD + 3),
        (),
        flops,
        moved,
    )(*pieces, *own_parts, turn_tested, tested_sq, pick)
    near_out = call(
        functools.partial(loco_near_kernel, near), [score_block] * len(near), [whole()] * 5, (), flops // 2, moved
    )(turn_tested, tested_sq, pick, loco, loco_sq)
    received = [swap(piece, "samp", partner) for partner, piece in zip(order, far_out + list(near_out[:-1]))]
    own_scores = call(
        functools.partial(score_kernel, total_rows), shape((test_width, n_traits)), [whole()] * (n_samp + 1)
    )(pick, near_out[-1], *received)
    scores = call(place_kernel, shape((tests, n_traits)), [whole()] * n_samp)(*samp_gather(own_scores))
    return (scores, residual)


def solution(mesh):
    placed = (
        P("samp", "chrom"),
        P("samp", None),
        P("chrom", None),
        P("chrom"),
        P("samp", "chrom"),
        P("chrom"),
    )
    return jax.shard_map(
        body,
        mesh=mesh,
        in_specs=placed,
        out_specs=(P("chrom", None), P("samp", None)),
        check_vma=False,
    )
```

time: 531 us -> 191 us (0.36)
  waiting for transfers between devices: 353 us -> 66.6 us
  blocking collectives: 86.6 us -> 22.5 us
  starting transfers between devices: 0.33 us -> 60.4 us
  matrix products: 59.3 us -> 0 us
  Pallas kernels: 0 us -> 27.3 us
  between operations: 18.2 us -> 1.1 us
  other arithmetic: 8.97 us -> 2.05 us
  local copies, waits for them, and re-layouts: 4.26 us -> 10.2 us
    psum x6 -> x0, waiting for transfers between devices: 293 us -> none  [the longest x3 170 us: total_prediction(): return lax.psum(partial_value, 'chrom')]
    psum x3 -> x0, blocking collectives: 86.6 us -> none  [the longest x2 76.4 us: body(): grad_sq, image_sq = lax.psum((grad_sq, image_sq), ('samp', 'chrom'))]
    ppermute x0 -> x59, waiting for transfers between devices: none -> 66.6 us  [swap(): return lax.ppermute(value, axis, [(i, i ^ bits) for i in range(size)])]
    ppermute x0 -> x59, starting transfers between devices: none -> 60.4 us  [swap(): return lax.ppermute(value, axis, [(i, i ^ bits) for i in range(size)])]
    dot_general x11 -> x0, matrix products: 59.3 us -> none  [the longest x7 46.5 us: matmul(): jnp.dot(left, right, precision=lax.Precision.HIGHEST, preferred_element_t...]
    reduce_scatter x2 -> x0, waiting for transfers between devices: 59.3 us -> none  [body(): lax.psum_scatter(image_rows(jnp.int32(0), rows_dev // lax.axis_size('chro...]
    pallas_call x0 -> x26, Pallas kernels: none -> 27.3 us  [the longest x2 9.29 us: first(): call(functools.partial(first_kernel, bits), [part, part, half_out] + outs...]
    all_to_all x0 -> x2, blocking collectives: none -> 22.5 us  [body(): sums = lax.all_to_all(sums, ('samp', 'chrom'), 0, 0)]
  transfers between devices with their start and end apart: 8 -> 59, of which waited for: 8 -> 39; matrix products, arithmetic and copies ran while one was open for 1% -> 0% of each run, Pallas kernels for 0% -> 7%
where the time goes in v2:
time: 191 us; the launch traced here: 190 us
  waiting for transfers between devices  66.6 us (35%)
  starting transfers between devices  60.4 us (32%)
  Pallas kernels  27.3 us (14%)
  blocking collectives  22.5 us (12%)
  local copies, waits for them, and re-layouts  10.2 us (5%)
  other arithmetic  2.05 us (1%)
    ppermute x59, waiting for transfers between devices, swap(): return lax.ppermute(value, axis, [(i, i ^ bits) for i in range(size)])  66.6 us
    ppermute x59, starting transfers between devices, swap(): return lax.ppermute(value, axis, [(i, i ^ bits) for i in range(size)])  60.4 us
    all_to_all x2, blocking collectives, body(): sums = lax.all_to_all(sums, ('samp', 'chrom'), 0, 0)  22.5 us
    unnamed x46, local copies, waits for them, and re-layouts  9.79 us
    pallas_call x2, Pallas kernels, first(): call(functools.partial(first_kernel, bits), [part, part, half_out] + outs...  9.29 us
  transfers between devices with their start and end apart: 59, of which 39 were waited for; matrix products, arithmetic and copies ran while one was open for 0% of the time, Pallas kernels for 7%

profile of v2, /device:TPU:0, one launch (start us, length us, event | category | flops | bytes accessed | tf_op | source)
XLA Modules:
  0.0 190.1 jit_solution(9808524955990079775)
XLA Ops:
  0.6 4.6 %shard_map.78 = (bf16[512,1024]{1,0:T(8,128)(2,1)}, bf16[512,1024]{1,0:T(8,128)(2,1)}, f32[4,128,128]{2,1,0:T(8,128)}, bf16[1024,256]{1,0:T(8,128)(2,1)}) custom-call(f32[4,2,128,1024]{3,2,1,0:T(8,128)} %bitcast.41, f32[1024,128]{1,0:T(8,128)} %coef_ref.3), custom_call_target="tpu_custom_call" | custom-call | flops 536870912 | bytes 4194304 | tf_op jit(solution)/shard_map/pallas_call | solution.py:348
  5.8 4.7 %shard_map.79 = (bf16[512,1024]{1,0:T(8,128)(2,1)}, bf16[512,1024]{1,0:T(8,128)(2,1)}, f32[4,128,128]{2,1,0:T(8,128)}) custom-call(f32[4,2,128,1024]{3,2,1,0:T(8,128)} %bitcast.42, bf16[1024,256]{1,0:T(8,128)(2,1)} %get-tuple-element.48.coef_ref), custom_call_target="tpu_custom_call" | custom-call | flops 536870912 | bytes 4194304 | tf_op jit(solution)/shard_map/pallas_call | solution.py:348
  11.4 2.7 %collective-permute-start.3 = (f32[128,128]{1,0:T(8,128)S(1)}, f32[128,128]{1,0:T(8,128)S(1)}, u32[]{:S(2)}, u32[]{:S(2)}) collective-permute-start(f32[128,128]{1,0:T(8,128)S(1)} %get-tuple-element.106), channel_id=1, source_target_pairs={{0,2},{1,3},{2,0},{3,1},{4,6},{5,7},{6,4},{7,5},{8,10},{9,11},{10,... | collective-permute-start | bytes 196616 | tf_op jit(solution)/shard_map/ppermute | solution.py:20
  14.1 2.6 %collective-permute-start.2 = (f32[128,128]{1,0:T(8,128)S(1)}, f32[128,128]{1,0:T(8,128)S(1)}, u32[]{:S(2)}, u32[]{:S(2)}) collective-permute-start(f32[128,128]{1,0:T(8,128)S(1)} %get-tuple-element.107), channel_id=1, source_target_pairs={{0,4},{1,5},{2,6},{3,7},{4,0},{5,1},{6,2},{7,3},{8,12},{9,13},{10,... | collective-permute-start | bytes 196616 | tf_op jit(solution)/shard_map/ppermute | solution.py:20
  19.2 1.9 %shard_map.80 = (bf16[4,256,512]{2,1,0:T(8,128)(2,1)S(1)}, bf16[4,256,512]{2,1,0:T(8,128)(2,1)S(1)}, bf16[4,256,512]{2,1,0:T(8,128)(2,1)S(1)}, bf16[4,256,512]{2,1,0:T(8,128)(2,1)S(1)}) custom-call(bf16[512,1024]{1,0:T(8,128)(2,1)S(1)} %copy-done.3, bf16[512,1024]{1,0:T(8,128)(2,1)S(1)} %copy-done.5, bf16[512,1024]{1,0:T(8,128)(2,1)S(1)} %copy-done.1, ...), custom_call_target="tpu_custom_call" | custom-call | bytes 16777216 | tf_op jit(solution)/shard_map/pallas_call | solution.py:95
  23.1 3.8 %collective-permute-start.9 = (f32[128,128]{1,0:T(8,128)S(1)}, f32[128,128]{1,0:T(8,128)S(1)}, u32[]{:S(2)}, u32[]{:S(2)}) collective-permute-start(f32[128,128]{1,0:T(8,128)S(1)} %shard_map.81.refs_0_), channel_id=1, source_target_pairs={{0,6},{1,7},{2,4},{3,5},{4,2},{5,3},{6,0},{7,1},{8,14},{9,15},{10,... | collective-permute-start | bytes 196616 | tf_op jit(solution)/shard_map/ppermute | solution.py:20
  27.5 2.2 %collective-permute-done.9.refs_6_ = f32[128,128]{1,0:T(8,128)S(1)} collective-permute-done((f32[128,128]{1,0:T(8,128)S(1)}, f32[128,128]{1,0:T(8,128)S(1)}, u32[]{:S(2)}, u32[]{:S(2)}) %collective-permute-start.9) | collective-permute-done | bytes 65568 | tf_op jit(solution)/shard_map/ppermute | solution.py:20
  29.7 2.5 %collective-permute-done.7.refs_4_ = f32[128,128]{1,0:T(8,128)S(1)} collective-permute-done((f32[128,128]{1,0:T(8,128)S(1)}, f32[128,128]{1,0:T(8,128)S(1)}, u32[]{:S(2)}, u32[]{:S(2)}) %collective-permute-start.7) | collective-permute-done | bytes 65568 | tf_op jit(solution)/shard_map/ppermute | solution.py:20
  46.4 3.3 %collective-permute-done.11 = f32[256,128]{1,0:T(8,128)S(1)} collective-permute-done((f32[256,128]{1,0:T(8,128)S(1)}, f32[256,128]{1,0:T(8,128)S(1)}, u32[]{:S(2)}, u32[]{:S(2)}) %collective-permute-start.11) | collective-permute-done | bytes 131104 | tf_op jit(solution)/shard_map/ppermute | solution.py:20
  55.6 3.4 %collective-permute-done.16.refs_3_ = f32[256,128]{1,0:T(8,128)S(1)} collective-permute-done((f32[256,128]{1,0:T(8,128)S(1)}, f32[256,128]{1,0:T(8,128)S(1)}, u32[]{:S(2)}, u32[]{:S(2)}) %collective-permute-start.16) | collective-permute-done | bytes 131104 | tf_op jit(solution)/shard_map/ppermute | solution.py:20
  64.1 2.1 %collective-permute-start.19 = (f32[128,128]{1,0:T(8,128)S(1)}, f32[128,128]{1,0:T(8,128)S(1)}, u32[]{:S(2)}, u32[]{:S(2)}) collective-permute-start(f32[128,128]{1,0:T(8,128)S(1)} %get-tuple-element.103), channel_id=1, source_target_pairs={{0,4},{1,5},{2,6},{3,7},{4,0},{5,1},{6,2},{7,3},{8,12},{9,13},{10,... | collective-permute-start | bytes 196616 | tf_op jit(solution)/shard_map/ppermute | solution.py:20
  68.3 4.2 %collective-permute-done.19.refs_3_ = f32[128,128]{1,0:T(8,128)S(1)} collective-permute-done((f32[128,128]{1,0:T(8,128)S(1)}, f32[128,128]{1,0:T(8,128)S(1)}, u32[]{:S(2)}, u32[]{:S(2)}) %collective-permute-start.19) | collective-permute-done | bytes 65568 | tf_op jit(solution)/shard_map/ppermute | solution.py:20
  72.6 11.4 %all_to_all.10.sums_ref = f32[32,8,128]{2,1,0:T(8,128)S(1)} all-to-all(f32[32,8,128]{2,1,0:T(8,128)S(1)} %shard_map.86), channel_id=1, replica_groups=mesh['samp'=4,'chrom'=8] {'samp','chrom'}, dimensions={0} | all-to-all | bytes 262144 | tf_op jit(solution)/shard_map/all_to_all | solution.py:398
  88.4 2.8 %collective-permute-start.22 = (f32[128,128]{1,0:T(8,128)S(1)}, f32[128,128]{1,0:T(8,128)S(1)}, u32[]{:S(2)}, u32[]{:S(2)}) collective-permute-start(f32[128,128]{1,0:T(8,128)S(1)} %get-tuple-element.100), channel_id=1, source_target_pairs={{0,6},{1,7},{2,4},{3,5},{4,2},{5,3},{6,0},{7,1},{8,14},{9,15},{10,... | collective-permute-start | bytes 196616 | tf_op jit(solution)/shard_map/ppermute | solution.py:20
  91.9 3.8 %collective-permute-done.23.refs_2_ = f32[128,128]{1,0:T(8,128)S(1)} collective-permute-done((f32[128,128]{1,0:T(8,128)S(1)}, f32[128,128]{1,0:T(8,128)S(1)}, u32[]{:S(2)}, u32[]{:S(2)}) %collective-permute-start.23) | collective-permute-done | bytes 65568 | tf_op jit(solution)/shard_map/ppermute | solution.py:20
  95.8 1.8 collective-permute-start.30
  100.2 1.8 collective-permute-done.30.refs_6_
  110.0 2.8 %collective-permute-done.34 = f32[256,128]{1,0:T(8,128)S(1)} collective-permute-done((f32[256,128]{1,0:T(8,128)S(1)}, f32[256,128]{1,0:T(8,128)S(1)}, u32[]{:S(2)}, u32[]{:S(2)}) %collective-permute-start.34) | collective-permute-done | bytes 131104 | tf_op jit(solution)/shard_map/ppermute | solution.py:20
  112.8 2.5 %collective-permute-done.32 = f32[256,128]{1,0:T(8,128)S(1)} collective-permute-done((f32[256,128]{1,0:T(8,128)S(1)}, f32[256,128]{1,0:T(8,128)S(1)}, u32[]{:S(2)}, u32[]{:S(2)}) %collective-permute-start.32) | collective-permute-done | bytes 131104 | tf_op jit(solution)/shard_map/ppermute | solution.py:20
  120.3 3.5 %collective-permute-done.37.refs_3_ = f32[256,128]{1,0:T(8,128)S(1)} collective-permute-done((f32[256,128]{1,0:T(8,128)S(1)}, f32[256,128]{1,0:T(8,128)S(1)}, u32[]{:S(2)}, u32[]{:S(2)}) %collective-permute-start.37) | collective-permute-done | bytes 131104 | tf_op jit(solution)/shard_map/ppermute | solution.py:20
  128.1 1.9 collective-permute-start.40
  130.0 2.0 %collective-permute-start.39 = (f32[128,128]{1,0:T(8,128)S(1)}, f32[128,128]{1,0:T(8,128)S(1)}, u32[]{:S(2)}, u32[]{:S(2)}) collective-permute-start(f32[128,128]{1,0:T(8,128)S(1)} %get-tuple-element.96), channel_id=1, source_target_pairs={{0,6},{1,7},{2,4},{3,5},{4,2},{5,3},{6,0},{7,1},{8,14},{9,15},{10,... | collective-permute-start | bytes 196616 | tf_op jit(solution)/shard_map/ppermute | solution.py:20
  132.6 3.8 %collective-permute-done.40.refs_3_ = f32[128,128]{1,0:T(8,128)S(1)} collective-permute-done((f32[128,128]{1,0:T(8,128)S(1)}, f32[128,128]{1,0:T(8,128)S(1)}, u32[]{:S(2)}, u32[]{:S(2)}) %collective-permute-start.40) | collective-permute-done | bytes 65568 | tf_op jit(solution)/shard_map/ppermute | solution.py:20
  136.4 11.2 %all_to_all.11.sums_ref = f32[32,8,128]{2,1,0:T(8,128)S(1)} all-to-all(f32[32,8,128]{2,1,0:T(8,128)S(1)} %shard_map.94), channel_id=1, replica_groups=mesh['samp'=4,'chrom'=8] {'samp','chrom'}, dimensions={0} | all-to-all | bytes 262144 | tf_op jit(solution)/shard_map/all_to_all | solution.py:398
  152.0 2.8 %collective-permute-start.43 = (f32[128,128]{1,0:T(8,128)S(1)}, f32[128,128]{1,0:T(8,128)S(1)}, u32[]{:S(2)}, u32[]{:S(2)}) collective-permute-start(f32[128,128]{1,0:T(8,128)S(1)} %get-tuple-element.92), channel_id=1, source_target_pairs={{0,6},{1,7},{2,4},{3,5},{4,2},{5,3},{6,0},{7,1},{8,14},{9,15},{10,... | collective-permute-start | bytes 196616 | tf_op jit(solution)/shard_map/ppermute | solution.py:20
  154.9 2.4 %shard_map.97 = (f32[1024,128]{1,0:T(8,128)S(1)}, f32[1024,128]{1,0:T(8,128)S(1)}) custom-call(f32[1024,128]{1,0:T(8,128)S(1)} %get-tuple-element.80.coef_ref, s32[1024,128]{1,0:T(8,128)S(1)} %broadcast_in_dim.16.refs_8_.mask_ref, bf16[512,1024]{1,0:T(8,128)(2,1)S(1)} %copy-done.4, bf16[512,1024]{1,0:T(8,128)(2,1)S(1)} %copy-done.6, ...), custom_call_target="tpu_custom_call" | custom-call | flops 2147483648 | bytes 8388608 | tf_op jit(solution)/shard_map/pallas_call | solution.py:409
  157.2 2.1 %collective-permute-done.44.refs_2_ = f32[128,128]{1,0:T(8,128)S(1)} collective-permute-done((f32[128,128]{1,0:T(8,128)S(1)}, f32[128,128]{1,0:T(8,128)S(1)}, u32[]{:S(2)}, u32[]{:S(2)}) %collective-permute-start.44) | collective-permute-done | bytes 65568 | tf_op jit(solution)/shard_map/ppermute | solution.py:20
  159.3 1.8 collective-permute-start.51
  163.8 1.8 collective-permute-done.51.refs_6_
  173.7 3.0 %collective-permute-done.55.refs_3_ = f32[272,128]{1,0:T(8,128)S(1)} collective-permute-done((f32[272,128]{1,0:T(8,128)S(1)}, f32[272,128]{1,0:T(8,128)S(1)}, u32[]{:S(2)}, u32[]{:S(2)}) %collective-permute-start.55) | collective-permute-done | bytes 139296 | tf_op jit(solution)/shard_map/ppermute | solution.py:20
  176.7 2.7 %collective-permute-done.53.refs_1_ = f32[272,128]{1,0:T(8,128)S(1)} collective-permute-done((f32[272,128]{1,0:T(8,128)S(1)}, f32[272,128]{1,0:T(8,128)S(1)}, u32[]{:S(2)}, u32[]{:S(2)}) %collective-permute-start.53) | collective-permute-done | bytes 139296 | tf_op jit(solution)/shard_map/ppermute | solution.py:20
  184.6 3.4 %collective-permute-done.58.refs_3_ = f32[256,128]{1,0:T(8,128)S(1)} collective-permute-done((f32[256,128]{1,0:T(8,128)S(1)}, f32[256,128]{1,0:T(8,128)S(1)}, u32[]{:S(2)}, u32[]{:S(2)}) %collective-permute-start.58) | collective-permute-done | bytes 131104 | tf_op jit(solution)/shard_map/ppermute | solution.py:20
  (173 shorter events, 81.8 us)
Async XLA Ops:
  11.4 9.7 %collective-permute-start.3 = (f32[128,128]{1,0:T(8,128)S(1)}, f32[128,128]{1,0:T(8,128)S(1)}, u32[]{:S(2)}, u32[]{:S(2)}) collective-permute-start(f32[128,128]{1,0:T(8,128)S(1)} %get-tuple-element.106), channel_id=1, source_target_pairs={{0,2},{1,3},{2,0},{3,1},{4,6},{5,7},{6,4},{7,5},{8,10},{9,11},{10,... | collective-permute-start | bytes 196616 | tf_op jit(solution)/shard_map/ppermute | solution.py:20
  14.1 7.1 %collective-permute-start.2 = (f32[128,128]{1,0:T(8,128)S(1)}, f32[128,128]{1,0:T(8,128)S(1)}, u32[]{:S(2)}, u32[]{:S(2)}) collective-permute-start(f32[128,128]{1,0:T(8,128)S(1)} %get-tuple-element.107), channel_id=1, source_target_pairs={{0,4},{1,5},{2,6},{3,7},{4,0},{5,1},{6,2},{7,3},{8,12},{9,13},{10,... | collective-permute-start | bytes 196616 | tf_op jit(solution)/shard_map/ppermute | solution.py:20
  16.7 6.1 %collective-permute-start.1 = (f32[128,128]{1,0:T(8,128)S(1)}, f32[128,128]{1,0:T(8,128)S(1)}, u32[]{:S(2)}, u32[]{:S(2)}) collective-permute-start(f32[128,128]{1,0:T(8,128)S(1)} %get-tuple-element.108), channel_id=1, source_target_pairs={{0,6},{1,7},{2,4},{3,5},{4,2},{5,3},{6,0},{7,1},{8,14},{9,15},{10,... | collective-permute-start | bytes 196616 | tf_op jit(solution)/shard_map/ppermute | solution.py:20
  23.1 6.6 %collective-permute-start.9 = (f32[128,128]{1,0:T(8,128)S(1)}, f32[128,128]{1,0:T(8,128)S(1)}, u32[]{:S(2)}, u32[]{:S(2)}) collective-permute-start(f32[128,128]{1,0:T(8,128)S(1)} %shard_map.81.refs_0_), channel_id=1, source_target_pairs={{0,6},{1,7},{2,4},{3,5},{4,2},{5,3},{6,0},{7,1},{8,14},{9,15},{10,... | collective-permute-start | bytes 196616 | tf_op jit(solution)/shard_map/ppermute | solution.py:20
  40.1 6.3 %collective-permute-start.13 = (f32[256,128]{1,0:T(8,128)S(1)}, f32[256,128]{1,0:T(8,128)S(1)}, u32[]{:S(2)}, u32[]{:S(2)}) collective-permute-start(f32[256,128]{1,0:T(8,128)S(1)} %get-tuple-element.63), channel_id=1, source_target_pairs={{0,8},{8,0},{16,24},{24,16},{1,9},{9,1},{17,25},{25,17},{2,10},{10... | collective-permute-start | bytes 393224 | tf_op jit(solution)/shard_map/ppermute | solution.py:20
  41.7 8.0 %collective-permute-start.11 = (f32[256,128]{1,0:T(8,128)S(1)}, f32[256,128]{1,0:T(8,128)S(1)}, u32[]{:S(2)}, u32[]{:S(2)}) collective-permute-start(f32[256,128]{1,0:T(8,128)S(1)} %get-tuple-element.61), channel_id=1, source_target_pairs={{0,24},{8,16},{16,8},{24,0},{1,25},{9,17},{17,9},{25,1},{2,26},{10... | collective-permute-start | bytes 393224 | tf_op jit(solution)/shard_map/ppermute | solution.py:20
  43.2 8.0 %collective-permute-start.12 = (f32[256,128]{1,0:T(8,128)S(1)}, f32[256,128]{1,0:T(8,128)}, u32[]{:S(2)}, u32[]{:S(2)}) collective-permute-start(f32[256,128]{1,0:T(8,128)S(1)} %get-tuple-element.62), channel_id=1, source_target_pairs={{0,16},{8,24},{16,0},{24,8},{1,17},{9,25},{17,1},{25,9},{2,18},{10... | collective-permute-start | bytes 393224 | tf_op jit(solution)/shard_map/ppermute | solution.py:20
  52.1 7.0 %collective-permute-start.16 = (f32[256,128]{1,0:T(8,128)S(1)}, f32[256,128]{1,0:T(8,128)S(1)}, u32[]{:S(2)}, u32[]{:S(2)}) collective-permute-start(f32[256,128]{1,0:T(8,128)S(1)} %add_multiply_fusion.1.refs_0_), channel_id=1, source_target_pairs={{0,24},{8,16},{16,8},{24,0},{1,25},{9,17},{17,9},{25,1},{2,26},{10... | collective-permute-start | bytes 393224 | tf_op jit(solution)/shard_map/ppermute | solution.py:20
  53.6 6.8 %collective-permute-start.15 = (f32[256,128]{1,0:T(8,128)S(1)}, f32[256,128]{1,0:T(8,128)S(1)}, u32[]{:S(2)}, u32[]{:S(2)}) collective-permute-start(f32[256,128]{1,0:T(8,128)S(1)} %add_multiply_fusion.1.refs_0_), channel_id=1, source_target_pairs={{0,16},{8,24},{16,0},{24,8},{1,17},{9,25},{17,1},{25,9},{2,18},{10... | collective-permute-start | bytes 393224 | tf_op jit(solution)/shard_map/ppermute | solution.py:20
  64.1 8.4 %collective-permute-start.19 = (f32[128,128]{1,0:T(8,128)S(1)}, f32[128,128]{1,0:T(8,128)S(1)}, u32[]{:S(2)}, u32[]{:S(2)}) collective-permute-start(f32[128,128]{1,0:T(8,128)S(1)} %get-tuple-element.103), channel_id=1, source_target_pairs={{0,4},{1,5},{2,6},{3,7},{4,0},{5,1},{6,2},{7,3},{8,12},{9,13},{10,... | collective-permute-start | bytes 196616 | tf_op jit(solution)/shard_map/ppermute | solution.py:20
  66.2 6.3 %collective-permute-start.18 = (f32[128,128]{1,0:T(8,128)S(1)}, f32[128,128]{1,0:T(8,128)S(1)}, u32[]{:S(2)}, u32[]{:S(2)}) collective-permute-start(f32[128,128]{1,0:T(8,128)S(1)} %get-tuple-element.104), channel_id=1, source_target_pairs={{0,6},{1,7},{2,4},{3,5},{4,2},{5,3},{6,0},{7,1},{8,14},{9,15},{10,... | collective-permute-start | bytes 196616 | tf_op jit(solution)/shard_map/ppermute | solution.py:20
  87.5 8.3 %collective-permute-start.23 = (f32[128,128]{1,0:T(8,128)S(1)}, f32[128,128]{1,0:T(8,128)S(1)}, u32[]{:S(2)}, u32[]{:S(2)}) collective-permute-start(f32[128,128]{1,0:T(8,128)S(1)} %get-tuple-element.99), channel_id=1, source_target_pairs={{0,4},{1,5},{2,6},{3,7},{4,0},{5,1},{6,2},{7,3},{8,12},{9,13},{10,... | collective-permute-start | bytes 196616 | tf_op jit(solution)/shard_map/ppermute | solution.py:20
  88.4 7.3 %collective-permute-start.22 = (f32[128,128]{1,0:T(8,128)S(1)}, f32[128,128]{1,0:T(8,128)S(1)}, u32[]{:S(2)}, u32[]{:S(2)}) collective-permute-start(f32[128,128]{1,0:T(8,128)S(1)} %get-tuple-element.100), channel_id=1, source_target_pairs={{0,6},{1,7},{2,4},{3,5},{4,2},{5,3},{6,0},{7,1},{8,14},{9,15},{10,... | collective-permute-start | bytes 196616 | tf_op jit(solution)/shard_map/ppermute | solution.py:20
  95.8 6.2 %collective-permute-start.30 = (f32[128,128]{1,0:T(8,128)S(1)}, f32[128,128]{1,0:T(8,128)S(1)}, u32[]{:S(2)}, u32[]{:S(2)}) collective-permute-start(f32[128,128]{1,0:T(8,128)S(1)} %shard_map.89.refs_0_), channel_id=1, source_target_pairs={{0,6},{1,7},{2,4},{3,5},{4,2},{5,3},{6,0},{7,1},{8,14},{9,15},{10,... | collective-permute-start | bytes 196616 | tf_op jit(solution)/shard_map/ppermute | solution.py:20
  106.4 6.4 %collective-permute-start.34 = (f32[256,128]{1,0:T(8,128)S(1)}, f32[256,128]{1,0:T(8,128)S(1)}, u32[]{:S(2)}, u32[]{:S(2)}) collective-permute-start(f32[256,128]{1,0:T(8,128)S(1)} %get-tuple-element.74), channel_id=1, source_target_pairs={{0,8},{8,0},{16,24},{24,16},{1,9},{9,1},{17,25},{25,17},{2,10},{10... | collective-permute-start | bytes 393224 | tf_op jit(solution)/shard_map/ppermute | solution.py:20
  107.3 8.1 %collective-permute-start.32 = (f32[256,128]{1,0:T(8,128)S(1)}, f32[256,128]{1,0:T(8,128)S(1)}, u32[]{:S(2)}, u32[]{:S(2)}) collective-permute-start(f32[256,128]{1,0:T(8,128)S(1)} %get-tuple-element.72), channel_id=1, source_target_pairs={{0,24},{8,16},{16,8},{24,0},{1,25},{9,17},{17,9},{25,1},{2,26},{10... | collective-permute-start | bytes 393224 | tf_op jit(solution)/shard_map/ppermute | solution.py:20
  108.7 8.0 %collective-permute-start.33 = (f32[256,128]{1,0:T(8,128)S(1)}, f32[256,128]{1,0:T(8,128)S(1)}, u32[]{:S(2)}, u32[]{:S(2)}) collective-permute-start(f32[256,128]{1,0:T(8,128)S(1)} %get-tuple-element.73), channel_id=1, source_target_pairs={{0,16},{8,24},{16,0},{24,8},{1,17},{9,25},{17,1},{25,9},{2,18},{10... | collective-permute-start | bytes 393224 | tf_op jit(solution)/shard_map/ppermute | solution.py:20
  116.7 7.0 %collective-permute-start.37 = (f32[256,128]{1,0:T(8,128)S(1)}, f32[256,128]{1,0:T(8,128)S(1)}, u32[]{:S(2)}, u32[]{:S(2)}) collective-permute-start(f32[256,128]{1,0:T(8,128)S(1)} %add_multiply_fusion.refs_0_), channel_id=1, source_target_pairs={{0,24},{8,16},{16,8},{24,0},{1,25},{9,17},{17,9},{25,1},{2,26},{10... | collective-permute-start | bytes 393224 | tf_op jit(solution)/shard_map/ppermute | solution.py:20
  118.3 6.7 %collective-permute-start.36 = (f32[256,128]{1,0:T(8,128)S(1)}, f32[256,128]{1,0:T(8,128)S(1)}, u32[]{:S(2)}, u32[]{:S(2)}) collective-permute-start(f32[256,128]{1,0:T(8,128)S(1)} %add_multiply_fusion.refs_0_), channel_id=1, source_target_pairs={{0,16},{8,24},{16,0},{24,8},{1,17},{9,25},{17,1},{25,9},{2,18},{10... | collective-permute-start | bytes 393224 | tf_op jit(solution)/shard_map/ppermute | solution.py:20
  118.8 6.2 %collective-permute-start.35 = (f32[256,128]{1,0:T(8,128)S(1)}, f32[256,128]{1,0:T(8,128)S(1)}, u32[]{:S(2)}, u32[]{:S(2)}) collective-permute-start(f32[256,128]{1,0:T(8,128)S(1)} %add_multiply_fusion.refs_0_), channel_id=1, source_target_pairs={{0,8},{8,0},{16,24},{24,16},{1,9},{9,1},{17,25},{25,17},{2,10},{10... | collective-permute-start | bytes 393224 | tf_op jit(solution)/shard_map/ppermute | solution.py:20
  128.1 8.3 %collective-permute-start.40 = (f32[128,128]{1,0:T(8,128)S(1)}, f32[128,128]{1,0:T(8,128)S(1)}, u32[]{:S(2)}, u32[]{:S(2)}) collective-permute-start(f32[128,128]{1,0:T(8,128)S(1)} %get-tuple-element.95), channel_id=1, source_target_pairs={{0,4},{1,5},{2,6},{3,7},{4,0},{5,1},{6,2},{7,3},{8,12},{9,13},{10,... | collective-permute-start | bytes 196616 | tf_op jit(solution)/shard_map/ppermute | solution.py:20
  130.0 6.4 %collective-permute-start.39 = (f32[128,128]{1,0:T(8,128)S(1)}, f32[128,128]{1,0:T(8,128)S(1)}, u32[]{:S(2)}, u32[]{:S(2)}) collective-permute-start(f32[128,128]{1,0:T(8,128)S(1)} %get-tuple-element.96), channel_id=1, source_target_pairs={{0,6},{1,7},{2,4},{3,5},{4,2},{5,3},{6,0},{7,1},{8,14},{9,15},{10,... | collective-permute-start | bytes 196616 | tf_op jit(solution)/shard_map/ppermute | solution.py:20
  150.4 6.8 %collective-permute-start.45 = (f32[128,128]{1,0:T(8,128)S(1)}, f32[128,128]{1,0:T(8,128)S(1)}, u32[]{:S(2)}, u32[]{:S(2)}) collective-permute-start(f32[128,128]{1,0:T(8,128)S(1)} %get-tuple-element.90), channel_id=1, source_target_pairs={{0,2},{1,3},{2,0},{3,1},{4,6},{5,7},{6,4},{7,5},{8,10},{9,11},{10,... | collective-permute-start | bytes 196616 | tf_op jit(solution)/shard_map/ppermute | solution.py:20
  151.0 8.3 %collective-permute-start.44 = (f32[128,128]{1,0:T(8,128)S(1)}, f32[128,128]{1,0:T(8,128)S(1)}, u32[]{:S(2)}, u32[]{:S(2)}) collective-permute-start(f32[128,128]{1,0:T(8,128)S(1)} %get-tuple-element.91), channel_id=1, source_target_pairs={{0,4},{1,5},{2,6},{3,7},{4,0},{5,1},{6,2},{7,3},{8,12},{9,13},{10,... | collective-permute-start | bytes 196616 | tf_op jit(solution)/shard_map/ppermute | solution.py:20
  152.0 7.3 %collective-permute-start.43 = (f32[128,128]{1,0:T(8,128)S(1)}, f32[128,128]{1,0:T(8,128)S(1)}, u32[]{:S(2)}, u32[]{:S(2)}) collective-permute-start(f32[128,128]{1,0:T(8,128)S(1)} %get-tuple-element.92), channel_id=1, source_target_pairs={{0,6},{1,7},{2,4},{3,5},{4,2},{5,3},{6,0},{7,1},{8,14},{9,15},{10,... | collective-permute-start | bytes 196616 | tf_op jit(solution)/shard_map/ppermute | solution.py:20
  159.3 6.2 %collective-permute-start.51 = (f32[128,128]{1,0:T(8,128)S(1)}, f32[128,128]{1,0:T(8,128)S(1)}, u32[]{:S(2)}, u32[]{:S(2)}) collective-permute-start(f32[128,128]{1,0:T(8,128)S(1)} %shard_map.98.refs_0_), channel_id=1, source_target_pairs={{0,6},{1,7},{2,4},{3,5},{4,2},{5,3},{6,0},{7,1},{8,14},{9,15},{10,... | collective-permute-start | bytes 196616 | tf_op jit(solution)/shard_map/ppermute | solution.py:20
  170.1 6.6 %collective-permute-start.55 = (f32[272,128]{1,0:T(8,128)S(1)}, f32[272,128]{1,0:T(8,128)S(1)}, u32[]{:S(2)}, u32[]{:S(2)}) collective-permute-start(f32[272,128]{1,0:T(8,128)S(1)} %get-tuple-element.88), channel_id=1, source_target_pairs={{0,8},{8,0},{16,24},{24,16},{1,9},{9,1},{17,25},{25,17},{2,10},{10... | collective-permute-start | bytes 417800 | tf_op jit(solution)/shard_map/ppermute | solution.py:20
  171.0 8.4 %collective-permute-start.53 = (f32[272,128]{1,0:T(8,128)S(1)}, f32[272,128]{1,0:T(8,128)S(1)}, u32[]{:S(2)}, u32[]{:S(2)}) collective-permute-start(f32[272,128]{1,0:T(8,128)S(1)} %get-tuple-element.86), channel_id=1, source_target_pairs={{0,24},{8,16},{16,8},{24,0},{1,25},{9,17},{17,9},{25,1},{2,26},{10... | collective-permute-start | bytes 417800 | tf_op jit(solution)/shard_map/ppermute | solution.py:20
  172.4 8.4 %collective-permute-start.54 = (f32[272,128]{1,0:T(8,128)S(1)}, f32[272,128]{1,0:T(8,128)S(1)}, u32[]{:S(2)}, u32[]{:S(2)}) collective-permute-start(f32[272,128]{1,0:T(8,128)S(1)} %get-tuple-element.87), channel_id=1, source_target_pairs={{0,16},{8,24},{16,0},{24,8},{1,17},{9,25},{17,1},{25,9},{2,18},{10... | collective-permute-start | bytes 417800 | tf_op jit(solution)/shard_map/ppermute | solution.py:20
  181.0 6.9 %collective-permute-start.58 = (f32[256,128]{1,0:T(8,128)S(1)}, f32[256,128]{1,0:T(8,128)S(1)}, u32[]{:S(2)}, u32[]{:S(2)}) collective-permute-start(f32[256,128]{1,0:T(8,128)S(1)} %shard_map.101.refs_0_), channel_id=1, source_target_pairs={{0,24},{8,16},{16,8},{24,0},{1,25},{9,17},{17,9},{25,1},{2,26},{10... | collective-permute-start | bytes 393224 | tf_op jit(solution)/shard_map/ppermute | solution.py:20
  182.6 6.6 %collective-permute-start.57 = (f32[256,128]{1,0:T(8,128)S(1)}, f32[256,128]{1,0:T(8,128)S(1)}, u32[]{:S(2)}, u32[]{:S(2)}) collective-permute-start(f32[256,128]{1,0:T(8,128)S(1)} %shard_map.101.refs_0_), channel_id=1, source_target_pairs={{0,16},{8,24},{16,0},{24,8},{1,17},{9,25},{17,1},{25,9},{2,18},{10... | collective-permute-start | bytes 393224 | tf_op jit(solution)/shard_map/ppermute | solution.py:20
  183.1 6.1 %collective-permute-start.56 = (f32[256,128]{1,0:T(8,128)S(1)}, f32[256,128]{1,0:T(8,128)S(1)}, u32[]{:S(2)}, u32[]{:S(2)}) collective-permute-start(f32[256,128]{1,0:T(8,128)S(1)} %shard_map.101.refs_0_), channel_id=1, source_target_pairs={{0,8},{8,0},{16,24},{24,16},{1,9},{9,1},{17,25},{25,17},{2,10},{10... | collective-permute-start | bytes 393224 | tf_op jit(solution)/shard_map/ppermute | solution.py:20
  (50 other events, 271.4 us)

commit v3 on v2

--- a/solution.py
+++ b/solution.py
@@ -12,7 +12,6 @@
 ITERS = 2
 STATS = 16
 VMEM_LIMIT = 14 * 1024 * 1024
-FIRST_LIMIT = 60 * 1024 * 1024
 
 
 def swap(value, axis, bits):
@@ -49,39 +48,54 @@
     return jax.ShapeDtypeStruct(dims, dtype)
 
 
-def call(kernel, outs, specs, scratch=(), flops=0, moved=0, limit=VMEM_LIMIT):
+def call(kernel, outs, specs, scratch=(), flops=0, moved=0):
     return pl.pallas_call(
         kernel,
         out_shape=outs,
         in_specs=specs,
         out_specs=jax.tree.map(lambda _: whole(), outs),
         scratch_shapes=list(scratch),
-        compiler_params=pltpu.CompilerParams(vmem_limit_bytes=limit),
+        compiler_params=pltpu.CompilerParams(vmem_limit_bytes=VMEM_LIMIT),
         cost_estimate=pl.CostEstimate(flops=flops, bytes_accessed=moved, transcendentals=0),
     )
 
 
-def first_kernel(bits, dosage_ref, coef_ref, high_ref, low_ref, out_ref, *rest):
-    *packed_out, buffer_ref, sems = rest
+def split_rows(source_ref, ready, packed_ref, high_ref, low_ref, out_ref):
+    half, block = source_ref.shape[0], source_ref.shape[1]
+    group = max(1, half // 2)
+    for first in range(0, half, group):
+        for k in range(first, first + group):
+            ready(k)
+            high, low = split(source_ref[k])
+            high_ref[k * block : (k + 1) * block] = high
+            low_ref[k * block : (k + 1) * block] = low
+        rows = slice(first * block, (first + group) * block)
+        total = wide_dot(high_ref[rows], low_ref[rows], packed_ref[...])
+        out_ref[first : first + group] = total.reshape((group,) + out_ref.shape[1:])
+
+
+def first_kernel(dosage_ref, coef_ref, high_ref, low_ref, out_ref, packed_ref, kept_ref, buffer_ref, coef_buffer, sems):
     me = lax.axis_index("chrom")
     place, core = me // 2, me % 2
-    half, block = buffer_ref.shape[0], buffer_ref.shape[1]
+    half = buffer_ref.shape[0]
+    coef_copy = pltpu.make_async_copy(coef_ref, coef_buffer, sems.at[2 * half])
     copies = [
-        pltpu.make_async_copy(dosage_ref.at[place ^ k, core ^ bits], buffer_ref.at[k], sems.at[k]) for k in range(half)
+        pltpu.make_async_copy(dosage_ref.at[place ^ k, core ^ bits], target.at[k], sems.at[bits * half + k])
+        for bits, target in ((1, buffer_ref), (0, kept_ref))
+        for k in range(half)
     ]
+    coef_copy.start()
     for copy in copies:
         copy.start()
-    if packed_out:
-        packed_out[0][...] = pack(coef_ref[...])
-        packed = packed_out[0][...]
-    else:
-        packed = coef_ref[...]
-    for k, copy in enumerate(copies):
+    coef_copy.wait()
+    packed_ref[...] = pack(coef_buffer[...])
+    split_rows(buffer_ref, lambda k: copies[k].wait(), packed_ref, high_ref, low_ref, out_ref)
+    for copy in copies[half:]:
         copy.wait()
-        high, low = split(buffer_ref[k])
-        high_ref[k * block : (k + 1) * block] = high
-        low_ref[k * block : (k + 1) * block] = low
-    out_ref[...] = wide_dot(high_ref[...], low_ref[...], packed).reshape(out_ref.shape)
+
+
+def second_kernel(kept_ref, packed_ref, high_ref, low_ref, out_ref):
+    split_rows(kept_ref, lambda k: None, packed_ref, high_ref, low_ref, out_ref)
 
 
 def turn_kernel(count, *refs):
@@ -184,8 +198,7 @@
     grad = grad_ref[...]
     grad_sq = jnp.sum(grad * grad, axis=0, keepdims=True)
     image_sq = jnp.sum(total * total, axis=0, keepdims=True)
-    row = lax.broadcasted_iota(jnp.int32, out.shape[1:], 0)
-    sums = jnp.where(row == 0, grad_sq, jnp.where(row == 1, image_sq, 0.0))
+    sums = jnp.concatenate([grad_sq, image_sq])
     for place in range(out.shape[0]):
         out[place] = sums
 
@@ -319,7 +332,7 @@
     flops = 4 * rows * cols * n_traits
     moved = 2 * rows * cols
     order = samp_order(n_samp)
-    far, near = order[: n_samp // 2], order[n_samp // 2 :]
+    far, near = order[:-1], order[-1:]
 
     part = shape((rows // 2, cols), jnp.bfloat16)
     half_out = shape((half, block, n_traits))
@@ -328,8 +341,6 @@
     grad_block = shape((width, n_traits))
     score_block = shape((test_width + STATS, n_traits))
     coef_out = shape((cols, n_traits))
-    buffers = [pltpu.VMEM((half, block, cols), jnp.float32), pltpu.SemaphoreType.DMA((half,))]
-
     mask = jnp.broadcast_to((groups - me * GPD)[:, None], (cols, n_traits))
     pick = jnp.broadcast_to((owners - me * GPD)[:, None], (tests, n_traits)).reshape(n_samp, test_width, n_traits)
     own_traits = lax.dynamic_slice_in_dim(traits, me * block, block, 0)
@@ -344,20 +355,20 @@
             [whole()] * (1 + len(summands)) + [anywhere()] * len(after),
         )(own_traits, *summands, *after)
 
-    def first(bits, coefficients, outs):
-        return call(
-            functools.partial(first_kernel, bits),
-            [part, part, half_out] + outs,
-            [pl.BlockSpec(memory_space=pltpu.HBM), whole()],
-            buffers,
-            flops,
-            2 * moved,
-            FIRST_LIMIT,
-        )(dosages.reshape(half, 2, block, cols), coefficients)
-
     coefficients = start_coef
-    high1, low1, give, packed = first(1, coefficients, [packed_cols])
-    high0, low0, keep = first(0, packed, [])
+    kept_shape = (half, block, cols)
+    high1, low1, give, packed, kept = call(
+        first_kernel,
+        [part, part, half_out, packed_cols, shape(kept_shape)],
+        [pl.BlockSpec(memory_space=pltpu.HBM)] * 2,
+        [pltpu.VMEM(kept_shape, jnp.float32), pltpu.VMEM(coefficients.shape, jnp.float32), pltpu.SemaphoreType.DMA((n_chrom + 1,))],
+        flops,
+        4 * moved,
+    )(
+        pltpu.with_memory_space_constraint(dosages.reshape(half, 2, block, cols), pltpu.HBM),
+        pltpu.with_memory_space_constraint(coefficients, pltpu.HBM),
+    )
+    high0, low0, keep = call(second_kernel, [part, part, half_out], [whole()] * 2, (), flops, moved)(kept, packed)
     summands = chrom_scatter(give, keep)
     turns = turned([high0, low0, high1, low1], n_samp, summands[0])
     turn_tested, tested_sq = tested_parts(tested, n_samp)
@@ -393,7 +404,7 @@
         summands = chrom_scatter(give, rest(high0, low0, packed))
         size = n_samp * n_chrom
         sums = call(
-            functools.partial(norm_kernel, half), shape((size, 8, n_traits)), [whole()] * (half + 1)
+            functools.partial(norm_kernel, half), shape((size, 2, n_traits)), [whole()] * (half + 1)
         )(own_grad, *summands)
         sums = lax.all_to_all(sums, ("samp", "chrom"), 0, 0)
         coefficients, packed, give = call(

time: 191 us -> 187 us (0.979)
  local copies, waits for them, and re-layouts: 10.2 us -> 17.7 us
  waiting for transfers between devices: 66.6 us -> 61.5 us
  Pallas kernels: 27.3 us -> 22.4 us
  blocking collectives: 22.5 us -> 20.5 us
    unnamed x46 -> x62, local copies, waits for them, and re-layouts: 9.79 us -> 17.3 us
    pallas_call x4, Pallas kernels: 9.39 us -> 3.87 us  [the longest x1 2.97 us: body(): call(first_kernel, [part, part, half_out, packed_cols, shape(kept_shape)]...]
    ppermute x59, waiting for transfers between devices: 66.6 us -> 61.5 us  [swap(): return lax.ppermute(value, axis, [(i, i ^ bits) for i in range(size)])]
    all_to_all x2, blocking collectives: 22.5 us -> 20.5 us  [body(): sums = lax.all_to_all(sums, ('samp', 'chrom'), 0, 0)]
  transfers between devices with their start and end apart: 59 -> 59, of which waited for: 39 -> 37; matrix products, arithmetic and copies ran while one was open for 0% -> 0% of each run, Pallas kernels for 7% -> 5%
where the time goes in v3:
time: 187 us; the launch traced here: 186 us
  waiting for transfers between devices  61.5 us (33%)
  starting transfers between devices  60.1 us (32%)
  Pallas kernels  22.4 us (12%)
  blocking collectives  20.5 us (11%)
  local copies, waits for them, and re-layouts  17.7 us (9%)
  other arithmetic  2.4 us (1%)
    ppermute x59, waiting for transfers between devices, swap(): return lax.ppermute(value, axis, [(i, i ^ bits) for i in range(size)])  61.5 us
    ppermute x59, starting transfers between devices, swap(): return lax.ppermute(value, axis, [(i, i ^ bits) for i in range(size)])  60.1 us
    all_to_all x2, blocking collectives, body(): sums = lax.all_to_all(sums, ('samp', 'chrom'), 0, 0)  20.5 us
    unnamed x62, local copies, waits for them, and re-layouts  17.3 us
  transfers between devices with their start and end apart: 59, of which 37 were waited for; matrix products, arithmetic and copies ran while one was open for 0% of the time, Pallas kernels for 5%

profile of v3, /device:TPU:0, one launch (start us, length us, event | category | flops | bytes accessed | tf_op | source)
XLA Modules:
  0.0 185.8 jit_solution(2301222696551890034)
XLA Ops:
  0.6 3.0 %shard_map.78 = (bf16[512,1024]{1,0:T(8,128)(2,1)S(1)}, bf16[512,1024]{1,0:T(8,128)(2,1)S(1)}, f32[4,128,128]{2,1,0:T(8,128)S(1)}, bf16[1024,256]{1,0:T(8,128)(2,1)S(1)}, f32[4,128,1024]{2,1,0:T(8,128)S(1)}) custom-call(f32[4,2,128,1024]{3,2,1,0:T(8,128)} %bitcast.41, f32[1024,128]{1,0:T(8,128)} %coef_ref.3), custom_call_target="tpu_custom_call" | custom-call | flops 536870912 | bytes 8388608 | tf_op jit(solution)/shard_map/pallas_call | solution.py:360
  9.1 2.6 %collective-permute-start.3 = (f32[128,128]{1,0:T(8,128)S(1)}, f32[128,128]{1,0:T(8,128)S(1)}, u32[]{:S(2)}, u32[]{:S(2)}) collective-permute-start(f32[128,128]{1,0:T(8,128)S(1)} %get-tuple-element.102), channel_id=1, source_target_pairs={{0,2},{1,3},{2,0},{3,1},{4,6},{5,7},{6,4},{7,5},{8,10},{9,11},{10,... | collective-permute-start | bytes 196616 | tf_op jit(solution)/shard_map/ppermute | solution.py:19
  11.7 2.6 %collective-permute-start.2 = (f32[128,128]{1,0:T(8,128)S(1)}, f32[128,128]{1,0:T(8,128)S(1)}, u32[]{:S(2)}, u32[]{:S(2)}) collective-permute-start(f32[128,128]{1,0:T(8,128)S(1)} %get-tuple-element.103), channel_id=1, source_target_pairs={{0,4},{1,5},{2,6},{3,7},{4,0},{5,1},{6,2},{7,3},{8,12},{9,13},{10,... | collective-permute-start | bytes 196616 | tf_op jit(solution)/shard_map/ppermute | solution.py:19
  14.4 1.9 %shard_map.80 = (bf16[4,256,512]{2,1,0:T(8,128)(2,1)S(1)}, bf16[4,256,512]{2,1,0:T(8,128)(2,1)S(1)}, bf16[4,256,512]{2,1,0:T(8,128)(2,1)S(1)}, bf16[4,256,512]{2,1,0:T(8,128)(2,1)S(1)}) custom-call(bf16[512,1024]{1,0:T(8,128)(2,1)S(1)} %get-tuple-element.48.refs_0_.high_ref, bf16[512,1024]{1,0:T(8,128)(2,1)S(1)} %get-tuple-element.49.refs_1_.low_ref, ...), custom_call_target="tpu_custom_call" | custom-call | bytes 16777216 | tf_op jit(solution)/shard_map/pallas_call | solution.py:109
  16.4 2.3 %collective-permute-done.2.refs_2_ = f32[128,128]{1,0:T(8,128)S(1)} collective-permute-done((f32[128,128]{1,0:T(8,128)S(1)}, f32[128,128]{1,0:T(8,128)S(1)}, u32[]{:S(2)}, u32[]{:S(2)}) %collective-permute-start.2) | collective-permute-done | bytes 65568 | tf_op jit(solution)/shard_map/ppermute | solution.py:19
  18.7 1.8 collective-permute-done.1.refs_1_
  20.5 2.5 %collective-permute-start.9 = (f32[128,128]{1,0:T(8,128)S(1)}, f32[128,128]{1,0:T(8,128)S(1)}, u32[]{:S(2)}, u32[]{:S(2)}) collective-permute-start(f32[128,128]{1,0:T(8,128)S(1)} %shard_map.81.refs_0_), channel_id=1, source_target_pairs={{0,6},{1,7},{2,4},{3,5},{4,2},{5,3},{6,0},{7,1},{8,14},{9,15},{10,... | collective-permute-start | bytes 196616 | tf_op jit(solution)/shard_map/ppermute | solution.py:19
  25.0 2.2 %collective-permute-done.9.refs_6_ = f32[128,128]{1,0:T(8,128)S(1)} collective-permute-done((f32[128,128]{1,0:T(8,128)S(1)}, f32[128,128]{1,0:T(8,128)S(1)}, u32[]{:S(2)}, u32[]{:S(2)}) %collective-permute-start.9) | collective-permute-done | bytes 65568 | tf_op jit(solution)/shard_map/ppermute | solution.py:19
  27.2 2.0 %collective-permute-done.7.refs_4_ = f32[128,128]{1,0:T(8,128)S(1)} collective-permute-done((f32[128,128]{1,0:T(8,128)S(1)}, f32[128,128]{1,0:T(8,128)S(1)}, u32[]{:S(2)}, u32[]{:S(2)}) %collective-permute-start.7) | collective-permute-done | bytes 65568 | tf_op jit(solution)/shard_map/ppermute | solution.py:19
  40.8 2.4 %collective-permute-start.11 = (f32[256,128]{1,0:T(8,128)}, f32[256,128]{1,0:T(8,128)S(1)}, u32[]{:S(2)}, u32[]{:S(2)}) collective-permute-start(f32[256,128]{1,0:T(8,128)} %get-tuple-element.59), channel_id=1, source_target_pairs={{0,24},{8,16},{16,8},{24,0},{1,25},{9,17},{17,9},{25,1},{2,26},{10... | collective-permute-start | bytes 393224 | tf_op jit(solution)/shard_map/ppermute | solution.py:19
  51.4 2.5 %collective-permute-start.16 = (f32[256,128]{1,0:T(8,128)S(1)}, f32[256,128]{1,0:T(8,128)S(1)}, u32[]{:S(2)}, u32[]{:S(2)}) collective-permute-start(f32[256,128]{1,0:T(8,128)S(1)} %add_multiply_fusion.1.refs_0_), channel_id=1, source_target_pairs={{0,24},{8,16},{16,8},{24,0},{1,25},{9,17},{17,9},{25,1},{2,26},{10... | collective-permute-start | bytes 393224 | tf_op jit(solution)/shard_map/ppermute | solution.py:19
  54.9 3.8 %collective-permute-done.16.refs_3_ = f32[256,128]{1,0:T(8,128)S(1)} collective-permute-done((f32[256,128]{1,0:T(8,128)S(1)}, f32[256,128]{1,0:T(8,128)S(1)}, u32[]{:S(2)}, u32[]{:S(2)}) %collective-permute-start.16) | collective-permute-done | bytes 131104 | tf_op jit(solution)/shard_map/ppermute | solution.py:19
  58.7 1.8 collective-permute-done.15.refs_2_
  63.8 2.3 %collective-permute-start.19 = (f32[128,128]{1,0:T(8,128)S(1)}, f32[128,128]{1,0:T(8,128)S(1)}, u32[]{:S(2)}, u32[]{:S(2)}) collective-permute-start(f32[128,128]{1,0:T(8,128)S(1)} %get-tuple-element.99), channel_id=1, source_target_pairs={{0,4},{1,5},{2,6},{3,7},{4,0},{5,1},{6,2},{7,3},{8,12},{9,13},{10,... | collective-permute-start | bytes 196616 | tf_op jit(solution)/shard_map/ppermute | solution.py:19
  68.5 3.9 %collective-permute-done.19.refs_3_ = f32[128,128]{1,0:T(8,128)S(1)} collective-permute-done((f32[128,128]{1,0:T(8,128)S(1)}, f32[128,128]{1,0:T(8,128)S(1)}, u32[]{:S(2)}, u32[]{:S(2)}) %collective-permute-start.19) | collective-permute-done | bytes 65568 | tf_op jit(solution)/shard_map/ppermute | solution.py:19
  72.5 10.3 %all_to_all.10.sums_ref = f32[32,2,128]{2,1,0:T(2,128)S(1)} all-to-all(f32[32,2,128]{2,1,0:T(2,128)S(1)} %shard_map.86), channel_id=1, replica_groups=mesh['samp'=4,'chrom'=8] {'samp','chrom'}, dimensions={0} | all-to-all | bytes 65536 | tf_op jit(solution)/shard_map/all_to_all | solution.py:409
  86.8 3.3 %collective-permute-start.22 = (f32[128,128]{1,0:T(8,128)S(1)}, f32[128,128]{1,0:T(8,128)S(1)}, u32[]{:S(2)}, u32[]{:S(2)}) collective-permute-start(f32[128,128]{1,0:T(8,128)S(1)} %get-tuple-element.96), channel_id=1, source_target_pairs={{0,6},{1,7},{2,4},{3,5},{4,2},{5,3},{6,0},{7,1},{8,14},{9,15},{10,... | collective-permute-start | bytes 196616 | tf_op jit(solution)/shard_map/ppermute | solution.py:19
  90.6 3.8 %collective-permute-done.23.refs_2_ = f32[128,128]{1,0:T(8,128)S(1)} collective-permute-done((f32[128,128]{1,0:T(8,128)S(1)}, f32[128,128]{1,0:T(8,128)S(1)}, u32[]{:S(2)}, u32[]{:S(2)}) %collective-permute-start.23) | collective-permute-done | bytes 65568 | tf_op jit(solution)/shard_map/ppermute | solution.py:19
  94.5 1.8 collective-permute-start.30
  108.7 3.3 %collective-permute-done.32 = f32[256,128]{1,0:T(8,128)S(1)} collective-permute-done((f32[256,128]{1,0:T(8,128)S(1)}, f32[256,128]{1,0:T(8,128)S(1)}, u32[]{:S(2)}, u32[]{:S(2)}) %collective-permute-start.32) | collective-permute-done | bytes 131104 | tf_op jit(solution)/shard_map/ppermute | solution.py:19
  117.3 3.5 %collective-permute-done.37.refs_3_ = f32[256,128]{1,0:T(8,128)S(1)} collective-permute-done((f32[256,128]{1,0:T(8,128)S(1)}, f32[256,128]{1,0:T(8,128)S(1)}, u32[]{:S(2)}, u32[]{:S(2)}) %collective-permute-start.37) | collective-permute-done | bytes 131104 | tf_op jit(solution)/shard_map/ppermute | solution.py:19
  125.7 1.8 collective-permute-start.40
  127.6 2.0 %collective-permute-start.39 = (f32[128,128]{1,0:T(8,128)S(1)}, f32[128,128]{1,0:T(8,128)S(1)}, u32[]{:S(2)}, u32[]{:S(2)}) collective-permute-start(f32[128,128]{1,0:T(8,128)S(1)} %get-tuple-element.92), channel_id=1, source_target_pairs={{0,6},{1,7},{2,4},{3,5},{4,2},{5,3},{6,0},{7,1},{8,14},{9,15},{10,... | collective-permute-start | bytes 196616 | tf_op jit(solution)/shard_map/ppermute | solution.py:19
  130.1 3.9 %collective-permute-done.40.refs_3_ = f32[128,128]{1,0:T(8,128)S(1)} collective-permute-done((f32[128,128]{1,0:T(8,128)S(1)}, f32[128,128]{1,0:T(8,128)S(1)}, u32[]{:S(2)}, u32[]{:S(2)}) %collective-permute-start.40) | collective-permute-done | bytes 65568 | tf_op jit(solution)/shard_map/ppermute | solution.py:19
  134.1 10.3 %all_to_all.11.sums_ref = f32[32,2,128]{2,1,0:T(2,128)S(1)} all-to-all(f32[32,2,128]{2,1,0:T(2,128)S(1)} %shard_map.94), channel_id=1, replica_groups=mesh['samp'=4,'chrom'=8] {'samp','chrom'}, dimensions={0} | all-to-all | bytes 65536 | tf_op jit(solution)/shard_map/all_to_all | solution.py:409
  148.4 3.3 %collective-permute-start.43 = (f32[128,128]{1,0:T(8,128)S(1)}, f32[128,128]{1,0:T(8,128)S(1)}, u32[]{:S(2)}, u32[]{:S(2)}) collective-permute-start(f32[128,128]{1,0:T(8,128)S(1)} %get-tuple-element.88), channel_id=1, source_target_pairs={{0,6},{1,7},{2,4},{3,5},{4,2},{5,3},{6,0},{7,1},{8,14},{9,15},{10,... | collective-permute-start | bytes 196616 | tf_op jit(solution)/shard_map/ppermute | solution.py:19
  151.6 2.4 %shard_map.97 = (f32[1024,128]{1,0:T(8,128)S(1)}, f32[1024,128]{1,0:T(8,128)S(1)}) custom-call(f32[1024,128]{1,0:T(8,128)S(1)} %get-tuple-element.77.coef_ref, s32[1024,128]{1,0:T(8,128)S(1)} %broadcast_in_dim.16.refs_8_.mask_ref, bf16[512,1024]{1,0:T(8,128)(2,1)S(1)} %copy-done.16, bf16[512,1024]{1,0:T(8,128)(2,1)S(1)} %copy-done.18, ...), custom_call_target="tpu_custom_call" | custom-call | flops 2147483648 | bytes 8388608 | tf_op jit(solution)/shard_map/pallas_call | solution.py:420
  154.0 2.0 %collective-permute-done.44.refs_2_ = f32[128,128]{1,0:T(8,128)S(1)} collective-permute-done((f32[128,128]{1,0:T(8,128)S(1)}, f32[128,128]{1,0:T(8,128)S(1)}, u32[]{:S(2)}, u32[]{:S(2)}) %collective-permute-start.44) | collective-permute-done | bytes 65568 | tf_op jit(solution)/shard_map/ppermute | solution.py:19
  156.0 1.8 collective-permute-start.51
  170.4 3.6 %collective-permute-done.53.refs_1_ = f32[272,128]{1,0:T(8,128)S(1)} collective-permute-done((f32[272,128]{1,0:T(8,128)S(1)}, f32[272,128]{1,0:T(8,128)S(1)}, u32[]{:S(2)}, u32[]{:S(2)}) %collective-permute-start.53) | collective-permute-done | bytes 139296 | tf_op jit(solution)/shard_map/ppermute | solution.py:19
  174.0 1.8 collective-permute-done.54.refs_2_
  179.6 3.5 %collective-permute-done.58.refs_3_ = f32[256,128]{1,0:T(8,128)S(1)} collective-permute-done((f32[256,128]{1,0:T(8,128)S(1)}, f32[256,128]{1,0:T(8,128)S(1)}, u32[]{:S(2)}, u32[]{:S(2)}) %collective-permute-start.58) | collective-permute-done | bytes 131104 | tf_op jit(solution)/shard_map/ppermute | solution.py:19
  (189 shorter events, 84.6 us)
Async XLA Ops:
  9.1 7.2 %collective-permute-start.3 = (f32[128,128]{1,0:T(8,128)S(1)}, f32[128,128]{1,0:T(8,128)S(1)}, u32[]{:S(2)}, u32[]{:S(2)}) collective-permute-start(f32[128,128]{1,0:T(8,128)S(1)} %get-tuple-element.102), channel_id=1, source_target_pairs={{0,2},{1,3},{2,0},{3,1},{4,6},{5,7},{6,4},{7,5},{8,10},{9,11},{10,... | collective-permute-start | bytes 196616 | tf_op jit(solution)/shard_map/ppermute | solution.py:19
  11.7 6.9 %collective-permute-start.2 = (f32[128,128]{1,0:T(8,128)S(1)}, f32[128,128]{1,0:T(8,128)S(1)}, u32[]{:S(2)}, u32[]{:S(2)}) collective-permute-start(f32[128,128]{1,0:T(8,128)S(1)} %get-tuple-element.103), channel_id=1, source_target_pairs={{0,4},{1,5},{2,6},{3,7},{4,0},{5,1},{6,2},{7,3},{8,12},{9,13},{10,... | collective-permute-start | bytes 196616 | tf_op jit(solution)/shard_map/ppermute | solution.py:19
  20.5 6.6 %collective-permute-start.9 = (f32[128,128]{1,0:T(8,128)S(1)}, f32[128,128]{1,0:T(8,128)S(1)}, u32[]{:S(2)}, u32[]{:S(2)}) collective-permute-start(f32[128,128]{1,0:T(8,128)S(1)} %shard_map.81.refs_0_), channel_id=1, source_target_pairs={{0,6},{1,7},{2,4},{3,5},{4,2},{5,3},{6,0},{7,1},{8,14},{9,15},{10,... | collective-permute-start | bytes 196616 | tf_op jit(solution)/shard_map/ppermute | solution.py:19
  23.0 6.2 %collective-permute-start.7 = (f32[128,128]{1,0:T(8,128)S(1)}, f32[128,128]{1,0:T(8,128)S(1)}, u32[]{:S(2)}, u32[]{:S(2)}) collective-permute-start(f32[128,128]{1,0:T(8,128)S(1)} %shard_map.81.refs_0_), channel_id=1, source_target_pairs={{0,4},{1,5},{2,6},{3,7},{4,0},{5,1},{6,2},{7,3},{8,12},{9,13},{10,... | collective-permute-start | bytes 196616 | tf_op jit(solution)/shard_map/ppermute | solution.py:19
  40.8 9.5 %collective-permute-start.11 = (f32[256,128]{1,0:T(8,128)}, f32[256,128]{1,0:T(8,128)S(1)}, u32[]{:S(2)}, u32[]{:S(2)}) collective-permute-start(f32[256,128]{1,0:T(8,128)} %get-tuple-element.59), channel_id=1, source_target_pairs={{0,24},{8,16},{16,8},{24,0},{1,25},{9,17},{17,9},{25,1},{2,26},{10... | collective-permute-start | bytes 393224 | tf_op jit(solution)/shard_map/ppermute | solution.py:19
  43.3 7.1 %collective-permute-start.12 = (f32[256,128]{1,0:T(8,128)}, f32[256,128]{1,0:T(8,128)S(1)}, u32[]{:S(2)}, u32[]{:S(2)}) collective-permute-start(f32[256,128]{1,0:T(8,128)} %get-tuple-element.60), channel_id=1, source_target_pairs={{0,16},{8,24},{16,0},{24,8},{1,17},{9,25},{17,1},{25,9},{2,18},{10... | collective-permute-start | bytes 393224 | tf_op jit(solution)/shard_map/ppermute | solution.py:19
  43.7 6.7 %collective-permute-start.13 = (f32[256,128]{1,0:T(8,128)}, f32[256,128]{1,0:T(8,128)}, u32[]{:S(2)}, u32[]{:S(2)}) collective-permute-start(f32[256,128]{1,0:T(8,128)} %get-tuple-element.61), channel_id=1, source_target_pairs={{0,8},{8,0},{16,24},{24,16},{1,9},{9,1},{17,25},{25,17},{2,10},{10... | collective-permute-start | bytes 393224 | tf_op jit(solution)/shard_map/ppermute | solution.py:19
  51.4 7.3 %collective-permute-start.16 = (f32[256,128]{1,0:T(8,128)S(1)}, f32[256,128]{1,0:T(8,128)S(1)}, u32[]{:S(2)}, u32[]{:S(2)}) collective-permute-start(f32[256,128]{1,0:T(8,128)S(1)} %add_multiply_fusion.1.refs_0_), channel_id=1, source_target_pairs={{0,24},{8,16},{16,8},{24,0},{1,25},{9,17},{17,9},{25,1},{2,26},{10... | collective-permute-start | bytes 393224 | tf_op jit(solution)/shard_map/ppermute | solution.py:19
  53.8 6.7 %collective-permute-start.15 = (f32[256,128]{1,0:T(8,128)S(1)}, f32[256,128]{1,0:T(8,128)S(1)}, u32[]{:S(2)}, u32[]{:S(2)}) collective-permute-start(f32[256,128]{1,0:T(8,128)S(1)} %add_multiply_fusion.1.refs_0_), channel_id=1, source_target_pairs={{0,16},{8,24},{16,0},{24,8},{1,17},{9,25},{17,1},{25,9},{2,18},{10... | collective-permute-start | bytes 393224 | tf_op jit(solution)/shard_map/ppermute | solution.py:19
  63.8 8.6 %collective-permute-start.19 = (f32[128,128]{1,0:T(8,128)S(1)}, f32[128,128]{1,0:T(8,128)S(1)}, u32[]{:S(2)}, u32[]{:S(2)}) collective-permute-start(f32[128,128]{1,0:T(8,128)S(1)} %get-tuple-element.99), channel_id=1, source_target_pairs={{0,4},{1,5},{2,6},{3,7},{4,0},{5,1},{6,2},{7,3},{8,12},{9,13},{10,... | collective-permute-start | bytes 196616 | tf_op jit(solution)/shard_map/ppermute | solution.py:19
  66.1 6.3 %collective-permute-start.18 = (f32[128,128]{1,0:T(8,128)S(1)}, f32[128,128]{1,0:T(8,128)S(1)}, u32[]{:S(2)}, u32[]{:S(2)}) collective-permute-start(f32[128,128]{1,0:T(8,128)S(1)} %get-tuple-element.100), channel_id=1, source_target_pairs={{0,6},{1,7},{2,4},{3,5},{4,2},{5,3},{6,0},{7,1},{8,14},{9,15},{10,... | collective-permute-start | bytes 196616 | tf_op jit(solution)/shard_map/ppermute | solution.py:19
  86.2 8.3 %collective-permute-start.23 = (f32[128,128]{1,0:T(8,128)S(1)}, f32[128,128]{1,0:T(8,128)S(1)}, u32[]{:S(2)}, u32[]{:S(2)}) collective-permute-start(f32[128,128]{1,0:T(8,128)S(1)} %get-tuple-element.95), channel_id=1, source_target_pairs={{0,4},{1,5},{2,6},{3,7},{4,0},{5,1},{6,2},{7,3},{8,12},{9,13},{10,... | collective-permute-start | bytes 196616 | tf_op jit(solution)/shard_map/ppermute | solution.py:19
  86.8 7.7 %collective-permute-start.22 = (f32[128,128]{1,0:T(8,128)S(1)}, f32[128,128]{1,0:T(8,128)S(1)}, u32[]{:S(2)}, u32[]{:S(2)}) collective-permute-start(f32[128,128]{1,0:T(8,128)S(1)} %get-tuple-element.96), channel_id=1, source_target_pairs={{0,6},{1,7},{2,4},{3,5},{4,2},{5,3},{6,0},{7,1},{8,14},{9,15},{10,... | collective-permute-start | bytes 196616 | tf_op jit(solution)/shard_map/ppermute | solution.py:19
  94.5 6.2 %collective-permute-start.30 = (f32[128,128]{1,0:T(8,128)S(1)}, f32[128,128]{1,0:T(8,128)S(1)}, u32[]{:S(2)}, u32[]{:S(2)}) collective-permute-start(f32[128,128]{1,0:T(8,128)S(1)} %shard_map.89.refs_0_), channel_id=1, source_target_pairs={{0,6},{1,7},{2,4},{3,5},{4,2},{5,3},{6,0},{7,1},{8,14},{9,15},{10,... | collective-permute-start | bytes 196616 | tf_op jit(solution)/shard_map/ppermute | solution.py:19
  104.7 7.3 %collective-permute-start.32 = (f32[256,128]{1,0:T(8,128)S(1)}, f32[256,128]{1,0:T(8,128)S(1)}, u32[]{:S(2)}, u32[]{:S(2)}) collective-permute-start(f32[256,128]{1,0:T(8,128)S(1)} %get-tuple-element.69), channel_id=1, source_target_pairs={{0,24},{8,16},{16,8},{24,0},{1,25},{9,17},{17,9},{25,1},{2,26},{10... | collective-permute-start | bytes 393224 | tf_op jit(solution)/shard_map/ppermute | solution.py:19
  105.4 8.3 %collective-permute-start.33 = (f32[256,128]{1,0:T(8,128)S(1)}, f32[256,128]{1,0:T(8,128)S(1)}, u32[]{:S(2)}, u32[]{:S(2)}) collective-permute-start(f32[256,128]{1,0:T(8,128)S(1)} %get-tuple-element.70), channel_id=1, source_target_pairs={{0,16},{8,24},{16,0},{24,8},{1,17},{9,25},{17,1},{25,9},{2,18},{10... | collective-permute-start | bytes 393224 | tf_op jit(solution)/shard_map/ppermute | solution.py:19
  106.8 6.9 %collective-permute-start.34 = (f32[256,128]{1,0:T(8,128)S(1)}, f32[256,128]{1,0:T(8,128)S(1)}, u32[]{:S(2)}, u32[]{:S(2)}) collective-permute-start(f32[256,128]{1,0:T(8,128)S(1)} %get-tuple-element.71), channel_id=1, source_target_pairs={{0,8},{8,0},{16,24},{24,16},{1,9},{9,1},{17,25},{25,17},{2,10},{10... | collective-permute-start | bytes 393224 | tf_op jit(solution)/shard_map/ppermute | solution.py:19
  113.7 7.1 %collective-permute-start.37 = (f32[256,128]{1,0:T(8,128)S(1)}, f32[256,128]{1,0:T(8,128)S(1)}, u32[]{:S(2)}, u32[]{:S(2)}) collective-permute-start(f32[256,128]{1,0:T(8,128)S(1)} %add_multiply_fusion.refs_0_), channel_id=1, source_target_pairs={{0,24},{8,16},{16,8},{24,0},{1,25},{9,17},{17,9},{25,1},{2,26},{10... | collective-permute-start | bytes 393224 | tf_op jit(solution)/shard_map/ppermute | solution.py:19
  114.9 7.4 %collective-permute-start.36 = (f32[256,128]{1,0:T(8,128)S(1)}, f32[256,128]{1,0:T(8,128)S(1)}, u32[]{:S(2)}, u32[]{:S(2)}) collective-permute-start(f32[256,128]{1,0:T(8,128)S(1)} %add_multiply_fusion.refs_0_), channel_id=1, source_target_pairs={{0,16},{8,24},{16,0},{24,8},{1,17},{9,25},{17,1},{25,9},{2,18},{10... | collective-permute-start | bytes 393224 | tf_op jit(solution)/shard_map/ppermute | solution.py:19
  116.4 6.2 %collective-permute-start.35 = (f32[256,128]{1,0:T(8,128)S(1)}, f32[256,128]{1,0:T(8,128)S(1)}, u32[]{:S(2)}, u32[]{:S(2)}) collective-permute-start(f32[256,128]{1,0:T(8,128)S(1)} %add_multiply_fusion.refs_0_), channel_id=1, source_target_pairs={{0,8},{8,0},{16,24},{24,16},{1,9},{9,1},{17,25},{25,17},{2,10},{10... | collective-permute-start | bytes 393224 | tf_op jit(solution)/shard_map/ppermute | solution.py:19
  125.7 8.3 %collective-permute-start.40 = (f32[128,128]{1,0:T(8,128)S(1)}, f32[128,128]{1,0:T(8,128)S(1)}, u32[]{:S(2)}, u32[]{:S(2)}) collective-permute-start(f32[128,128]{1,0:T(8,128)S(1)} %get-tuple-element.91), channel_id=1, source_target_pairs={{0,4},{1,5},{2,6},{3,7},{4,0},{5,1},{6,2},{7,3},{8,12},{9,13},{10,... | collective-permute-start | bytes 196616 | tf_op jit(solution)/shard_map/ppermute | solution.py:19
  127.6 6.5 %collective-permute-start.39 = (f32[128,128]{1,0:T(8,128)S(1)}, f32[128,128]{1,0:T(8,128)S(1)}, u32[]{:S(2)}, u32[]{:S(2)}) collective-permute-start(f32[128,128]{1,0:T(8,128)S(1)} %get-tuple-element.92), channel_id=1, source_target_pairs={{0,6},{1,7},{2,4},{3,5},{4,2},{5,3},{6,0},{7,1},{8,14},{9,15},{10,... | collective-permute-start | bytes 196616 | tf_op jit(solution)/shard_map/ppermute | solution.py:19
  147.2 6.8 %collective-permute-start.45 = (f32[128,128]{1,0:T(8,128)S(1)}, f32[128,128]{1,0:T(8,128)S(1)}, u32[]{:S(2)}, u32[]{:S(2)}) collective-permute-start(f32[128,128]{1,0:T(8,128)S(1)} %get-tuple-element.86), channel_id=1, source_target_pairs={{0,2},{1,3},{2,0},{3,1},{4,6},{5,7},{6,4},{7,5},{8,10},{9,11},{10,... | collective-permute-start | bytes 196616 | tf_op jit(solution)/shard_map/ppermute | solution.py:19
  147.8 8.3 %collective-permute-start.44 = (f32[128,128]{1,0:T(8,128)S(1)}, f32[128,128]{1,0:T(8,128)S(1)}, u32[]{:S(2)}, u32[]{:S(2)}) collective-permute-start(f32[128,128]{1,0:T(8,128)S(1)} %get-tuple-element.87), channel_id=1, source_target_pairs={{0,4},{1,5},{2,6},{3,7},{4,0},{5,1},{6,2},{7,3},{8,12},{9,13},{10,... | collective-permute-start | bytes 196616 | tf_op jit(solution)/shard_map/ppermute | solution.py:19
  148.4 7.7 %collective-permute-start.43 = (f32[128,128]{1,0:T(8,128)S(1)}, f32[128,128]{1,0:T(8,128)S(1)}, u32[]{:S(2)}, u32[]{:S(2)}) collective-permute-start(f32[128,128]{1,0:T(8,128)S(1)} %get-tuple-element.88), channel_id=1, source_target_pairs={{0,6},{1,7},{2,4},{3,5},{4,2},{5,3},{6,0},{7,1},{8,14},{9,15},{10,... | collective-permute-start | bytes 196616 | tf_op jit(solution)/shard_map/ppermute | solution.py:19
  156.0 6.2 %collective-permute-start.51 = (f32[128,128]{1,0:T(8,128)S(1)}, f32[128,128]{1,0:T(8,128)S(1)}, u32[]{:S(2)}, u32[]{:S(2)}) collective-permute-start(f32[128,128]{1,0:T(8,128)S(1)} %shard_map.98.refs_0_), channel_id=1, source_target_pairs={{0,6},{1,7},{2,4},{3,5},{4,2},{5,3},{6,0},{7,1},{8,14},{9,15},{10,... | collective-permute-start | bytes 196616 | tf_op jit(solution)/shard_map/ppermute | solution.py:19
  166.6 7.4 %collective-permute-start.53 = (f32[272,128]{1,0:T(8,128)S(1)}, f32[272,128]{1,0:T(8,128)S(1)}, u32[]{:S(2)}, u32[]{:S(2)}) collective-permute-start(f32[272,128]{1,0:T(8,128)S(1)} %get-tuple-element.82), channel_id=1, source_target_pairs={{0,24},{8,16},{16,8},{24,0},{1,25},{9,17},{17,9},{25,1},{2,26},{10... | collective-permute-start | bytes 417800 | tf_op jit(solution)/shard_map/ppermute | solution.py:19
  167.2 8.6 %collective-permute-start.54 = (f32[272,128]{1,0:T(8,128)S(1)}, f32[272,128]{1,0:T(8,128)S(1)}, u32[]{:S(2)}, u32[]{:S(2)}) collective-permute-start(f32[272,128]{1,0:T(8,128)S(1)} %get-tuple-element.83), channel_id=1, source_target_pairs={{0,16},{8,24},{16,0},{24,8},{1,17},{9,25},{17,1},{25,9},{2,18},{10... | collective-permute-start | bytes 417800 | tf_op jit(solution)/shard_map/ppermute | solution.py:19
  168.6 7.2 %collective-permute-start.55 = (f32[272,128]{1,0:T(8,128)S(1)}, f32[272,128]{1,0:T(8,128)S(1)}, u32[]{:S(2)}, u32[]{:S(2)}) collective-permute-start(f32[272,128]{1,0:T(8,128)S(1)} %get-tuple-element.84), channel_id=1, source_target_pairs={{0,8},{8,0},{16,24},{24,16},{1,9},{9,1},{17,25},{25,17},{2,10},{10... | collective-permute-start | bytes 417800 | tf_op jit(solution)/shard_map/ppermute | solution.py:19
  176.1 7.1 %collective-permute-start.58 = (f32[256,128]{1,0:T(8,128)S(1)}, f32[256,128]{1,0:T(8,128)S(1)}, u32[]{:S(2)}, u32[]{:S(2)}) collective-permute-start(f32[256,128]{1,0:T(8,128)S(1)} %shard_map.101.refs_0_), channel_id=1, source_target_pairs={{0,24},{8,16},{16,8},{24,0},{1,25},{9,17},{17,9},{25,1},{2,26},{10... | collective-permute-start | bytes 393224 | tf_op jit(solution)/shard_map/ppermute | solution.py:19
  177.3 7.4 %collective-permute-start.57 = (f32[256,128]{1,0:T(8,128)S(1)}, f32[256,128]{1,0:T(8,128)S(1)}, u32[]{:S(2)}, u32[]{:S(2)}) collective-permute-start(f32[256,128]{1,0:T(8,128)S(1)} %shard_map.101.refs_0_), channel_id=1, source_target_pairs={{0,16},{8,24},{16,0},{24,8},{1,17},{9,25},{17,1},{25,9},{2,18},{10... | collective-permute-start | bytes 393224 | tf_op jit(solution)/shard_map/ppermute | solution.py:19
  178.7 6.2 %collective-permute-start.56 = (f32[256,128]{1,0:T(8,128)S(1)}, f32[256,128]{1,0:T(8,128)S(1)}, u32[]{:S(2)}, u32[]{:S(2)}) collective-permute-start(f32[256,128]{1,0:T(8,128)S(1)} %shard_map.101.refs_0_), channel_id=1, source_target_pairs={{0,8},{8,0},{16,24},{24,16},{1,9},{9,1},{17,25},{25,17},{2,10},{10... | collective-permute-start | bytes 393224 | tf_op jit(solution)/shard_map/ppermute | solution.py:19
  (58 other events, 231.6 us)

commit v4 on v3

--- a/solution.py
+++ b/solution.py
@@ -11,7 +11,7 @@
 GPD = 2
 ITERS = 2
 STATS = 16
-VMEM_LIMIT = 14 * 1024 * 1024
+VMEM_LIMIT = 10 * 1024 * 1024
 
 
 def swap(value, axis, bits):
@@ -98,47 +98,21 @@
     split_rows(kept_ref, lambda k: None, packed_ref, high_ref, low_ref, out_ref)
 
 
-def turn_kernel(count, *refs):
-    for source, target in zip(refs[:count], refs[-count:]):
-        target[0] = source[...].T
-
-
-def turned(parts, blocks, after):
-    rows, cols = parts[0].shape
-    width = cols // blocks
-    return pl.pallas_call(
-        functools.partial(turn_kernel, len(parts)),
-        grid=(blocks,),
-        in_specs=[pl.BlockSpec((rows, width), lambda step: (0, step))] * len(parts) + [anywhere()],
-        out_specs=[pl.BlockSpec((1, width, rows), lambda step: (step, 0, 0))] * len(parts),
-        out_shape=[shape((blocks, width, rows), jnp.bfloat16)] * len(parts),
-        compiler_params=pltpu.CompilerParams(vmem_limit_bytes=VMEM_LIMIT),
-        cost_estimate=pl.CostEstimate(flops=0, bytes_accessed=8 * rows * cols * len(parts), transcendentals=0),
-    )(*parts, after)
-
-
-def tested_kernel(tested_ref, turned_ref, square_ref):
-    value = tested_ref[...]
-    turned_ref[0] = value.T
-    wide = value.astype(jnp.float32)
-    square_ref[0] = jnp.sum(wide * wide, axis=0).reshape(square_ref.shape[1:])
-
-
-def tested_parts(tested, blocks):
-    rows, cols = tested.shape
-    width = cols // blocks
-    return pl.pallas_call(
-        tested_kernel,
-        grid=(blocks,),
-        in_specs=[pl.BlockSpec((rows, width), lambda step: (0, step))],
-        out_specs=[
-            pl.BlockSpec((1, width, rows), lambda step: (step, 0, 0)),
-            pl.BlockSpec((1, width // 128, 128), lambda step: (step, 0, 0)),
-        ],
-        out_shape=[shape((blocks, width, rows), jnp.bfloat16), shape((blocks, width // 128, 128))],
-        compiler_params=pltpu.CompilerParams(vmem_limit_bytes=VMEM_LIMIT),
-        cost_estimate=pl.CostEstimate(flops=0, bytes_accessed=8 * rows * cols, transcendentals=0),
-    )(tested)
+def square_kernel(tested_ref, square_ref):
+    for place in range(square_ref.shape[0]):
+        width = square_ref.shape[1] * square_ref.shape[2]
+        value = tested_ref[:, place * width : (place + 1) * width].astype(jnp.float32)
+        square_ref[place] = jnp.sum(value * value, axis=0).reshape(square_ref.shape[1:])
+
+
+def column(row):
+    down = lax.broadcasted_iota(jnp.int32, (128, 128), 0)
+    across = lax.broadcasted_iota(jnp.int32, (128, 128), 1)
+    return jnp.sum(jnp.where(down == across, row, 0.0), axis=1, keepdims=True)
+
+
+def columns(ref):
+    return jnp.concatenate([column(ref[k : k + 1]) for k in range(ref.shape[0])])
 
 
 def rest_kernel(high_ref, low_ref, packed_ref, out_ref):
@@ -152,28 +126,36 @@
     refs[-1][...] = traits_ref[...] - total
 
 
-def grad_dot(turn_refs, packed_ref, which):
-    half = packed_ref.shape[0] // 2
-    own = wide_dot(turn_refs[0][which], turn_refs[1][which], packed_ref[0:half])
-    return own + wide_dot(turn_refs[2][which], turn_refs[3][which], packed_ref[half:])
+def grad_dot(packed_ref, parts, which, width):
+    half = packed_ref.shape[1] // 2
+    cols = pl.ds(pl.multiple_of(which * width, width), width)
+    total = None
+    for place, part in enumerate(parts):
+        left = packed_ref[:, (place // 2) * half : (place // 2 + 1) * half]
+        term = jnp.dot(left, part[:, cols], preferred_element_type=jnp.float32)
+        total = term if total is None else total + term
+    traits = packed_ref.shape[0] // 2
+    return (total[:traits] + total[traits:]).T
 
 
 def grad_far_kernel(count, partners, *refs):
-    pieces, turn_refs, (packed_ref, *outs) = refs[:count], refs[count : count + 4], refs[count + 4 :]
+    pieces, parts, (packed_ref, *outs) = refs[:count], refs[count : count + 4], refs[count + 4 : -1]
+    rows_ref = refs[-1]
     samp = lax.axis_index("samp")
     block = pieces[0].shape[0]
     for bits, piece in enumerate(pieces):
         start = ((bits % 2) * (count // 2) + bits // 2) * block
-        packed_ref[start : start + block] = pack(piece[...])
+        rows_ref[start : start + block] = pack(piece[...])
+    packed_ref[...] = rows_ref[...].T
     for partner, out in zip(partners, outs):
-        out[...] = grad_dot(turn_refs, packed_ref, samp ^ partner)
+        out[...] = grad_dot(packed_ref, parts, samp ^ partner, out.shape[0])
 
 
 def grad_near_kernel(partners, *refs):
-    packed_ref, turn_refs, outs = refs[0], refs[1:5], refs[5:]
+    packed_ref, parts, outs = refs[0], refs[1:5], refs[5:]
     samp = lax.axis_index("samp")
     for partner, out in zip(partners, outs):
-        out[...] = grad_dot(turn_refs, packed_ref, samp ^ partner)
+        out[...] = grad_dot(packed_ref, parts, samp ^ partner, out.shape[0])
 
 
 def image_kernel(count, *refs):
@@ -220,34 +202,36 @@
     rest_kernel(high_ref, low_ref, packed_ref, give_ref)
 
 
-def own_kernel(coef_ref, mask_ref, *refs):
+def own_kernel(coef_ref, group_ref, *refs):
     parts, outs = refs[:4], refs[4:]
     coef = coef_ref[...]
-    mask = mask_ref[...]
+    base = lax.axis_index("chrom") * GPD
+    local = columns((group_ref[...] - base).astype(jnp.float32))
     half = parts[0].shape[0]
     for which, out in enumerate(outs):
-        packed = pack(jnp.where(mask == which, coef, 0.0))
+        packed = pack(jnp.where(local == which, coef, 0.0))
         out[0:half] = wide_dot(parts[0][...], parts[1][...], packed)
         out[half:] = wide_dot(parts[2][...], parts[3][...], packed)
 
 
-def score_products(partner, out, tested_ref, square_ref, pick_ref, loco_ref, sums_ref):
-    cols, traits = tested_ref.shape[1], out.shape[1]
-    products = jnp.dot(tested_ref[partner], loco_ref[...], preferred_element_type=jnp.float32)
-    pick = pick_ref[partner]
-    chosen = products[:, :traits]
+def score_products(partner, out, tested_ref, square_ref, owner_ref, loco_ref, sums_ref):
+    width, traits = out.shape[0] - STATS, out.shape[1]
+    cols = pl.ds(pl.multiple_of(partner * width, width), width)
+    products = jnp.dot(loco_ref[...], tested_ref[:, cols], preferred_element_type=jnp.float32)
+    local = owner_ref[partner] - lax.axis_index("chrom") * GPD
+    chosen = products[:traits]
     for which in range(1, GPD):
-        chosen = jnp.where(pick == which, products[:, which * traits : (which + 1) * traits], chosen)
-    out[0:cols] = chosen
-    out[cols : cols + 8] = sums_ref[...]
-    out[cols + 8 : cols + STATS] = jnp.zeros((STATS - 8, traits), jnp.float32)
-    out[cols + 8 : cols + 8 + square_ref.shape[1]] = square_ref[partner]
+        chosen = jnp.where(local == which, products[which * traits : (which + 1) * traits], chosen)
+    out[0:width] = chosen.T
+    out[width : width + 8] = sums_ref[...]
+    out[width + 8 : width + STATS] = jnp.zeros((STATS - 8, traits), jnp.float32)
+    out[width + 8 : width + 8 + square_ref.shape[1]] = square_ref[partner]
 
 
 def loco_kernel(count, partners, *refs):
     pieces, own_refs = refs[:count], refs[count : count + GPD]
-    tested_ref, square_ref, pick_ref, residual_ref, loco_ref, sums_ref = refs[count + GPD : count + GPD + 6]
-    outs = refs[count + GPD + 6 :]
+    tested_ref, square_ref, owner_ref, residual_ref, loco_ref, sums_ref = refs[count + GPD : count + GPD + 6]
+    outs, rows_ref = refs[count + GPD + 6 : -1], refs[-1]
     me, samp = lax.axis_index("chrom"), lax.axis_index("samp")
     block, traits = pieces[0].shape
     sums_ref[...] = jnp.zeros_like(sums_ref)
@@ -259,9 +243,10 @@
         for which in range(GPD):
             loco = value + own_refs[which][start : start + block]
             sums_ref[which : which + 1] += jnp.sum(loco * loco, axis=0, keepdims=True)
-            loco_ref[rows, which * traits : (which + 1) * traits] = loco.astype(jnp.bfloat16)
+            rows_ref[rows, which * traits : (which + 1) * traits] = loco.astype(jnp.bfloat16)
+    loco_ref[...] = rows_ref[...].T
     for partner, out in zip(partners, outs):
-        score_products(samp ^ partner, out, tested_ref, square_ref, pick_ref, loco_ref, sums_ref)
+        score_products(samp ^ partner, out, tested_ref, square_ref, owner_ref, loco_ref, sums_ref)
 
 
 def loco_near_kernel(partners, *refs):
@@ -270,22 +255,19 @@
         score_products(samp ^ partner, out, *refs[:5])
 
 
-def score_kernel(total_rows, pick_ref, *refs):
+def score_kernel(total_rows, owner_ref, *refs):
     pieces, out = refs[:-1], refs[-1]
     total = pieces[0][...]
     for piece in pieces[1:]:
         total = total + piece[...]
     cols, traits = out.shape
-    pick = pick_ref[lax.axis_index("samp")]
+    base = lax.axis_index("chrom") * GPD
+    owner = (owner_ref[lax.axis_index("samp")] - base).astype(jnp.float32)
+    local = jnp.concatenate([column(owner[:, k * 128 : (k + 1) * 128]) for k in range(cols // 128)])
     loco_sq = jnp.broadcast_to(total[cols : cols + 1], (cols, traits))
     for which in range(1, GPD):
-        loco_sq = jnp.where(pick == which, total[cols + which : cols + which + 1], loco_sq)
-    diagonal = lax.broadcasted_iota(jnp.int32, (128, 128), 0) == lax.broadcasted_iota(jnp.int32, (128, 128), 1)
-    columns = []
-    for row in range(cols // 128):
-        squares = total[cols + 8 + row : cols + 9 + row, :128]
-        columns.append(jnp.sum(jnp.where(diagonal, squares, 0.0), axis=1, keepdims=True))
-    tested_sq = jnp.concatenate(columns)
+        loco_sq = jnp.where(local == which, total[cols + which : cols + which + 1], loco_sq)
+    tested_sq = columns(total[cols + 8 : cols + 8 + cols // 128])
     denom = math.sqrt(total_rows) * jnp.sqrt((tested_sq / total_rows + 1e-06) * (loco_sq / total_rows + 1e-06))
     out[...] = total[:cols] / denom
 
@@ -337,12 +319,13 @@
     part = shape((rows // 2, cols), jnp.bfloat16)
     half_out = shape((half, block, n_traits))
     packed_cols = shape((cols, 2 * n_traits), jnp.bfloat16)
-    packed_rows = shape((rows, 2 * n_traits), jnp.bfloat16)
+    packed_rows = shape((2 * n_traits, rows), jnp.bfloat16)
+    rows_buffer = [pltpu.VMEM((rows, 2 * n_traits), jnp.bfloat16)]
     grad_block = shape((width, n_traits))
     score_block = shape((test_width + STATS, n_traits))
     coef_out = shape((cols, n_traits))
-    mask = jnp.broadcast_to((groups - me * GPD)[:, None], (cols, n_traits))
-    pick = jnp.broadcast_to((owners - me * GPD)[:, None], (tests, n_traits)).reshape(n_samp, test_width, n_traits)
+    group_rows = groups.reshape(cols // 128, 128)
+    owner_rows = owners.reshape(n_samp, 1, test_width)
     own_traits = lax.dynamic_slice_in_dim(traits, me * block, block, 0)
 
     def rest(high, low, packed):
@@ -370,29 +353,29 @@
     )
     high0, low0, keep = call(second_kernel, [part, part, half_out], [whole()] * 2, (), flops, moved)(kept, packed)
     summands = chrom_scatter(give, keep)
-    turns = turned([high0, low0, high1, low1], n_samp, summands[0])
-    turn_tested, tested_sq = tested_parts(tested, n_samp)
+    parts = [high0, low0, high1, low1]
+    tested_sq = call(square_kernel, shape((n_samp, test_width // 128, 128)), [whole()], (), 0, 2 * rows * tests)(tested)
 
     for iteration in range(ITERS):
-        own = own_residual(summands, turns if iteration == 0 else ())
+        own = own_residual(summands)
         pieces = chrom_gather(own)
         packed, *far_out = call(
             functools.partial(grad_far_kernel, n_chrom, far),
             [packed_rows] + [grad_block] * len(far),
             [whole()] * (n_chrom + 4),
-            (),
+            rows_buffer,
             flops,
             moved,
-        )(*pieces, *turns)
+        )(*pieces, *parts)
         near_out = call(
             functools.partial(grad_near_kernel, near), [grad_block] * len(near), [whole()] * 5, (), flops, moved
-        )(packed, *turns)
+        )(packed, *parts)
         own_grad = near_out[-1]
         for partner, piece in zip(order, far_out + list(near_out[:-1])):
             own_grad = own_grad + swap(piece, "samp", partner)
         own_grad = own_grad / total_rows
         pieces = samp_gather(own_grad)
-        after = (turn_tested, tested_sq, mask, pick) if iteration == 0 else ()
+        after = (tested_sq,) if iteration == 0 else ()
         gradient, packed, give = call(
             functools.partial(image_kernel, n_samp),
             [coef_out, packed_cols, half_out],
@@ -418,25 +401,25 @@
         summands = chrom_scatter(give, rest(high0, low0, packed))
 
     own_parts = call(own_kernel, [shape((rows, n_traits))] * GPD, [whole()] * 6, (), 4 * flops, 4 * moved)(
-        coefficients, mask, high0, low0, high1, low1
+        coefficients, group_rows, *parts
     )
     pieces = chrom_gather(own_residual(summands, own_parts))
     residual, loco, loco_sq, *far_out = call(
         functools.partial(loco_kernel, n_chrom, far),
-        [shape((rows, n_traits)), shape((rows, GPD * n_traits), jnp.bfloat16), shape((8, n_traits))]
+        [shape((rows, n_traits)), shape((GPD * n_traits, rows), jnp.bfloat16), shape((8, n_traits))]
         + [score_block] * len(far),
         [whole()] * (n_chrom + GPD + 3),
-        (),
+        [pltpu.VMEM((rows, GPD * n_traits), jnp.bfloat16)],
         flops,
         moved,
-    )(*pieces, *own_parts, turn_tested, tested_sq, pick)
+    )(*pieces, *own_parts, tested, tested_sq, owner_rows)
     near_out = call(
         functools.partial(loco_near_kernel, near), [score_block] * len(near), [whole()] * 5, (), flops // 2, moved
-    )(turn_tested, tested_sq, pick, loco, loco_sq)
+    )(tested, tested_sq, owner_rows, loco, loco_sq)
     received = [swap(piece, "samp", partner) for partner, piece in zip(order, far_out + list(near_out[:-1]))]
     own_scores = call(
         functools.partial(score_kernel, total_rows), shape((test_width, n_traits)), [whole()] * (n_samp + 1)
-    )(pick, near_out[-1], *received)
+    )(owner_rows, near_out[-1], *received)
     scores = call(place_kernel, shape((tests, n_traits)), [whole()] * n_samp)(*samp_gather(own_scores))
     return (scores, residual)
 

time: 187 us -> 175 us (0.936)
  local copies, waits for them, and re-layouts: 17.7 us -> 2.94 us
  waiting for transfers between devices: 61.5 us -> 69.9 us
  Pallas kernels: 22.4 us -> 19.8 us
    unnamed x62 -> x14, local copies, waits for them, and re-layouts: 17.3 us -> 2.93 us
    ppermute x59, waiting for transfers between devices: 61.5 us -> 69.9 us  [swap(): return lax.ppermute(value, axis, [(i, i ^ bits) for i in range(size)])]
    pallas_call x2 -> x1, Pallas kernels: 3.04 us -> 0.1 us  [body(): call(square_kernel, shape((n_samp, test_width // 128, 128)), [whole()], (...]
  transfers between devices with their start and end apart: 59 -> 59, of which waited for: 37 -> 41; matrix products, arithmetic and copies ran while one was open for 0% -> 0% of each run, Pallas kernels for 5% -> 4%
where the time goes in v4:
time: 175 us
  waiting for transfers between devices  69.9 us (40%)
  starting transfers between devices  59.7 us (34%)
  blocking collectives  20.5 us (12%)
  Pallas kernels  19.8 us (11%)
  local copies, waits for them, and re-layouts  2.94 us (2%)
    ppermute x59, waiting for transfers between devices, swap(): return lax.ppermute(value, axis, [(i, i ^ bits) for i in range(size)])  69.9 us
    ppermute x59, starting transfers between devices, swap(): return lax.ppermute(value, axis, [(i, i ^ bits) for i in range(size)])  59.7 us
    all_to_all x2, blocking collectives, body(): sums = lax.all_to_all(sums, ('samp', 'chrom'), 0, 0)  20.5 us
  transfers between devices with their start and end apart: 59, of which 41 were waited for; matrix products, arithmetic and copies ran while one was open for 0% of the time, Pallas kernels for 4%

profile of v4, /device:TPU:0, one launch (start us, length us, event | category | flops | bytes accessed | tf_op | source)
XLA Modules:
  0.0 174.9 jit_solution(10263557006396785002)
XLA Ops:
  0.6 3.0 %shard_map.78 = (bf16[512,1024]{1,0:T(8,128)(2,1)S(1)}, bf16[512,1024]{1,0:T(8,128)(2,1)S(1)}, f32[4,128,128]{2,1,0:T(8,128)S(1)}, bf16[1024,256]{1,0:T(8,128)(2,1)S(1)}, f32[4,128,1024]{2,1,0:T(8,128)S(1)}) custom-call(f32[4,2,128,1024]{3,2,1,0:T(8,128)} %bitcast.47, f32[1024,128]{1,0:T(8,128)} %coef_ref.3), custom_call_target="tpu_custom_call" | custom-call | flops 536870912 | bytes 8388608 | tf_op jit(solution)/shard_map/pallas_call | solution.py:343
  8.8 4.7 %collective-permute-start.1 = (f32[128,128]{1,0:T(8,128)S(1)}, f32[128,128]{1,0:T(8,128)S(1)}, u32[]{:S(2)}, u32[]{:S(2)}) collective-permute-start(f32[128,128]{1,0:T(8,128)S(1)} %get-tuple-element.92), channel_id=1, source_target_pairs={{0,6},{1,7},{2,4},{3,5},{4,2},{5,3},{6,0},{7,1},{8,14},{9,15},{10,... | collective-permute-start | bytes 196616 | tf_op jit(solution)/shard_map/ppermute | solution.py:19
  14.1 2.3 %collective-permute-done.1.refs_1_ = f32[128,128]{1,0:T(8,128)S(1)} collective-permute-done((f32[128,128]{1,0:T(8,128)S(1)}, f32[128,128]{1,0:T(8,128)S(1)}, u32[]{:S(2)}, u32[]{:S(2)}) %collective-permute-start.1) | collective-permute-done | bytes 65568 | tf_op jit(solution)/shard_map/ppermute | solution.py:19
  16.4 3.2 %collective-permute-done.2.refs_2_ = f32[128,128]{1,0:T(8,128)S(1)} collective-permute-done((f32[128,128]{1,0:T(8,128)S(1)}, f32[128,128]{1,0:T(8,128)S(1)}, u32[]{:S(2)}, u32[]{:S(2)}) %collective-permute-start.2) | collective-permute-done | bytes 65568 | tf_op jit(solution)/shard_map/ppermute | solution.py:19
  19.6 2.5 %collective-permute-start.9 = (f32[128,128]{1,0:T(8,128)S(1)}, f32[128,128]{1,0:T(8,128)S(1)}, u32[]{:S(2)}, u32[]{:S(2)}) collective-permute-start(f32[128,128]{1,0:T(8,128)S(1)} %shard_map.80.refs_0_), channel_id=1, source_target_pairs={{0,6},{1,7},{2,4},{3,5},{4,2},{5,3},{6,0},{7,1},{8,14},{9,15},{10,... | collective-permute-start | bytes 196616 | tf_op jit(solution)/shard_map/ppermute | solution.py:19
  22.1 1.9 %collective-permute-start.7 = (f32[128,128]{1,0:T(8,128)S(1)}, f32[128,128]{1,0:T(8,128)S(1)}, u32[]{:S(2)}, u32[]{:S(2)}) collective-permute-start(f32[128,128]{1,0:T(8,128)S(1)} %shard_map.80.refs_0_), channel_id=1, source_target_pairs={{0,4},{1,5},{2,6},{3,7},{4,0},{5,1},{6,2},{7,3},{8,12},{9,13},{10,... | collective-permute-start | bytes 196616 | tf_op jit(solution)/shard_map/ppermute | solution.py:19
  24.0 2.0 %collective-permute-done.9.refs_6_ = f32[128,128]{1,0:T(8,128)S(1)} collective-permute-done((f32[128,128]{1,0:T(8,128)S(1)}, f32[128,128]{1,0:T(8,128)S(1)}, u32[]{:S(2)}, u32[]{:S(2)}) %collective-permute-start.9) | collective-permute-done | bytes 65568 | tf_op jit(solution)/shard_map/ppermute | solution.py:19
  30.4 2.5 %collective-permute-start.11 = (f32[256,128]{1,0:T(8,128)S(1)}, f32[256,128]{1,0:T(8,128)S(1)}, u32[]{:S(2)}, u32[]{:S(2)}) collective-permute-start(f32[256,128]{1,0:T(8,128)S(1)} %get-tuple-element.47), channel_id=1, source_target_pairs={{0,24},{8,16},{16,8},{24,0},{1,25},{9,17},{17,9},{25,1},{2,26},{10... | collective-permute-start | bytes 393224 | tf_op jit(solution)/shard_map/ppermute | solution.py:19
  34.5 2.7 %collective-permute-done.11 = f32[256,128]{1,0:T(8,128)S(1)} collective-permute-done((f32[256,128]{1,0:T(8,128)S(1)}, f32[256,128]{1,0:T(8,128)S(1)}, u32[]{:S(2)}, u32[]{:S(2)}) %collective-permute-start.11) | collective-permute-done | bytes 131104 | tf_op jit(solution)/shard_map/ppermute | solution.py:19
  37.2 2.5 %collective-permute-done.12 = f32[256,128]{1,0:T(8,128)S(1)} collective-permute-done((f32[256,128]{1,0:T(8,128)S(1)}, f32[256,128]{1,0:T(8,128)S(1)}, u32[]{:S(2)}, u32[]{:S(2)}) %collective-permute-start.12) | collective-permute-done | bytes 131104 | tf_op jit(solution)/shard_map/ppermute | solution.py:19
  43.5 2.1 %collective-permute-done.14.refs_1_ = f32[256,128]{1,0:T(8,128)S(1)} collective-permute-done((f32[256,128]{1,0:T(8,128)S(1)}, f32[256,128]{1,0:T(8,128)S(1)}, u32[]{:S(2)}, u32[]{:S(2)}) %collective-permute-start.14) | collective-permute-done | bytes 131104 | tf_op jit(solution)/shard_map/ppermute | solution.py:19
  45.6 3.7 %collective-permute-done.15.refs_2_ = f32[256,128]{1,0:T(8,128)S(1)} collective-permute-done((f32[256,128]{1,0:T(8,128)S(1)}, f32[256,128]{1,0:T(8,128)S(1)}, u32[]{:S(2)}, u32[]{:S(2)}) %collective-permute-start.15) | collective-permute-done | bytes 131104 | tf_op jit(solution)/shard_map/ppermute | solution.py:19
  51.8 1.8 %collective-permute-start.18 = (f32[128,128]{1,0:T(8,128)S(1)}, f32[128,128]{1,0:T(8,128)S(1)}, u32[]{:S(2)}, u32[]{:S(2)}) collective-permute-start(f32[128,128]{1,0:T(8,128)S(1)} %get-tuple-element.88), channel_id=1, source_target_pairs={{0,6},{1,7},{2,4},{3,5},{4,2},{5,3},{6,0},{7,1},{8,14},{9,15},{10,... | collective-permute-start | bytes 196616 | tf_op jit(solution)/shard_map/ppermute | solution.py:19
  56.2 2.4 %collective-permute-done.18.refs_2_ = f32[128,128]{1,0:T(8,128)S(1)} collective-permute-done((f32[128,128]{1,0:T(8,128)S(1)}, f32[128,128]{1,0:T(8,128)S(1)}, u32[]{:S(2)}, u32[]{:S(2)}) %collective-permute-start.18) | collective-permute-done | bytes 65568 | tf_op jit(solution)/shard_map/ppermute | solution.py:19
  58.6 2.4 %collective-permute-done.19.refs_3_ = f32[128,128]{1,0:T(8,128)S(1)} collective-permute-done((f32[128,128]{1,0:T(8,128)S(1)}, f32[128,128]{1,0:T(8,128)S(1)}, u32[]{:S(2)}, u32[]{:S(2)}) %collective-permute-start.19) | collective-permute-done | bytes 65568 | tf_op jit(solution)/shard_map/ppermute | solution.py:19
  61.1 10.1 %all_to_all.10.sums_ref = f32[32,2,128]{2,1,0:T(2,128)S(1)} all-to-all(f32[32,2,128]{2,1,0:T(2,128)S(1)} %shard_map.85), channel_id=1, replica_groups=mesh['samp'=4,'chrom'=8] {'samp','chrom'}, dimensions={0} | all-to-all | bytes 65536 | tf_op jit(solution)/shard_map/all_to_all | solution.py:392
  76.0 2.4 %collective-permute-start.24 = (f32[128,128]{1,0:T(8,128)S(1)}, f32[128,128]{1,0:T(8,128)S(1)}, u32[]{:S(2)}, u32[]{:S(2)}) collective-permute-start(f32[128,128]{1,0:T(8,128)S(1)} %get-tuple-element.82), channel_id=1, source_target_pairs={{0,2},{1,3},{2,0},{3,1},{4,6},{5,7},{6,4},{7,5},{8,10},{9,11},{10,... | collective-permute-start | bytes 196616 | tf_op jit(solution)/shard_map/ppermute | solution.py:19
  78.5 2.4 %collective-permute-done.22.refs_1_ = f32[128,128]{1,0:T(8,128)S(1)} collective-permute-done((f32[128,128]{1,0:T(8,128)S(1)}, f32[128,128]{1,0:T(8,128)S(1)}, u32[]{:S(2)}, u32[]{:S(2)}) %collective-permute-start.22) | collective-permute-done | bytes 65568 | tf_op jit(solution)/shard_map/ppermute | solution.py:19
  84.6 2.4 %collective-permute-start.30 = (f32[128,128]{1,0:T(8,128)S(1)}, f32[128,128]{1,0:T(8,128)S(1)}, u32[]{:S(2)}, u32[]{:S(2)}) collective-permute-start(f32[128,128]{1,0:T(8,128)S(1)} %shard_map.88.refs_0_), channel_id=1, source_target_pairs={{0,6},{1,7},{2,4},{3,5},{4,2},{5,3},{6,0},{7,1},{8,14},{9,15},{10,... | collective-permute-start | bytes 196616 | tf_op jit(solution)/shard_map/ppermute | solution.py:19
  87.5 2.4 %collective-permute-done.28.refs_4_ = f32[128,128]{1,0:T(8,128)S(1)} collective-permute-done((f32[128,128]{1,0:T(8,128)S(1)}, f32[128,128]{1,0:T(8,128)S(1)}, u32[]{:S(2)}, u32[]{:S(2)}) %collective-permute-start.28) | collective-permute-done | bytes 65568 | tf_op jit(solution)/shard_map/ppermute | solution.py:19
  97.1 3.3 %collective-permute-done.32 = f32[256,128]{1,0:T(8,128)S(1)} collective-permute-done((f32[256,128]{1,0:T(8,128)S(1)}, f32[256,128]{1,0:T(8,128)S(1)}, u32[]{:S(2)}, u32[]{:S(2)}) %collective-permute-start.32) | collective-permute-done | bytes 131104 | tf_op jit(solution)/shard_map/ppermute | solution.py:19
  107.2 3.9 %collective-permute-done.36.refs_2_ = f32[256,128]{1,0:T(8,128)S(1)} collective-permute-done((f32[256,128]{1,0:T(8,128)S(1)}, f32[256,128]{1,0:T(8,128)S(1)}, u32[]{:S(2)}, u32[]{:S(2)}) %collective-permute-start.36) | collective-permute-done | bytes 131104 | tf_op jit(solution)/shard_map/ppermute | solution.py:19
  113.5 2.5 %collective-permute-start.39 = (f32[128,128]{1,0:T(8,128)S(1)}, f32[128,128]{1,0:T(8,128)S(1)}, u32[]{:S(2)}, u32[]{:S(2)}) collective-permute-start(f32[128,128]{1,0:T(8,128)S(1)} %get-tuple-element.80), channel_id=1, source_target_pairs={{0,6},{1,7},{2,4},{3,5},{4,2},{5,3},{6,0},{7,1},{8,14},{9,15},{10,... | collective-permute-start | bytes 196616 | tf_op jit(solution)/shard_map/ppermute | solution.py:19
  118.0 2.4 %collective-permute-done.39.refs_2_ = f32[128,128]{1,0:T(8,128)S(1)} collective-permute-done((f32[128,128]{1,0:T(8,128)S(1)}, f32[128,128]{1,0:T(8,128)S(1)}, u32[]{:S(2)}, u32[]{:S(2)}) %collective-permute-start.39) | collective-permute-done | bytes 65568 | tf_op jit(solution)/shard_map/ppermute | solution.py:19
  120.3 2.3 %collective-permute-done.40.refs_3_ = f32[128,128]{1,0:T(8,128)S(1)} collective-permute-done((f32[128,128]{1,0:T(8,128)S(1)}, f32[128,128]{1,0:T(8,128)S(1)}, u32[]{:S(2)}, u32[]{:S(2)}) %collective-permute-start.40) | collective-permute-done | bytes 65568 | tf_op jit(solution)/shard_map/ppermute | solution.py:19
  122.7 10.5 %all_to_all.11.sums_ref = f32[32,2,128]{2,1,0:T(2,128)S(1)} all-to-all(f32[32,2,128]{2,1,0:T(2,128)S(1)} %shard_map.93), channel_id=1, replica_groups=mesh['samp'=4,'chrom'=8] {'samp','chrom'}, dimensions={0} | all-to-all | bytes 65536 | tf_op jit(solution)/shard_map/all_to_all | solution.py:392
  138.1 2.4 %collective-permute-start.45 = (f32[128,128]{1,0:T(8,128)S(1)}, f32[128,128]{1,0:T(8,128)S(1)}, u32[]{:S(2)}, u32[]{:S(2)}) collective-permute-start(f32[128,128]{1,0:T(8,128)S(1)} %get-tuple-element.74), channel_id=1, source_target_pairs={{0,2},{1,3},{2,0},{3,1},{4,6},{5,7},{6,4},{7,5},{8,10},{9,11},{10,... | collective-permute-start | bytes 196616 | tf_op jit(solution)/shard_map/ppermute | solution.py:19
  140.5 2.5 %shard_map.96 = (f32[1024,128]{1,0:T(8,128)S(1)}, f32[1024,128]{1,0:T(8,128)S(1)}) custom-call(f32[1024,128]{1,0:T(8,128)S(1)} %get-tuple-element.65.coef_ref, s32[8,128]{1,0:T(8,128)S(1)} %bitcast.46, bf16[512,1024]{1,0:T(8,128)(2,1)S(1)} %get-tuple-element.40.refs_8_.refs_1_.high_ref.refs_0_, ...), custom_call_target="tpu_custom_call" | custom-call | flops 2147483648 | bytes 8388608 | tf_op jit(solution)/shard_map/pallas_call | solution.py:403
  146.6 2.4 %collective-permute-start.51 = (f32[128,128]{1,0:T(8,128)S(1)}, f32[128,128]{1,0:T(8,128)S(1)}, u32[]{:S(2)}, u32[]{:S(2)}) collective-permute-start(f32[128,128]{1,0:T(8,128)S(1)} %shard_map.97.refs_0_), channel_id=1, source_target_pairs={{0,6},{1,7},{2,4},{3,5},{4,2},{5,3},{6,0},{7,1},{8,14},{9,15},{10,... | collective-permute-start | bytes 196616 | tf_op jit(solution)/shard_map/ppermute | solution.py:19
  149.5 2.4 %collective-permute-done.49.refs_4_ = f32[128,128]{1,0:T(8,128)S(1)} collective-permute-done((f32[128,128]{1,0:T(8,128)S(1)}, f32[128,128]{1,0:T(8,128)S(1)}, u32[]{:S(2)}, u32[]{:S(2)}) %collective-permute-start.49) | collective-permute-done | bytes 65568 | tf_op jit(solution)/shard_map/ppermute | solution.py:19
  159.4 3.6 %collective-permute-done.53.refs_1_ = f32[272,128]{1,0:T(8,128)S(1)} collective-permute-done((f32[272,128]{1,0:T(8,128)S(1)}, f32[272,128]{1,0:T(8,128)S(1)}, u32[]{:S(2)}, u32[]{:S(2)}) %collective-permute-start.53) | collective-permute-done | bytes 139296 | tf_op jit(solution)/shard_map/ppermute | solution.py:19
  170.2 3.8 %collective-permute-done.57.refs_2_ = f32[256,128]{1,0:T(8,128)S(1)} collective-permute-done((f32[256,128]{1,0:T(8,128)S(1)}, f32[256,128]{1,0:T(8,128)S(1)}, u32[]{:S(2)}, u32[]{:S(2)}) %collective-permute-start.57) | collective-permute-done | bytes 131104 | tf_op jit(solution)/shard_map/ppermute | solution.py:19
  (135 shorter events, 72.6 us)
Async XLA Ops:
  8.8 7.6 %collective-permute-start.1 = (f32[128,128]{1,0:T(8,128)S(1)}, f32[128,128]{1,0:T(8,128)S(1)}, u32[]{:S(2)}, u32[]{:S(2)}) collective-permute-start(f32[128,128]{1,0:T(8,128)S(1)} %get-tuple-element.92), channel_id=1, source_target_pairs={{0,6},{1,7},{2,4},{3,5},{4,2},{5,3},{6,0},{7,1},{8,14},{9,15},{10,... | collective-permute-start | bytes 196616 | tf_op jit(solution)/shard_map/ppermute | solution.py:19
  13.4 6.1 %collective-permute-start.2 = (f32[128,128]{1,0:T(8,128)S(1)}, f32[128,128]{1,0:T(8,128)S(1)}, u32[]{:S(2)}, u32[]{:S(2)}) collective-permute-start(f32[128,128]{1,0:T(8,128)S(1)} %get-tuple-element.91), channel_id=1, source_target_pairs={{0,4},{1,5},{2,6},{3,7},{4,0},{5,1},{6,2},{7,3},{8,12},{9,13},{10,... | collective-permute-start | bytes 196616 | tf_op jit(solution)/shard_map/ppermute | solution.py:19
  19.6 6.4 %collective-permute-start.9 = (f32[128,128]{1,0:T(8,128)S(1)}, f32[128,128]{1,0:T(8,128)S(1)}, u32[]{:S(2)}, u32[]{:S(2)}) collective-permute-start(f32[128,128]{1,0:T(8,128)S(1)} %shard_map.80.refs_0_), channel_id=1, source_target_pairs={{0,6},{1,7},{2,4},{3,5},{4,2},{5,3},{6,0},{7,1},{8,14},{9,15},{10,... | collective-permute-start | bytes 196616 | tf_op jit(solution)/shard_map/ppermute | solution.py:19
  30.4 6.8 %collective-permute-start.11 = (f32[256,128]{1,0:T(8,128)S(1)}, f32[256,128]{1,0:T(8,128)S(1)}, u32[]{:S(2)}, u32[]{:S(2)}) collective-permute-start(f32[256,128]{1,0:T(8,128)S(1)} %get-tuple-element.47), channel_id=1, source_target_pairs={{0,24},{8,16},{16,8},{24,0},{1,25},{9,17},{17,9},{25,1},{2,26},{10... | collective-permute-start | bytes 393224 | tf_op jit(solution)/shard_map/ppermute | solution.py:19
  32.9 6.8 %collective-permute-start.12 = (f32[256,128]{1,0:T(8,128)S(1)}, f32[256,128]{1,0:T(8,128)S(1)}, u32[]{:S(2)}, u32[]{:S(2)}) collective-permute-start(f32[256,128]{1,0:T(8,128)S(1)} %get-tuple-element.48), channel_id=1, source_target_pairs={{0,16},{8,24},{16,0},{24,8},{1,17},{9,25},{17,1},{25,9},{2,18},{10... | collective-permute-start | bytes 393224 | tf_op jit(solution)/shard_map/ppermute | solution.py:19
  33.4 6.4 %collective-permute-start.13 = (f32[256,128]{1,0:T(8,128)S(1)}, f32[256,128]{1,0:T(8,128)S(1)}, u32[]{:S(2)}, u32[]{:S(2)}) collective-permute-start(f32[256,128]{1,0:T(8,128)S(1)} %get-tuple-element.49), channel_id=1, source_target_pairs={{0,8},{8,0},{16,24},{24,16},{1,9},{9,1},{17,25},{25,17},{2,10},{10... | collective-permute-start | bytes 393224 | tf_op jit(solution)/shard_map/ppermute | solution.py:19
  41.4 7.9 %collective-permute-start.15 = (f32[256,128]{1,0:T(8,128)S(1)}, f32[256,128]{1,0:T(8,128)S(1)}, u32[]{:S(2)}, u32[]{:S(2)}) collective-permute-start(f32[256,128]{1,0:T(8,128)S(1)} %add_multiply_fusion.1.refs_0_), channel_id=1, source_target_pairs={{0,16},{8,24},{16,0},{24,8},{1,17},{9,25},{17,1},{25,9},{2,18},{10... | collective-permute-start | bytes 393224 | tf_op jit(solution)/shard_map/ppermute | solution.py:19
  42.1 7.2 %collective-permute-start.16 = (f32[256,128]{1,0:T(8,128)S(1)}, f32[256,128]{1,0:T(8,128)S(1)}, u32[]{:S(2)}, u32[]{:S(2)}) collective-permute-start(f32[256,128]{1,0:T(8,128)S(1)} %add_multiply_fusion.1.refs_0_), channel_id=1, source_target_pairs={{0,24},{8,16},{16,8},{24,0},{1,25},{9,17},{17,9},{25,1},{2,26},{10... | collective-permute-start | bytes 393224 | tf_op jit(solution)/shard_map/ppermute | solution.py:19
  51.8 6.8 %collective-permute-start.18 = (f32[128,128]{1,0:T(8,128)S(1)}, f32[128,128]{1,0:T(8,128)S(1)}, u32[]{:S(2)}, u32[]{:S(2)}) collective-permute-start(f32[128,128]{1,0:T(8,128)S(1)} %get-tuple-element.88), channel_id=1, source_target_pairs={{0,6},{1,7},{2,4},{3,5},{4,2},{5,3},{6,0},{7,1},{8,14},{9,15},{10,... | collective-permute-start | bytes 196616 | tf_op jit(solution)/shard_map/ppermute | solution.py:19
  53.6 7.5 %collective-permute-start.19 = (f32[128,128]{1,0:T(8,128)S(1)}, f32[128,128]{1,0:T(8,128)S(1)}, u32[]{:S(2)}, u32[]{:S(2)}) collective-permute-start(f32[128,128]{1,0:T(8,128)S(1)} %get-tuple-element.87), channel_id=1, source_target_pairs={{0,4},{1,5},{2,6},{3,7},{4,0},{5,1},{6,2},{7,3},{8,12},{9,13},{10,... | collective-permute-start | bytes 196616 | tf_op jit(solution)/shard_map/ppermute | solution.py:19
  54.6 6.5 %collective-permute-start.20 = (f32[128,128]{1,0:T(8,128)S(1)}, f32[128,128]{1,0:T(8,128)S(1)}, u32[]{:S(2)}, u32[]{:S(2)}) collective-permute-start(f32[128,128]{1,0:T(8,128)S(1)} %get-tuple-element.86), channel_id=1, source_target_pairs={{0,2},{1,3},{2,0},{3,1},{4,6},{5,7},{6,4},{7,5},{8,10},{9,11},{10,... | collective-permute-start | bytes 196616 | tf_op jit(solution)/shard_map/ppermute | solution.py:19
  74.0 6.9 %collective-permute-start.22 = (f32[128,128]{1,0:T(8,128)S(1)}, f32[128,128]{1,0:T(8,128)S(1)}, u32[]{:S(2)}, u32[]{:S(2)}) collective-permute-start(f32[128,128]{1,0:T(8,128)S(1)} %get-tuple-element.84), channel_id=1, source_target_pairs={{0,6},{1,7},{2,4},{3,5},{4,2},{5,3},{6,0},{7,1},{8,14},{9,15},{10,... | collective-permute-start | bytes 196616 | tf_op jit(solution)/shard_map/ppermute | solution.py:19
  74.6 7.9 %collective-permute-start.23 = (f32[128,128]{1,0:T(8,128)S(1)}, f32[128,128]{1,0:T(8,128)S(1)}, u32[]{:S(2)}, u32[]{:S(2)}) collective-permute-start(f32[128,128]{1,0:T(8,128)S(1)} %get-tuple-element.83), channel_id=1, source_target_pairs={{0,4},{1,5},{2,6},{3,7},{4,0},{5,1},{6,2},{7,3},{8,12},{9,13},{10,... | collective-permute-start | bytes 196616 | tf_op jit(solution)/shard_map/ppermute | solution.py:19
  76.0 6.5 %collective-permute-start.24 = (f32[128,128]{1,0:T(8,128)S(1)}, f32[128,128]{1,0:T(8,128)S(1)}, u32[]{:S(2)}, u32[]{:S(2)}) collective-permute-start(f32[128,128]{1,0:T(8,128)S(1)} %get-tuple-element.82), channel_id=1, source_target_pairs={{0,2},{1,3},{2,0},{3,1},{4,6},{5,7},{6,4},{7,5},{8,10},{9,11},{10,... | collective-permute-start | bytes 196616 | tf_op jit(solution)/shard_map/ppermute | solution.py:19
  82.8 7.1 %collective-permute-start.28 = (f32[128,128]{1,0:T(8,128)S(1)}, f32[128,128]{1,0:T(8,128)S(1)}, u32[]{:S(2)}, u32[]{:S(2)}) collective-permute-start(f32[128,128]{1,0:T(8,128)S(1)} %shard_map.88.refs_0_), channel_id=1, source_target_pairs={{0,4},{1,5},{2,6},{3,7},{4,0},{5,1},{6,2},{7,3},{8,12},{9,13},{10,... | collective-permute-start | bytes 196616 | tf_op jit(solution)/shard_map/ppermute | solution.py:19
  93.1 7.4 %collective-permute-start.32 = (f32[256,128]{1,0:T(8,128)S(1)}, f32[256,128]{1,0:T(8,128)S(1)}, u32[]{:S(2)}, u32[]{:S(2)}) collective-permute-start(f32[256,128]{1,0:T(8,128)S(1)} %get-tuple-element.57), channel_id=1, source_target_pairs={{0,24},{8,16},{16,8},{24,0},{1,25},{9,17},{17,9},{25,1},{2,26},{10... | collective-permute-start | bytes 393224 | tf_op jit(solution)/shard_map/ppermute | solution.py:19
  93.7 8.1 %collective-permute-start.33 = (f32[256,128]{1,0:T(8,128)S(1)}, f32[256,128]{1,0:T(8,128)S(1)}, u32[]{:S(2)}, u32[]{:S(2)}) collective-permute-start(f32[256,128]{1,0:T(8,128)S(1)} %get-tuple-element.58), channel_id=1, source_target_pairs={{0,16},{8,24},{16,0},{24,8},{1,17},{9,25},{17,1},{25,9},{2,18},{10... | collective-permute-start | bytes 393224 | tf_op jit(solution)/shard_map/ppermute | solution.py:19
  95.2 6.6 %collective-permute-start.34 = (f32[256,128]{1,0:T(8,128)S(1)}, f32[256,128]{1,0:T(8,128)S(1)}, u32[]{:S(2)}, u32[]{:S(2)}) collective-permute-start(f32[256,128]{1,0:T(8,128)S(1)} %get-tuple-element.59), channel_id=1, source_target_pairs={{0,8},{8,0},{16,24},{24,16},{1,9},{9,1},{17,25},{25,17},{2,10},{10... | collective-permute-start | bytes 393224 | tf_op jit(solution)/shard_map/ppermute | solution.py:19
  103.1 7.9 %collective-permute-start.36 = (f32[256,128]{1,0:T(8,128)S(1)}, f32[256,128]{1,0:T(8,128)S(1)}, u32[]{:S(2)}, u32[]{:S(2)}) collective-permute-start(f32[256,128]{1,0:T(8,128)S(1)} %add_multiply_fusion.refs_0_), channel_id=1, source_target_pairs={{0,16},{8,24},{16,0},{24,8},{1,17},{9,25},{17,1},{25,9},{2,18},{10... | collective-permute-start | bytes 393224 | tf_op jit(solution)/shard_map/ppermute | solution.py:19
  103.7 7.4 %collective-permute-start.37 = (f32[256,128]{1,0:T(8,128)S(1)}, f32[256,128]{1,0:T(8,128)S(1)}, u32[]{:S(2)}, u32[]{:S(2)}) collective-permute-start(f32[256,128]{1,0:T(8,128)S(1)} %add_multiply_fusion.refs_0_), channel_id=1, source_target_pairs={{0,24},{8,16},{16,8},{24,0},{1,25},{9,17},{17,9},{25,1},{2,26},{10... | collective-permute-start | bytes 393224 | tf_op jit(solution)/shard_map/ppermute | solution.py:19
  113.5 6.8 %collective-permute-start.39 = (f32[128,128]{1,0:T(8,128)S(1)}, f32[128,128]{1,0:T(8,128)S(1)}, u32[]{:S(2)}, u32[]{:S(2)}) collective-permute-start(f32[128,128]{1,0:T(8,128)S(1)} %get-tuple-element.80), channel_id=1, source_target_pairs={{0,6},{1,7},{2,4},{3,5},{4,2},{5,3},{6,0},{7,1},{8,14},{9,15},{10,... | collective-permute-start | bytes 196616 | tf_op jit(solution)/shard_map/ppermute | solution.py:19
  116.1 6.6 %collective-permute-start.40 = (f32[128,128]{1,0:T(8,128)S(1)}, f32[128,128]{1,0:T(8,128)S(1)}, u32[]{:S(2)}, u32[]{:S(2)}) collective-permute-start(f32[128,128]{1,0:T(8,128)S(1)} %get-tuple-element.79), channel_id=1, source_target_pairs={{0,4},{1,5},{2,6},{3,7},{4,0},{5,1},{6,2},{7,3},{8,12},{9,13},{10,... | collective-permute-start | bytes 196616 | tf_op jit(solution)/shard_map/ppermute | solution.py:19
  116.2 6.5 %collective-permute-start.41 = (f32[128,128]{1,0:T(8,128)S(1)}, f32[128,128]{1,0:T(8,128)S(1)}, u32[]{:S(2)}, u32[]{:S(2)}) collective-permute-start(f32[128,128]{1,0:T(8,128)S(1)} %get-tuple-element.78), channel_id=1, source_target_pairs={{0,2},{1,3},{2,0},{3,1},{4,6},{5,7},{6,4},{7,5},{8,10},{9,11},{10,... | collective-permute-start | bytes 196616 | tf_op jit(solution)/shard_map/ppermute | solution.py:19
  136.0 7.0 %collective-permute-start.43 = (f32[128,128]{1,0:T(8,128)S(1)}, f32[128,128]{1,0:T(8,128)S(1)}, u32[]{:S(2)}, u32[]{:S(2)}) collective-permute-start(f32[128,128]{1,0:T(8,128)S(1)} %get-tuple-element.76), channel_id=1, source_target_pairs={{0,6},{1,7},{2,4},{3,5},{4,2},{5,3},{6,0},{7,1},{8,14},{9,15},{10,... | collective-permute-start | bytes 196616 | tf_op jit(solution)/shard_map/ppermute | solution.py:19
  136.6 7.9 %collective-permute-start.44 = (f32[128,128]{1,0:T(8,128)S(1)}, f32[128,128]{1,0:T(8,128)S(1)}, u32[]{:S(2)}, u32[]{:S(2)}) collective-permute-start(f32[128,128]{1,0:T(8,128)S(1)} %get-tuple-element.75), channel_id=1, source_target_pairs={{0,4},{1,5},{2,6},{3,7},{4,0},{5,1},{6,2},{7,3},{8,12},{9,13},{10,... | collective-permute-start | bytes 196616 | tf_op jit(solution)/shard_map/ppermute | solution.py:19
  138.1 6.5 %collective-permute-start.45 = (f32[128,128]{1,0:T(8,128)S(1)}, f32[128,128]{1,0:T(8,128)S(1)}, u32[]{:S(2)}, u32[]{:S(2)}) collective-permute-start(f32[128,128]{1,0:T(8,128)S(1)} %get-tuple-element.74), channel_id=1, source_target_pairs={{0,2},{1,3},{2,0},{3,1},{4,6},{5,7},{6,4},{7,5},{8,10},{9,11},{10,... | collective-permute-start | bytes 196616 | tf_op jit(solution)/shard_map/ppermute | solution.py:19
  144.8 7.0 %collective-permute-start.49 = (f32[128,128]{1,0:T(8,128)S(1)}, f32[128,128]{1,0:T(8,128)S(1)}, u32[]{:S(2)}, u32[]{:S(2)}) collective-permute-start(f32[128,128]{1,0:T(8,128)S(1)} %shard_map.97.refs_0_), channel_id=1, source_target_pairs={{0,4},{1,5},{2,6},{3,7},{4,0},{5,1},{6,2},{7,3},{8,12},{9,13},{10,... | collective-permute-start | bytes 196616 | tf_op jit(solution)/shard_map/ppermute | solution.py:19
  155.5 7.5 %collective-permute-start.53 = (f32[272,128]{1,0:T(8,128)S(1)}, f32[272,128]{1,0:T(8,128)S(1)}, u32[]{:S(2)}, u32[]{:S(2)}) collective-permute-start(f32[272,128]{1,0:T(8,128)S(1)} %get-tuple-element.70), channel_id=1, source_target_pairs={{0,24},{8,16},{16,8},{24,0},{1,25},{9,17},{17,9},{25,1},{2,26},{10... | collective-permute-start | bytes 417800 | tf_op jit(solution)/shard_map/ppermute | solution.py:19
  156.2 8.4 %collective-permute-start.54 = (f32[272,128]{1,0:T(8,128)S(1)}, f32[272,128]{1,0:T(8,128)S(1)}, u32[]{:S(2)}, u32[]{:S(2)}) collective-permute-start(f32[272,128]{1,0:T(8,128)S(1)} %get-tuple-element.71), channel_id=1, source_target_pairs={{0,16},{8,24},{16,0},{24,8},{1,17},{9,25},{17,1},{25,9},{2,18},{10... | collective-permute-start | bytes 417800 | tf_op jit(solution)/shard_map/ppermute | solution.py:19
  157.6 7.0 %collective-permute-start.55 = (f32[272,128]{1,0:T(8,128)S(1)}, f32[272,128]{1,0:T(8,128)S(1)}, u32[]{:S(2)}, u32[]{:S(2)}) collective-permute-start(f32[272,128]{1,0:T(8,128)S(1)} %get-tuple-element.72), channel_id=1, source_target_pairs={{0,8},{8,0},{16,24},{24,16},{1,9},{9,1},{17,25},{25,17},{2,10},{10... | collective-permute-start | bytes 417800 | tf_op jit(solution)/shard_map/ppermute | solution.py:19
  166.1 7.9 %collective-permute-start.57 = (f32[256,128]{1,0:T(8,128)S(1)}, f32[256,128]{1,0:T(8,128)S(1)}, u32[]{:S(2)}, u32[]{:S(2)}) collective-permute-start(f32[256,128]{1,0:T(8,128)S(1)} %shard_map.100.refs_0_), channel_id=1, source_target_pairs={{0,16},{8,24},{16,0},{24,8},{1,17},{9,25},{17,1},{25,9},{2,18},{10... | collective-permute-start | bytes 393224 | tf_op jit(solution)/shard_map/ppermute | solution.py:19
  166.7 7.3 %collective-permute-start.58 = (f32[256,128]{1,0:T(8,128)S(1)}, f32[256,128]{1,0:T(8,128)S(1)}, u32[]{:S(2)}, u32[]{:S(2)}) collective-permute-start(f32[256,128]{1,0:T(8,128)S(1)} %shard_map.100.refs_0_), channel_id=1, source_target_pairs={{0,24},{8,16},{16,8},{24,0},{1,25},{9,17},{17,9},{25,1},{2,26},{10... | collective-permute-start | bytes 393224 | tf_op jit(solution)/shard_map/ppermute | solution.py:19
  (34 other events, 159.1 us)

commit v5 on v4

--- a/solution.py
+++ b/solution.py
@@ -11,7 +11,7 @@
 GPD = 2
 ITERS = 2
 STATS = 16
-VMEM_LIMIT = 10 * 1024 * 1024
+VMEM_LIMIT = 12 * 1024 * 1024
 
 
 def swap(value, axis, bits):
@@ -60,42 +60,51 @@
     )
 
 
-def split_rows(source_ref, ready, packed_ref, high_ref, low_ref, out_ref):
-    half, block = source_ref.shape[0], source_ref.shape[1]
-    group = max(1, half // 2)
-    for first in range(0, half, group):
-        for k in range(first, first + group):
-            ready(k)
-            high, low = split(source_ref[k])
-            high_ref[k * block : (k + 1) * block] = high
-            low_ref[k * block : (k + 1) * block] = low
-        rows = slice(first * block, (first + group) * block)
-        total = wide_dot(high_ref[rows], low_ref[rows], packed_ref[...])
-        out_ref[first : first + group] = total.reshape((group,) + out_ref.shape[1:])
-
-
-def first_kernel(dosage_ref, coef_ref, high_ref, low_ref, out_ref, packed_ref, kept_ref, buffer_ref, coef_buffer, sems):
+def first_kernel(
+    dosage_ref,
+    coef_ref,
+    high1_ref,
+    low1_ref,
+    high0_ref,
+    low0_ref,
+    give_ref,
+    packed_ref,
+    buffer_ref,
+    coef_buffer,
+    sems,
+):
     me = lax.axis_index("chrom")
     place, core = me // 2, me % 2
-    half = buffer_ref.shape[0]
+    half, block = buffer_ref.shape[1], buffer_ref.shape[2]
     coef_copy = pltpu.make_async_copy(coef_ref, coef_buffer, sems.at[2 * half])
-    copies = [
-        pltpu.make_async_copy(dosage_ref.at[place ^ k, core ^ bits], target.at[k], sems.at[bits * half + k])
-        for bits, target in ((1, buffer_ref), (0, kept_ref))
+    copies = {
+        (bits, k): pltpu.make_async_copy(
+            dosage_ref.at[place ^ k, core ^ bits], buffer_ref.at[bits, k], sems.at[bits * half + k]
+        )
+        for bits in (1, 0)
         for k in range(half)
-    ]
+    }
     coef_copy.start()
-    for copy in copies:
+    for copy in copies.values():
         copy.start()
     coef_copy.wait()
     packed_ref[...] = pack(coef_buffer[...])
-    split_rows(buffer_ref, lambda k: copies[k].wait(), packed_ref, high_ref, low_ref, out_ref)
-    for copy in copies[half:]:
-        copy.wait()
-
-
-def second_kernel(kept_ref, packed_ref, high_ref, low_ref, out_ref):
-    split_rows(kept_ref, lambda k: None, packed_ref, high_ref, low_ref, out_ref)
+    group = max(1, half // 2)
+
+    def split_block(bits, k, high_ref, low_ref):
+        copies[bits, k].wait()
+        high, low = split(buffer_ref[bits, k])
+        high_ref[k * block : (k + 1) * block] = high
+        low_ref[k * block : (k + 1) * block] = low
+
+    for first in range(0, half, group):
+        for k in range(first, first + group):
+            split_block(1, k, high1_ref, low1_ref)
+        rows = slice(first * block, (first + group) * block)
+        total = wide_dot(high1_ref[rows], low1_ref[rows], packed_ref[...])
+        give_ref[first : first + group] = total.reshape((group,) + give_ref.shape[1:])
+    for k in range(half):
+        split_block(0, k, high0_ref, low0_ref)
 
 
 def square_kernel(tested_ref, square_ref):
@@ -143,7 +152,7 @@
     rows_ref = refs[-1]
     samp = lax.axis_index("samp")
     block = pieces[0].shape[0]
-    for bits, piece in enumerate(pieces):
+    for bits, piece in zip(chrom_order(count), pieces):
         start = ((bits % 2) * (count // 2) + bits // 2) * block
         rows_ref[start : start + block] = pack(piece[...])
     packed_ref[...] = rows_ref[...].T
@@ -178,11 +187,14 @@
     for piece in pieces[1:]:
         total = total + piece[...]
     grad = grad_ref[...]
-    grad_sq = jnp.sum(grad * grad, axis=0, keepdims=True)
-    image_sq = jnp.sum(total * total, axis=0, keepdims=True)
-    sums = jnp.concatenate([grad_sq, image_sq])
-    for place in range(out.shape[0]):
-        out[place] = sums
+    out[0:1] = jnp.sum(grad * grad, axis=0, keepdims=True)
+    out[1:2] = jnp.sum(total * total, axis=0, keepdims=True)
+
+
+def spread_kernel(own_ref, other_ref, out_ref):
+    total = own_ref[...] + other_ref[...]
+    for place in range(out_ref.shape[0]):
+        out_ref[place] = total
 
 
 def prox_kernel(total_rows, coef_ref, grad_ref, sums_ref, high_ref, low_ref, new_ref, packed_ref, give_ref):
@@ -230,16 +242,15 @@
 
 def loco_kernel(count, partners, *refs):
     pieces, own_refs = refs[:count], refs[count : count + GPD]
-    tested_ref, square_ref, owner_ref, residual_ref, loco_ref, sums_ref = refs[count + GPD : count + GPD + 6]
-    outs, rows_ref = refs[count + GPD + 6 : -1], refs[-1]
+    tested_ref, square_ref, owner_ref, loco_ref, sums_ref = refs[count + GPD : count + GPD + 5]
+    outs, rows_ref = refs[count + GPD + 5 : -1], refs[-1]
     me, samp = lax.axis_index("chrom"), lax.axis_index("samp")
     block, traits = pieces[0].shape
     sums_ref[...] = jnp.zeros_like(sums_ref)
-    for bits, piece in enumerate(pieces):
+    for bits, piece in zip(chrom_order(count), pieces):
         rows = pl.ds(pl.multiple_of((me ^ bits) * block, block), block)
         start = ((bits % 2) * (count // 2) + bits // 2) * block
         value = piece[...]
-        residual_ref[rows] = value
         for which in range(GPD):
             loco = value + own_refs[which][start : start + block]
             sums_ref[which : which + 1] += jnp.sum(loco * loco, axis=0, keepdims=True)
@@ -249,10 +260,14 @@
         score_products(samp ^ partner, out, tested_ref, square_ref, owner_ref, loco_ref, sums_ref)
 
 
-def loco_near_kernel(partners, *refs):
-    samp = lax.axis_index("samp")
-    for partner, out in zip(partners, refs[5:]):
-        score_products(samp ^ partner, out, *refs[:5])
+def loco_near_kernel(count, partners, *refs):
+    pieces, operands, residual_ref, outs = refs[:count], refs[count : count + 5], refs[count + 5], refs[count + 6 :]
+    me, samp = lax.axis_index("chrom"), lax.axis_index("samp")
+    block = pieces[0].shape[0]
+    for bits, piece in zip(chrom_order(count), pieces):
+        residual_ref[pl.ds(pl.multiple_of((me ^ bits) * block, block), block)] = piece[...]
+    for partner, out in zip(partners, outs):
+        score_products(samp ^ partner, out, *operands)
 
 
 def score_kernel(total_rows, owner_ref, *refs):
@@ -284,15 +299,20 @@
     got = swap(give, "chrom", 1)
     count = keep.shape[0]
     sums = [keep[k] + got[k] for k in range(count)]
-    return [sums[0]] + [swap(sums[k], "chrom", 2 * k) for k in reversed(range(1, count))]
+    return [sums[0]] + [swap(sums[k], "chrom", 2 * k) for k in range(1, count)]
 
 
 def chrom_gather(own):
     count = lax.axis_size("chrom") // 2
-    far = [swap(own, "chrom", 2 * k) for k in reversed(range(1, count))]
-    mine = [own] + far[::-1]
-    other = [swap(block, "chrom", 1) for block in mine]
-    return [block for pair in zip(mine, other) for block in pair]
+    blocks = []
+    for k in range(count):
+        block = swap(own, "chrom", 2 * k) if k else own
+        blocks += [block, swap(block, "chrom", 1)]
+    return blocks
+
+
+def chrom_order(size):
+    return [2 * k + bits for k in range(size // 2) for bits in range(2)]
 
 
 def samp_order(size):
@@ -339,19 +359,22 @@
         )(own_traits, *summands, *after)
 
     coefficients = start_coef
-    kept_shape = (half, block, cols)
-    high1, low1, give, packed, kept = call(
+    high1, low1, high0, low0, give, packed = call(
         first_kernel,
-        [part, part, half_out, packed_cols, shape(kept_shape)],
+        [part] * 4 + [half_out, packed_cols],
         [pl.BlockSpec(memory_space=pltpu.HBM)] * 2,
-        [pltpu.VMEM(kept_shape, jnp.float32), pltpu.VMEM(coefficients.shape, jnp.float32), pltpu.SemaphoreType.DMA((n_chrom + 1,))],
+        [
+            pltpu.VMEM((2, half, block, cols), jnp.float32),
+            pltpu.VMEM(coefficients.shape, jnp.float32),
+            pltpu.SemaphoreType.DMA((n_chrom + 1,)),
+        ],
         flops,
         4 * moved,
     )(
         pltpu.with_memory_space_constraint(dosages.reshape(half, 2, block, cols), pltpu.HBM),
         pltpu.with_memory_space_constraint(coefficients, pltpu.HBM),
     )
-    high0, low0, keep = call(second_kernel, [part, part, half_out], [whole()] * 2, (), flops, moved)(kept, packed)
+    keep = rest(high0, low0, packed)
     summands = chrom_scatter(give, keep)
     parts = [high0, low0, high1, low1]
     tested_sq = call(square_kernel, shape((n_samp, test_width // 128, 128)), [whole()], (), 0, 2 * rows * tests)(tested)
@@ -385,11 +408,13 @@
             moved,
         )(*pieces, high1, low1, *after)
         summands = chrom_scatter(give, rest(high0, low0, packed))
-        size = n_samp * n_chrom
-        sums = call(
-            functools.partial(norm_kernel, half), shape((size, 2, n_traits)), [whole()] * (half + 1)
-        )(own_grad, *summands)
-        sums = lax.all_to_all(sums, ("samp", "chrom"), 0, 0)
+        size = n_samp * half
+        sums = call(functools.partial(norm_kernel, half), shape((2, n_traits)), [whole()] * (half + 1))(
+            own_grad, *summands
+        )
+        sums = call(spread_kernel, shape((size, 2, n_traits)), [whole()] * 2)(sums, swap(sums, "chrom", 1))
+        cores = [list(range(core, n_samp * n_chrom, 2)) for core in range(2)]
+        sums = lax.all_to_all(sums, ("samp", "chrom"), 0, 0, axis_index_groups=cores)
         coefficients, packed, give = call(
             functools.partial(prox_kernel, total_rows),
             [coef_out, packed_cols, half_out],
@@ -404,18 +429,23 @@
         coefficients, group_rows, *parts
     )
     pieces = chrom_gather(own_residual(summands, own_parts))
-    residual, loco, loco_sq, *far_out = call(
+    loco, loco_sq, *far_out = call(
         functools.partial(loco_kernel, n_chrom, far),
-        [shape((rows, n_traits)), shape((GPD * n_traits, rows), jnp.bfloat16), shape((8, n_traits))]
+        [shape((GPD * n_traits, rows), jnp.bfloat16), shape((8, n_traits))]
         + [score_block] * len(far),
         [whole()] * (n_chrom + GPD + 3),
         [pltpu.VMEM((rows, GPD * n_traits), jnp.bfloat16)],
         flops,
         moved,
     )(*pieces, *own_parts, tested, tested_sq, owner_rows)
-    near_out = call(
-        functools.partial(loco_near_kernel, near), [score_block] * len(near), [whole()] * 5, (), flops // 2, moved
-    )(tested, tested_sq, owner_rows, loco, loco_sq)
+    residual, *near_out = call(
+        functools.partial(loco_near_kernel, n_chrom, near),
+        [shape((rows, n_traits))] + [score_block] * len(near),
+        [whole()] * (n_chrom + 5),
+        (),
+        flops // 2,
+        moved,
+    )(*pieces, tested, tested_sq, owner_rows, loco, loco_sq)
     received = [swap(piece, "samp", partner) for partner, piece in zip(order, far_out + list(near_out[:-1]))]
     own_scores = call(
         functools.partial(score_kernel, total_rows), shape((test_width, n_traits)), [whole()] * (n_samp + 1)

time: 175 us -> 179 us (1.023)
  waiting for transfers between devices: 69.9 us -> 72.2 us
  blocking collectives: 20.5 us -> 22.3 us
    ppermute x59 -> x61, waiting for transfers between devices: 69.9 us -> 72.2 us  [swap(): return lax.ppermute(value, axis, [(i, i ^ bits) for i in range(size)])]
    all_to_all x2, blocking collectives: 20.5 us -> 22.3 us  [body(): lax.all_to_all(sums, ('samp', 'chrom'), 0, 0, axis_index_groups=cores)]
    ppermute x59 -> x61, starting transfers between devices: 59.7 us -> 60.6 us  [swap(): return lax.ppermute(value, axis, [(i, i ^ bits) for i in range(size)])]
    pallas_call x6 -> x7, Pallas kernels: 5.84 us -> 5.33 us  [the longest x1 3.34 us: body(): call(first_kernel, [part] * 4 + [half_out, packed_cols], [pl.BlockSpec(me...]
  transfers between devices with their start and end apart: 59 -> 61, of which waited for: 41 -> 44; matrix products, arithmetic and copies ran while one was open for 0% -> 0% of each run, Pallas kernels for 4% -> 5%
where the time goes in v5:
time: 179 us
  waiting for transfers between devices  72.2 us (40%)
  starting transfers between devices  60.6 us (34%)
  blocking collectives  22.3 us (12%)
  Pallas kernels  20 us (11%)
  local copies, waits for them, and re-layouts  1.99 us (1%)
    ppermute x61, waiting for transfers between devices, swap(): return lax.ppermute(value, axis, [(i, i ^ bits) for i in range(size)])  72.2 us
    ppermute x61, starting transfers between devices, swap(): return lax.ppermute(value, axis, [(i, i ^ bits) for i in range(size)])  60.6 us
    all_to_all x2, blocking collectives, body(): lax.all_to_all(sums, ('samp', 'chrom'), 0, 0, axis_index_groups=cores)  22.3 us
  transfers between devices with their start and end apart: 61, of which 44 were waited for; matrix products, arithmetic and copies ran while one was open for 0% of the time, Pallas kernels for 5%

profile of v5, /device:TPU:0, one launch (start us, length us, event | category | flops | bytes accessed | tf_op | source)
XLA Modules:
  0.0 179.2 jit_solution(15192984007688316916)
XLA Ops:
  0.6 3.3 %shard_map.77 = (bf16[512,1024]{1,0:T(8,128)(2,1)S(1)}, bf16[512,1024]{1,0:T(8,128)(2,1)S(1)}, bf16[512,1024]{1,0:T(8,128)(2,1)S(1)}, bf16[512,1024]{1,0:T(8,128...) custom-call(f32[4,2,128,1024]{3,2,1,0:T(8,128)} %bitcast.47, f32[1024,128]{1,0:T(8,128)} %coef_ref.3), custom_call_target="tpu_custom_call" | custom-call | flops 536870912 | bytes 8388608 | tf_op jit(solution)/shard_map/pallas_call | solution.py:362
  8.7 5.0 %collective-permute-start.3 = (f32[128,128]{1,0:T(8,128)S(1)}, f32[128,128]{1,0:T(8,128)S(1)}, u32[]{:S(2)}, u32[]{:S(2)}) collective-permute-start(f32[128,128]{1,0:T(8,128)S(1)} %get-tuple-element.88), channel_id=1, source_target_pairs={{0,6},{1,7},{2,4},{3,5},{4,2},{5,3},{6,0},{7,1},{8,14},{9,15},{10,... | collective-permute-start | bytes 196616 | tf_op jit(solution)/shard_map/ppermute | solution.py:19
  14.4 2.0 %collective-permute-done.3.refs_3_ = f32[128,128]{1,0:T(8,128)S(1)} collective-permute-done((f32[128,128]{1,0:T(8,128)S(1)}, f32[128,128]{1,0:T(8,128)S(1)}, u32[]{:S(2)}, u32[]{:S(2)}) %collective-permute-start.3) | collective-permute-done | bytes 65568 | tf_op jit(solution)/shard_map/ppermute | solution.py:19
  16.3 3.2 %collective-permute-done.2.refs_2_ = f32[128,128]{1,0:T(8,128)S(1)} collective-permute-done((f32[128,128]{1,0:T(8,128)S(1)}, f32[128,128]{1,0:T(8,128)S(1)}, u32[]{:S(2)}, u32[]{:S(2)}) %collective-permute-start.2) | collective-permute-done | bytes 65568 | tf_op jit(solution)/shard_map/ppermute | solution.py:19
  19.6 2.5 %collective-permute-start.9 = (f32[128,128]{1,0:T(8,128)S(1)}, f32[128,128]{1,0:T(8,128)S(1)}, u32[]{:S(2)}, u32[]{:S(2)}) collective-permute-start(f32[128,128]{1,0:T(8,128)S(1)} %shard_map.79.refs_0_), channel_id=1, source_target_pairs={{0,6},{1,7},{2,4},{3,5},{4,2},{5,3},{6,0},{7,1},{8,14},{9,15},{10,... | collective-permute-start | bytes 196616 | tf_op jit(solution)/shard_map/ppermute | solution.py:19
  24.1 1.9 %collective-permute-done.9.refs_6_ = f32[128,128]{1,0:T(8,128)S(1)} collective-permute-done((f32[128,128]{1,0:T(8,128)S(1)}, f32[128,128]{1,0:T(8,128)S(1)}, u32[]{:S(2)}, u32[]{:S(2)}) %collective-permute-start.9) | collective-permute-done | bytes 65568 | tf_op jit(solution)/shard_map/ppermute | solution.py:19
  26.0 2.7 %collective-permute-done.7.refs_4_ = f32[128,128]{1,0:T(8,128)S(1)} collective-permute-done((f32[128,128]{1,0:T(8,128)S(1)}, f32[128,128]{1,0:T(8,128)S(1)}, u32[]{:S(2)}, u32[]{:S(2)}) %collective-permute-start.7) | collective-permute-done | bytes 65568 | tf_op jit(solution)/shard_map/ppermute | solution.py:19
  31.2 2.5 %collective-permute-start.11 = (f32[256,128]{1,0:T(8,128)S(1)}, f32[256,128]{1,0:T(8,128)S(1)}, u32[]{:S(2)}, u32[]{:S(2)}) collective-permute-start(f32[256,128]{1,0:T(8,128)S(1)} %get-tuple-element.44), channel_id=1, source_target_pairs={{0,24},{8,16},{16,8},{24,0},{1,25},{9,17},{17,9},{25,1},{2,26},{10... | collective-permute-start | bytes 393224 | tf_op jit(solution)/shard_map/ppermute | solution.py:19
  35.3 2.9 %collective-permute-done.11 = f32[256,128]{1,0:T(8,128)S(1)} collective-permute-done((f32[256,128]{1,0:T(8,128)S(1)}, f32[256,128]{1,0:T(8,128)S(1)}, u32[]{:S(2)}, u32[]{:S(2)}) %collective-permute-start.11) | collective-permute-done | bytes 131104 | tf_op jit(solution)/shard_map/ppermute | solution.py:19
  38.2 2.5 %collective-permute-done.12 = f32[256,128]{1,0:T(8,128)S(1)} collective-permute-done((f32[256,128]{1,0:T(8,128)S(1)}, f32[256,128]{1,0:T(8,128)S(1)}, u32[]{:S(2)}, u32[]{:S(2)}) %collective-permute-start.12) | collective-permute-done | bytes 131104 | tf_op jit(solution)/shard_map/ppermute | solution.py:19
  44.5 3.7 %collective-permute-done.16.refs_3_ = f32[256,128]{1,0:T(8,128)S(1)} collective-permute-done((f32[256,128]{1,0:T(8,128)S(1)}, f32[256,128]{1,0:T(8,128)S(1)}, u32[]{:S(2)}, u32[]{:S(2)}) %collective-permute-start.16) | collective-permute-done | bytes 131104 | tf_op jit(solution)/shard_map/ppermute | solution.py:19
  54.3 2.7 %collective-permute-start.18 = (f32[128,128]{1,0:T(8,128)S(1)}, f32[128,128]{1,0:T(8,128)S(1)}, u32[]{:S(2)}, u32[]{:S(2)}) collective-permute-start(f32[128,128]{1,0:T(8,128)S(1)} %get-tuple-element.86), channel_id=1, source_target_pairs={{0,2},{1,3},{2,0},{3,1},{4,6},{5,7},{6,4},{7,5},{8,10},{9,11},{10,... | collective-permute-start | bytes 196616 | tf_op jit(solution)/shard_map/ppermute | solution.py:19
  57.0 2.4 %collective-permute-done.20.refs_4_ = f32[128,128]{1,0:T(8,128)S(1)} collective-permute-done((f32[128,128]{1,0:T(8,128)S(1)}, f32[128,128]{1,0:T(8,128)S(1)}, u32[]{:S(2)}, u32[]{:S(2)}) %collective-permute-start.20) | collective-permute-done | bytes 65568 | tf_op jit(solution)/shard_map/ppermute | solution.py:19
  59.3 2.0 %collective-permute-done.19.refs_3_ = f32[128,128]{1,0:T(8,128)S(1)} collective-permute-done((f32[128,128]{1,0:T(8,128)S(1)}, f32[128,128]{1,0:T(8,128)S(1)}, u32[]{:S(2)}, u32[]{:S(2)}) %collective-permute-start.19) | collective-permute-done | bytes 65568 | tf_op jit(solution)/shard_map/ppermute | solution.py:19
  62.6 11.1 %all_to_all.10.sums_ref = f32[16,2,128]{2,1,0:T(2,128)S(1)} all-to-all(f32[16,2,128]{2,1,0:T(2,128)S(1)} %shard_map.86), channel_id=1, replica_groups={{0,2,4,6,8,10,12,14,16,18,20,22,24,26,28,30},{1,3,5,7,9,11,13,15,17,19,..., dimensions={0} | all-to-all | bytes 32768 | tf_op jit(solution)/shard_map/all_to_all | solution.py:417
  78.7 2.3 %collective-permute-start.23 = (f32[128,128]{1,0:T(8,128)S(1)}, f32[128,128]{1,0:T(8,128)S(1)}, u32[]{:S(2)}, u32[]{:S(2)}) collective-permute-start(f32[128,128]{1,0:T(8,128)S(1)} %get-tuple-element.82), channel_id=1, source_target_pairs={{0,2},{1,3},{2,0},{3,1},{4,6},{5,7},{6,4},{7,5},{8,10},{9,11},{10,... | collective-permute-start | bytes 196616 | tf_op jit(solution)/shard_map/ppermute | solution.py:19
  80.9 2.4 %collective-permute-done.25.refs_3_ = f32[128,128]{1,0:T(8,128)S(1)} collective-permute-done((f32[128,128]{1,0:T(8,128)S(1)}, f32[128,128]{1,0:T(8,128)S(1)}, u32[]{:S(2)}, u32[]{:S(2)}) %collective-permute-start.25) | collective-permute-done | bytes 65568 | tf_op jit(solution)/shard_map/ppermute | solution.py:19
  86.8 2.8 %collective-permute-start.27 = (f32[128,128]{1,0:T(8,128)S(1)}, f32[128,128]{1,0:T(8,128)S(1)}, u32[]{:S(2)}, u32[]{:S(2)}) collective-permute-start(f32[128,128]{1,0:T(8,128)S(1)} %shard_map.89.refs_0_), channel_id=1, source_target_pairs={{0,2},{1,3},{2,0},{3,1},{4,6},{5,7},{6,4},{7,5},{8,10},{9,11},{10,... | collective-permute-start | bytes 196616 | tf_op jit(solution)/shard_map/ppermute | solution.py:19
  89.6 2.5 %collective-permute-done.31.refs_6_ = f32[128,128]{1,0:T(8,128)S(1)} collective-permute-done((f32[128,128]{1,0:T(8,128)S(1)}, f32[128,128]{1,0:T(8,128)S(1)}, u32[]{:S(2)}, u32[]{:S(2)}) %collective-permute-start.31) | collective-permute-done | bytes 65568 | tf_op jit(solution)/shard_map/ppermute | solution.py:19
  100.1 3.2 %collective-permute-done.33 = f32[256,128]{1,0:T(8,128)S(1)} collective-permute-done((f32[256,128]{1,0:T(8,128)S(1)}, f32[256,128]{1,0:T(8,128)S(1)}, u32[]{:S(2)}, u32[]{:S(2)}) %collective-permute-start.33) | collective-permute-done | bytes 131104 | tf_op jit(solution)/shard_map/ppermute | solution.py:19
  108.6 3.5 %collective-permute-done.38.refs_3_ = f32[256,128]{1,0:T(8,128)S(1)} collective-permute-done((f32[256,128]{1,0:T(8,128)S(1)}, f32[256,128]{1,0:T(8,128)S(1)}, u32[]{:S(2)}, u32[]{:S(2)}) %collective-permute-start.38) | collective-permute-done | bytes 131104 | tf_op jit(solution)/shard_map/ppermute | solution.py:19
  116.4 2.0 %collective-permute-start.42 = (f32[128,128]{1,0:T(8,128)S(1)}, f32[128,128]{1,0:T(8,128)S(1)}, u32[]{:S(2)}, u32[]{:S(2)}) collective-permute-start(f32[128,128]{1,0:T(8,128)S(1)} %get-tuple-element.76), channel_id=1, source_target_pairs={{0,6},{1,7},{2,4},{3,5},{4,2},{5,3},{6,0},{7,1},{8,14},{9,15},{10,... | collective-permute-start | bytes 196616 | tf_op jit(solution)/shard_map/ppermute | solution.py:19
  118.4 2.5 %collective-permute-start.40 = (f32[128,128]{1,0:T(8,128)S(1)}, f32[128,128]{1,0:T(8,128)S(1)}, u32[]{:S(2)}, u32[]{:S(2)}) collective-permute-start(f32[128,128]{1,0:T(8,128)S(1)} %get-tuple-element.78), channel_id=1, source_target_pairs={{0,2},{1,3},{2,0},{3,1},{4,6},{5,7},{6,4},{7,5},{8,10},{9,11},{10,... | collective-permute-start | bytes 196616 | tf_op jit(solution)/shard_map/ppermute | solution.py:19
  120.9 2.4 %collective-permute-done.42.refs_4_ = f32[128,128]{1,0:T(8,128)S(1)} collective-permute-done((f32[128,128]{1,0:T(8,128)S(1)}, f32[128,128]{1,0:T(8,128)S(1)}, u32[]{:S(2)}, u32[]{:S(2)}) %collective-permute-start.42) | collective-permute-done | bytes 65568 | tf_op jit(solution)/shard_map/ppermute | solution.py:19
  123.2 2.0 %collective-permute-done.41.refs_3_ = f32[128,128]{1,0:T(8,128)S(1)} collective-permute-done((f32[128,128]{1,0:T(8,128)S(1)}, f32[128,128]{1,0:T(8,128)S(1)}, u32[]{:S(2)}, u32[]{:S(2)}) %collective-permute-start.41) | collective-permute-done | bytes 65568 | tf_op jit(solution)/shard_map/ppermute | solution.py:19
  126.5 11.3 %all_to_all.11.sums_ref = f32[16,2,128]{2,1,0:T(2,128)S(1)} all-to-all(f32[16,2,128]{2,1,0:T(2,128)S(1)} %shard_map.95), channel_id=1, replica_groups={{0,2,4,6,8,10,12,14,16,18,20,22,24,26,28,30},{1,3,5,7,9,11,13,15,17,19,..., dimensions={0} | all-to-all | bytes 32768 | tf_op jit(solution)/shard_map/all_to_all | solution.py:417
  142.8 2.3 %collective-permute-start.45 = (f32[128,128]{1,0:T(8,128)S(1)}, f32[128,128]{1,0:T(8,128)S(1)}, u32[]{:S(2)}, u32[]{:S(2)}) collective-permute-start(f32[128,128]{1,0:T(8,128)S(1)} %get-tuple-element.74), channel_id=1, source_target_pairs={{0,2},{1,3},{2,0},{3,1},{4,6},{5,7},{6,4},{7,5},{8,10},{9,11},{10,... | collective-permute-start | bytes 196616 | tf_op jit(solution)/shard_map/ppermute | solution.py:19
  145.0 2.5 %shard_map.98 = (f32[1024,128]{1,0:T(8,128)S(1)}, f32[1024,128]{1,0:T(8,128)S(1)}) custom-call(f32[1024,128]{1,0:T(8,128)S(1)} %get-tuple-element.62.coef_ref, s32[8,128]{1,0:T(8,128)S(1)} %bitcast.46, bf16[512,1024]{1,0:T(8,128)(2,1)S(1)} %get-tuple-element.37.high_ref.refs_8_.refs_1_.refs_0_, ...), custom_call_target="tpu_custom_call" | custom-call | flops 2147483648 | bytes 8388608 | tf_op jit(solution)/shard_map/pallas_call | solution.py:428
  150.9 2.8 %collective-permute-start.49 = (f32[128,128]{1,0:T(8,128)S(1)}, f32[128,128]{1,0:T(8,128)S(1)}, u32[]{:S(2)}, u32[]{:S(2)}) collective-permute-start(f32[128,128]{1,0:T(8,128)S(1)} %shard_map.99.refs_0_), channel_id=1, source_target_pairs={{0,2},{1,3},{2,0},{3,1},{4,6},{5,7},{6,4},{7,5},{8,10},{9,11},{10,... | collective-permute-start | bytes 196616 | tf_op jit(solution)/shard_map/ppermute | solution.py:19
  153.7 2.5 %collective-permute-done.53.refs_6_ = f32[128,128]{1,0:T(8,128)S(1)} collective-permute-done((f32[128,128]{1,0:T(8,128)S(1)}, f32[128,128]{1,0:T(8,128)S(1)}, u32[]{:S(2)}, u32[]{:S(2)}) %collective-permute-start.53) | collective-permute-done | bytes 65568 | tf_op jit(solution)/shard_map/ppermute | solution.py:19
  164.5 2.9 %collective-permute-done.55.refs_1_ = f32[272,128]{1,0:T(8,128)S(1)} collective-permute-done((f32[272,128]{1,0:T(8,128)S(1)}, f32[272,128]{1,0:T(8,128)S(1)}, u32[]{:S(2)}, u32[]{:S(2)}) %collective-permute-start.55) | collective-permute-done | bytes 139296 | tf_op jit(solution)/shard_map/ppermute | solution.py:19
  173.0 3.5 %collective-permute-done.60.refs_3_ = f32[256,128]{1,0:T(8,128)S(1)} collective-permute-done((f32[256,128]{1,0:T(8,128)S(1)}, f32[256,128]{1,0:T(8,128)S(1)}, u32[]{:S(2)}, u32[]{:S(2)}) %collective-permute-start.60) | collective-permute-done | bytes 131104 | tf_op jit(solution)/shard_map/ppermute | solution.py:19
  (145 shorter events, 74.4 us)
Async XLA Ops:
  8.7 7.7 %collective-permute-start.3 = (f32[128,128]{1,0:T(8,128)S(1)}, f32[128,128]{1,0:T(8,128)S(1)}, u32[]{:S(2)}, u32[]{:S(2)}) collective-permute-start(f32[128,128]{1,0:T(8,128)S(1)} %get-tuple-element.88), channel_id=1, source_target_pairs={{0,6},{1,7},{2,4},{3,5},{4,2},{5,3},{6,0},{7,1},{8,14},{9,15},{10,... | collective-permute-start | bytes 196616 | tf_op jit(solution)/shard_map/ppermute | solution.py:19
  31.2 7.0 %collective-permute-start.11 = (f32[256,128]{1,0:T(8,128)S(1)}, f32[256,128]{1,0:T(8,128)S(1)}, u32[]{:S(2)}, u32[]{:S(2)}) collective-permute-start(f32[256,128]{1,0:T(8,128)S(1)} %get-tuple-element.44), channel_id=1, source_target_pairs={{0,24},{8,16},{16,8},{24,0},{1,25},{9,17},{17,9},{25,1},{2,26},{10... | collective-permute-start | bytes 393224 | tf_op jit(solution)/shard_map/ppermute | solution.py:19
  33.7 7.0 %collective-permute-start.12 = (f32[256,128]{1,0:T(8,128)S(1)}, f32[256,128]{1,0:T(8,128)S(1)}, u32[]{:S(2)}, u32[]{:S(2)}) collective-permute-start(f32[256,128]{1,0:T(8,128)S(1)} %get-tuple-element.45), channel_id=1, source_target_pairs={{0,16},{8,24},{16,0},{24,8},{1,17},{9,25},{17,1},{25,9},{2,18},{10... | collective-permute-start | bytes 393224 | tf_op jit(solution)/shard_map/ppermute | solution.py:19
  34.2 6.6 %collective-permute-start.13 = (f32[256,128]{1,0:T(8,128)S(1)}, f32[256,128]{1,0:T(8,128)S(1)}, u32[]{:S(2)}, u32[]{:S(2)}) collective-permute-start(f32[256,128]{1,0:T(8,128)S(1)} %get-tuple-element.46), channel_id=1, source_target_pairs={{0,8},{8,0},{16,24},{24,16},{1,9},{9,1},{17,25},{25,17},{2,10},{10... | collective-permute-start | bytes 393224 | tf_op jit(solution)/shard_map/ppermute | solution.py:19
  40.9 7.4 %collective-permute-start.16 = (f32[256,128]{1,0:T(8,128)S(1)}, f32[256,128]{1,0:T(8,128)S(1)}, u32[]{:S(2)}, u32[]{:S(2)}) collective-permute-start(f32[256,128]{1,0:T(8,128)S(1)} %add_multiply_fusion.1.refs_0_), channel_id=1, source_target_pairs={{0,24},{8,16},{16,8},{24,0},{1,25},{9,17},{17,9},{25,1},{2,26},{10... | collective-permute-start | bytes 393224 | tf_op jit(solution)/shard_map/ppermute | solution.py:19
  42.6 7.4 %collective-permute-start.15 = (f32[256,128]{1,0:T(8,128)S(1)}, f32[256,128]{1,0:T(8,128)S(1)}, u32[]{:S(2)}, u32[]{:S(2)}) collective-permute-start(f32[256,128]{1,0:T(8,128)S(1)} %add_multiply_fusion.1.refs_0_), channel_id=1, source_target_pairs={{0,16},{8,24},{16,0},{24,8},{1,17},{9,25},{17,1},{25,9},{2,18},{10... | collective-permute-start | bytes 393224 | tf_op jit(solution)/shard_map/ppermute | solution.py:19
  52.5 6.8 %collective-permute-start.20 = (f32[128,128]{1,0:T(8,128)S(1)}, f32[128,128]{1,0:T(8,128)S(1)}, u32[]{:S(2)}, u32[]{:S(2)}) collective-permute-start(f32[128,128]{1,0:T(8,128)S(1)} %get-tuple-element.84), channel_id=1, source_target_pairs={{0,6},{1,7},{2,4},{3,5},{4,2},{5,3},{6,0},{7,1},{8,14},{9,15},{10,... | collective-permute-start | bytes 196616 | tf_op jit(solution)/shard_map/ppermute | solution.py:19
  54.3 7.1 %collective-permute-start.19 = (f32[128,128]{1,0:T(8,128)S(1)}, f32[128,128]{1,0:T(8,128)S(1)}, u32[]{:S(2)}, u32[]{:S(2)}) collective-permute-start(f32[128,128]{1,0:T(8,128)S(1)} %get-tuple-element.85), channel_id=1, source_target_pairs={{0,4},{1,5},{2,6},{3,7},{4,0},{5,1},{6,2},{7,3},{8,12},{9,13},{10,... | collective-permute-start | bytes 196616 | tf_op jit(solution)/shard_map/ppermute | solution.py:19
  54.3 7.1 %collective-permute-start.18 = (f32[128,128]{1,0:T(8,128)S(1)}, f32[128,128]{1,0:T(8,128)S(1)}, u32[]{:S(2)}, u32[]{:S(2)}) collective-permute-start(f32[128,128]{1,0:T(8,128)S(1)} %get-tuple-element.86), channel_id=1, source_target_pairs={{0,2},{1,3},{2,0},{3,1},{4,6},{5,7},{6,4},{7,5},{8,10},{9,11},{10,... | collective-permute-start | bytes 196616 | tf_op jit(solution)/shard_map/ppermute | solution.py:19
  76.5 6.8 %collective-permute-start.25 = (f32[128,128]{1,0:T(8,128)S(1)}, f32[128,128]{1,0:T(8,128)S(1)}, u32[]{:S(2)}, u32[]{:S(2)}) collective-permute-start(f32[128,128]{1,0:T(8,128)S(1)} %get-tuple-element.80), channel_id=1, source_target_pairs={{0,6},{1,7},{2,4},{3,5},{4,2},{5,3},{6,0},{7,1},{8,14},{9,15},{10,... | collective-permute-start | bytes 196616 | tf_op jit(solution)/shard_map/ppermute | solution.py:19
  77.2 8.0 %collective-permute-start.24 = (f32[128,128]{1,0:T(8,128)S(1)}, f32[128,128]{1,0:T(8,128)S(1)}, u32[]{:S(2)}, u32[]{:S(2)}) collective-permute-start(f32[128,128]{1,0:T(8,128)S(1)} %get-tuple-element.81), channel_id=1, source_target_pairs={{0,4},{1,5},{2,6},{3,7},{4,0},{5,1},{6,2},{7,3},{8,12},{9,13},{10,... | collective-permute-start | bytes 196616 | tf_op jit(solution)/shard_map/ppermute | solution.py:19
  85.1 6.9 %collective-permute-start.31 = (f32[128,128]{1,0:T(8,128)S(1)}, f32[128,128]{1,0:T(8,128)S(1)}, u32[]{:S(2)}, u32[]{:S(2)}) collective-permute-start(f32[128,128]{1,0:T(8,128)S(1)} %shard_map.89.refs_0_), channel_id=1, source_target_pairs={{0,6},{1,7},{2,4},{3,5},{4,2},{5,3},{6,0},{7,1},{8,14},{9,15},{10,... | collective-permute-start | bytes 196616 | tf_op jit(solution)/shard_map/ppermute | solution.py:19
  86.6 6.9 %collective-permute-start.29 = (f32[128,128]{1,0:T(8,128)S(1)}, f32[128,128]{1,0:T(8,128)S(1)}, u32[]{:S(2)}, u32[]{:S(2)}) collective-permute-start(f32[128,128]{1,0:T(8,128)S(1)} %shard_map.89.refs_0_), channel_id=1, source_target_pairs={{0,4},{1,5},{2,6},{3,7},{4,0},{5,1},{6,2},{7,3},{8,12},{9,13},{10,... | collective-permute-start | bytes 196616 | tf_op jit(solution)/shard_map/ppermute | solution.py:19
  86.8 6.8 %collective-permute-start.27 = (f32[128,128]{1,0:T(8,128)S(1)}, f32[128,128]{1,0:T(8,128)S(1)}, u32[]{:S(2)}, u32[]{:S(2)}) collective-permute-start(f32[128,128]{1,0:T(8,128)S(1)} %shard_map.89.refs_0_), channel_id=1, source_target_pairs={{0,2},{1,3},{2,0},{3,1},{4,6},{5,7},{6,4},{7,5},{8,10},{9,11},{10,... | collective-permute-start | bytes 196616 | tf_op jit(solution)/shard_map/ppermute | solution.py:19
  96.1 7.3 %collective-permute-start.33 = (f32[256,128]{1,0:T(8,128)S(1)}, f32[256,128]{1,0:T(8,128)S(1)}, u32[]{:S(2)}, u32[]{:S(2)}) collective-permute-start(f32[256,128]{1,0:T(8,128)S(1)} %get-tuple-element.54), channel_id=1, source_target_pairs={{0,24},{8,16},{16,8},{24,0},{1,25},{9,17},{17,9},{25,1},{2,26},{10... | collective-permute-start | bytes 393224 | tf_op jit(solution)/shard_map/ppermute | solution.py:19
  96.7 8.3 %collective-permute-start.34 = (f32[256,128]{1,0:T(8,128)S(1)}, f32[256,128]{1,0:T(8,128)S(1)}, u32[]{:S(2)}, u32[]{:S(2)}) collective-permute-start(f32[256,128]{1,0:T(8,128)S(1)} %get-tuple-element.55), channel_id=1, source_target_pairs={{0,16},{8,24},{16,0},{24,8},{1,17},{9,25},{17,1},{25,9},{2,18},{10... | collective-permute-start | bytes 393224 | tf_op jit(solution)/shard_map/ppermute | solution.py:19
  97.9 7.1 %collective-permute-start.35 = (f32[256,128]{1,0:T(8,128)S(1)}, f32[256,128]{1,0:T(8,128)S(1)}, u32[]{:S(2)}, u32[]{:S(2)}) collective-permute-start(f32[256,128]{1,0:T(8,128)S(1)} %get-tuple-element.56), channel_id=1, source_target_pairs={{0,8},{8,0},{16,24},{24,16},{1,9},{9,1},{17,25},{25,17},{2,10},{10... | collective-permute-start | bytes 393224 | tf_op jit(solution)/shard_map/ppermute | solution.py:19
  105.0 7.1 %collective-permute-start.38 = (f32[256,128]{1,0:T(8,128)S(1)}, f32[256,128]{1,0:T(8,128)S(1)}, u32[]{:S(2)}, u32[]{:S(2)}) collective-permute-start(f32[256,128]{1,0:T(8,128)S(1)} %add_multiply_fusion.refs_0_), channel_id=1, source_target_pairs={{0,24},{8,16},{16,8},{24,0},{1,25},{9,17},{17,9},{25,1},{2,26},{10... | collective-permute-start | bytes 393224 | tf_op jit(solution)/shard_map/ppermute | solution.py:19
  106.2 7.3 %collective-permute-start.37 = (f32[256,128]{1,0:T(8,128)S(1)}, f32[256,128]{1,0:T(8,128)S(1)}, u32[]{:S(2)}, u32[]{:S(2)}) collective-permute-start(f32[256,128]{1,0:T(8,128)S(1)} %add_multiply_fusion.refs_0_), channel_id=1, source_target_pairs={{0,16},{8,24},{16,0},{24,8},{1,17},{9,25},{17,1},{25,9},{2,18},{10... | collective-permute-start | bytes 393224 | tf_op jit(solution)/shard_map/ppermute | solution.py:19
  116.4 6.8 %collective-permute-start.42 = (f32[128,128]{1,0:T(8,128)S(1)}, f32[128,128]{1,0:T(8,128)S(1)}, u32[]{:S(2)}, u32[]{:S(2)}) collective-permute-start(f32[128,128]{1,0:T(8,128)S(1)} %get-tuple-element.76), channel_id=1, source_target_pairs={{0,6},{1,7},{2,4},{3,5},{4,2},{5,3},{6,0},{7,1},{8,14},{9,15},{10,... | collective-permute-start | bytes 196616 | tf_op jit(solution)/shard_map/ppermute | solution.py:19
  118.4 6.8 %collective-permute-start.41 = (f32[128,128]{1,0:T(8,128)S(1)}, f32[128,128]{1,0:T(8,128)S(1)}, u32[]{:S(2)}, u32[]{:S(2)}) collective-permute-start(f32[128,128]{1,0:T(8,128)S(1)} %get-tuple-element.77), channel_id=1, source_target_pairs={{0,4},{1,5},{2,6},{3,7},{4,0},{5,1},{6,2},{7,3},{8,12},{9,13},{10,... | collective-permute-start | bytes 196616 | tf_op jit(solution)/shard_map/ppermute | solution.py:19
  118.4 6.8 %collective-permute-start.40 = (f32[128,128]{1,0:T(8,128)S(1)}, f32[128,128]{1,0:T(8,128)S(1)}, u32[]{:S(2)}, u32[]{:S(2)}) collective-permute-start(f32[128,128]{1,0:T(8,128)S(1)} %get-tuple-element.78), channel_id=1, source_target_pairs={{0,2},{1,3},{2,0},{3,1},{4,6},{5,7},{6,4},{7,5},{8,10},{9,11},{10,... | collective-permute-start | bytes 196616 | tf_op jit(solution)/shard_map/ppermute | solution.py:19
  140.6 7.0 %collective-permute-start.47 = (f32[128,128]{1,0:T(8,128)S(1)}, f32[128,128]{1,0:T(8,128)S(1)}, u32[]{:S(2)}, u32[]{:S(2)}) collective-permute-start(f32[128,128]{1,0:T(8,128)S(1)} %get-tuple-element.72), channel_id=1, source_target_pairs={{0,6},{1,7},{2,4},{3,5},{4,2},{5,3},{6,0},{7,1},{8,14},{9,15},{10,... | collective-permute-start | bytes 196616 | tf_op jit(solution)/shard_map/ppermute | solution.py:19
  141.3 8.0 %collective-permute-start.46 = (f32[128,128]{1,0:T(8,128)S(1)}, f32[128,128]{1,0:T(8,128)S(1)}, u32[]{:S(2)}, u32[]{:S(2)}) collective-permute-start(f32[128,128]{1,0:T(8,128)S(1)} %get-tuple-element.73), channel_id=1, source_target_pairs={{0,4},{1,5},{2,6},{3,7},{4,0},{5,1},{6,2},{7,3},{8,12},{9,13},{10,... | collective-permute-start | bytes 196616 | tf_op jit(solution)/shard_map/ppermute | solution.py:19
  149.2 6.9 %collective-permute-start.53 = (f32[128,128]{1,0:T(8,128)S(1)}, f32[128,128]{1,0:T(8,128)S(1)}, u32[]{:S(2)}, u32[]{:S(2)}) collective-permute-start(f32[128,128]{1,0:T(8,128)S(1)} %shard_map.99.refs_0_), channel_id=1, source_target_pairs={{0,6},{1,7},{2,4},{3,5},{4,2},{5,3},{6,0},{7,1},{8,14},{9,15},{10,... | collective-permute-start | bytes 196616 | tf_op jit(solution)/shard_map/ppermute | solution.py:19
  150.7 6.9 %collective-permute-start.51 = (f32[128,128]{1,0:T(8,128)S(1)}, f32[128,128]{1,0:T(8,128)S(1)}, u32[]{:S(2)}, u32[]{:S(2)}) collective-permute-start(f32[128,128]{1,0:T(8,128)S(1)} %shard_map.99.refs_0_), channel_id=1, source_target_pairs={{0,4},{1,5},{2,6},{3,7},{4,0},{5,1},{6,2},{7,3},{8,12},{9,13},{10,... | collective-permute-start | bytes 196616 | tf_op jit(solution)/shard_map/ppermute | solution.py:19
  150.9 6.8 %collective-permute-start.49 = (f32[128,128]{1,0:T(8,128)S(1)}, f32[128,128]{1,0:T(8,128)S(1)}, u32[]{:S(2)}, u32[]{:S(2)}) collective-permute-start(f32[128,128]{1,0:T(8,128)S(1)} %shard_map.99.refs_0_), channel_id=1, source_target_pairs={{0,2},{1,3},{2,0},{3,1},{4,6},{5,7},{6,4},{7,5},{8,10},{9,11},{10,... | collective-permute-start | bytes 196616 | tf_op jit(solution)/shard_map/ppermute | solution.py:19
  159.9 7.5 %collective-permute-start.55 = (f32[272,128]{1,0:T(8,128)S(1)}, f32[272,128]{1,0:T(8,128)S(1)}, u32[]{:S(2)}, u32[]{:S(2)}) collective-permute-start(f32[272,128]{1,0:T(8,128)S(1)} %get-tuple-element.68), channel_id=1, source_target_pairs={{0,24},{8,16},{16,8},{24,0},{1,25},{9,17},{17,9},{25,1},{2,26},{10... | collective-permute-start | bytes 417800 | tf_op jit(solution)/shard_map/ppermute | solution.py:19
  160.6 8.6 %collective-permute-start.56 = (f32[272,128]{1,0:T(8,128)S(1)}, f32[272,128]{1,0:T(8,128)S(1)}, u32[]{:S(2)}, u32[]{:S(2)}) collective-permute-start(f32[272,128]{1,0:T(8,128)S(1)} %get-tuple-element.69), channel_id=1, source_target_pairs={{0,16},{8,24},{16,0},{24,8},{1,17},{9,25},{17,1},{25,9},{2,18},{10... | collective-permute-start | bytes 417800 | tf_op jit(solution)/shard_map/ppermute | solution.py:19
  161.8 7.4 %collective-permute-start.57 = (f32[272,128]{1,0:T(8,128)S(1)}, f32[272,128]{1,0:T(8,128)S(1)}, u32[]{:S(2)}, u32[]{:S(2)}) collective-permute-start(f32[272,128]{1,0:T(8,128)S(1)} %get-tuple-element.70), channel_id=1, source_target_pairs={{0,8},{8,0},{16,24},{24,16},{1,9},{9,1},{17,25},{25,17},{2,10},{10... | collective-permute-start | bytes 417800 | tf_op jit(solution)/shard_map/ppermute | solution.py:19
  169.5 7.1 %collective-permute-start.60 = (f32[256,128]{1,0:T(8,128)S(1)}, f32[256,128]{1,0:T(8,128)S(1)}, u32[]{:S(2)}, u32[]{:S(2)}) collective-permute-start(f32[256,128]{1,0:T(8,128)S(1)} %shard_map.102.refs_0_), channel_id=1, source_target_pairs={{0,24},{8,16},{16,8},{24,0},{1,25},{9,17},{17,9},{25,1},{2,26},{10... | collective-permute-start | bytes 393224 | tf_op jit(solution)/shard_map/ppermute | solution.py:19
  170.7 7.3 %collective-permute-start.59 = (f32[256,128]{1,0:T(8,128)S(1)}, f32[256,128]{1,0:T(8,128)S(1)}, u32[]{:S(2)}, u32[]{:S(2)}) collective-permute-start(f32[256,128]{1,0:T(8,128)S(1)} %shard_map.102.refs_0_), channel_id=1, source_target_pairs={{0,16},{8,24},{16,0},{24,8},{1,17},{9,25},{17,1},{25,9},{2,18},{10... | collective-permute-start | bytes 393224 | tf_op jit(solution)/shard_map/ppermute | solution.py:19
  (38 other events, 256.6 us)

commit v6 on v4

--- a/solution.py
+++ b/solution.py
@@ -85,11 +85,18 @@
         for k in range(half)
     ]
     coef_copy.start()
-    for copy in copies:
+    for copy in copies[:half]:
         copy.start()
     coef_copy.wait()
     packed_ref[...] = pack(coef_buffer[...])
-    split_rows(buffer_ref, lambda k: copies[k].wait(), packed_ref, high_ref, low_ref, out_ref)
+
+    def ready(k):
+        copies[k].wait()
+        if k == half // 2:
+            for copy in copies[half:]:
+                copy.start()
+
+    split_rows(buffer_ref, ready, packed_ref, high_ref, low_ref, out_ref)
     for copy in copies[half:]:
         copy.wait()
 
@@ -120,10 +127,13 @@
 
 
 def residual_kernel(count, traits_ref, *refs):
+    out = refs[-1]
+    block = out.shape[0]
     total = refs[0][...]
     for piece in refs[1:count]:
         total = total + piece[...]
-    refs[-1][...] = traits_ref[...] - total
+    start = pl.multiple_of(lax.axis_index("chrom") * block, block)
+    out[...] = traits_ref[pl.ds(start, block)] - total
 
 
 def grad_dot(packed_ref, parts, which, width):
@@ -230,8 +240,8 @@
 
 def loco_kernel(count, partners, *refs):
     pieces, own_refs = refs[:count], refs[count : count + GPD]
-    tested_ref, square_ref, owner_ref, residual_ref, loco_ref, sums_ref = refs[count + GPD : count + GPD + 6]
-    outs, rows_ref = refs[count + GPD + 6 : -1], refs[-1]
+    tested_ref, square_ref, owner_ref, loco_ref, sums_ref = refs[count + GPD : count + GPD + 5]
+    outs, rows_ref = refs[count + GPD + 5 : -1], refs[-1]
     me, samp = lax.axis_index("chrom"), lax.axis_index("samp")
     block, traits = pieces[0].shape
     sums_ref[...] = jnp.zeros_like(sums_ref)
@@ -239,7 +249,6 @@
         rows = pl.ds(pl.multiple_of((me ^ bits) * block, block), block)
         start = ((bits % 2) * (count // 2) + bits // 2) * block
         value = piece[...]
-        residual_ref[rows] = value
         for which in range(GPD):
             loco = value + own_refs[which][start : start + block]
             sums_ref[which : which + 1] += jnp.sum(loco * loco, axis=0, keepdims=True)
@@ -249,10 +258,14 @@
         score_products(samp ^ partner, out, tested_ref, square_ref, owner_ref, loco_ref, sums_ref)
 
 
-def loco_near_kernel(partners, *refs):
-    samp = lax.axis_index("samp")
-    for partner, out in zip(partners, refs[5:]):
-        score_products(samp ^ partner, out, *refs[:5])
+def loco_near_kernel(count, partners, *refs):
+    pieces, operands, residual_ref, outs = refs[:count], refs[count : count + 5], refs[count + 5], refs[count + 6 :]
+    me, samp = lax.axis_index("chrom"), lax.axis_index("samp")
+    block = pieces[0].shape[0]
+    for bits, piece in enumerate(pieces):
+        residual_ref[pl.ds(pl.multiple_of((me ^ bits) * block, block), block)] = piece[...]
+    for partner, out in zip(partners, outs):
+        score_products(samp ^ partner, out, *operands)
 
 
 def score_kernel(total_rows, owner_ref, *refs):
@@ -280,19 +293,31 @@
         out[pl.ds(pl.multiple_of((samp ^ bits) * block, block), block)] = piece[...]
 
 
+def chip_kernel(keep_ref, got_ref, *outs):
+    for k, out in enumerate(outs):
+        out[...] = keep_ref[k] + got_ref[k]
+
+
+def mean_kernel(total_rows, *refs):
+    total = refs[0][...]
+    for piece in refs[1:-1]:
+        total = total + piece[...]
+    refs[-1][...] = total / total_rows
+
+
 def chrom_scatter(give, keep):
     got = swap(give, "chrom", 1)
     count = keep.shape[0]
-    sums = [keep[k] + got[k] for k in range(count)]
+    sums = call(chip_kernel, [shape(keep.shape[1:])] * count, [whole()] * 2)(keep, got)
     return [sums[0]] + [swap(sums[k], "chrom", 2 * k) for k in reversed(range(1, count))]
 
 
 def chrom_gather(own):
-    count = lax.axis_size("chrom") // 2
-    far = [swap(own, "chrom", 2 * k) for k in reversed(range(1, count))]
-    mine = [own] + far[::-1]
-    other = [swap(block, "chrom", 1) for block in mine]
-    return [block for pair in zip(mine, other) for block in pair]
+    blocks = []
+    for k in range(lax.axis_size("chrom") // 2):
+        block = swap(own, "chrom", 2 * k) if k else own
+        blocks += [block, swap(block, "chrom", 1)]
+    return blocks
 
 
 def samp_order(size):
@@ -309,7 +334,6 @@
     rows, cols = dosages.shape
     tests, n_traits = tested.shape[1], traits.shape[1]
     total_rows = rows * n_samp
-    me = lax.axis_index("chrom")
     half, block, width, test_width = n_chrom // 2, rows // n_chrom, cols // n_samp, tests // n_samp
     flops = 4 * rows * cols * n_traits
     moved = 2 * rows * cols
@@ -326,7 +350,6 @@
     coef_out = shape((cols, n_traits))
     group_rows = groups.reshape(cols // 128, 128)
     owner_rows = owners.reshape(n_samp, 1, test_width)
-    own_traits = lax.dynamic_slice_in_dim(traits, me * block, block, 0)
 
     def rest(high, low, packed):
         return call(rest_kernel, half_out, [whole()] * 3, (), flops, moved)(high, low, packed)
@@ -336,7 +359,7 @@
             functools.partial(residual_kernel, len(summands)),
             shape((block, n_traits)),
             [whole()] * (1 + len(summands)) + [anywhere()] * len(after),
-        )(own_traits, *summands, *after)
+        )(traits, *summands, *after)
 
     coefficients = start_coef
     kept_shape = (half, block, cols)
@@ -370,10 +393,10 @@
         near_out = call(
             functools.partial(grad_near_kernel, near), [grad_block] * len(near), [whole()] * 5, (), flops, moved
         )(packed, *parts)
-        own_grad = near_out[-1]
-        for partner, piece in zip(order, far_out + list(near_out[:-1])):
-            own_grad = own_grad + swap(piece, "samp", partner)
-        own_grad = own_grad / total_rows
+        received = [swap(piece, "samp", partner) for partner, piece in zip(order, far_out)]
+        own_grad = call(functools.partial(mean_kernel, total_rows), grad_block, [whole()] * n_samp)(
+            near_out[-1], *received
+        )
         pieces = samp_gather(own_grad)
         after = (tested_sq,) if iteration == 0 else ()
         gradient, packed, give = call(
@@ -404,19 +427,24 @@
         coefficients, group_rows, *parts
     )
     pieces = chrom_gather(own_residual(summands, own_parts))
-    residual, loco, loco_sq, *far_out = call(
+    loco, loco_sq, *far_out = call(
         functools.partial(loco_kernel, n_chrom, far),
-        [shape((rows, n_traits)), shape((GPD * n_traits, rows), jnp.bfloat16), shape((8, n_traits))]
+        [shape((GPD * n_traits, rows), jnp.bfloat16), shape((8, n_traits))]
         + [score_block] * len(far),
         [whole()] * (n_chrom + GPD + 3),
         [pltpu.VMEM((rows, GPD * n_traits), jnp.bfloat16)],
         flops,
         moved,
     )(*pieces, *own_parts, tested, tested_sq, owner_rows)
-    near_out = call(
-        functools.partial(loco_near_kernel, near), [score_block] * len(near), [whole()] * 5, (), flops // 2, moved
-    )(tested, tested_sq, owner_rows, loco, loco_sq)
-    received = [swap(piece, "samp", partner) for partner, piece in zip(order, far_out + list(near_out[:-1]))]
+    residual, *near_out = call(
+        functools.partial(loco_near_kernel, n_chrom, near),
+        [shape((rows, n_traits))] + [score_block] * len(near),
+        [whole()] * (n_chrom + 5),
+        (),
+        flops // 2,
+        moved,
+    )(*pieces, tested, tested_sq, owner_rows, loco, loco_sq)
+    received = [swap(piece, "samp", partner) for partner, piece in zip(order, far_out)]
     own_scores = call(
         functools.partial(score_kernel, total_rows), shape((test_width, n_traits)), [whole()] * (n_samp + 1)
     )(owner_rows, near_out[-1], *received)

time: 175 us -> 172 us (0.983)
  local copies, waits for them, and re-layouts: 2.94 us -> 0.03 us
    unnamed x14 -> x10, local copies, waits for them, and re-layouts: 2.93 us -> 0.03 us
  transfers between devices with their start and end apart: 59 -> 59, of which waited for: 41 -> 42; matrix products, arithmetic and copies ran while one was open for 0% -> 0% of each run, Pallas kernels for 4% -> 5%
where the time goes in v6:
time: 172 us; the launch traced here: 171 us
  waiting for transfers between devices  69.4 us (40%)
  starting transfers between devices  60.1 us (35%)
  Pallas kernels  20.7 us (12%)
  blocking collectives  20.4 us (12%)
    ppermute x59, waiting for transfers between devices, swap(): return lax.ppermute(value, axis, [(i, i ^ bits) for i in range(size)])  69.4 us
    ppermute x59, starting transfers between devices, swap(): return lax.ppermute(value, axis, [(i, i ^ bits) for i in range(size)])  60.1 us
    all_to_all x2, blocking collectives, body(): sums = lax.all_to_all(sums, ('samp', 'chrom'), 0, 0)  20.4 us
    pallas_call x1, Pallas kernels, body(): call(first_kernel, [part, part, half_out, packed_cols, shape(kept_shape)]...  3.65 us
  transfers between devices with their start and end apart: 59, of which 42 were waited for; matrix products, arithmetic and copies ran while one was open for 0% of the time, Pallas kernels for 5%

profile of v6, /device:TPU:0, one launch (start us, length us, event | category | flops | bytes accessed | tf_op | source)
XLA Modules:
  0.0 171.5 jit_solution(4221554255305616297)
XLA Ops:
  0.6 3.6 %shard_map.77 = (bf16[512,1024]{1,0:T(8,128)(2,1)S(1)}, bf16[512,1024]{1,0:T(8,128)(2,1)S(1)}, f32[4,128,128]{2,1,0:T(8,128)S(1)}, bf16[1024,256]{1,0:T(8,128)(2,1)S(1)}, f32[4,128,1024]{2,1,0:T(8,128)S(1)}) custom-call(f32[4,2,128,1024]{3,2,1,0:T(8,128)} %bitcast.7, f32[1024,128]{1,0:T(8,128)} %coef_ref.3), custom_call_target="tpu_custom_call" | custom-call | flops 536870912 | bytes 8388608 | tf_op jit(solution)/shard_map/pallas_call | solution.py:366
  6.0 5.0 %collective-permute-start.1 = (f32[128,128]{1,0:T(8,128)S(1)}, f32[128,128]{1,0:T(8,128)S(1)}, u32[]{:S(2)}, u32[]{:S(2)}) collective-permute-start(f32[128,128]{1,0:T(8,128)S(1)} %get-tuple-element.66), channel_id=1, source_target_pairs={{0,6},{1,7},{2,4},{3,5},{4,2},{5,3},{6,0},{7,1},{8,14},{9,15},{10,... | collective-permute-start | bytes 196616 | tf_op jit(solution)/shard_map/ppermute | solution.py:19
  11.7 2.0 %collective-permute-done.1.refs_1_ = f32[128,128]{1,0:T(8,128)S(1)} collective-permute-done((f32[128,128]{1,0:T(8,128)S(1)}, f32[128,128]{1,0:T(8,128)S(1)}, u32[]{:S(2)}, u32[]{:S(2)}) %collective-permute-start.1) | collective-permute-done | bytes 65568 | tf_op jit(solution)/shard_map/ppermute | solution.py:19
  13.7 3.3 %collective-permute-done.2.refs_2_ = f32[128,128]{1,0:T(8,128)S(1)} collective-permute-done((f32[128,128]{1,0:T(8,128)S(1)}, f32[128,128]{1,0:T(8,128)S(1)}, u32[]{:S(2)}, u32[]{:S(2)}) %collective-permute-start.2) | collective-permute-done | bytes 65568 | tf_op jit(solution)/shard_map/ppermute | solution.py:19
  17.0 2.5 %collective-permute-start.9 = (f32[128,128]{1,0:T(8,128)S(1)}, f32[128,128]{1,0:T(8,128)S(1)}, u32[]{:S(2)}, u32[]{:S(2)}) collective-permute-start(f32[128,128]{1,0:T(8,128)S(1)} %shard_map.80.refs_0_), channel_id=1, source_target_pairs={{0,6},{1,7},{2,4},{3,5},{4,2},{5,3},{6,0},{7,1},{8,14},{9,15},{10,... | collective-permute-start | bytes 196616 | tf_op jit(solution)/shard_map/ppermute | solution.py:19
  19.5 1.9 %collective-permute-start.7 = (f32[128,128]{1,0:T(8,128)S(1)}, f32[128,128]{1,0:T(8,128)S(1)}, u32[]{:S(2)}, u32[]{:S(2)}) collective-permute-start(f32[128,128]{1,0:T(8,128)S(1)} %shard_map.80.refs_0_), channel_id=1, source_target_pairs={{0,4},{1,5},{2,6},{3,7},{4,0},{5,1},{6,2},{7,3},{8,12},{9,13},{10,... | collective-permute-start | bytes 196616 | tf_op jit(solution)/shard_map/ppermute | solution.py:19
  21.4 1.9 %collective-permute-done.9.refs_6_ = f32[128,128]{1,0:T(8,128)S(1)} collective-permute-done((f32[128,128]{1,0:T(8,128)S(1)}, f32[128,128]{1,0:T(8,128)S(1)}, u32[]{:S(2)}, u32[]{:S(2)}) %collective-permute-start.9) | collective-permute-done | bytes 65568 | tf_op jit(solution)/shard_map/ppermute | solution.py:19
  27.7 2.5 %collective-permute-start.11 = (f32[256,128]{1,0:T(8,128)S(1)}, f32[256,128]{1,0:T(8,128)S(1)}, u32[]{:S(2)}, u32[]{:S(2)}) collective-permute-start(f32[256,128]{1,0:T(8,128)S(1)} %get-tuple-element.72), channel_id=1, source_target_pairs={{0,24},{8,16},{16,8},{24,0},{1,25},{9,17},{17,9},{25,1},{2,26},{10... | collective-permute-start | bytes 393224 | tf_op jit(solution)/shard_map/ppermute | solution.py:19
  31.8 2.7 %collective-permute-done.11.refs_1_ = f32[256,128]{1,0:T(8,128)S(1)} collective-permute-done((f32[256,128]{1,0:T(8,128)S(1)}, f32[256,128]{1,0:T(8,128)S(1)}, u32[]{:S(2)}, u32[]{:S(2)}) %collective-permute-start.11) | collective-permute-done | bytes 131104 | tf_op jit(solution)/shard_map/ppermute | solution.py:19
  34.5 2.5 %collective-permute-done.12.refs_2_ = f32[256,128]{1,0:T(8,128)S(1)} collective-permute-done((f32[256,128]{1,0:T(8,128)S(1)}, f32[256,128]{1,0:T(8,128)S(1)}, u32[]{:S(2)}, u32[]{:S(2)}) %collective-permute-start.12) | collective-permute-done | bytes 131104 | tf_op jit(solution)/shard_map/ppermute | solution.py:19
  40.8 2.1 %collective-permute-done.14.refs_1_ = f32[256,128]{1,0:T(8,128)S(1)} collective-permute-done((f32[256,128]{1,0:T(8,128)S(1)}, f32[256,128]{1,0:T(8,128)S(1)}, u32[]{:S(2)}, u32[]{:S(2)}) %collective-permute-start.14) | collective-permute-done | bytes 131104 | tf_op jit(solution)/shard_map/ppermute | solution.py:19
  42.9 3.7 %collective-permute-done.15.refs_2_ = f32[256,128]{1,0:T(8,128)S(1)} collective-permute-done((f32[256,128]{1,0:T(8,128)S(1)}, f32[256,128]{1,0:T(8,128)S(1)}, u32[]{:S(2)}, u32[]{:S(2)}) %collective-permute-start.15) | collective-permute-done | bytes 131104 | tf_op jit(solution)/shard_map/ppermute | solution.py:19
  49.1 2.1 %collective-permute-start.18 = (f32[128,128]{1,0:T(8,128)S(1)}, f32[128,128]{1,0:T(8,128)S(1)}, u32[]{:S(2)}, u32[]{:S(2)}) collective-permute-start(f32[128,128]{1,0:T(8,128)S(1)} %get-tuple-element.79), channel_id=1, source_target_pairs={{0,6},{1,7},{2,4},{3,5},{4,2},{5,3},{6,0},{7,1},{8,14},{9,15},{10,... | collective-permute-start | bytes 196616 | tf_op jit(solution)/shard_map/ppermute | solution.py:19
  53.5 2.4 %collective-permute-done.18.refs_2_ = f32[128,128]{1,0:T(8,128)S(1)} collective-permute-done((f32[128,128]{1,0:T(8,128)S(1)}, f32[128,128]{1,0:T(8,128)S(1)}, u32[]{:S(2)}, u32[]{:S(2)}) %collective-permute-start.18) | collective-permute-done | bytes 65568 | tf_op jit(solution)/shard_map/ppermute | solution.py:19
  55.9 2.5 %collective-permute-done.19.refs_3_ = f32[128,128]{1,0:T(8,128)S(1)} collective-permute-done((f32[128,128]{1,0:T(8,128)S(1)}, f32[128,128]{1,0:T(8,128)S(1)}, u32[]{:S(2)}, u32[]{:S(2)}) %collective-permute-start.19) | collective-permute-done | bytes 65568 | tf_op jit(solution)/shard_map/ppermute | solution.py:19
  58.5 9.9 %all_to_all.10.sums_ref = f32[32,2,128]{2,1,0:T(2,128)S(1)} all-to-all(f32[32,2,128]{2,1,0:T(2,128)S(1)} %shard_map.88), channel_id=1, replica_groups=mesh['samp'=4,'chrom'=8] {'samp','chrom'}, dimensions={0} | all-to-all | bytes 65536 | tf_op jit(solution)/shard_map/all_to_all | solution.py:415
  73.3 2.4 %collective-permute-start.24 = (f32[128,128]{1,0:T(8,128)S(1)}, f32[128,128]{1,0:T(8,128)S(1)}, u32[]{:S(2)}, u32[]{:S(2)}) collective-permute-start(f32[128,128]{1,0:T(8,128)S(1)} %get-tuple-element.88), channel_id=1, source_target_pairs={{0,2},{1,3},{2,0},{3,1},{4,6},{5,7},{6,4},{7,5},{8,10},{9,11},{10,... | collective-permute-start | bytes 196616 | tf_op jit(solution)/shard_map/ppermute | solution.py:19
  75.7 2.4 %collective-permute-done.22.refs_1_ = f32[128,128]{1,0:T(8,128)S(1)} collective-permute-done((f32[128,128]{1,0:T(8,128)S(1)}, f32[128,128]{1,0:T(8,128)S(1)}, u32[]{:S(2)}, u32[]{:S(2)}) %collective-permute-start.22) | collective-permute-done | bytes 65568 | tf_op jit(solution)/shard_map/ppermute | solution.py:19
  81.8 2.4 %collective-permute-start.30 = (f32[128,128]{1,0:T(8,128)S(1)}, f32[128,128]{1,0:T(8,128)S(1)}, u32[]{:S(2)}, u32[]{:S(2)}) collective-permute-start(f32[128,128]{1,0:T(8,128)S(1)} %shard_map.92.refs_0_), channel_id=1, source_target_pairs={{0,6},{1,7},{2,4},{3,5},{4,2},{5,3},{6,0},{7,1},{8,14},{9,15},{10,... | collective-permute-start | bytes 196616 | tf_op jit(solution)/shard_map/ppermute | solution.py:19
  84.7 2.4 %collective-permute-done.28.refs_4_ = f32[128,128]{1,0:T(8,128)S(1)} collective-permute-done((f32[128,128]{1,0:T(8,128)S(1)}, f32[128,128]{1,0:T(8,128)S(1)}, u32[]{:S(2)}, u32[]{:S(2)}) %collective-permute-start.28) | collective-permute-done | bytes 65568 | tf_op jit(solution)/shard_map/ppermute | solution.py:19
  94.4 3.3 %collective-permute-done.32.refs_1_ = f32[256,128]{1,0:T(8,128)S(1)} collective-permute-done((f32[256,128]{1,0:T(8,128)S(1)}, f32[256,128]{1,0:T(8,128)S(1)}, u32[]{:S(2)}, u32[]{:S(2)}) %collective-permute-start.32) | collective-permute-done | bytes 131104 | tf_op jit(solution)/shard_map/ppermute | solution.py:19
  104.5 3.8 %collective-permute-done.36.refs_2_ = f32[256,128]{1,0:T(8,128)S(1)} collective-permute-done((f32[256,128]{1,0:T(8,128)S(1)}, f32[256,128]{1,0:T(8,128)S(1)}, u32[]{:S(2)}, u32[]{:S(2)}) %collective-permute-start.36) | collective-permute-done | bytes 131104 | tf_op jit(solution)/shard_map/ppermute | solution.py:19
  110.8 2.5 %collective-permute-start.39 = (f32[128,128]{1,0:T(8,128)S(1)}, f32[128,128]{1,0:T(8,128)S(1)}, u32[]{:S(2)}, u32[]{:S(2)}) collective-permute-start(f32[128,128]{1,0:T(8,128)S(1)} %get-tuple-element.97), channel_id=1, source_target_pairs={{0,6},{1,7},{2,4},{3,5},{4,2},{5,3},{6,0},{7,1},{8,14},{9,15},{10,... | collective-permute-start | bytes 196616 | tf_op jit(solution)/shard_map/ppermute | solution.py:19
  115.2 2.4 %collective-permute-done.39.refs_2_ = f32[128,128]{1,0:T(8,128)S(1)} collective-permute-done((f32[128,128]{1,0:T(8,128)S(1)}, f32[128,128]{1,0:T(8,128)S(1)}, u32[]{:S(2)}, u32[]{:S(2)}) %collective-permute-start.39) | collective-permute-done | bytes 65568 | tf_op jit(solution)/shard_map/ppermute | solution.py:19
  117.6 2.3 %collective-permute-done.40.refs_3_ = f32[128,128]{1,0:T(8,128)S(1)} collective-permute-done((f32[128,128]{1,0:T(8,128)S(1)}, f32[128,128]{1,0:T(8,128)S(1)}, u32[]{:S(2)}, u32[]{:S(2)}) %collective-permute-start.40) | collective-permute-done | bytes 65568 | tf_op jit(solution)/shard_map/ppermute | solution.py:19
  119.9 10.5 %all_to_all.11.sums_ref = f32[32,2,128]{2,1,0:T(2,128)S(1)} all-to-all(f32[32,2,128]{2,1,0:T(2,128)S(1)} %shard_map.99), channel_id=1, replica_groups=mesh['samp'=4,'chrom'=8] {'samp','chrom'}, dimensions={0} | all-to-all | bytes 65536 | tf_op jit(solution)/shard_map/all_to_all | solution.py:415
  135.3 2.4 %collective-permute-start.45 = (f32[128,128]{1,0:T(8,128)S(1)}, f32[128,128]{1,0:T(8,128)S(1)}, u32[]{:S(2)}, u32[]{:S(2)}) collective-permute-start(f32[128,128]{1,0:T(8,128)S(1)} %get-tuple-element.105), channel_id=1, source_target_pairs={{0,2},{1,3},{2,0},{3,1},{4,6},{5,7},{6,4},{7,5},{8,10},{9,11},{10,... | collective-permute-start | bytes 196616 | tf_op jit(solution)/shard_map/ppermute | solution.py:19
  137.7 2.6 %shard_map.103 = (f32[1024,128]{1,0:T(8,128)S(1)}, f32[1024,128]{1,0:T(8,128)S(1)}) custom-call(f32[1024,128]{1,0:T(8,128)S(1)} %get-tuple-element.106.coef_ref, s32[8,128]{1,0:T(8,128)S(1)} %bitcast.6, bf16[512,1024]{1,0:T(8,128)(2,1)S(1)} %get-tuple-element.61.refs_8_.refs_1_.high_ref.refs_0_, ...), custom_call_target="tpu_custom_call" | custom-call | flops 2147483648 | bytes 8388608 | tf_op jit(solution)/shard_map/pallas_call | solution.py:426
  143.8 2.4 %collective-permute-start.51 = (f32[128,128]{1,0:T(8,128)S(1)}, f32[128,128]{1,0:T(8,128)S(1)}, u32[]{:S(2)}, u32[]{:S(2)}) collective-permute-start(f32[128,128]{1,0:T(8,128)S(1)} %shard_map.104.refs_0_), channel_id=1, source_target_pairs={{0,6},{1,7},{2,4},{3,5},{4,2},{5,3},{6,0},{7,1},{8,14},{9,15},{10,... | collective-permute-start | bytes 196616 | tf_op jit(solution)/shard_map/ppermute | solution.py:19
  146.7 2.4 %collective-permute-done.49.refs_4_ = f32[128,128]{1,0:T(8,128)S(1)} collective-permute-done((f32[128,128]{1,0:T(8,128)S(1)}, f32[128,128]{1,0:T(8,128)S(1)}, u32[]{:S(2)}, u32[]{:S(2)}) %collective-permute-start.49) | collective-permute-done | bytes 65568 | tf_op jit(solution)/shard_map/ppermute | solution.py:19
  156.6 3.0 %collective-permute-done.53.refs_1_ = f32[272,128]{1,0:T(8,128)S(1)} collective-permute-done((f32[272,128]{1,0:T(8,128)S(1)}, f32[272,128]{1,0:T(8,128)S(1)}, u32[]{:S(2)}, u32[]{:S(2)}) %collective-permute-start.53) | collective-permute-done | bytes 139296 | tf_op jit(solution)/shard_map/ppermute | solution.py:19
  166.8 3.9 %collective-permute-done.57.refs_2_ = f32[256,128]{1,0:T(8,128)S(1)} collective-permute-done((f32[256,128]{1,0:T(8,128)S(1)}, f32[256,128]{1,0:T(8,128)S(1)}, u32[]{:S(2)}, u32[]{:S(2)}) %collective-permute-start.57) | collective-permute-done | bytes 131104 | tf_op jit(solution)/shard_map/ppermute | solution.py:19
  (130 shorter events, 68.9 us)
Async XLA Ops:
  6.0 7.7 %collective-permute-start.1 = (f32[128,128]{1,0:T(8,128)S(1)}, f32[128,128]{1,0:T(8,128)S(1)}, u32[]{:S(2)}, u32[]{:S(2)}) collective-permute-start(f32[128,128]{1,0:T(8,128)S(1)} %get-tuple-element.66), channel_id=1, source_target_pairs={{0,6},{1,7},{2,4},{3,5},{4,2},{5,3},{6,0},{7,1},{8,14},{9,15},{10,... | collective-permute-start | bytes 196616 | tf_op jit(solution)/shard_map/ppermute | solution.py:19
  17.0 6.4 %collective-permute-start.9 = (f32[128,128]{1,0:T(8,128)S(1)}, f32[128,128]{1,0:T(8,128)S(1)}, u32[]{:S(2)}, u32[]{:S(2)}) collective-permute-start(f32[128,128]{1,0:T(8,128)S(1)} %shard_map.80.refs_0_), channel_id=1, source_target_pairs={{0,6},{1,7},{2,4},{3,5},{4,2},{5,3},{6,0},{7,1},{8,14},{9,15},{10,... | collective-permute-start | bytes 196616 | tf_op jit(solution)/shard_map/ppermute | solution.py:19
  27.7 6.8 %collective-permute-start.11 = (f32[256,128]{1,0:T(8,128)S(1)}, f32[256,128]{1,0:T(8,128)S(1)}, u32[]{:S(2)}, u32[]{:S(2)}) collective-permute-start(f32[256,128]{1,0:T(8,128)S(1)} %get-tuple-element.72), channel_id=1, source_target_pairs={{0,24},{8,16},{16,8},{24,0},{1,25},{9,17},{17,9},{25,1},{2,26},{10... | collective-permute-start | bytes 393224 | tf_op jit(solution)/shard_map/ppermute | solution.py:19
  30.2 6.8 %collective-permute-start.12 = (f32[256,128]{1,0:T(8,128)S(1)}, f32[256,128]{1,0:T(8,128)S(1)}, u32[]{:S(2)}, u32[]{:S(2)}) collective-permute-start(f32[256,128]{1,0:T(8,128)S(1)} %get-tuple-element.73), channel_id=1, source_target_pairs={{0,16},{8,24},{16,0},{24,8},{1,17},{9,25},{17,1},{25,9},{2,18},{10... | collective-permute-start | bytes 393224 | tf_op jit(solution)/shard_map/ppermute | solution.py:19
  30.7 6.4 %collective-permute-start.13 = (f32[256,128]{1,0:T(8,128)S(1)}, f32[256,128]{1,0:T(8,128)S(1)}, u32[]{:S(2)}, u32[]{:S(2)}) collective-permute-start(f32[256,128]{1,0:T(8,128)S(1)} %get-tuple-element.74), channel_id=1, source_target_pairs={{0,8},{8,0},{16,24},{24,16},{1,9},{9,1},{17,25},{25,17},{2,10},{10... | collective-permute-start | bytes 393224 | tf_op jit(solution)/shard_map/ppermute | solution.py:19
  38.7 7.8 %collective-permute-start.15 = (f32[256,128]{1,0:T(8,128)S(1)}, f32[256,128]{1,0:T(8,128)S(1)}, u32[]{:S(2)}, u32[]{:S(2)}) collective-permute-start(f32[256,128]{1,0:T(8,128)S(1)} %shard_map.83.refs_0_), channel_id=1, source_target_pairs={{0,16},{8,24},{16,0},{24,8},{1,17},{9,25},{17,1},{25,9},{2,18},{10... | collective-permute-start | bytes 393224 | tf_op jit(solution)/shard_map/ppermute | solution.py:19
  39.4 7.1 %collective-permute-start.16 = (f32[256,128]{1,0:T(8,128)S(1)}, f32[256,128]{1,0:T(8,128)S(1)}, u32[]{:S(2)}, u32[]{:S(2)}) collective-permute-start(f32[256,128]{1,0:T(8,128)S(1)} %shard_map.83.refs_0_), channel_id=1, source_target_pairs={{0,24},{8,16},{16,8},{24,0},{1,25},{9,17},{17,9},{25,1},{2,26},{10... | collective-permute-start | bytes 393224 | tf_op jit(solution)/shard_map/ppermute | solution.py:19
  49.1 6.8 %collective-permute-start.18 = (f32[128,128]{1,0:T(8,128)S(1)}, f32[128,128]{1,0:T(8,128)S(1)}, u32[]{:S(2)}, u32[]{:S(2)}) collective-permute-start(f32[128,128]{1,0:T(8,128)S(1)} %get-tuple-element.79), channel_id=1, source_target_pairs={{0,6},{1,7},{2,4},{3,5},{4,2},{5,3},{6,0},{7,1},{8,14},{9,15},{10,... | collective-permute-start | bytes 196616 | tf_op jit(solution)/shard_map/ppermute | solution.py:19
  51.1 7.3 %collective-permute-start.19 = (f32[128,128]{1,0:T(8,128)S(1)}, f32[128,128]{1,0:T(8,128)S(1)}, u32[]{:S(2)}, u32[]{:S(2)}) collective-permute-start(f32[128,128]{1,0:T(8,128)S(1)} %get-tuple-element.80), channel_id=1, source_target_pairs={{0,4},{1,5},{2,6},{3,7},{4,0},{5,1},{6,2},{7,3},{8,12},{9,13},{10,... | collective-permute-start | bytes 196616 | tf_op jit(solution)/shard_map/ppermute | solution.py:19
  52.0 6.5 %collective-permute-start.20 = (f32[128,128]{1,0:T(8,128)S(1)}, f32[128,128]{1,0:T(8,128)S(1)}, u32[]{:S(2)}, u32[]{:S(2)}) collective-permute-start(f32[128,128]{1,0:T(8,128)S(1)} %get-tuple-element.81), channel_id=1, source_target_pairs={{0,2},{1,3},{2,0},{3,1},{4,6},{5,7},{6,4},{7,5},{8,10},{9,11},{10,... | collective-permute-start | bytes 196616 | tf_op jit(solution)/shard_map/ppermute | solution.py:19
  71.2 6.9 %collective-permute-start.22 = (f32[128,128]{1,0:T(8,128)S(1)}, f32[128,128]{1,0:T(8,128)S(1)}, u32[]{:S(2)}, u32[]{:S(2)}) collective-permute-start(f32[128,128]{1,0:T(8,128)S(1)} %get-tuple-element.86), channel_id=1, source_target_pairs={{0,6},{1,7},{2,4},{3,5},{4,2},{5,3},{6,0},{7,1},{8,14},{9,15},{10,... | collective-permute-start | bytes 196616 | tf_op jit(solution)/shard_map/ppermute | solution.py:19
  71.9 7.9 %collective-permute-start.23 = (f32[128,128]{1,0:T(8,128)S(1)}, f32[128,128]{1,0:T(8,128)S(1)}, u32[]{:S(2)}, u32[]{:S(2)}) collective-permute-start(f32[128,128]{1,0:T(8,128)S(1)} %get-tuple-element.87), channel_id=1, source_target_pairs={{0,4},{1,5},{2,6},{3,7},{4,0},{5,1},{6,2},{7,3},{8,12},{9,13},{10,... | collective-permute-start | bytes 196616 | tf_op jit(solution)/shard_map/ppermute | solution.py:19
  73.3 6.5 %collective-permute-start.24 = (f32[128,128]{1,0:T(8,128)S(1)}, f32[128,128]{1,0:T(8,128)S(1)}, u32[]{:S(2)}, u32[]{:S(2)}) collective-permute-start(f32[128,128]{1,0:T(8,128)S(1)} %get-tuple-element.88), channel_id=1, source_target_pairs={{0,2},{1,3},{2,0},{3,1},{4,6},{5,7},{6,4},{7,5},{8,10},{9,11},{10,... | collective-permute-start | bytes 196616 | tf_op jit(solution)/shard_map/ppermute | solution.py:19
  80.0 7.1 %collective-permute-start.28 = (f32[128,128]{1,0:T(8,128)S(1)}, f32[128,128]{1,0:T(8,128)S(1)}, u32[]{:S(2)}, u32[]{:S(2)}) collective-permute-start(f32[128,128]{1,0:T(8,128)S(1)} %shard_map.92.refs_0_), channel_id=1, source_target_pairs={{0,4},{1,5},{2,6},{3,7},{4,0},{5,1},{6,2},{7,3},{8,12},{9,13},{10,... | collective-permute-start | bytes 196616 | tf_op jit(solution)/shard_map/ppermute | solution.py:19
  90.3 7.4 %collective-permute-start.32 = (f32[256,128]{1,0:T(8,128)S(1)}, f32[256,128]{1,0:T(8,128)S(1)}, u32[]{:S(2)}, u32[]{:S(2)}) collective-permute-start(f32[256,128]{1,0:T(8,128)S(1)} %get-tuple-element.90), channel_id=1, source_target_pairs={{0,24},{8,16},{16,8},{24,0},{1,25},{9,17},{17,9},{25,1},{2,26},{10... | collective-permute-start | bytes 393224 | tf_op jit(solution)/shard_map/ppermute | solution.py:19
  91.0 8.1 %collective-permute-start.33 = (f32[256,128]{1,0:T(8,128)S(1)}, f32[256,128]{1,0:T(8,128)S(1)}, u32[]{:S(2)}, u32[]{:S(2)}) collective-permute-start(f32[256,128]{1,0:T(8,128)S(1)} %get-tuple-element.91), channel_id=1, source_target_pairs={{0,16},{8,24},{16,0},{24,8},{1,17},{9,25},{17,1},{25,9},{2,18},{10... | collective-permute-start | bytes 393224 | tf_op jit(solution)/shard_map/ppermute | solution.py:19
  92.4 6.7 %collective-permute-start.34 = (f32[256,128]{1,0:T(8,128)S(1)}, f32[256,128]{1,0:T(8,128)S(1)}, u32[]{:S(2)}, u32[]{:S(2)}) collective-permute-start(f32[256,128]{1,0:T(8,128)S(1)} %get-tuple-element.92), channel_id=1, source_target_pairs={{0,8},{8,0},{16,24},{24,16},{1,9},{9,1},{17,25},{25,17},{2,10},{10... | collective-permute-start | bytes 393224 | tf_op jit(solution)/shard_map/ppermute | solution.py:19
  100.3 7.9 %collective-permute-start.36 = (f32[256,128]{1,0:T(8,128)S(1)}, f32[256,128]{1,0:T(8,128)S(1)}, u32[]{:S(2)}, u32[]{:S(2)}) collective-permute-start(f32[256,128]{1,0:T(8,128)S(1)} %shard_map.95.refs_0_), channel_id=1, source_target_pairs={{0,16},{8,24},{16,0},{24,8},{1,17},{9,25},{17,1},{25,9},{2,18},{10... | collective-permute-start | bytes 393224 | tf_op jit(solution)/shard_map/ppermute | solution.py:19
  100.9 7.3 %collective-permute-start.37 = (f32[256,128]{1,0:T(8,128)S(1)}, f32[256,128]{1,0:T(8,128)S(1)}, u32[]{:S(2)}, u32[]{:S(2)}) collective-permute-start(f32[256,128]{1,0:T(8,128)S(1)} %shard_map.95.refs_0_), channel_id=1, source_target_pairs={{0,24},{8,16},{16,8},{24,0},{1,25},{9,17},{17,9},{25,1},{2,26},{10... | collective-permute-start | bytes 393224 | tf_op jit(solution)/shard_map/ppermute | solution.py:19
  110.8 6.8 %collective-permute-start.39 = (f32[128,128]{1,0:T(8,128)S(1)}, f32[128,128]{1,0:T(8,128)S(1)}, u32[]{:S(2)}, u32[]{:S(2)}) collective-permute-start(f32[128,128]{1,0:T(8,128)S(1)} %get-tuple-element.97), channel_id=1, source_target_pairs={{0,6},{1,7},{2,4},{3,5},{4,2},{5,3},{6,0},{7,1},{8,14},{9,15},{10,... | collective-permute-start | bytes 196616 | tf_op jit(solution)/shard_map/ppermute | solution.py:19
  113.3 6.5 %collective-permute-start.40 = (f32[128,128]{1,0:T(8,128)S(1)}, f32[128,128]{1,0:T(8,128)S(1)}, u32[]{:S(2)}, u32[]{:S(2)}) collective-permute-start(f32[128,128]{1,0:T(8,128)S(1)} %get-tuple-element.98), channel_id=1, source_target_pairs={{0,4},{1,5},{2,6},{3,7},{4,0},{5,1},{6,2},{7,3},{8,12},{9,13},{10,... | collective-permute-start | bytes 196616 | tf_op jit(solution)/shard_map/ppermute | solution.py:19
  113.4 6.5 %collective-permute-start.41 = (f32[128,128]{1,0:T(8,128)S(1)}, f32[128,128]{1,0:T(8,128)S(1)}, u32[]{:S(2)}, u32[]{:S(2)}) collective-permute-start(f32[128,128]{1,0:T(8,128)S(1)} %get-tuple-element.99), channel_id=1, source_target_pairs={{0,2},{1,3},{2,0},{3,1},{4,6},{5,7},{6,4},{7,5},{8,10},{9,11},{10,... | collective-permute-start | bytes 196616 | tf_op jit(solution)/shard_map/ppermute | solution.py:19
  133.3 7.0 %collective-permute-start.43 = (f32[128,128]{1,0:T(8,128)S(1)}, f32[128,128]{1,0:T(8,128)S(1)}, u32[]{:S(2)}, u32[]{:S(2)}) collective-permute-start(f32[128,128]{1,0:T(8,128)S(1)} %get-tuple-element.103), channel_id=1, source_target_pairs={{0,6},{1,7},{2,4},{3,5},{4,2},{5,3},{6,0},{7,1},{8,14},{9,15},{10,... | collective-permute-start | bytes 196616 | tf_op jit(solution)/shard_map/ppermute | solution.py:19
  133.9 7.9 %collective-permute-start.44 = (f32[128,128]{1,0:T(8,128)S(1)}, f32[128,128]{1,0:T(8,128)S(1)}, u32[]{:S(2)}, u32[]{:S(2)}) collective-permute-start(f32[128,128]{1,0:T(8,128)S(1)} %get-tuple-element.104), channel_id=1, source_target_pairs={{0,4},{1,5},{2,6},{3,7},{4,0},{5,1},{6,2},{7,3},{8,12},{9,13},{10,... | collective-permute-start | bytes 196616 | tf_op jit(solution)/shard_map/ppermute | solution.py:19
  135.3 6.5 %collective-permute-start.45 = (f32[128,128]{1,0:T(8,128)S(1)}, f32[128,128]{1,0:T(8,128)S(1)}, u32[]{:S(2)}, u32[]{:S(2)}) collective-permute-start(f32[128,128]{1,0:T(8,128)S(1)} %get-tuple-element.105), channel_id=1, source_target_pairs={{0,2},{1,3},{2,0},{3,1},{4,6},{5,7},{6,4},{7,5},{8,10},{9,11},{10,... | collective-permute-start | bytes 196616 | tf_op jit(solution)/shard_map/ppermute | solution.py:19
  142.1 7.0 %collective-permute-start.49 = (f32[128,128]{1,0:T(8,128)S(1)}, f32[128,128]{1,0:T(8,128)S(1)}, u32[]{:S(2)}, u32[]{:S(2)}) collective-permute-start(f32[128,128]{1,0:T(8,128)S(1)} %shard_map.104.refs_0_), channel_id=1, source_target_pairs={{0,4},{1,5},{2,6},{3,7},{4,0},{5,1},{6,2},{7,3},{8,12},{9,13},{10,... | collective-permute-start | bytes 196616 | tf_op jit(solution)/shard_map/ppermute | solution.py:19
  143.8 6.1 %collective-permute-start.51 = (f32[128,128]{1,0:T(8,128)S(1)}, f32[128,128]{1,0:T(8,128)S(1)}, u32[]{:S(2)}, u32[]{:S(2)}) collective-permute-start(f32[128,128]{1,0:T(8,128)S(1)} %shard_map.104.refs_0_), channel_id=1, source_target_pairs={{0,6},{1,7},{2,4},{3,5},{4,2},{5,3},{6,0},{7,1},{8,14},{9,15},{10,... | collective-permute-start | bytes 196616 | tf_op jit(solution)/shard_map/ppermute | solution.py:19
  152.1 7.5 %collective-permute-start.53 = (f32[272,128]{1,0:T(8,128)S(1)}, f32[272,128]{1,0:T(8,128)S(1)}, u32[]{:S(2)}, u32[]{:S(2)}) collective-permute-start(f32[272,128]{1,0:T(8,128)S(1)} %get-tuple-element.112), channel_id=1, source_target_pairs={{0,24},{8,16},{16,8},{24,0},{1,25},{9,17},{17,9},{25,1},{2,26},{10... | collective-permute-start | bytes 417800 | tf_op jit(solution)/shard_map/ppermute | solution.py:19
  152.8 8.4 %collective-permute-start.54 = (f32[272,128]{1,0:T(8,128)S(1)}, f32[272,128]{1,0:T(8,128)S(1)}, u32[]{:S(2)}, u32[]{:S(2)}) collective-permute-start(f32[272,128]{1,0:T(8,128)S(1)} %get-tuple-element.113), channel_id=1, source_target_pairs={{0,16},{8,24},{16,0},{24,8},{1,17},{9,25},{17,1},{25,9},{2,18},{10... | collective-permute-start | bytes 417800 | tf_op jit(solution)/shard_map/ppermute | solution.py:19
  154.2 7.0 %collective-permute-start.55 = (f32[272,128]{1,0:T(8,128)S(1)}, f32[272,128]{1,0:T(8,128)S(1)}, u32[]{:S(2)}, u32[]{:S(2)}) collective-permute-start(f32[272,128]{1,0:T(8,128)S(1)} %get-tuple-element.114), channel_id=1, source_target_pairs={{0,8},{8,0},{16,24},{24,16},{1,9},{9,1},{17,25},{25,17},{2,10},{10... | collective-permute-start | bytes 417800 | tf_op jit(solution)/shard_map/ppermute | solution.py:19
  162.7 7.9 %collective-permute-start.57 = (f32[256,128]{1,0:T(8,128)S(1)}, f32[256,128]{1,0:T(8,128)S(1)}, u32[]{:S(2)}, u32[]{:S(2)}) collective-permute-start(f32[256,128]{1,0:T(8,128)S(1)} %shard_map.107.refs_0_), channel_id=1, source_target_pairs={{0,16},{8,24},{16,0},{24,8},{1,17},{9,25},{17,1},{25,9},{2,18},{10... | collective-permute-start | bytes 393224 | tf_op jit(solution)/shard_map/ppermute | solution.py:19
  163.3 7.3 %collective-permute-start.58 = (f32[256,128]{1,0:T(8,128)S(1)}, f32[256,128]{1,0:T(8,128)S(1)}, u32[]{:S(2)}, u32[]{:S(2)}) collective-permute-start(f32[256,128]{1,0:T(8,128)S(1)} %shard_map.107.refs_0_), channel_id=1, source_target_pairs={{0,24},{8,16},{16,8},{24,0},{1,25},{9,17},{17,9},{25,1},{2,26},{10... | collective-permute-start | bytes 393224 | tf_op jit(solution)/shard_map/ppermute | solution.py:19
  (32 other events, 153.2 us)

commit v7 on v6

--- a/solution.py
+++ b/solution.py
@@ -11,6 +11,7 @@
 GPD = 2
 ITERS = 2
 STATS = 16
+PARTS = 2
 VMEM_LIMIT = 10 * 1024 * 1024
 
 
@@ -78,27 +79,35 @@
     me = lax.axis_index("chrom")
     place, core = me // 2, me % 2
     half = buffer_ref.shape[0]
-    coef_copy = pltpu.make_async_copy(coef_ref, coef_buffer, sems.at[2 * half])
+    coef_copy = pltpu.make_async_copy(coef_ref, coef_buffer, sems.at[2 * half * PARTS])
+    part = buffer_ref.shape[1] // PARTS
     copies = [
-        pltpu.make_async_copy(dosage_ref.at[place ^ k, core ^ bits], target.at[k], sems.at[bits * half + k])
+        [
+            pltpu.make_async_copy(
+                dosage_ref.at[place ^ k, core ^ bits, pl.ds(p * part, part)],
+                target.at[k, pl.ds(p * part, part)],
+                sems.at[(bits * half + k) * PARTS + p],
+            )
+            for p in range(PARTS)
+        ]
         for bits, target in ((1, buffer_ref), (0, kept_ref))
         for k in range(half)
     ]
     coef_copy.start()
-    for copy in copies[:half]:
-        copy.start()
+    for group in copies:
+        for copy in group:
+            copy.start()
+
+    def ready(k):
+        for copy in copies[k]:
+            copy.wait()
+
     coef_copy.wait()
     packed_ref[...] = pack(coef_buffer[...])
-
-    def ready(k):
-        copies[k].wait()
-        if k == half // 2:
-            for copy in copies[half:]:
-                copy.start()
-
     split_rows(buffer_ref, ready, packed_ref, high_ref, low_ref, out_ref)
-    for copy in copies[half:]:
-        copy.wait()
+    for group in copies[half:]:
+        for copy in group:
+            copy.wait()
 
 
 def second_kernel(kept_ref, packed_ref, high_ref, low_ref, out_ref):
@@ -153,7 +162,7 @@
     rows_ref = refs[-1]
     samp = lax.axis_index("samp")
     block = pieces[0].shape[0]
-    for bits, piece in enumerate(pieces):
+    for bits, piece in zip(chrom_order(count), pieces):
         start = ((bits % 2) * (count // 2) + bits // 2) * block
         rows_ref[start : start + block] = pack(piece[...])
     packed_ref[...] = rows_ref[...].T
@@ -245,7 +254,7 @@
     me, samp = lax.axis_index("chrom"), lax.axis_index("samp")
     block, traits = pieces[0].shape
     sums_ref[...] = jnp.zeros_like(sums_ref)
-    for bits, piece in enumerate(pieces):
+    for bits, piece in zip(chrom_order(count), pieces):
         rows = pl.ds(pl.multiple_of((me ^ bits) * block, block), block)
         start = ((bits % 2) * (count // 2) + bits // 2) * block
         value = piece[...]
@@ -262,7 +271,7 @@
     pieces, operands, residual_ref, outs = refs[:count], refs[count : count + 5], refs[count + 5], refs[count + 6 :]
     me, samp = lax.axis_index("chrom"), lax.axis_index("samp")
     block = pieces[0].shape[0]
-    for bits, piece in enumerate(pieces):
+    for bits, piece in zip(chrom_order(count), pieces):
         residual_ref[pl.ds(pl.multiple_of((me ^ bits) * block, block), block)] = piece[...]
     for partner, out in zip(partners, outs):
         score_products(samp ^ partner, out, *operands)
@@ -312,12 +321,15 @@
     return [sums[0]] + [swap(sums[k], "chrom", 2 * k) for k in reversed(range(1, count))]
 
 
+def chrom_order(size):
+    return list(reversed(range(size)))
+
+
 def chrom_gather(own):
-    blocks = []
-    for k in range(lax.axis_size("chrom") // 2):
-        block = swap(own, "chrom", 2 * k) if k else own
-        blocks += [block, swap(block, "chrom", 1)]
-    return blocks
+    size = lax.axis_size("chrom")
+    direct = {bits: swap(own, "chrom", bits) for bits in chrom_order(size)[:-1] if bits < 4 or bits % 2 == 0}
+    direct[0] = own
+    return [direct[bits] if bits in direct else swap(direct[bits - 1], "chrom", 1) for bits in chrom_order(size)]
 
 
 def samp_order(size):
@@ -367,7 +379,7 @@
         first_kernel,
         [part, part, half_out, packed_cols, shape(kept_shape)],
         [pl.BlockSpec(memory_space=pltpu.HBM)] * 2,
-        [pltpu.VMEM(kept_shape, jnp.float32), pltpu.VMEM(coefficients.shape, jnp.float32), pltpu.SemaphoreType.DMA((n_chrom + 1,))],
+        [pltpu.VMEM(kept_shape, jnp.float32), pltpu.VMEM(coefficients.shape, jnp.float32), pltpu.SemaphoreType.DMA((n_chrom * PARTS + 1,))],
         flops,
         4 * moved,
     )(
@@ -395,7 +407,7 @@
         )(packed, *parts)
         received = [swap(piece, "samp", partner) for partner, piece in zip(order, far_out)]
         own_grad = call(functools.partial(mean_kernel, total_rows), grad_block, [whole()] * n_samp)(
-            near_out[-1], *received
+            near_out[-1], *received[::-1]
         )
         pieces = samp_gather(own_grad)
         after = (tested_sq,) if iteration == 0 else ()
@@ -447,7 +459,7 @@
     received = [swap(piece, "samp", partner) for partner, piece in zip(order, far_out)]
     own_scores = call(
         functools.partial(score_kernel, total_rows), shape((test_width, n_traits)), [whole()] * (n_samp + 1)
-    )(owner_rows, near_out[-1], *received)
+    )(owner_rows, near_out[-1], *received[::-1])
     scores = call(place_kernel, shape((tests, n_traits)), [whole()] * n_samp)(*samp_gather(own_scores))
     return (scores, residual)
 

time: 172 us -> 170 us (0.988)
  transfers between devices with their start and end apart: 59 -> 59, of which waited for: 42 -> 35; matrix products, arithmetic and copies ran while one was open for 0% -> 0% of each run, Pallas kernels for 5% -> 5%
where the time goes in v7:
time: 170 us
  waiting for transfers between devices  68.4 us (40%)
  starting transfers between devices  59.7 us (35%)
  blocking collectives  20.9 us (12%)
  Pallas kernels  20 us (12%)
    ppermute x59, waiting for transfers between devices, swap(): return lax.ppermute(value, axis, [(i, i ^ bits) for i in range(size)])  68.4 us
    ppermute x59, starting transfers between devices, swap(): return lax.ppermute(value, axis, [(i, i ^ bits) for i in range(size)])  59.7 us
    all_to_all x2, blocking collectives, body(): sums = lax.all_to_all(sums, ('samp', 'chrom'), 0, 0)  20.9 us
  transfers between devices with their start and end apart: 59, of which 35 were waited for; matrix products, arithmetic and copies ran while one was open for 0% of the time, Pallas kernels for 5%

profile of v7, /device:TPU:0, one launch (start us, length us, event | category | flops | bytes accessed | tf_op | source)
XLA Modules:
  0.0 170.0 jit_solution(18090106960851609215)
XLA Ops:
  0.6 3.0 %shard_map.77 = (bf16[512,1024]{1,0:T(8,128)(2,1)S(1)}, bf16[512,1024]{1,0:T(8,128)(2,1)S(1)}, f32[4,128,128]{2,1,0:T(8,128)S(1)}, bf16[1024,256]{1,0:T(8,128)(2,1)S(1)}, f32[4,128,1024]{2,1,0:T(8,128)S(1)}) custom-call(f32[4,2,128,1024]{3,2,1,0:T(8,128)} %bitcast.7, f32[1024,128]{1,0:T(8,128)} %coef_ref.3), custom_call_target="tpu_custom_call" | custom-call | flops 536870912 | bytes 8388608 | tf_op jit(solution)/shard_map/pallas_call | solution.py:378
  5.4 5.0 %collective-permute-start.1 = (f32[128,128]{1,0:T(8,128)S(1)}, f32[128,128]{1,0:T(8,128)S(1)}, u32[]{:S(2)}, u32[]{:S(2)}) collective-permute-start(f32[128,128]{1,0:T(8,128)S(1)} %get-tuple-element.66), channel_id=1, source_target_pairs={{0,6},{1,7},{2,4},{3,5},{4,2},{5,3},{6,0},{7,1},{8,14},{9,15},{10,... | collective-permute-start | bytes 196616 | tf_op jit(solution)/shard_map/ppermute | solution.py:20
  13.0 3.3 %collective-permute-done.2.refs_2_ = f32[128,128]{1,0:T(8,128)S(1)} collective-permute-done((f32[128,128]{1,0:T(8,128)S(1)}, f32[128,128]{1,0:T(8,128)S(1)}, u32[]{:S(2)}, u32[]{:S(2)}) %collective-permute-start.2) | collective-permute-done | bytes 65568 | tf_op jit(solution)/shard_map/ppermute | solution.py:20
  16.3 2.5 %collective-permute-start.4 = (f32[128,128]{1,0:T(8,128)S(1)}, f32[128,128]{1,0:T(8,128)S(1)}, u32[]{:S(2)}, u32[]{:S(2)}) collective-permute-start(f32[128,128]{1,0:T(8,128)S(1)} %shard_map.80.refs_7_), channel_id=1, source_target_pairs={{0,6},{1,7},{2,4},{3,5},{4,2},{5,3},{6,0},{7,1},{8,14},{9,15},{10,... | collective-permute-start | bytes 196616 | tf_op jit(solution)/shard_map/ppermute | solution.py:20
  22.7 2.8 %collective-permute-done.6.refs_3_ = f32[128,128]{1,0:T(8,128)S(1)} collective-permute-done((f32[128,128]{1,0:T(8,128)S(1)}, f32[128,128]{1,0:T(8,128)S(1)}, u32[]{:S(2)}, u32[]{:S(2)}) %collective-permute-start.6) | collective-permute-done | bytes 65568 | tf_op jit(solution)/shard_map/ppermute | solution.py:20
  33.9 3.7 %collective-permute-done.12.refs_2_ = f32[256,128]{1,0:T(8,128)S(1)} collective-permute-done((f32[256,128]{1,0:T(8,128)S(1)}, f32[256,128]{1,0:T(8,128)S(1)}, u32[]{:S(2)}, u32[]{:S(2)}) %collective-permute-start.12) | collective-permute-done | bytes 131104 | tf_op jit(solution)/shard_map/ppermute | solution.py:20
  41.2 2.5 %collective-permute-done.14.refs_1_ = f32[256,128]{1,0:T(8,128)S(1)} collective-permute-done((f32[256,128]{1,0:T(8,128)S(1)}, f32[256,128]{1,0:T(8,128)S(1)}, u32[]{:S(2)}, u32[]{:S(2)}) %collective-permute-start.14) | collective-permute-done | bytes 131104 | tf_op jit(solution)/shard_map/ppermute | solution.py:20
  43.7 2.3 %collective-permute-done.15.refs_2_ = f32[256,128]{1,0:T(8,128)S(1)} collective-permute-done((f32[256,128]{1,0:T(8,128)S(1)}, f32[256,128]{1,0:T(8,128)S(1)}, u32[]{:S(2)}, u32[]{:S(2)}) %collective-permute-start.15) | collective-permute-done | bytes 131104 | tf_op jit(solution)/shard_map/ppermute | solution.py:20
  48.5 2.3 %collective-permute-start.18 = (f32[128,128]{1,0:T(8,128)S(1)}, f32[128,128]{1,0:T(8,128)S(1)}, u32[]{:S(2)}, u32[]{:S(2)}) collective-permute-start(f32[128,128]{1,0:T(8,128)S(1)} %get-tuple-element.79), channel_id=1, source_target_pairs={{0,6},{1,7},{2,4},{3,5},{4,2},{5,3},{6,0},{7,1},{8,14},{9,15},{10,... | collective-permute-start | bytes 196616 | tf_op jit(solution)/shard_map/ppermute | solution.py:20
  50.9 2.1 %collective-permute-start.20 = (f32[128,128]{1,0:T(8,128)S(1)}, f32[128,128]{1,0:T(8,128)S(1)}, u32[]{:S(2)}, u32[]{:S(2)}) collective-permute-start(f32[128,128]{1,0:T(8,128)S(1)} %get-tuple-element.81), channel_id=1, source_target_pairs={{0,2},{1,3},{2,0},{3,1},{4,6},{5,7},{6,4},{7,5},{8,10},{9,11},{10,... | collective-permute-start | bytes 196616 | tf_op jit(solution)/shard_map/ppermute | solution.py:20
  53.0 2.4 %collective-permute-done.18.refs_2_ = f32[128,128]{1,0:T(8,128)S(1)} collective-permute-done((f32[128,128]{1,0:T(8,128)S(1)}, f32[128,128]{1,0:T(8,128)S(1)}, u32[]{:S(2)}, u32[]{:S(2)}) %collective-permute-start.18) | collective-permute-done | bytes 65568 | tf_op jit(solution)/shard_map/ppermute | solution.py:20
  57.4 10.7 %all_to_all.10.sums_ref = f32[32,2,128]{2,1,0:T(2,128)S(1)} all-to-all(f32[32,2,128]{2,1,0:T(2,128)S(1)} %shard_map.88), channel_id=1, replica_groups=mesh['samp'=4,'chrom'=8] {'samp','chrom'}, dimensions={0} | all-to-all | bytes 65536 | tf_op jit(solution)/shard_map/all_to_all | solution.py:427
  73.0 2.4 %collective-permute-start.24 = (f32[128,128]{1,0:T(8,128)S(1)}, f32[128,128]{1,0:T(8,128)S(1)}, u32[]{:S(2)}, u32[]{:S(2)}) collective-permute-start(f32[128,128]{1,0:T(8,128)S(1)} %get-tuple-element.88), channel_id=1, source_target_pairs={{0,2},{1,3},{2,0},{3,1},{4,6},{5,7},{6,4},{7,5},{8,10},{9,11},{10,... | collective-permute-start | bytes 196616 | tf_op jit(solution)/shard_map/ppermute | solution.py:20
  75.4 2.4 %collective-permute-done.22.refs_1_ = f32[128,128]{1,0:T(8,128)S(1)} collective-permute-done((f32[128,128]{1,0:T(8,128)S(1)}, f32[128,128]{1,0:T(8,128)S(1)}, u32[]{:S(2)}, u32[]{:S(2)}) %collective-permute-start.22) | collective-permute-done | bytes 65568 | tf_op jit(solution)/shard_map/ppermute | solution.py:20
  85.7 2.1 %collective-permute-done.27.refs_3_ = f32[128,128]{1,0:T(8,128)S(1)} collective-permute-done((f32[128,128]{1,0:T(8,128)S(1)}, f32[128,128]{1,0:T(8,128)S(1)}, u32[]{:S(2)}, u32[]{:S(2)}) %collective-permute-start.27) | collective-permute-done | bytes 65568 | tf_op jit(solution)/shard_map/ppermute | solution.py:20
  91.5 2.2 %collective-permute-start.34 = (f32[256,128]{1,0:T(8,128)S(1)}, f32[256,128]{1,0:T(8,128)S(1)}, u32[]{:S(2)}, u32[]{:S(2)}) collective-permute-start(f32[256,128]{1,0:T(8,128)S(1)} %get-tuple-element.92), channel_id=1, source_target_pairs={{0,24},{8,16},{16,8},{24,0},{1,25},{9,17},{17,9},{25,1},{2,26},{10... | collective-permute-start | bytes 393224 | tf_op jit(solution)/shard_map/ppermute | solution.py:20
  94.2 2.3 %collective-permute-done.32.refs_1_ = f32[256,128]{1,0:T(8,128)S(1)} collective-permute-done((f32[256,128]{1,0:T(8,128)S(1)}, f32[256,128]{1,0:T(8,128)S(1)}, u32[]{:S(2)}, u32[]{:S(2)}) %collective-permute-start.32) | collective-permute-done | bytes 131104 | tf_op jit(solution)/shard_map/ppermute | solution.py:20
  96.5 2.4 %collective-permute-done.33.refs_2_ = f32[256,128]{1,0:T(8,128)S(1)} collective-permute-done((f32[256,128]{1,0:T(8,128)S(1)}, f32[256,128]{1,0:T(8,128)S(1)}, u32[]{:S(2)}, u32[]{:S(2)}) %collective-permute-start.33) | collective-permute-done | bytes 131104 | tf_op jit(solution)/shard_map/ppermute | solution.py:20
  102.5 2.4 %collective-permute-done.35.refs_1_ = f32[256,128]{1,0:T(8,128)S(1)} collective-permute-done((f32[256,128]{1,0:T(8,128)S(1)}, f32[256,128]{1,0:T(8,128)S(1)}, u32[]{:S(2)}, u32[]{:S(2)}) %collective-permute-start.35) | collective-permute-done | bytes 131104 | tf_op jit(solution)/shard_map/ppermute | solution.py:20
  104.9 2.7 %collective-permute-done.36.refs_2_ = f32[256,128]{1,0:T(8,128)S(1)} collective-permute-done((f32[256,128]{1,0:T(8,128)S(1)}, f32[256,128]{1,0:T(8,128)S(1)}, u32[]{:S(2)}, u32[]{:S(2)}) %collective-permute-start.36) | collective-permute-done | bytes 131104 | tf_op jit(solution)/shard_map/ppermute | solution.py:20
  110.0 2.1 %collective-permute-start.39 = (f32[128,128]{1,0:T(8,128)S(1)}, f32[128,128]{1,0:T(8,128)S(1)}, u32[]{:S(2)}, u32[]{:S(2)}) collective-permute-start(f32[128,128]{1,0:T(8,128)S(1)} %get-tuple-element.97), channel_id=1, source_target_pairs={{0,6},{1,7},{2,4},{3,5},{4,2},{5,3},{6,0},{7,1},{8,14},{9,15},{10,... | collective-permute-start | bytes 196616 | tf_op jit(solution)/shard_map/ppermute | solution.py:20
  112.2 2.3 %collective-permute-start.41 = (f32[128,128]{1,0:T(8,128)S(1)}, f32[128,128]{1,0:T(8,128)S(1)}, u32[]{:S(2)}, u32[]{:S(2)}) collective-permute-start(f32[128,128]{1,0:T(8,128)S(1)} %get-tuple-element.99), channel_id=1, source_target_pairs={{0,2},{1,3},{2,0},{3,1},{4,6},{5,7},{6,4},{7,5},{8,10},{9,11},{10,... | collective-permute-start | bytes 196616 | tf_op jit(solution)/shard_map/ppermute | solution.py:20
  114.5 2.4 %collective-permute-done.39.refs_2_ = f32[128,128]{1,0:T(8,128)S(1)} collective-permute-done((f32[128,128]{1,0:T(8,128)S(1)}, f32[128,128]{1,0:T(8,128)S(1)}, u32[]{:S(2)}, u32[]{:S(2)}) %collective-permute-start.39) | collective-permute-done | bytes 65568 | tf_op jit(solution)/shard_map/ppermute | solution.py:20
  118.9 10.3 %all_to_all.11.sums_ref = f32[32,2,128]{2,1,0:T(2,128)S(1)} all-to-all(f32[32,2,128]{2,1,0:T(2,128)S(1)} %shard_map.99), channel_id=1, replica_groups=mesh['samp'=4,'chrom'=8] {'samp','chrom'}, dimensions={0} | all-to-all | bytes 65536 | tf_op jit(solution)/shard_map/all_to_all | solution.py:427
  134.0 2.4 %collective-permute-start.45 = (f32[128,128]{1,0:T(8,128)S(1)}, f32[128,128]{1,0:T(8,128)S(1)}, u32[]{:S(2)}, u32[]{:S(2)}) collective-permute-start(f32[128,128]{1,0:T(8,128)S(1)} %get-tuple-element.105), channel_id=1, source_target_pairs={{0,2},{1,3},{2,0},{3,1},{4,6},{5,7},{6,4},{7,5},{8,10},{9,11},{10,... | collective-permute-start | bytes 196616 | tf_op jit(solution)/shard_map/ppermute | solution.py:20
  136.5 2.6 %shard_map.103 = (f32[1024,128]{1,0:T(8,128)S(1)}, f32[1024,128]{1,0:T(8,128)S(1)}) custom-call(f32[1024,128]{1,0:T(8,128)S(1)} %get-tuple-element.106.coef_ref, s32[8,128]{1,0:T(8,128)S(1)} %bitcast.6, bf16[512,1024]{1,0:T(8,128)(2,1)S(1)} %get-tuple-element.61.refs_8_.refs_1_.high_ref.refs_0_, ...), custom_call_target="tpu_custom_call" | custom-call | flops 2147483648 | bytes 8388608 | tf_op jit(solution)/shard_map/pallas_call | solution.py:438
  146.7 2.1 %collective-permute-done.48.refs_3_ = f32[128,128]{1,0:T(8,128)S(1)} collective-permute-done((f32[128,128]{1,0:T(8,128)S(1)}, f32[128,128]{1,0:T(8,128)S(1)}, u32[]{:S(2)}, u32[]{:S(2)}) %collective-permute-start.48) | collective-permute-done | bytes 65568 | tf_op jit(solution)/shard_map/ppermute | solution.py:20
  152.3 2.2 %collective-permute-start.55 = (f32[272,128]{1,0:T(8,128)S(1)}, f32[272,128]{1,0:T(8,128)S(1)}, u32[]{:S(2)}, u32[]{:S(2)}) collective-permute-start(f32[272,128]{1,0:T(8,128)S(1)} %get-tuple-element.114), channel_id=1, source_target_pairs={{0,24},{8,16},{16,8},{24,0},{1,25},{9,17},{17,9},{25,1},{2,26},{10... | collective-permute-start | bytes 417800 | tf_op jit(solution)/shard_map/ppermute | solution.py:20
  155.6 2.0 %collective-permute-done.53.refs_1_ = f32[272,128]{1,0:T(8,128)S(1)} collective-permute-done((f32[272,128]{1,0:T(8,128)S(1)}, f32[272,128]{1,0:T(8,128)S(1)}, u32[]{:S(2)}, u32[]{:S(2)}) %collective-permute-start.53) | collective-permute-done | bytes 139296 | tf_op jit(solution)/shard_map/ppermute | solution.py:20
  157.6 2.5 %collective-permute-done.54.refs_2_ = f32[272,128]{1,0:T(8,128)S(1)} collective-permute-done((f32[272,128]{1,0:T(8,128)S(1)}, f32[272,128]{1,0:T(8,128)S(1)}, u32[]{:S(2)}, u32[]{:S(2)}) %collective-permute-start.54) | collective-permute-done | bytes 139296 | tf_op jit(solution)/shard_map/ppermute | solution.py:20
  163.9 2.5 %collective-permute-done.56.refs_1_ = f32[256,128]{1,0:T(8,128)S(1)} collective-permute-done((f32[256,128]{1,0:T(8,128)S(1)}, f32[256,128]{1,0:T(8,128)S(1)}, u32[]{:S(2)}, u32[]{:S(2)}) %collective-permute-start.56) | collective-permute-done | bytes 131104 | tf_op jit(solution)/shard_map/ppermute | solution.py:20
  166.4 2.8 %collective-permute-done.57.refs_2_ = f32[256,128]{1,0:T(8,128)S(1)} collective-permute-done((f32[256,128]{1,0:T(8,128)S(1)}, f32[256,128]{1,0:T(8,128)S(1)}, u32[]{:S(2)}, u32[]{:S(2)}) %collective-permute-start.57) | collective-permute-done | bytes 131104 | tf_op jit(solution)/shard_map/ppermute | solution.py:20
  (130 shorter events, 71.5 us)
Async XLA Ops:
  5.4 7.7 %collective-permute-start.1 = (f32[128,128]{1,0:T(8,128)S(1)}, f32[128,128]{1,0:T(8,128)S(1)}, u32[]{:S(2)}, u32[]{:S(2)}) collective-permute-start(f32[128,128]{1,0:T(8,128)S(1)} %get-tuple-element.66), channel_id=1, source_target_pairs={{0,6},{1,7},{2,4},{3,5},{4,2},{5,3},{6,0},{7,1},{8,14},{9,15},{10,... | collective-permute-start | bytes 196616 | tf_op jit(solution)/shard_map/ppermute | solution.py:20
  18.8 6.6 %collective-permute-start.6 = (f32[128,128]{1,0:T(8,128)S(1)}, f32[128,128]{1,0:T(8,128)S(1)}, u32[]{:S(2)}, u32[]{:S(2)}) collective-permute-start(f32[128,128]{1,0:T(8,128)S(1)} %shard_map.80.refs_7_), channel_id=1, source_target_pairs={{0,4},{1,5},{2,6},{3,7},{4,0},{5,1},{6,2},{7,3},{8,12},{9,13},{10,... | collective-permute-start | bytes 196616 | tf_op jit(solution)/shard_map/ppermute | solution.py:20
  18.9 6.5 %collective-permute-start.10 = (f32[128,128]{1,0:T(8,128)S(1)}, f32[128,128]{1,0:T(8,128)S(1)}, u32[]{:S(2)}, u32[]{:S(2)}) collective-permute-start(f32[128,128]{1,0:T(8,128)S(1)} %shard_map.80.refs_7_), channel_id=1, source_target_pairs={{0,1},{1,0},{2,3},{3,2},{4,5},{5,4},{6,7},{7,6},{8,9},{9,8},{10,11... | collective-permute-start | bytes 196616 | tf_op jit(solution)/shard_map/ppermute | solution.py:20
  18.9 6.5 %collective-permute-start.8 = (f32[128,128]{1,0:T(8,128)S(1)}, f32[128,128]{1,0:T(8,128)S(1)}, u32[]{:S(2)}, u32[]{:S(2)}) collective-permute-start(f32[128,128]{1,0:T(8,128)S(1)} %shard_map.80.refs_7_), channel_id=1, source_target_pairs={{0,3},{1,2},{2,1},{3,0},{4,7},{5,6},{6,5},{7,4},{8,11},{9,10},{10,... | collective-permute-start | bytes 196616 | tf_op jit(solution)/shard_map/ppermute | solution.py:20
  29.5 8.0 %collective-permute-start.12 = (f32[256,128]{1,0:T(8,128)S(1)}, f32[256,128]{1,0:T(8,128)S(1)}, u32[]{:S(2)}, u32[]{:S(2)}) collective-permute-start(f32[256,128]{1,0:T(8,128)S(1)} %get-tuple-element.73), channel_id=1, source_target_pairs={{0,16},{8,24},{16,0},{24,8},{1,17},{9,25},{17,1},{25,9},{2,18},{10... | collective-permute-start | bytes 393224 | tf_op jit(solution)/shard_map/ppermute | solution.py:20
  31.1 6.5 %collective-permute-start.13 = (f32[256,128]{1,0:T(8,128)S(1)}, f32[256,128]{1,0:T(8,128)S(1)}, u32[]{:S(2)}, u32[]{:S(2)}) collective-permute-start(f32[256,128]{1,0:T(8,128)S(1)} %get-tuple-element.74), channel_id=1, source_target_pairs={{0,24},{8,16},{16,8},{24,0},{1,25},{9,17},{17,9},{25,1},{2,26},{10... | collective-permute-start | bytes 393224 | tf_op jit(solution)/shard_map/ppermute | solution.py:20
  38.9 7.2 %collective-permute-start.15 = (f32[256,128]{1,0:T(8,128)S(1)}, f32[256,128]{1,0:T(8,128)S(1)}, u32[]{:S(2)}, u32[]{:S(2)}) collective-permute-start(f32[256,128]{1,0:T(8,128)S(1)} %shard_map.83.refs_0_), channel_id=1, source_target_pairs={{0,16},{8,24},{16,0},{24,8},{1,17},{9,25},{17,1},{25,9},{2,18},{10... | collective-permute-start | bytes 393224 | tf_op jit(solution)/shard_map/ppermute | solution.py:20
  48.5 6.8 %collective-permute-start.18 = (f32[128,128]{1,0:T(8,128)S(1)}, f32[128,128]{1,0:T(8,128)S(1)}, u32[]{:S(2)}, u32[]{:S(2)}) collective-permute-start(f32[128,128]{1,0:T(8,128)S(1)} %get-tuple-element.79), channel_id=1, source_target_pairs={{0,6},{1,7},{2,4},{3,5},{4,2},{5,3},{6,0},{7,1},{8,14},{9,15},{10,... | collective-permute-start | bytes 196616 | tf_op jit(solution)/shard_map/ppermute | solution.py:20
  50.9 6.5 %collective-permute-start.19 = (f32[128,128]{1,0:T(8,128)S(1)}, f32[128,128]{1,0:T(8,128)S(1)}, u32[]{:S(2)}, u32[]{:S(2)}) collective-permute-start(f32[128,128]{1,0:T(8,128)S(1)} %get-tuple-element.80), channel_id=1, source_target_pairs={{0,4},{1,5},{2,6},{3,7},{4,0},{5,1},{6,2},{7,3},{8,12},{9,13},{10,... | collective-permute-start | bytes 196616 | tf_op jit(solution)/shard_map/ppermute | solution.py:20
  50.9 6.5 %collective-permute-start.20 = (f32[128,128]{1,0:T(8,128)S(1)}, f32[128,128]{1,0:T(8,128)S(1)}, u32[]{:S(2)}, u32[]{:S(2)}) collective-permute-start(f32[128,128]{1,0:T(8,128)S(1)} %get-tuple-element.81), channel_id=1, source_target_pairs={{0,2},{1,3},{2,0},{3,1},{4,6},{5,7},{6,4},{7,5},{8,10},{9,11},{10,... | collective-permute-start | bytes 196616 | tf_op jit(solution)/shard_map/ppermute | solution.py:20
  70.9 6.9 %collective-permute-start.22 = (f32[128,128]{1,0:T(8,128)S(1)}, f32[128,128]{1,0:T(8,128)S(1)}, u32[]{:S(2)}, u32[]{:S(2)}) collective-permute-start(f32[128,128]{1,0:T(8,128)S(1)} %get-tuple-element.86), channel_id=1, source_target_pairs={{0,6},{1,7},{2,4},{3,5},{4,2},{5,3},{6,0},{7,1},{8,14},{9,15},{10,... | collective-permute-start | bytes 196616 | tf_op jit(solution)/shard_map/ppermute | solution.py:20
  71.6 7.9 %collective-permute-start.23 = (f32[128,128]{1,0:T(8,128)S(1)}, f32[128,128]{1,0:T(8,128)S(1)}, u32[]{:S(2)}, u32[]{:S(2)}) collective-permute-start(f32[128,128]{1,0:T(8,128)S(1)} %get-tuple-element.87), channel_id=1, source_target_pairs={{0,4},{1,5},{2,6},{3,7},{4,0},{5,1},{6,2},{7,3},{8,12},{9,13},{10,... | collective-permute-start | bytes 196616 | tf_op jit(solution)/shard_map/ppermute | solution.py:20
  80.9 6.8 %collective-permute-start.27 = (f32[128,128]{1,0:T(8,128)S(1)}, f32[128,128]{1,0:T(8,128)S(1)}, u32[]{:S(2)}, u32[]{:S(2)}) collective-permute-start(f32[128,128]{1,0:T(8,128)S(1)} %shard_map.92.refs_7_), channel_id=1, source_target_pairs={{0,4},{1,5},{2,6},{3,7},{4,0},{5,1},{6,2},{7,3},{8,12},{9,13},{10,... | collective-permute-start | bytes 196616 | tf_op jit(solution)/shard_map/ppermute | solution.py:20
  81.2 6.6 %collective-permute-start.29 = (f32[128,128]{1,0:T(8,128)S(1)}, f32[128,128]{1,0:T(8,128)S(1)}, u32[]{:S(2)}, u32[]{:S(2)}) collective-permute-start(f32[128,128]{1,0:T(8,128)S(1)} %shard_map.92.refs_7_), channel_id=1, source_target_pairs={{0,3},{1,2},{2,1},{3,0},{4,7},{5,6},{6,5},{7,4},{8,11},{9,10},{10,... | collective-permute-start | bytes 196616 | tf_op jit(solution)/shard_map/ppermute | solution.py:20
  82.5 6.5 %collective-permute-start.30 = (f32[128,128]{1,0:T(8,128)S(1)}, f32[128,128]{1,0:T(8,128)S(1)}, u32[]{:S(2)}, u32[]{:S(2)}) collective-permute-start(f32[128,128]{1,0:T(8,128)S(1)} %shard_map.92.refs_7_), channel_id=1, source_target_pairs={{0,2},{1,3},{2,0},{3,1},{4,6},{5,7},{6,4},{7,5},{8,10},{9,11},{10,... | collective-permute-start | bytes 196616 | tf_op jit(solution)/shard_map/ppermute | solution.py:20
  90.9 8.1 %collective-permute-start.33 = (f32[256,128]{1,0:T(8,128)S(1)}, f32[256,128]{1,0:T(8,128)S(1)}, u32[]{:S(2)}, u32[]{:S(2)}) collective-permute-start(f32[256,128]{1,0:T(8,128)S(1)} %get-tuple-element.91), channel_id=1, source_target_pairs={{0,16},{8,24},{16,0},{24,8},{1,17},{9,25},{17,1},{25,9},{2,18},{10... | collective-permute-start | bytes 393224 | tf_op jit(solution)/shard_map/ppermute | solution.py:20
  91.5 7.4 %collective-permute-start.34 = (f32[256,128]{1,0:T(8,128)S(1)}, f32[256,128]{1,0:T(8,128)S(1)}, u32[]{:S(2)}, u32[]{:S(2)}) collective-permute-start(f32[256,128]{1,0:T(8,128)S(1)} %get-tuple-element.92), channel_id=1, source_target_pairs={{0,24},{8,16},{16,8},{24,0},{1,25},{9,17},{17,9},{25,1},{2,26},{10... | collective-permute-start | bytes 393224 | tf_op jit(solution)/shard_map/ppermute | solution.py:20
  100.4 7.1 %collective-permute-start.36 = (f32[256,128]{1,0:T(8,128)S(1)}, f32[256,128]{1,0:T(8,128)S(1)}, u32[]{:S(2)}, u32[]{:S(2)}) collective-permute-start(f32[256,128]{1,0:T(8,128)S(1)} %shard_map.95.refs_0_), channel_id=1, source_target_pairs={{0,16},{8,24},{16,0},{24,8},{1,17},{9,25},{17,1},{25,9},{2,18},{10... | collective-permute-start | bytes 393224 | tf_op jit(solution)/shard_map/ppermute | solution.py:20
  101.1 6.5 %collective-permute-start.37 = (f32[256,128]{1,0:T(8,128)S(1)}, f32[256,128]{1,0:T(8,128)S(1)}, u32[]{:S(2)}, u32[]{:S(2)}) collective-permute-start(f32[256,128]{1,0:T(8,128)S(1)} %shard_map.95.refs_0_), channel_id=1, source_target_pairs={{0,24},{8,16},{16,8},{24,0},{1,25},{9,17},{17,9},{25,1},{2,26},{10... | collective-permute-start | bytes 393224 | tf_op jit(solution)/shard_map/ppermute | solution.py:20
  110.0 6.8 %collective-permute-start.39 = (f32[128,128]{1,0:T(8,128)S(1)}, f32[128,128]{1,0:T(8,128)S(1)}, u32[]{:S(2)}, u32[]{:S(2)}) collective-permute-start(f32[128,128]{1,0:T(8,128)S(1)} %get-tuple-element.97), channel_id=1, source_target_pairs={{0,6},{1,7},{2,4},{3,5},{4,2},{5,3},{6,0},{7,1},{8,14},{9,15},{10,... | collective-permute-start | bytes 196616 | tf_op jit(solution)/shard_map/ppermute | solution.py:20
  112.1 6.7 %collective-permute-start.40 = (f32[128,128]{1,0:T(8,128)S(1)}, f32[128,128]{1,0:T(8,128)S(1)}, u32[]{:S(2)}, u32[]{:S(2)}) collective-permute-start(f32[128,128]{1,0:T(8,128)S(1)} %get-tuple-element.98), channel_id=1, source_target_pairs={{0,4},{1,5},{2,6},{3,7},{4,0},{5,1},{6,2},{7,3},{8,12},{9,13},{10,... | collective-permute-start | bytes 196616 | tf_op jit(solution)/shard_map/ppermute | solution.py:20
  112.2 6.7 %collective-permute-start.41 = (f32[128,128]{1,0:T(8,128)S(1)}, f32[128,128]{1,0:T(8,128)S(1)}, u32[]{:S(2)}, u32[]{:S(2)}) collective-permute-start(f32[128,128]{1,0:T(8,128)S(1)} %get-tuple-element.99), channel_id=1, source_target_pairs={{0,2},{1,3},{2,0},{3,1},{4,6},{5,7},{6,4},{7,5},{8,10},{9,11},{10,... | collective-permute-start | bytes 196616 | tf_op jit(solution)/shard_map/ppermute | solution.py:20
  132.0 7.0 %collective-permute-start.43 = (f32[128,128]{1,0:T(8,128)S(1)}, f32[128,128]{1,0:T(8,128)S(1)}, u32[]{:S(2)}, u32[]{:S(2)}) collective-permute-start(f32[128,128]{1,0:T(8,128)S(1)} %get-tuple-element.103), channel_id=1, source_target_pairs={{0,6},{1,7},{2,4},{3,5},{4,2},{5,3},{6,0},{7,1},{8,14},{9,15},{10,... | collective-permute-start | bytes 196616 | tf_op jit(solution)/shard_map/ppermute | solution.py:20
  132.6 7.9 %collective-permute-start.44 = (f32[128,128]{1,0:T(8,128)S(1)}, f32[128,128]{1,0:T(8,128)S(1)}, u32[]{:S(2)}, u32[]{:S(2)}) collective-permute-start(f32[128,128]{1,0:T(8,128)S(1)} %get-tuple-element.104), channel_id=1, source_target_pairs={{0,4},{1,5},{2,6},{3,7},{4,0},{5,1},{6,2},{7,3},{8,12},{9,13},{10,... | collective-permute-start | bytes 196616 | tf_op jit(solution)/shard_map/ppermute | solution.py:20
  142.0 6.8 %collective-permute-start.48 = (f32[128,128]{1,0:T(8,128)S(1)}, f32[128,128]{1,0:T(8,128)S(1)}, u32[]{:S(2)}, u32[]{:S(2)}) collective-permute-start(f32[128,128]{1,0:T(8,128)S(1)} %shard_map.104.refs_7_), channel_id=1, source_target_pairs={{0,4},{1,5},{2,6},{3,7},{4,0},{5,1},{6,2},{7,3},{8,12},{9,13},{10,... | collective-permute-start | bytes 196616 | tf_op jit(solution)/shard_map/ppermute | solution.py:20
  142.3 6.6 %collective-permute-start.50 = (f32[128,128]{1,0:T(8,128)S(1)}, f32[128,128]{1,0:T(8,128)S(1)}, u32[]{:S(2)}, u32[]{:S(2)}) collective-permute-start(f32[128,128]{1,0:T(8,128)S(1)} %shard_map.104.refs_7_), channel_id=1, source_target_pairs={{0,3},{1,2},{2,1},{3,0},{4,7},{5,6},{6,5},{7,4},{8,11},{9,10},{10,... | collective-permute-start | bytes 196616 | tf_op jit(solution)/shard_map/ppermute | solution.py:20
  143.5 6.5 %collective-permute-start.51 = (f32[128,128]{1,0:T(8,128)S(1)}, f32[128,128]{1,0:T(8,128)S(1)}, u32[]{:S(2)}, u32[]{:S(2)}) collective-permute-start(f32[128,128]{1,0:T(8,128)S(1)} %shard_map.104.refs_7_), channel_id=1, source_target_pairs={{0,2},{1,3},{2,0},{3,1},{4,6},{5,7},{6,4},{7,5},{8,10},{9,11},{10,... | collective-permute-start | bytes 196616 | tf_op jit(solution)/shard_map/ppermute | solution.py:20
  151.0 6.6 %collective-permute-start.53 = (f32[272,128]{1,0:T(8,128)S(1)}, f32[272,128]{1,0:T(8,128)S(1)}, u32[]{:S(2)}, u32[]{:S(2)}) collective-permute-start(f32[272,128]{1,0:T(8,128)S(1)} %get-tuple-element.112), channel_id=1, source_target_pairs={{0,8},{8,0},{16,24},{24,16},{1,9},{9,1},{17,25},{25,17},{2,10},{10... | collective-permute-start | bytes 417800 | tf_op jit(solution)/shard_map/ppermute | solution.py:20
  151.7 8.4 %collective-permute-start.54 = (f32[272,128]{1,0:T(8,128)S(1)}, f32[272,128]{1,0:T(8,128)S(1)}, u32[]{:S(2)}, u32[]{:S(2)}) collective-permute-start(f32[272,128]{1,0:T(8,128)S(1)} %get-tuple-element.113), channel_id=1, source_target_pairs={{0,16},{8,24},{16,0},{24,8},{1,17},{9,25},{17,1},{25,9},{2,18},{10... | collective-permute-start | bytes 417800 | tf_op jit(solution)/shard_map/ppermute | solution.py:20
  152.3 7.8 %collective-permute-start.55 = (f32[272,128]{1,0:T(8,128)S(1)}, f32[272,128]{1,0:T(8,128)S(1)}, u32[]{:S(2)}, u32[]{:S(2)}) collective-permute-start(f32[272,128]{1,0:T(8,128)S(1)} %get-tuple-element.114), channel_id=1, source_target_pairs={{0,24},{8,16},{16,8},{24,0},{1,25},{9,17},{17,9},{25,1},{2,26},{10... | collective-permute-start | bytes 417800 | tf_op jit(solution)/shard_map/ppermute | solution.py:20
  161.9 7.3 %collective-permute-start.57 = (f32[256,128]{1,0:T(8,128)S(1)}, f32[256,128]{1,0:T(8,128)S(1)}, u32[]{:S(2)}, u32[]{:S(2)}) collective-permute-start(f32[256,128]{1,0:T(8,128)S(1)} %shard_map.107.refs_0_), channel_id=1, source_target_pairs={{0,16},{8,24},{16,0},{24,8},{1,17},{9,25},{17,1},{25,9},{2,18},{10... | collective-permute-start | bytes 393224 | tf_op jit(solution)/shard_map/ppermute | solution.py:20
  162.5 6.7 %collective-permute-start.58 = (f32[256,128]{1,0:T(8,128)S(1)}, f32[256,128]{1,0:T(8,128)S(1)}, u32[]{:S(2)}, u32[]{:S(2)}) collective-permute-start(f32[256,128]{1,0:T(8,128)S(1)} %shard_map.107.refs_0_), channel_id=1, source_target_pairs={{0,24},{8,16},{16,8},{24,0},{1,25},{9,17},{17,9},{25,1},{2,26},{10... | collective-permute-start | bytes 393224 | tf_op jit(solution)/shard_map/ppermute | solution.py:20
  (32 other events, 182.4 us)

commit v8 on v7

--- a/solution.py
+++ b/solution.py
@@ -12,6 +12,7 @@
 ITERS = 2
 STATS = 16
 PARTS = 2
+GIVEN = 2
 VMEM_LIMIT = 10 * 1024 * 1024
 
 
@@ -61,7 +62,17 @@
     )
 
 
-def split_rows(source_ref, ready, packed_ref, high_ref, low_ref, out_ref):
+def store_places(total, out_refs, first=0):
+    block = out_refs[0].shape[1]
+    for k in range(total.shape[0] // block):
+        place = first + k
+        for out in out_refs:
+            if 0 <= place < out.shape[0]:
+                out[place] = total[k * block : (k + 1) * block]
+            place -= out.shape[0]
+
+
+def split_rows(source_ref, ready, packed_ref, high_ref, low_ref, out_refs):
     half, block = source_ref.shape[0], source_ref.shape[1]
     group = max(1, half // 2)
     for first in range(0, half, group):
@@ -72,10 +83,11 @@
             low_ref[k * block : (k + 1) * block] = low
         rows = slice(first * block, (first + group) * block)
         total = wide_dot(high_ref[rows], low_ref[rows], packed_ref[...])
-        out_ref[first : first + group] = total.reshape((group,) + out_ref.shape[1:])
-
-
-def first_kernel(dosage_ref, coef_ref, high_ref, low_ref, out_ref, packed_ref, kept_ref, buffer_ref, coef_buffer, sems):
+        store_places(total, out_refs, first)
+
+
+def first_kernel(dosage_ref, coef_ref, high_ref, low_ref, *refs):
+    *out_refs, packed_ref, kept_ref, buffer_ref, coef_buffer, sems = refs
     me = lax.axis_index("chrom")
     place, core = me // 2, me % 2
     half = buffer_ref.shape[0]
@@ -104,14 +116,14 @@
 
     coef_copy.wait()
     packed_ref[...] = pack(coef_buffer[...])
-    split_rows(buffer_ref, ready, packed_ref, high_ref, low_ref, out_ref)
+    split_rows(buffer_ref, ready, packed_ref, high_ref, low_ref, out_refs)
     for group in copies[half:]:
         for copy in group:
             copy.wait()
 
 
 def second_kernel(kept_ref, packed_ref, high_ref, low_ref, out_ref):
-    split_rows(kept_ref, lambda k: None, packed_ref, high_ref, low_ref, out_ref)
+    split_rows(kept_ref, lambda k: None, packed_ref, high_ref, low_ref, [out_ref])
 
 
 def square_kernel(tested_ref, square_ref):
@@ -131,8 +143,8 @@
     return jnp.concatenate([column(ref[k : k + 1]) for k in range(ref.shape[0])])
 
 
-def rest_kernel(high_ref, low_ref, packed_ref, out_ref):
-    out_ref[...] = wide_dot(high_ref[...], low_ref[...], packed_ref[...]).reshape(out_ref.shape)
+def rest_kernel(high_ref, low_ref, packed_ref, *out_refs):
+    store_places(wide_dot(high_ref[...], low_ref[...], packed_ref[...]), out_refs)
 
 
 def residual_kernel(count, traits_ref, *refs):
@@ -180,7 +192,7 @@
 def image_kernel(count, *refs):
     pieces = refs[:count]
     high_ref, low_ref = refs[count : count + 2]
-    grad_ref, packed_ref, give_ref = refs[-3:]
+    grad_ref, packed_ref, *give_refs = refs[-2 - GIVEN :]
     samp = lax.axis_index("samp")
     block = pieces[0].shape[0]
     for bits, piece in enumerate(pieces):
@@ -188,7 +200,7 @@
         value = piece[...]
         grad_ref[rows] = value
         packed_ref[rows] = pack(value)
-    rest_kernel(high_ref, low_ref, packed_ref, give_ref)
+    rest_kernel(high_ref, low_ref, packed_ref, *give_refs)
 
 
 def norm_kernel(count, *refs):
@@ -204,7 +216,7 @@
         out[place] = sums
 
 
-def prox_kernel(total_rows, coef_ref, grad_ref, sums_ref, high_ref, low_ref, new_ref, packed_ref, give_ref):
+def prox_kernel(total_rows, coef_ref, grad_ref, sums_ref, high_ref, low_ref, new_ref, packed_ref, *give_refs):
     sums = sums_ref[0]
     for place in range(1, sums_ref.shape[0]):
         sums = sums + sums_ref[place]
@@ -218,7 +230,7 @@
     new = moved * (jnp.maximum(length - cut, 0.0) / jnp.maximum(length, cut))
     new_ref[...] = new
     packed_ref[...] = pack(new)
-    rest_kernel(high_ref, low_ref, packed_ref, give_ref)
+    rest_kernel(high_ref, low_ref, packed_ref, *give_refs)
 
 
 def own_kernel(coef_ref, group_ref, *refs):
@@ -295,16 +307,24 @@
 
 
 def place_kernel(*refs):
-    pieces, out = refs[:-1], refs[-1]
+    pieces, out, sems = refs[:-2], refs[-2], refs[-1]
     samp = lax.axis_index("samp")
     block = pieces[0].shape[0]
-    for bits, piece in enumerate(pieces):
-        out[pl.ds(pl.multiple_of((samp ^ bits) * block, block), block)] = piece[...]
-
-
-def chip_kernel(keep_ref, got_ref, *outs):
+    copies = [
+        pltpu.make_async_copy(
+            piece, out.at[pl.ds(pl.multiple_of((samp ^ bits) * block, block), block)], sems.at[bits]
+        )
+        for bits, piece in enumerate(pieces)
+    ]
+    for copy in copies:
+        copy.start()
+    for copy in copies:
+        copy.wait()
+
+
+def chip_kernel(first, keep_ref, got_ref, *outs):
     for k, out in enumerate(outs):
-        out[...] = keep_ref[k] + got_ref[k]
+        out[...] = keep_ref[first + k] + got_ref[k]
 
 
 def mean_kernel(total_rows, *refs):
@@ -314,11 +334,14 @@
     refs[-1][...] = total / total_rows
 
 
-def chrom_scatter(give, keep):
-    got = swap(give, "chrom", 1)
-    count = keep.shape[0]
-    sums = call(chip_kernel, [shape(keep.shape[1:])] * count, [whole()] * 2)(keep, got)
-    return [sums[0]] + [swap(sums[k], "chrom", 2 * k) for k in reversed(range(1, count))]
+def chrom_scatter(gives, keep):
+    sums, first = [], keep.shape[0]
+    for part in gives[::-1]:
+        count = part.shape[0]
+        first -= count
+        kernel = functools.partial(chip_kernel, first)
+        sums = list(call(kernel, [shape(keep.shape[1:])] * count, [whole()] * 2)(keep, swap(part, "chrom", 1))) + sums
+    return [sums[0]] + [swap(sums[k], "chrom", 2 * k) for k in reversed(range(1, len(sums)))]
 
 
 def chrom_order(size):
@@ -354,6 +377,7 @@
 
     part = shape((rows // 2, cols), jnp.bfloat16)
     half_out = shape((half, block, n_traits))
+    give_outs = [shape((count, block, n_traits)) for count in (half // 2, half - half // 2)]
     packed_cols = shape((cols, 2 * n_traits), jnp.bfloat16)
     packed_rows = shape((2 * n_traits, rows), jnp.bfloat16)
     rows_buffer = [pltpu.VMEM((rows, 2 * n_traits), jnp.bfloat16)]
@@ -375,9 +399,9 @@
 
     coefficients = start_coef
     kept_shape = (half, block, cols)
-    high1, low1, give, packed, kept = call(
+    high1, low1, *gives, packed, kept = call(
         first_kernel,
-        [part, part, half_out, packed_cols, shape(kept_shape)],
+        [part, part] + give_outs + [packed_cols, shape(kept_shape)],
         [pl.BlockSpec(memory_space=pltpu.HBM)] * 2,
         [pltpu.VMEM(kept_shape, jnp.float32), pltpu.VMEM(coefficients.shape, jnp.float32), pltpu.SemaphoreType.DMA((n_chrom * PARTS + 1,))],
         flops,
@@ -387,7 +411,7 @@
         pltpu.with_memory_space_constraint(coefficients, pltpu.HBM),
     )
     high0, low0, keep = call(second_kernel, [part, part, half_out], [whole()] * 2, (), flops, moved)(kept, packed)
-    summands = chrom_scatter(give, keep)
+    summands = chrom_scatter(gives, keep)
     parts = [high0, low0, high1, low1]
     tested_sq = call(square_kernel, shape((n_samp, test_width // 128, 128)), [whole()], (), 0, 2 * rows * tests)(tested)
 
@@ -411,29 +435,29 @@
         )
         pieces = samp_gather(own_grad)
         after = (tested_sq,) if iteration == 0 else ()
-        gradient, packed, give = call(
+        gradient, packed, *gives = call(
             functools.partial(image_kernel, n_samp),
-            [coef_out, packed_cols, half_out],
+            [coef_out, packed_cols] + give_outs,
             [whole()] * (n_samp + 2) + [anywhere()] * len(after),
             (),
             flops,
             moved,
         )(*pieces, high1, low1, *after)
-        summands = chrom_scatter(give, rest(high0, low0, packed))
+        summands = chrom_scatter(gives, rest(high0, low0, packed))
         size = n_samp * n_chrom
         sums = call(
             functools.partial(norm_kernel, half), shape((size, 2, n_traits)), [whole()] * (half + 1)
         )(own_grad, *summands)
         sums = lax.all_to_all(sums, ("samp", "chrom"), 0, 0)
-        coefficients, packed, give = call(
+        coefficients, packed, *gives = call(
             functools.partial(prox_kernel, total_rows),
-            [coef_out, packed_cols, half_out],
+            [coef_out, packed_cols] + give_outs,
             [whole()] * 5,
             (),
             flops,
             moved,
         )(coefficients, gradient, sums, high1, low1)
-        summands = chrom_scatter(give, rest(high0, low0, packed))
+        summands = chrom_scatter(gives, rest(high0, low0, packed))
 
     own_parts = call(own_kernel, [shape((rows, n_traits))] * GPD, [whole()] * 6, (), 4 * flops, 4 * moved)(
         coefficients, group_rows, *parts
@@ -460,7 +484,14 @@
     own_scores = call(
         functools.partial(score_kernel, total_rows), shape((test_width, n_traits)), [whole()] * (n_samp + 1)
     )(owner_rows, near_out[-1], *received[::-1])
-    scores = call(place_kernel, shape((tests, n_traits)), [whole()] * n_samp)(*samp_gather(own_scores))
+    scores = pl.pallas_call(
+        place_kernel,
+        out_shape=shape((tests, n_traits)),
+        in_specs=[whole()] * n_samp,
+        out_specs=anywhere(),
+        scratch_shapes=[pltpu.SemaphoreType.DMA((n_samp,))],
+        compiler_params=pltpu.CompilerParams(vmem_limit_bytes=VMEM_LIMIT),
+    )(*samp_gather(own_scores))
     return (scores, residual)
 
 

time: 170 us -> 169 us (level)
  waiting for transfers between devices: 68.4 us -> 65.2 us
  starting transfers between devices: 59.7 us -> 62 us
    ppermute x59 -> x64, waiting for transfers between devices: 68.4 us -> 65.2 us  [swap(): return lax.ppermute(value, axis, [(i, i ^ bits) for i in range(size)])]
    ppermute x59 -> x64, starting transfers between devices: 59.7 us -> 62 us  [swap(): return lax.ppermute(value, axis, [(i, i ^ bits) for i in range(size)])]
    pallas_call x11 -> x16, Pallas kernels: 8.06 us -> 8.04 us  [the longest x1 2.99 us: body(): call(first_kernel, [part, part] + give_outs + [packed_cols, shape(kept_sh...]
  transfers between devices with their start and end apart: 59 -> 64, of which waited for: 35 -> 35; matrix products, arithmetic and copies ran while one was open for 0% -> 0% of each run, Pallas kernels for 5% -> 5%
where the time goes in v8:
time: 169 us
  waiting for transfers between devices  65.2 us (39%)
  starting transfers between devices  62 us (37%)
  blocking collectives  20.4 us (12%)
  Pallas kernels  20 us (12%)
    ppermute x64, waiting for transfers between devices, swap(): return lax.ppermute(value, axis, [(i, i ^ bits) for i in range(size)])  65.2 us
    ppermute x64, starting transfers between devices, swap(): return lax.ppermute(value, axis, [(i, i ^ bits) for i in range(size)])  62 us
    all_to_all x2, blocking collectives, body(): sums = lax.all_to_all(sums, ('samp', 'chrom'), 0, 0)  20.4 us
  transfers between devices with their start and end apart: 64, of which 35 were waited for; matrix products, arithmetic and copies ran while one was open for 0% of the time, Pallas kernels for 5%

profile of v8, /device:TPU:0, one launch (start us, length us, event | category | flops | bytes accessed | tf_op | source)
XLA Modules:
  0.0 168.8 jit_solution(1259181453438058525)
XLA Ops:
  0.6 3.0 %shard_map.77 = (bf16[512,1024]{1,0:T(8,128)(2,1)S(1)}, bf16[512,1024]{1,0:T(8,128)(2,1)S(1)}, f32[2,128,128]{2,1,0:T(8,128)S(1)}, f32[2,128,128]{2,1,0:T(8,128)...) custom-call(f32[4,2,128,1024]{3,2,1,0:T(8,128)} %bitcast.7, f32[1024,128]{1,0:T(8,128)} %coef_ref.3), custom_call_target="tpu_custom_call" | custom-call | flops 536870912 | bytes 8388608 | tf_op jit(solution)/shard_map/pallas_call | solution.py:402
  5.2 5.1 %collective-permute-start.2 = (f32[128,128]{1,0:T(8,128)S(1)}, f32[128,128]{1,0:T(8,128)S(1)}, u32[]{:S(2)}, u32[]{:S(2)}) collective-permute-start(f32[128,128]{1,0:T(8,128)S(1)} %get-tuple-element.72), channel_id=1, source_target_pairs={{0,6},{1,7},{2,4},{3,5},{4,2},{5,3},{6,0},{7,1},{8,14},{9,15},{10,... | collective-permute-start | bytes 196616 | tf_op jit(solution)/shard_map/ppermute | solution.py:21
  12.8 3.3 %collective-permute-done.3.refs_2_ = f32[128,128]{1,0:T(8,128)S(1)} collective-permute-done((f32[128,128]{1,0:T(8,128)S(1)}, f32[128,128]{1,0:T(8,128)S(1)}, u32[]{:S(2)}, u32[]{:S(2)}) %collective-permute-start.3) | collective-permute-done | bytes 65568 | tf_op jit(solution)/shard_map/ppermute | solution.py:21
  16.1 2.6 %collective-permute-start.5 = (f32[128,128]{1,0:T(8,128)S(1)}, f32[128,128]{1,0:T(8,128)S(1)}, u32[]{:S(2)}, u32[]{:S(2)}) collective-permute-start(f32[128,128]{1,0:T(8,128)S(1)} %shard_map.81.refs_7_), channel_id=1, source_target_pairs={{0,6},{1,7},{2,4},{3,5},{4,2},{5,3},{6,0},{7,1},{8,14},{9,15},{10,... | collective-permute-start | bytes 196616 | tf_op jit(solution)/shard_map/ppermute | solution.py:21
  22.5 2.8 %collective-permute-done.7.refs_3_ = f32[128,128]{1,0:T(8,128)S(1)} collective-permute-done((f32[128,128]{1,0:T(8,128)S(1)}, f32[128,128]{1,0:T(8,128)S(1)}, u32[]{:S(2)}, u32[]{:S(2)}) %collective-permute-start.7) | collective-permute-done | bytes 65568 | tf_op jit(solution)/shard_map/ppermute | solution.py:21
  33.6 3.7 %collective-permute-done.13.refs_2_ = f32[256,128]{1,0:T(8,128)S(1)} collective-permute-done((f32[256,128]{1,0:T(8,128)S(1)}, f32[256,128]{1,0:T(8,128)S(1)}, u32[]{:S(2)}, u32[]{:S(2)}) %collective-permute-start.13) | collective-permute-done | bytes 131104 | tf_op jit(solution)/shard_map/ppermute | solution.py:21
  40.9 2.4 %collective-permute-done.15.refs_1_ = f32[256,128]{1,0:T(8,128)S(1)} collective-permute-done((f32[256,128]{1,0:T(8,128)S(1)}, f32[256,128]{1,0:T(8,128)S(1)}, u32[]{:S(2)}, u32[]{:S(2)}) %collective-permute-start.15) | collective-permute-done | bytes 131104 | tf_op jit(solution)/shard_map/ppermute | solution.py:21
  43.3 2.5 %collective-permute-done.16.refs_2_ = f32[256,128]{1,0:T(8,128)S(1)} collective-permute-done((f32[256,128]{1,0:T(8,128)S(1)}, f32[256,128]{1,0:T(8,128)S(1)}, u32[]{:S(2)}, u32[]{:S(2)}) %collective-permute-start.16) | collective-permute-done | bytes 131104 | tf_op jit(solution)/shard_map/ppermute | solution.py:21
  50.0 2.7 %collective-permute-start.22 = (f32[128,128]{1,0:T(8,128)S(1)}, f32[128,128]{1,0:T(8,128)S(1)}, u32[]{:S(2)}, u32[]{:S(2)}) collective-permute-start(f32[128,128]{1,0:T(8,128)S(1)} %get-tuple-element.88), channel_id=1, source_target_pairs={{0,2},{1,3},{2,0},{3,1},{4,6},{5,7},{6,4},{7,5},{8,10},{9,11},{10,... | collective-permute-start | bytes 196616 | tf_op jit(solution)/shard_map/ppermute | solution.py:21
  52.7 2.3 %collective-permute-done.20.refs_2_ = f32[128,128]{1,0:T(8,128)S(1)} collective-permute-done((f32[128,128]{1,0:T(8,128)S(1)}, f32[128,128]{1,0:T(8,128)S(1)}, u32[]{:S(2)}, u32[]{:S(2)}) %collective-permute-start.20) | collective-permute-done | bytes 65568 | tf_op jit(solution)/shard_map/ppermute | solution.py:21
  55.0 2.0 %collective-permute-done.21.refs_3_ = f32[128,128]{1,0:T(8,128)S(1)} collective-permute-done((f32[128,128]{1,0:T(8,128)S(1)}, f32[128,128]{1,0:T(8,128)S(1)}, u32[]{:S(2)}, u32[]{:S(2)}) %collective-permute-start.21) | collective-permute-done | bytes 65568 | tf_op jit(solution)/shard_map/ppermute | solution.py:21
  57.0 10.2 %all_to_all.10.sums_ref = f32[32,2,128]{2,1,0:T(2,128)S(1)} all-to-all(f32[32,2,128]{2,1,0:T(2,128)S(1)} %shard_map.90), channel_id=1, replica_groups=mesh['samp'=4,'chrom'=8] {'samp','chrom'}, dimensions={0} | all-to-all | bytes 65536 | tf_op jit(solution)/shard_map/all_to_all | solution.py:451
  71.9 2.5 %collective-permute-start.27 = (f32[128,128]{1,0:T(8,128)S(1)}, f32[128,128]{1,0:T(8,128)S(1)}, u32[]{:S(2)}, u32[]{:S(2)}) collective-permute-start(f32[128,128]{1,0:T(8,128)S(1)} %get-tuple-element.96), channel_id=1, source_target_pairs={{0,2},{1,3},{2,0},{3,1},{4,6},{5,7},{6,4},{7,5},{8,10},{9,11},{10,... | collective-permute-start | bytes 196616 | tf_op jit(solution)/shard_map/ppermute | solution.py:21
  74.4 2.3 %collective-permute-done.25.refs_1_ = f32[128,128]{1,0:T(8,128)S(1)} collective-permute-done((f32[128,128]{1,0:T(8,128)S(1)}, f32[128,128]{1,0:T(8,128)S(1)}, u32[]{:S(2)}, u32[]{:S(2)}) %collective-permute-start.25) | collective-permute-done | bytes 65568 | tf_op jit(solution)/shard_map/ppermute | solution.py:21
  84.6 2.2 %collective-permute-done.30.refs_3_ = f32[128,128]{1,0:T(8,128)S(1)} collective-permute-done((f32[128,128]{1,0:T(8,128)S(1)}, f32[128,128]{1,0:T(8,128)S(1)}, u32[]{:S(2)}, u32[]{:S(2)}) %collective-permute-start.30) | collective-permute-done | bytes 65568 | tf_op jit(solution)/shard_map/ppermute | solution.py:21
  90.5 2.2 %collective-permute-start.37 = (f32[256,128]{1,0:T(8,128)S(1)}, f32[256,128]{1,0:T(8,128)S(1)}, u32[]{:S(2)}, u32[]{:S(2)}) collective-permute-start(f32[256,128]{1,0:T(8,128)S(1)} %get-tuple-element.100), channel_id=1, source_target_pairs={{0,24},{8,16},{16,8},{24,0},{1,25},{9,17},{17,9},{25,1},{2,26},{10... | collective-permute-start | bytes 393224 | tf_op jit(solution)/shard_map/ppermute | solution.py:21
  93.3 2.3 %collective-permute-done.35.refs_1_ = f32[256,128]{1,0:T(8,128)S(1)} collective-permute-done((f32[256,128]{1,0:T(8,128)S(1)}, f32[256,128]{1,0:T(8,128)S(1)}, u32[]{:S(2)}, u32[]{:S(2)}) %collective-permute-start.35) | collective-permute-done | bytes 131104 | tf_op jit(solution)/shard_map/ppermute | solution.py:21
  95.6 2.3 %collective-permute-done.36.refs_2_ = f32[256,128]{1,0:T(8,128)S(1)} collective-permute-done((f32[256,128]{1,0:T(8,128)S(1)}, f32[256,128]{1,0:T(8,128)S(1)}, u32[]{:S(2)}, u32[]{:S(2)}) %collective-permute-start.36) | collective-permute-done | bytes 131104 | tf_op jit(solution)/shard_map/ppermute | solution.py:21
  101.5 2.4 %collective-permute-done.38.refs_1_ = f32[256,128]{1,0:T(8,128)S(1)} collective-permute-done((f32[256,128]{1,0:T(8,128)S(1)}, f32[256,128]{1,0:T(8,128)S(1)}, u32[]{:S(2)}, u32[]{:S(2)}) %collective-permute-start.38) | collective-permute-done | bytes 131104 | tf_op jit(solution)/shard_map/ppermute | solution.py:21
  103.9 2.6 %collective-permute-done.39.refs_2_ = f32[256,128]{1,0:T(8,128)S(1)} collective-permute-done((f32[256,128]{1,0:T(8,128)S(1)}, f32[256,128]{1,0:T(8,128)S(1)}, u32[]{:S(2)}, u32[]{:S(2)}) %collective-permute-start.39) | collective-permute-done | bytes 131104 | tf_op jit(solution)/shard_map/ppermute | solution.py:21
  108.8 2.1 %collective-permute-start.43 = (f32[128,128]{1,0:T(8,128)S(1)}, f32[128,128]{1,0:T(8,128)S(1)}, u32[]{:S(2)}, u32[]{:S(2)}) collective-permute-start(f32[128,128]{1,0:T(8,128)S(1)} %get-tuple-element.106), channel_id=1, source_target_pairs={{0,6},{1,7},{2,4},{3,5},{4,2},{5,3},{6,0},{7,1},{8,14},{9,15},{10,... | collective-permute-start | bytes 196616 | tf_op jit(solution)/shard_map/ppermute | solution.py:21
  110.9 2.5 %collective-permute-start.45 = (f32[128,128]{1,0:T(8,128)S(1)}, f32[128,128]{1,0:T(8,128)S(1)}, u32[]{:S(2)}, u32[]{:S(2)}) collective-permute-start(f32[128,128]{1,0:T(8,128)S(1)} %get-tuple-element.108), channel_id=1, source_target_pairs={{0,2},{1,3},{2,0},{3,1},{4,6},{5,7},{6,4},{7,5},{8,10},{9,11},{10,... | collective-permute-start | bytes 196616 | tf_op jit(solution)/shard_map/ppermute | solution.py:21
  113.4 2.3 %collective-permute-done.43.refs_2_ = f32[128,128]{1,0:T(8,128)S(1)} collective-permute-done((f32[128,128]{1,0:T(8,128)S(1)}, f32[128,128]{1,0:T(8,128)S(1)}, u32[]{:S(2)}, u32[]{:S(2)}) %collective-permute-start.43) | collective-permute-done | bytes 65568 | tf_op jit(solution)/shard_map/ppermute | solution.py:21
  117.7 10.2 %all_to_all.11.sums_ref = f32[32,2,128]{2,1,0:T(2,128)S(1)} all-to-all(f32[32,2,128]{2,1,0:T(2,128)S(1)} %shard_map.103), channel_id=1, replica_groups=mesh['samp'=4,'chrom'=8] {'samp','chrom'}, dimensions={0} | all-to-all | bytes 65536 | tf_op jit(solution)/shard_map/all_to_all | solution.py:451
  132.6 2.5 %collective-permute-start.50 = (f32[128,128]{1,0:T(8,128)S(1)}, f32[128,128]{1,0:T(8,128)S(1)}, u32[]{:S(2)}, u32[]{:S(2)}) collective-permute-start(f32[128,128]{1,0:T(8,128)S(1)} %get-tuple-element.115), channel_id=1, source_target_pairs={{0,2},{1,3},{2,0},{3,1},{4,6},{5,7},{6,4},{7,5},{8,10},{9,11},{10,... | collective-permute-start | bytes 196616 | tf_op jit(solution)/shard_map/ppermute | solution.py:21
  135.1 2.5 %shard_map.108 = (f32[1024,128]{1,0:T(8,128)S(1)}, f32[1024,128]{1,0:T(8,128)S(1)}) custom-call(f32[1024,128]{1,0:T(8,128)S(1)} %get-tuple-element.116.coef_ref, s32[8,128]{1,0:T(8,128)S(1)} %bitcast.6, bf16[512,1024]{1,0:T(8,128)(2,1)S(1)} %get-tuple-element.66.refs_8_.refs_1_.high_ref.refs_0_, ...), custom_call_target="tpu_custom_call" | custom-call | flops 2147483648 | bytes 8388608 | tf_op jit(solution)/shard_map/pallas_call | solution.py:462
  145.3 2.2 %collective-permute-done.53.refs_3_ = f32[128,128]{1,0:T(8,128)S(1)} collective-permute-done((f32[128,128]{1,0:T(8,128)S(1)}, f32[128,128]{1,0:T(8,128)S(1)}, u32[]{:S(2)}, u32[]{:S(2)}) %collective-permute-start.53) | collective-permute-done | bytes 65568 | tf_op jit(solution)/shard_map/ppermute | solution.py:21
  151.0 2.2 %collective-permute-start.60 = (f32[272,128]{1,0:T(8,128)S(1)}, f32[272,128]{1,0:T(8,128)S(1)}, u32[]{:S(2)}, u32[]{:S(2)}) collective-permute-start(f32[272,128]{1,0:T(8,128)S(1)} %get-tuple-element.124), channel_id=1, source_target_pairs={{0,24},{8,16},{16,8},{24,0},{1,25},{9,17},{17,9},{25,1},{2,26},{10... | collective-permute-start | bytes 417800 | tf_op jit(solution)/shard_map/ppermute | solution.py:21
  154.2 2.0 %collective-permute-done.58.refs_1_ = f32[272,128]{1,0:T(8,128)S(1)} collective-permute-done((f32[272,128]{1,0:T(8,128)S(1)}, f32[272,128]{1,0:T(8,128)S(1)}, u32[]{:S(2)}, u32[]{:S(2)}) %collective-permute-start.58) | collective-permute-done | bytes 139296 | tf_op jit(solution)/shard_map/ppermute | solution.py:21
  156.2 2.5 %collective-permute-done.59.refs_2_ = f32[272,128]{1,0:T(8,128)S(1)} collective-permute-done((f32[272,128]{1,0:T(8,128)S(1)}, f32[272,128]{1,0:T(8,128)S(1)}, u32[]{:S(2)}, u32[]{:S(2)}) %collective-permute-start.59) | collective-permute-done | bytes 139296 | tf_op jit(solution)/shard_map/ppermute | solution.py:21
  162.6 2.5 %collective-permute-done.61.refs_1_ = f32[256,128]{1,0:T(8,128)S(1)} collective-permute-done((f32[256,128]{1,0:T(8,128)S(1)}, f32[256,128]{1,0:T(8,128)S(1)}, u32[]{:S(2)}, u32[]{:S(2)}) %collective-permute-start.61) | collective-permute-done | bytes 131104 | tf_op jit(solution)/shard_map/ppermute | solution.py:21
  165.1 2.7 %collective-permute-done.62.refs_2_ = f32[256,128]{1,0:T(8,128)S(1)} collective-permute-done((f32[256,128]{1,0:T(8,128)S(1)}, f32[256,128]{1,0:T(8,128)S(1)}, u32[]{:S(2)}, u32[]{:S(2)}) %collective-permute-start.62) | collective-permute-done | bytes 131104 | tf_op jit(solution)/shard_map/ppermute | solution.py:21
  (145 shorter events, 70.3 us)
Async XLA Ops:
  5.2 7.6 %collective-permute-start.2 = (f32[128,128]{1,0:T(8,128)S(1)}, f32[128,128]{1,0:T(8,128)S(1)}, u32[]{:S(2)}, u32[]{:S(2)}) collective-permute-start(f32[128,128]{1,0:T(8,128)S(1)} %get-tuple-element.72), channel_id=1, source_target_pairs={{0,6},{1,7},{2,4},{3,5},{4,2},{5,3},{6,0},{7,1},{8,14},{9,15},{10,... | collective-permute-start | bytes 196616 | tf_op jit(solution)/shard_map/ppermute | solution.py:21
  18.7 6.5 %collective-permute-start.7 = (f32[128,128]{1,0:T(8,128)S(1)}, f32[128,128]{1,0:T(8,128)S(1)}, u32[]{:S(2)}, u32[]{:S(2)}) collective-permute-start(f32[128,128]{1,0:T(8,128)S(1)} %shard_map.81.refs_7_), channel_id=1, source_target_pairs={{0,4},{1,5},{2,6},{3,7},{4,0},{5,1},{6,2},{7,3},{8,12},{9,13},{10,... | collective-permute-start | bytes 196616 | tf_op jit(solution)/shard_map/ppermute | solution.py:21
  18.7 6.5 %collective-permute-start.10 = (f32[128,128]{1,0:T(8,128)S(1)}, f32[128,128]{1,0:T(8,128)S(1)}, u32[]{:S(2)}, u32[]{:S(2)}) collective-permute-start(f32[128,128]{1,0:T(8,128)S(1)} %shard_map.81.refs_7_), channel_id=1, source_target_pairs={{0,2},{1,3},{2,0},{3,1},{4,6},{5,7},{6,4},{7,5},{8,10},{9,11},{10,... | collective-permute-start | bytes 196616 | tf_op jit(solution)/shard_map/ppermute | solution.py:21
  29.2 8.1 %collective-permute-start.13 = (f32[256,128]{1,0:T(8,128)S(1)}, f32[256,128]{1,0:T(8,128)S(1)}, u32[]{:S(2)}, u32[]{:S(2)}) collective-permute-start(f32[256,128]{1,0:T(8,128)S(1)} %get-tuple-element.79), channel_id=1, source_target_pairs={{0,16},{8,24},{16,0},{24,8},{1,17},{9,25},{17,1},{25,9},{2,18},{10... | collective-permute-start | bytes 393224 | tf_op jit(solution)/shard_map/ppermute | solution.py:21
  30.7 6.6 %collective-permute-start.14 = (f32[256,128]{1,0:T(8,128)S(1)}, f32[256,128]{1,0:T(8,128)S(1)}, u32[]{:S(2)}, u32[]{:S(2)}) collective-permute-start(f32[256,128]{1,0:T(8,128)S(1)} %get-tuple-element.80), channel_id=1, source_target_pairs={{0,24},{8,16},{16,8},{24,0},{1,25},{9,17},{17,9},{25,1},{2,26},{10... | collective-permute-start | bytes 393224 | tf_op jit(solution)/shard_map/ppermute | solution.py:21
  38.6 7.3 %collective-permute-start.16 = (f32[256,128]{1,0:T(8,128)S(1)}, f32[256,128]{1,0:T(8,128)S(1)}, u32[]{:S(2)}, u32[]{:S(2)}) collective-permute-start(f32[256,128]{1,0:T(8,128)S(1)} %shard_map.84.refs_0_), channel_id=1, source_target_pairs={{0,16},{8,24},{16,0},{24,8},{1,17},{9,25},{17,1},{25,9},{2,18},{10... | collective-permute-start | bytes 393224 | tf_op jit(solution)/shard_map/ppermute | solution.py:21
  39.4 6.4 %collective-permute-start.17 = (f32[256,128]{1,0:T(8,128)S(1)}, f32[256,128]{1,0:T(8,128)S(1)}, u32[]{:S(2)}, u32[]{:S(2)}) collective-permute-start(f32[256,128]{1,0:T(8,128)S(1)} %shard_map.84.refs_0_), channel_id=1, source_target_pairs={{0,24},{8,16},{16,8},{24,0},{1,25},{9,17},{17,9},{25,1},{2,26},{10... | collective-permute-start | bytes 393224 | tf_op jit(solution)/shard_map/ppermute | solution.py:21
  48.1 6.8 %collective-permute-start.20 = (f32[128,128]{1,0:T(8,128)S(1)}, f32[128,128]{1,0:T(8,128)S(1)}, u32[]{:S(2)}, u32[]{:S(2)}) collective-permute-start(f32[128,128]{1,0:T(8,128)S(1)} %get-tuple-element.86), channel_id=1, source_target_pairs={{0,6},{1,7},{2,4},{3,5},{4,2},{5,3},{6,0},{7,1},{8,14},{9,15},{10,... | collective-permute-start | bytes 196616 | tf_op jit(solution)/shard_map/ppermute | solution.py:21
  50.0 7.0 %collective-permute-start.21 = (f32[128,128]{1,0:T(8,128)S(1)}, f32[128,128]{1,0:T(8,128)S(1)}, u32[]{:S(2)}, u32[]{:S(2)}) collective-permute-start(f32[128,128]{1,0:T(8,128)S(1)} %get-tuple-element.87), channel_id=1, source_target_pairs={{0,4},{1,5},{2,6},{3,7},{4,0},{5,1},{6,2},{7,3},{8,12},{9,13},{10,... | collective-permute-start | bytes 196616 | tf_op jit(solution)/shard_map/ppermute | solution.py:21
  50.0 6.9 %collective-permute-start.22 = (f32[128,128]{1,0:T(8,128)S(1)}, f32[128,128]{1,0:T(8,128)S(1)}, u32[]{:S(2)}, u32[]{:S(2)}) collective-permute-start(f32[128,128]{1,0:T(8,128)S(1)} %get-tuple-element.88), channel_id=1, source_target_pairs={{0,2},{1,3},{2,0},{3,1},{4,6},{5,7},{6,4},{7,5},{8,10},{9,11},{10,... | collective-permute-start | bytes 196616 | tf_op jit(solution)/shard_map/ppermute | solution.py:21
  69.9 6.9 %collective-permute-start.25 = (f32[128,128]{1,0:T(8,128)S(1)}, f32[128,128]{1,0:T(8,128)S(1)}, u32[]{:S(2)}, u32[]{:S(2)}) collective-permute-start(f32[128,128]{1,0:T(8,128)S(1)} %get-tuple-element.94), channel_id=1, source_target_pairs={{0,6},{1,7},{2,4},{3,5},{4,2},{5,3},{6,0},{7,1},{8,14},{9,15},{10,... | collective-permute-start | bytes 196616 | tf_op jit(solution)/shard_map/ppermute | solution.py:21
  70.5 7.9 %collective-permute-start.26 = (f32[128,128]{1,0:T(8,128)S(1)}, f32[128,128]{1,0:T(8,128)S(1)}, u32[]{:S(2)}, u32[]{:S(2)}) collective-permute-start(f32[128,128]{1,0:T(8,128)S(1)} %get-tuple-element.95), channel_id=1, source_target_pairs={{0,4},{1,5},{2,6},{3,7},{4,0},{5,1},{6,2},{7,3},{8,12},{9,13},{10,... | collective-permute-start | bytes 196616 | tf_op jit(solution)/shard_map/ppermute | solution.py:21
  79.9 6.9 %collective-permute-start.30 = (f32[128,128]{1,0:T(8,128)S(1)}, f32[128,128]{1,0:T(8,128)S(1)}, u32[]{:S(2)}, u32[]{:S(2)}) collective-permute-start(f32[128,128]{1,0:T(8,128)S(1)} %shard_map.95.refs_7_), channel_id=1, source_target_pairs={{0,4},{1,5},{2,6},{3,7},{4,0},{5,1},{6,2},{7,3},{8,12},{9,13},{10,... | collective-permute-start | bytes 196616 | tf_op jit(solution)/shard_map/ppermute | solution.py:21
  80.2 6.6 %collective-permute-start.32 = (f32[128,128]{1,0:T(8,128)S(1)}, f32[128,128]{1,0:T(8,128)S(1)}, u32[]{:S(2)}, u32[]{:S(2)}) collective-permute-start(f32[128,128]{1,0:T(8,128)S(1)} %shard_map.95.refs_7_), channel_id=1, source_target_pairs={{0,3},{1,2},{2,1},{3,0},{4,7},{5,6},{6,5},{7,4},{8,11},{9,10},{10,... | collective-permute-start | bytes 196616 | tf_op jit(solution)/shard_map/ppermute | solution.py:21
  81.4 6.7 %collective-permute-start.33 = (f32[128,128]{1,0:T(8,128)S(1)}, f32[128,128]{1,0:T(8,128)S(1)}, u32[]{:S(2)}, u32[]{:S(2)}) collective-permute-start(f32[128,128]{1,0:T(8,128)S(1)} %shard_map.95.refs_7_), channel_id=1, source_target_pairs={{0,2},{1,3},{2,0},{3,1},{4,6},{5,7},{6,4},{7,5},{8,10},{9,11},{10,... | collective-permute-start | bytes 196616 | tf_op jit(solution)/shard_map/ppermute | solution.py:21
  89.9 8.1 %collective-permute-start.36 = (f32[256,128]{1,0:T(8,128)S(1)}, f32[256,128]{1,0:T(8,128)S(1)}, u32[]{:S(2)}, u32[]{:S(2)}) collective-permute-start(f32[256,128]{1,0:T(8,128)S(1)} %get-tuple-element.99), channel_id=1, source_target_pairs={{0,16},{8,24},{16,0},{24,8},{1,17},{9,25},{17,1},{25,9},{2,18},{10... | collective-permute-start | bytes 393224 | tf_op jit(solution)/shard_map/ppermute | solution.py:21
  90.5 7.4 %collective-permute-start.37 = (f32[256,128]{1,0:T(8,128)S(1)}, f32[256,128]{1,0:T(8,128)S(1)}, u32[]{:S(2)}, u32[]{:S(2)}) collective-permute-start(f32[256,128]{1,0:T(8,128)S(1)} %get-tuple-element.100), channel_id=1, source_target_pairs={{0,24},{8,16},{16,8},{24,0},{1,25},{9,17},{17,9},{25,1},{2,26},{10... | collective-permute-start | bytes 393224 | tf_op jit(solution)/shard_map/ppermute | solution.py:21
  99.4 7.1 %collective-permute-start.39 = (f32[256,128]{1,0:T(8,128)S(1)}, f32[256,128]{1,0:T(8,128)S(1)}, u32[]{:S(2)}, u32[]{:S(2)}) collective-permute-start(f32[256,128]{1,0:T(8,128)S(1)} %shard_map.98.refs_0_), channel_id=1, source_target_pairs={{0,16},{8,24},{16,0},{24,8},{1,17},{9,25},{17,1},{25,9},{2,18},{10... | collective-permute-start | bytes 393224 | tf_op jit(solution)/shard_map/ppermute | solution.py:21
  100.1 6.5 %collective-permute-start.40 = (f32[256,128]{1,0:T(8,128)S(1)}, f32[256,128]{1,0:T(8,128)S(1)}, u32[]{:S(2)}, u32[]{:S(2)}) collective-permute-start(f32[256,128]{1,0:T(8,128)S(1)} %shard_map.98.refs_0_), channel_id=1, source_target_pairs={{0,24},{8,16},{16,8},{24,0},{1,25},{9,17},{17,9},{25,1},{2,26},{10... | collective-permute-start | bytes 393224 | tf_op jit(solution)/shard_map/ppermute | solution.py:21
  108.8 6.8 %collective-permute-start.43 = (f32[128,128]{1,0:T(8,128)S(1)}, f32[128,128]{1,0:T(8,128)S(1)}, u32[]{:S(2)}, u32[]{:S(2)}) collective-permute-start(f32[128,128]{1,0:T(8,128)S(1)} %get-tuple-element.106), channel_id=1, source_target_pairs={{0,6},{1,7},{2,4},{3,5},{4,2},{5,3},{6,0},{7,1},{8,14},{9,15},{10,... | collective-permute-start | bytes 196616 | tf_op jit(solution)/shard_map/ppermute | solution.py:21
  110.9 6.8 %collective-permute-start.44 = (f32[128,128]{1,0:T(8,128)S(1)}, f32[128,128]{1,0:T(8,128)S(1)}, u32[]{:S(2)}, u32[]{:S(2)}) collective-permute-start(f32[128,128]{1,0:T(8,128)S(1)} %get-tuple-element.107), channel_id=1, source_target_pairs={{0,4},{1,5},{2,6},{3,7},{4,0},{5,1},{6,2},{7,3},{8,12},{9,13},{10,... | collective-permute-start | bytes 196616 | tf_op jit(solution)/shard_map/ppermute | solution.py:21
  110.9 6.7 %collective-permute-start.45 = (f32[128,128]{1,0:T(8,128)S(1)}, f32[128,128]{1,0:T(8,128)S(1)}, u32[]{:S(2)}, u32[]{:S(2)}) collective-permute-start(f32[128,128]{1,0:T(8,128)S(1)} %get-tuple-element.108), channel_id=1, source_target_pairs={{0,2},{1,3},{2,0},{3,1},{4,6},{5,7},{6,4},{7,5},{8,10},{9,11},{10,... | collective-permute-start | bytes 196616 | tf_op jit(solution)/shard_map/ppermute | solution.py:21
  130.6 7.1 %collective-permute-start.48 = (f32[128,128]{1,0:T(8,128)S(1)}, f32[128,128]{1,0:T(8,128)S(1)}, u32[]{:S(2)}, u32[]{:S(2)}) collective-permute-start(f32[128,128]{1,0:T(8,128)S(1)} %get-tuple-element.113), channel_id=1, source_target_pairs={{0,6},{1,7},{2,4},{3,5},{4,2},{5,3},{6,0},{7,1},{8,14},{9,15},{10,... | collective-permute-start | bytes 196616 | tf_op jit(solution)/shard_map/ppermute | solution.py:21
  131.2 7.9 %collective-permute-start.49 = (f32[128,128]{1,0:T(8,128)S(1)}, f32[128,128]{1,0:T(8,128)S(1)}, u32[]{:S(2)}, u32[]{:S(2)}) collective-permute-start(f32[128,128]{1,0:T(8,128)S(1)} %get-tuple-element.114), channel_id=1, source_target_pairs={{0,4},{1,5},{2,6},{3,7},{4,0},{5,1},{6,2},{7,3},{8,12},{9,13},{10,... | collective-permute-start | bytes 196616 | tf_op jit(solution)/shard_map/ppermute | solution.py:21
  140.6 6.9 %collective-permute-start.53 = (f32[128,128]{1,0:T(8,128)S(1)}, f32[128,128]{1,0:T(8,128)S(1)}, u32[]{:S(2)}, u32[]{:S(2)}) collective-permute-start(f32[128,128]{1,0:T(8,128)S(1)} %shard_map.109.refs_7_), channel_id=1, source_target_pairs={{0,4},{1,5},{2,6},{3,7},{4,0},{5,1},{6,2},{7,3},{8,12},{9,13},{10,... | collective-permute-start | bytes 196616 | tf_op jit(solution)/shard_map/ppermute | solution.py:21
  140.9 6.6 %collective-permute-start.55 = (f32[128,128]{1,0:T(8,128)S(1)}, f32[128,128]{1,0:T(8,128)S(1)}, u32[]{:S(2)}, u32[]{:S(2)}) collective-permute-start(f32[128,128]{1,0:T(8,128)S(1)} %shard_map.109.refs_7_), channel_id=1, source_target_pairs={{0,3},{1,2},{2,1},{3,0},{4,7},{5,6},{6,5},{7,4},{8,11},{9,10},{10,... | collective-permute-start | bytes 196616 | tf_op jit(solution)/shard_map/ppermute | solution.py:21
  142.0 6.7 %collective-permute-start.56 = (f32[128,128]{1,0:T(8,128)S(1)}, f32[128,128]{1,0:T(8,128)S(1)}, u32[]{:S(2)}, u32[]{:S(2)}) collective-permute-start(f32[128,128]{1,0:T(8,128)S(1)} %shard_map.109.refs_7_), channel_id=1, source_target_pairs={{0,2},{1,3},{2,0},{3,1},{4,6},{5,7},{6,4},{7,5},{8,10},{9,11},{10,... | collective-permute-start | bytes 196616 | tf_op jit(solution)/shard_map/ppermute | solution.py:21
  149.7 6.6 %collective-permute-start.58 = (f32[272,128]{1,0:T(8,128)S(1)}, f32[272,128]{1,0:T(8,128)S(1)}, u32[]{:S(2)}, u32[]{:S(2)}) collective-permute-start(f32[272,128]{1,0:T(8,128)S(1)} %get-tuple-element.122), channel_id=1, source_target_pairs={{0,8},{8,0},{16,24},{24,16},{1,9},{9,1},{17,25},{25,17},{2,10},{10... | collective-permute-start | bytes 417800 | tf_op jit(solution)/shard_map/ppermute | solution.py:21
  150.4 8.4 %collective-permute-start.59 = (f32[272,128]{1,0:T(8,128)S(1)}, f32[272,128]{1,0:T(8,128)S(1)}, u32[]{:S(2)}, u32[]{:S(2)}) collective-permute-start(f32[272,128]{1,0:T(8,128)S(1)} %get-tuple-element.123), channel_id=1, source_target_pairs={{0,16},{8,24},{16,0},{24,8},{1,17},{9,25},{17,1},{25,9},{2,18},{10... | collective-permute-start | bytes 417800 | tf_op jit(solution)/shard_map/ppermute | solution.py:21
  151.0 7.8 %collective-permute-start.60 = (f32[272,128]{1,0:T(8,128)S(1)}, f32[272,128]{1,0:T(8,128)S(1)}, u32[]{:S(2)}, u32[]{:S(2)}) collective-permute-start(f32[272,128]{1,0:T(8,128)S(1)} %get-tuple-element.124), channel_id=1, source_target_pairs={{0,24},{8,16},{16,8},{24,0},{1,25},{9,17},{17,9},{25,1},{2,26},{10... | collective-permute-start | bytes 417800 | tf_op jit(solution)/shard_map/ppermute | solution.py:21
  160.5 7.3 %collective-permute-start.62 = (f32[256,128]{1,0:T(8,128)S(1)}, f32[256,128]{1,0:T(8,128)S(1)}, u32[]{:S(2)}, u32[]{:S(2)}) collective-permute-start(f32[256,128]{1,0:T(8,128)S(1)} %shard_map.112.refs_0_), channel_id=1, source_target_pairs={{0,16},{8,24},{16,0},{24,8},{1,17},{9,25},{17,1},{25,9},{2,18},{10... | collective-permute-start | bytes 393224 | tf_op jit(solution)/shard_map/ppermute | solution.py:21
  161.2 6.6 %collective-permute-start.63 = (f32[256,128]{1,0:T(8,128)S(1)}, f32[256,128]{1,0:T(8,128)S(1)}, u32[]{:S(2)}, u32[]{:S(2)}) collective-permute-start(f32[256,128]{1,0:T(8,128)S(1)} %shard_map.112.refs_0_), channel_id=1, source_target_pairs={{0,24},{8,16},{16,8},{24,0},{1,25},{9,17},{17,9},{25,1},{2,26},{10... | collective-permute-start | bytes 393224 | tf_op jit(solution)/shard_map/ppermute | solution.py:21
  (37 other events, 196.8 us)

commit v9 on v8

--- a/solution.py
+++ b/solution.py
@@ -10,9 +10,8 @@
 
 GPD = 2
 ITERS = 2
-STATS = 16
+STATS = 8
 PARTS = 2
-GIVEN = 2
 VMEM_LIMIT = 10 * 1024 * 1024
 
 
@@ -143,10 +142,6 @@
     return jnp.concatenate([column(ref[k : k + 1]) for k in range(ref.shape[0])])
 
 
-def rest_kernel(high_ref, low_ref, packed_ref, *out_refs):
-    store_places(wide_dot(high_ref[...], low_ref[...], packed_ref[...]), out_refs)
-
-
 def residual_kernel(count, traits_ref, *refs):
     out = refs[-1]
     block = out.shape[0]
@@ -192,7 +187,7 @@
 def image_kernel(count, *refs):
     pieces = refs[:count]
     high_ref, low_ref = refs[count : count + 2]
-    grad_ref, packed_ref, *give_refs = refs[-2 - GIVEN :]
+    grad_ref, packed_ref, far_ref = refs[-3:]
     samp = lax.axis_index("samp")
     block = pieces[0].shape[0]
     for bits, piece in enumerate(pieces):
@@ -200,7 +195,7 @@
         value = piece[...]
         grad_ref[rows] = value
         packed_ref[rows] = pack(value)
-    rest_kernel(high_ref, low_ref, packed_ref, *give_refs)
+    far_kernel(high_ref, low_ref, packed_ref, far_ref)
 
 
 def norm_kernel(count, *refs):
@@ -216,7 +211,18 @@
         out[place] = sums
 
 
-def prox_kernel(total_rows, coef_ref, grad_ref, sums_ref, high_ref, low_ref, new_ref, packed_ref, *give_refs):
+def far_kernel(high_ref, low_ref, packed_ref, out_ref):
+    rows = pl.ds(high_ref.shape[0] - out_ref.shape[0] * out_ref.shape[1], out_ref.shape[0] * out_ref.shape[1])
+    store_places(wide_dot(high_ref[rows], low_ref[rows], packed_ref[...]), [out_ref])
+
+
+def near_kernel(high1_ref, low1_ref, high0_ref, low0_ref, packed_ref, near_ref, keep_ref):
+    rows = pl.ds(0, near_ref.shape[0] * near_ref.shape[1])
+    store_places(wide_dot(high1_ref[rows], low1_ref[rows], packed_ref[...]), [near_ref])
+    store_places(wide_dot(high0_ref[...], low0_ref[...], packed_ref[...]), [keep_ref])
+
+
+def prox_kernel(total_rows, coef_ref, grad_ref, sums_ref, high_ref, low_ref, new_ref, packed_ref, far_ref):
     sums = sums_ref[0]
     for place in range(1, sums_ref.shape[0]):
         sums = sums + sums_ref[place]
@@ -230,7 +236,7 @@
     new = moved * (jnp.maximum(length - cut, 0.0) / jnp.maximum(length, cut))
     new_ref[...] = new
     packed_ref[...] = pack(new)
-    rest_kernel(high_ref, low_ref, packed_ref, *give_refs)
+    far_kernel(high_ref, low_ref, packed_ref, far_ref)
 
 
 def own_kernel(coef_ref, group_ref, *refs):
@@ -254,9 +260,8 @@
     for which in range(1, GPD):
         chosen = jnp.where(local == which, products[which * traits : (which + 1) * traits], chosen)
     out[0:width] = chosen.T
-    out[width : width + 8] = sums_ref[...]
-    out[width + 8 : width + STATS] = jnp.zeros((STATS - 8, traits), jnp.float32)
-    out[width + 8 : width + 8 + square_ref.shape[1]] = square_ref[partner]
+    out[width : width + STATS] = sums_ref[...]
+    out[width + GPD : width + GPD + square_ref.shape[1]] = square_ref[partner]
 
 
 def loco_kernel(count, partners, *refs):
@@ -301,7 +306,7 @@
     loco_sq = jnp.broadcast_to(total[cols : cols + 1], (cols, traits))
     for which in range(1, GPD):
         loco_sq = jnp.where(local == which, total[cols + which : cols + which + 1], loco_sq)
-    tested_sq = columns(total[cols + 8 : cols + 8 + cols // 128])
+    tested_sq = columns(total[cols + GPD : cols + GPD + cols // 128])
     denom = math.sqrt(total_rows) * jnp.sqrt((tested_sq / total_rows + 1e-06) * (loco_sq / total_rows + 1e-06))
     out[...] = total[:cols] / denom
 
@@ -373,7 +378,7 @@
     flops = 4 * rows * cols * n_traits
     moved = 2 * rows * cols
     order = samp_order(n_samp)
-    far, near = order[:-1], order[-1:]
+    others, own = order[:-1], order[-1:]
 
     part = shape((rows // 2, cols), jnp.bfloat16)
     half_out = shape((half, block, n_traits))
@@ -387,8 +392,10 @@
     group_rows = groups.reshape(cols // 128, 128)
     owner_rows = owners.reshape(n_samp, 1, test_width)
 
-    def rest(high, low, packed):
-        return call(rest_kernel, half_out, [whole()] * 3, (), flops, moved)(high, low, packed)
+    def near(packed):
+        return call(near_kernel, [give_outs[0], half_out], [whole()] * 5, (), 2 * flops, 2 * moved)(
+            high1, low1, high0, low0, packed
+        )
 
     def own_residual(summands, after=()):
         return call(
@@ -416,18 +423,17 @@
     tested_sq = call(square_kernel, shape((n_samp, test_width // 128, 128)), [whole()], (), 0, 2 * rows * tests)(tested)
 
     for iteration in range(ITERS):
-        own = own_residual(summands)
-        pieces = chrom_gather(own)
+        pieces = chrom_gather(own_residual(summands))
         packed, *far_out = call(
-            functools.partial(grad_far_kernel, n_chrom, far),
-            [packed_rows] + [grad_block] * len(far),
+            functools.partial(grad_far_kernel, n_chrom, others),
+            [packed_rows] + [grad_block] * len(others),
             [whole()] * (n_chrom + 4),
             rows_buffer,
             flops,
             moved,
         )(*pieces, *parts)
         near_out = call(
-            functools.partial(grad_near_kernel, near), [grad_block] * len(near), [whole()] * 5, (), flops, moved
+            functools.partial(grad_near_kernel, own), [grad_block] * len(own), [whole()] * 5, (), flops, moved
         )(packed, *parts)
         received = [swap(piece, "samp", partner) for partner, piece in zip(order, far_out)]
         own_grad = call(functools.partial(mean_kernel, total_rows), grad_block, [whole()] * n_samp)(
@@ -435,46 +441,48 @@
         )
         pieces = samp_gather(own_grad)
         after = (tested_sq,) if iteration == 0 else ()
-        gradient, packed, *gives = call(
+        gradient, packed, far_give = call(
             functools.partial(image_kernel, n_samp),
-            [coef_out, packed_cols] + give_outs,
+            [coef_out, packed_cols, give_outs[1]],
             [whole()] * (n_samp + 2) + [anywhere()] * len(after),
             (),
             flops,
             moved,
         )(*pieces, high1, low1, *after)
-        summands = chrom_scatter(gives, rest(high0, low0, packed))
+        near_give, keep = near(packed)
+        summands = chrom_scatter([near_give, far_give], keep)
         size = n_samp * n_chrom
         sums = call(
             functools.partial(norm_kernel, half), shape((size, 2, n_traits)), [whole()] * (half + 1)
         )(own_grad, *summands)
         sums = lax.all_to_all(sums, ("samp", "chrom"), 0, 0)
-        coefficients, packed, *gives = call(
+        coefficients, packed, far_give = call(
             functools.partial(prox_kernel, total_rows),
-            [coef_out, packed_cols] + give_outs,
+            [coef_out, packed_cols, give_outs[1]],
             [whole()] * 5,
             (),
             flops,
             moved,
         )(coefficients, gradient, sums, high1, low1)
-        summands = chrom_scatter(gives, rest(high0, low0, packed))
+        near_give, keep = near(packed)
+        summands = chrom_scatter([near_give, far_give], keep)
 
     own_parts = call(own_kernel, [shape((rows, n_traits))] * GPD, [whole()] * 6, (), 4 * flops, 4 * moved)(
         coefficients, group_rows, *parts
     )
     pieces = chrom_gather(own_residual(summands, own_parts))
     loco, loco_sq, *far_out = call(
-        functools.partial(loco_kernel, n_chrom, far),
-        [shape((GPD * n_traits, rows), jnp.bfloat16), shape((8, n_traits))]
-        + [score_block] * len(far),
+        functools.partial(loco_kernel, n_chrom, others),
+        [shape((GPD * n_traits, rows), jnp.bfloat16), shape((STATS, n_traits))]
+        + [score_block] * len(others),
         [whole()] * (n_chrom + GPD + 3),
         [pltpu.VMEM((rows, GPD * n_traits), jnp.bfloat16)],
         flops,
         moved,
     )(*pieces, *own_parts, tested, tested_sq, owner_rows)
     residual, *near_out = call(
-        functools.partial(loco_near_kernel, n_chrom, near),
-        [shape((rows, n_traits))] + [score_block] * len(near),
+        functools.partial(loco_near_kernel, n_chrom, own),
+        [shape((rows, n_traits))] + [score_block] * len(own),
         [whole()] * (n_chrom + 5),
         (),
         flops // 2,

time: 169 us -> 168 us (level)
  transfers between devices with their start and end apart: 64 -> 64, of which waited for: 35 -> 31; matrix products, arithmetic and copies ran while one was open for 0% -> 0% of each run, Pallas kernels for 5% -> 6%
where the time goes in v9:
time: 168 us
  waiting for transfers between devices  64.5 us (38%)
  starting transfers between devices  62.2 us (37%)
  Pallas kernels  20.2 us (12%)
  blocking collectives  20.2 us (12%)
    ppermute x64, waiting for transfers between devices, swap(): return lax.ppermute(value, axis, [(i, i ^ bits) for i in range(size)])  64.5 us
    ppermute x64, starting transfers between devices, swap(): return lax.ppermute(value, axis, [(i, i ^ bits) for i in range(size)])  62.2 us
    all_to_all x2, blocking collectives, body(): sums = lax.all_to_all(sums, ('samp', 'chrom'), 0, 0)  20.2 us
    pallas_call x4, Pallas kernels, near(): call(near_kernel, [give_outs[0], half_out], [whole()] * 5, (), 2 * flops,...  3.94 us
  transfers between devices with their start and end apart: 64, of which 31 were waited for; matrix products, arithmetic and copies ran while one was open for 0% of the time, Pallas kernels for 6%

profile of v9, /device:TPU:0, one launch (start us, length us, event | category | flops | bytes accessed | tf_op | source)
XLA Modules:
  0.0 168.2 jit_solution(8103134107185922894)
XLA Ops:
  0.6 3.0 %shard_map.77 = (bf16[512,1024]{1,0:T(8,128)(2,1)S(1)}, bf16[512,1024]{1,0:T(8,128)(2,1)S(1)}, f32[2,128,128]{2,1,0:T(8,128)S(1)}, f32[2,128,128]{2,1,0:T(8,128)...) custom-call(f32[4,2,128,1024]{3,2,1,0:T(8,128)} %bitcast.7, f32[1024,128]{1,0:T(8,128)} %coef_ref.3), custom_call_target="tpu_custom_call" | custom-call | flops 536870912 | bytes 8388608 | tf_op jit(solution)/shard_map/pallas_call | solution.py:409
  5.2 5.1 %collective-permute-start.2 = (f32[128,128]{1,0:T(8,128)S(1)}, f32[128,128]{1,0:T(8,128)S(1)}, u32[]{:S(2)}, u32[]{:S(2)}) collective-permute-start(f32[128,128]{1,0:T(8,128)S(1)} %get-tuple-element.78), channel_id=1, source_target_pairs={{0,6},{1,7},{2,4},{3,5},{4,2},{5,3},{6,0},{7,1},{8,14},{9,15},{10,... | collective-permute-start | bytes 196616 | tf_op jit(solution)/shard_map/ppermute | solution.py:20
  12.8 3.3 %collective-permute-done.3.refs_2_ = f32[128,128]{1,0:T(8,128)S(1)} collective-permute-done((f32[128,128]{1,0:T(8,128)S(1)}, f32[128,128]{1,0:T(8,128)S(1)}, u32[]{:S(2)}, u32[]{:S(2)}) %collective-permute-start.3) | collective-permute-done | bytes 65568 | tf_op jit(solution)/shard_map/ppermute | solution.py:20
  16.1 2.6 %collective-permute-start.5 = (f32[128,128]{1,0:T(8,128)S(1)}, f32[128,128]{1,0:T(8,128)S(1)}, u32[]{:S(2)}, u32[]{:S(2)}) collective-permute-start(f32[128,128]{1,0:T(8,128)S(1)} %shard_map.81.refs_7_), channel_id=1, source_target_pairs={{0,6},{1,7},{2,4},{3,5},{4,2},{5,3},{6,0},{7,1},{8,14},{9,15},{10,... | collective-permute-start | bytes 196616 | tf_op jit(solution)/shard_map/ppermute | solution.py:20
  22.5 2.8 %collective-permute-done.7.refs_3_ = f32[128,128]{1,0:T(8,128)S(1)} collective-permute-done((f32[128,128]{1,0:T(8,128)S(1)}, f32[128,128]{1,0:T(8,128)S(1)}, u32[]{:S(2)}, u32[]{:S(2)}) %collective-permute-start.7) | collective-permute-done | bytes 65568 | tf_op jit(solution)/shard_map/ppermute | solution.py:20
  31.7 1.9 %collective-permute-done.12.refs_1_ = f32[256,128]{1,0:T(8,128)S(1)} collective-permute-done((f32[256,128]{1,0:T(8,128)S(1)}, f32[256,128]{1,0:T(8,128)S(1)}, u32[]{:S(2)}, u32[]{:S(2)}) %collective-permute-start.12) | collective-permute-done | bytes 131104 | tf_op jit(solution)/shard_map/ppermute | solution.py:20
  33.6 3.7 %collective-permute-done.13.refs_2_ = f32[256,128]{1,0:T(8,128)S(1)} collective-permute-done((f32[256,128]{1,0:T(8,128)S(1)}, f32[256,128]{1,0:T(8,128)S(1)}, u32[]{:S(2)}, u32[]{:S(2)}) %collective-permute-start.13) | collective-permute-done | bytes 131104 | tf_op jit(solution)/shard_map/ppermute | solution.py:20
  40.9 2.4 %collective-permute-done.15.refs_1_ = f32[256,128]{1,0:T(8,128)S(1)} collective-permute-done((f32[256,128]{1,0:T(8,128)S(1)}, f32[256,128]{1,0:T(8,128)S(1)}, u32[]{:S(2)}, u32[]{:S(2)}) %collective-permute-start.15) | collective-permute-done | bytes 131104 | tf_op jit(solution)/shard_map/ppermute | solution.py:20
  43.3 2.5 %collective-permute-done.16.refs_2_ = f32[256,128]{1,0:T(8,128)S(1)} collective-permute-done((f32[256,128]{1,0:T(8,128)S(1)}, f32[256,128]{1,0:T(8,128)S(1)}, u32[]{:S(2)}, u32[]{:S(2)}) %collective-permute-start.16) | collective-permute-done | bytes 131104 | tf_op jit(solution)/shard_map/ppermute | solution.py:20
  48.1 1.9 %collective-permute-start.20 = (f32[128,128]{1,0:T(8,128)S(1)}, f32[128,128]{1,0:T(8,128)S(1)}, u32[]{:S(2)}, u32[]{:S(2)}) collective-permute-start(f32[128,128]{1,0:T(8,128)S(1)} %get-tuple-element.91), channel_id=1, source_target_pairs={{0,6},{1,7},{2,4},{3,5},{4,2},{5,3},{6,0},{7,1},{8,14},{9,15},{10,... | collective-permute-start | bytes 196616 | tf_op jit(solution)/shard_map/ppermute | solution.py:20
  49.9 2.7 %collective-permute-start.22 = (f32[128,128]{1,0:T(8,128)S(1)}, f32[128,128]{1,0:T(8,128)S(1)}, u32[]{:S(2)}, u32[]{:S(2)}) collective-permute-start(f32[128,128]{1,0:T(8,128)S(1)} %get-tuple-element.93), channel_id=1, source_target_pairs={{0,2},{1,3},{2,0},{3,1},{4,6},{5,7},{6,4},{7,5},{8,10},{9,11},{10,... | collective-permute-start | bytes 196616 | tf_op jit(solution)/shard_map/ppermute | solution.py:20
  52.6 2.3 %collective-permute-done.20.refs_2_ = f32[128,128]{1,0:T(8,128)S(1)} collective-permute-done((f32[128,128]{1,0:T(8,128)S(1)}, f32[128,128]{1,0:T(8,128)S(1)}, u32[]{:S(2)}, u32[]{:S(2)}) %collective-permute-start.20) | collective-permute-done | bytes 65568 | tf_op jit(solution)/shard_map/ppermute | solution.py:20
  56.8 10.2 %all_to_all.10.sums_ref = f32[32,2,128]{2,1,0:T(2,128)S(1)} all-to-all(f32[32,2,128]{2,1,0:T(2,128)S(1)} %shard_map.90), channel_id=1, replica_groups=mesh['samp'=4,'chrom'=8] {'samp','chrom'}, dimensions={0} | all-to-all | bytes 65536 | tf_op jit(solution)/shard_map/all_to_all | solution.py:458
  71.8 2.5 %collective-permute-start.27 = (f32[128,128]{1,0:T(8,128)S(1)}, f32[128,128]{1,0:T(8,128)S(1)}, u32[]{:S(2)}, u32[]{:S(2)}) collective-permute-start(f32[128,128]{1,0:T(8,128)S(1)} %get-tuple-element.102), channel_id=1, source_target_pairs={{0,2},{1,3},{2,0},{3,1},{4,6},{5,7},{6,4},{7,5},{8,10},{9,11},{10,... | collective-permute-start | bytes 196616 | tf_op jit(solution)/shard_map/ppermute | solution.py:20
  74.3 2.3 %collective-permute-done.25.refs_1_ = f32[128,128]{1,0:T(8,128)S(1)} collective-permute-done((f32[128,128]{1,0:T(8,128)S(1)}, f32[128,128]{1,0:T(8,128)S(1)}, u32[]{:S(2)}, u32[]{:S(2)}) %collective-permute-start.25) | collective-permute-done | bytes 65568 | tf_op jit(solution)/shard_map/ppermute | solution.py:20
  84.5 2.2 %collective-permute-done.30.refs_3_ = f32[128,128]{1,0:T(8,128)S(1)} collective-permute-done((f32[128,128]{1,0:T(8,128)S(1)}, f32[128,128]{1,0:T(8,128)S(1)}, u32[]{:S(2)}, u32[]{:S(2)}) %collective-permute-start.30) | collective-permute-done | bytes 65568 | tf_op jit(solution)/shard_map/ppermute | solution.py:20
  90.4 2.2 %collective-permute-start.37 = (f32[256,128]{1,0:T(8,128)S(1)}, f32[256,128]{1,0:T(8,128)S(1)}, u32[]{:S(2)}, u32[]{:S(2)}) collective-permute-start(f32[256,128]{1,0:T(8,128)S(1)} %get-tuple-element.106), channel_id=1, source_target_pairs={{0,24},{8,16},{16,8},{24,0},{1,25},{9,17},{17,9},{25,1},{2,26},{10... | collective-permute-start | bytes 393224 | tf_op jit(solution)/shard_map/ppermute | solution.py:20
  93.1 2.3 %collective-permute-done.35.refs_1_ = f32[256,128]{1,0:T(8,128)S(1)} collective-permute-done((f32[256,128]{1,0:T(8,128)S(1)}, f32[256,128]{1,0:T(8,128)S(1)}, u32[]{:S(2)}, u32[]{:S(2)}) %collective-permute-start.35) | collective-permute-done | bytes 131104 | tf_op jit(solution)/shard_map/ppermute | solution.py:20
  95.5 2.4 %collective-permute-done.36.refs_2_ = f32[256,128]{1,0:T(8,128)S(1)} collective-permute-done((f32[256,128]{1,0:T(8,128)S(1)}, f32[256,128]{1,0:T(8,128)S(1)}, u32[]{:S(2)}, u32[]{:S(2)}) %collective-permute-start.36) | collective-permute-done | bytes 131104 | tf_op jit(solution)/shard_map/ppermute | solution.py:20
  101.4 2.4 %collective-permute-done.38.refs_1_ = f32[256,128]{1,0:T(8,128)S(1)} collective-permute-done((f32[256,128]{1,0:T(8,128)S(1)}, f32[256,128]{1,0:T(8,128)S(1)}, u32[]{:S(2)}, u32[]{:S(2)}) %collective-permute-start.38) | collective-permute-done | bytes 131104 | tf_op jit(solution)/shard_map/ppermute | solution.py:20
  103.8 2.7 %collective-permute-done.39.refs_2_ = f32[256,128]{1,0:T(8,128)S(1)} collective-permute-done((f32[256,128]{1,0:T(8,128)S(1)}, f32[256,128]{1,0:T(8,128)S(1)}, u32[]{:S(2)}, u32[]{:S(2)}) %collective-permute-start.39) | collective-permute-done | bytes 131104 | tf_op jit(solution)/shard_map/ppermute | solution.py:20
  110.6 2.7 %collective-permute-start.45 = (f32[128,128]{1,0:T(8,128)S(1)}, f32[128,128]{1,0:T(8,128)S(1)}, u32[]{:S(2)}, u32[]{:S(2)}) collective-permute-start(f32[128,128]{1,0:T(8,128)S(1)} %get-tuple-element.115), channel_id=1, source_target_pairs={{0,2},{1,3},{2,0},{3,1},{4,6},{5,7},{6,4},{7,5},{8,10},{9,11},{10,... | collective-permute-start | bytes 196616 | tf_op jit(solution)/shard_map/ppermute | solution.py:20
  113.3 2.3 %collective-permute-done.43.refs_2_ = f32[128,128]{1,0:T(8,128)S(1)} collective-permute-done((f32[128,128]{1,0:T(8,128)S(1)}, f32[128,128]{1,0:T(8,128)S(1)}, u32[]{:S(2)}, u32[]{:S(2)}) %collective-permute-start.43) | collective-permute-done | bytes 65568 | tf_op jit(solution)/shard_map/ppermute | solution.py:20
  117.5 10.0 %all_to_all.11.sums_ref = f32[32,2,128]{2,1,0:T(2,128)S(1)} all-to-all(f32[32,2,128]{2,1,0:T(2,128)S(1)} %shard_map.103), channel_id=1, replica_groups=mesh['samp'=4,'chrom'=8] {'samp','chrom'}, dimensions={0} | all-to-all | bytes 65536 | tf_op jit(solution)/shard_map/all_to_all | solution.py:458
  132.2 2.5 %collective-permute-start.50 = (f32[128,128]{1,0:T(8,128)S(1)}, f32[128,128]{1,0:T(8,128)S(1)}, u32[]{:S(2)}, u32[]{:S(2)}) collective-permute-start(f32[128,128]{1,0:T(8,128)S(1)} %get-tuple-element.123), channel_id=1, source_target_pairs={{0,2},{1,3},{2,0},{3,1},{4,6},{5,7},{6,4},{7,5},{8,10},{9,11},{10,... | collective-permute-start | bytes 196616 | tf_op jit(solution)/shard_map/ppermute | solution.py:20
  134.7 2.6 %shard_map.108 = (f32[1024,128]{1,0:T(8,128)S(1)}, f32[1024,128]{1,0:T(8,128)S(1)}) custom-call(f32[1024,128]{1,0:T(8,128)S(1)} %get-tuple-element.124.coef_ref, s32[8,128]{1,0:T(8,128)S(1)} %bitcast.6, bf16[512,1024]{1,0:T(8,128)(2,1)S(1)} %get-tuple-element.72.refs_8_.refs_1_.high0_ref.refs_0_, ...), custom_call_target="tpu_custom_call" | custom-call | flops 2147483648 | bytes 8388608 | tf_op jit(solution)/shard_map/pallas_call | solution.py:470
  145.0 2.1 %collective-permute-done.53.refs_3_ = f32[128,128]{1,0:T(8,128)S(1)} collective-permute-done((f32[128,128]{1,0:T(8,128)S(1)}, f32[128,128]{1,0:T(8,128)S(1)}, u32[]{:S(2)}, u32[]{:S(2)}) %collective-permute-start.53) | collective-permute-done | bytes 65568 | tf_op jit(solution)/shard_map/ppermute | solution.py:20
  150.6 2.2 %collective-permute-start.60 = (f32[264,128]{1,0:T(8,128)S(1)}, f32[264,128]{1,0:T(8,128)S(1)}, u32[]{:S(2)}, u32[]{:S(2)}) collective-permute-start(f32[264,128]{1,0:T(8,128)S(1)} %get-tuple-element.132), channel_id=1, source_target_pairs={{0,24},{8,16},{16,8},{24,0},{1,25},{9,17},{17,9},{25,1},{2,26},{10... | collective-permute-start | bytes 405512 | tf_op jit(solution)/shard_map/ppermute | solution.py:20
  153.8 1.9 %collective-permute-done.58.refs_1_ = f32[264,128]{1,0:T(8,128)S(1)} collective-permute-done((f32[264,128]{1,0:T(8,128)S(1)}, f32[264,128]{1,0:T(8,128)S(1)}, u32[]{:S(2)}, u32[]{:S(2)}) %collective-permute-start.58) | collective-permute-done | bytes 135200 | tf_op jit(solution)/shard_map/ppermute | solution.py:20
  155.8 2.5 %collective-permute-done.59.refs_2_ = f32[264,128]{1,0:T(8,128)S(1)} collective-permute-done((f32[264,128]{1,0:T(8,128)S(1)}, f32[264,128]{1,0:T(8,128)S(1)}, u32[]{:S(2)}, u32[]{:S(2)}) %collective-permute-start.59) | collective-permute-done | bytes 135200 | tf_op jit(solution)/shard_map/ppermute | solution.py:20
  162.1 2.4 %collective-permute-done.61.refs_1_ = f32[256,128]{1,0:T(8,128)S(1)} collective-permute-done((f32[256,128]{1,0:T(8,128)S(1)}, f32[256,128]{1,0:T(8,128)S(1)}, u32[]{:S(2)}, u32[]{:S(2)}) %collective-permute-start.61) | collective-permute-done | bytes 131104 | tf_op jit(solution)/shard_map/ppermute | solution.py:20
  164.5 2.8 %collective-permute-done.62.refs_2_ = f32[256,128]{1,0:T(8,128)S(1)} collective-permute-done((f32[256,128]{1,0:T(8,128)S(1)}, f32[256,128]{1,0:T(8,128)S(1)}, u32[]{:S(2)}, u32[]{:S(2)}) %collective-permute-start.62) | collective-permute-done | bytes 131104 | tf_op jit(solution)/shard_map/ppermute | solution.py:20
  (145 shorter events, 70.1 us)
Async XLA Ops:
  5.2 7.6 %collective-permute-start.2 = (f32[128,128]{1,0:T(8,128)S(1)}, f32[128,128]{1,0:T(8,128)S(1)}, u32[]{:S(2)}, u32[]{:S(2)}) collective-permute-start(f32[128,128]{1,0:T(8,128)S(1)} %get-tuple-element.78), channel_id=1, source_target_pairs={{0,6},{1,7},{2,4},{3,5},{4,2},{5,3},{6,0},{7,1},{8,14},{9,15},{10,... | collective-permute-start | bytes 196616 | tf_op jit(solution)/shard_map/ppermute | solution.py:20
  18.7 6.5 %collective-permute-start.7 = (f32[128,128]{1,0:T(8,128)S(1)}, f32[128,128]{1,0:T(8,128)S(1)}, u32[]{:S(2)}, u32[]{:S(2)}) collective-permute-start(f32[128,128]{1,0:T(8,128)S(1)} %shard_map.81.refs_7_), channel_id=1, source_target_pairs={{0,4},{1,5},{2,6},{3,7},{4,0},{5,1},{6,2},{7,3},{8,12},{9,13},{10,... | collective-permute-start | bytes 196616 | tf_op jit(solution)/shard_map/ppermute | solution.py:20
  18.7 6.5 %collective-permute-start.10 = (f32[128,128]{1,0:T(8,128)S(1)}, f32[128,128]{1,0:T(8,128)S(1)}, u32[]{:S(2)}, u32[]{:S(2)}) collective-permute-start(f32[128,128]{1,0:T(8,128)S(1)} %shard_map.81.refs_7_), channel_id=1, source_target_pairs={{0,2},{1,3},{2,0},{3,1},{4,6},{5,7},{6,4},{7,5},{8,10},{9,11},{10,... | collective-permute-start | bytes 196616 | tf_op jit(solution)/shard_map/ppermute | solution.py:20
  29.2 8.1 %collective-permute-start.13 = (f32[256,128]{1,0:T(8,128)S(1)}, f32[256,128]{1,0:T(8,128)S(1)}, u32[]{:S(2)}, u32[]{:S(2)}) collective-permute-start(f32[256,128]{1,0:T(8,128)S(1)} %get-tuple-element.83), channel_id=1, source_target_pairs={{0,16},{8,24},{16,0},{24,8},{1,17},{9,25},{17,1},{25,9},{2,18},{10... | collective-permute-start | bytes 393224 | tf_op jit(solution)/shard_map/ppermute | solution.py:20
  30.7 6.6 %collective-permute-start.14 = (f32[256,128]{1,0:T(8,128)S(1)}, f32[256,128]{1,0:T(8,128)S(1)}, u32[]{:S(2)}, u32[]{:S(2)}) collective-permute-start(f32[256,128]{1,0:T(8,128)S(1)} %get-tuple-element.84), channel_id=1, source_target_pairs={{0,24},{8,16},{16,8},{24,0},{1,25},{9,17},{17,9},{25,1},{2,26},{10... | collective-permute-start | bytes 393224 | tf_op jit(solution)/shard_map/ppermute | solution.py:20
  38.6 7.3 %collective-permute-start.16 = (f32[256,128]{1,0:T(8,128)S(1)}, f32[256,128]{1,0:T(8,128)S(1)}, u32[]{:S(2)}, u32[]{:S(2)}) collective-permute-start(f32[256,128]{1,0:T(8,128)S(1)} %shard_map.84.refs_0_), channel_id=1, source_target_pairs={{0,16},{8,24},{16,0},{24,8},{1,17},{9,25},{17,1},{25,9},{2,18},{10... | collective-permute-start | bytes 393224 | tf_op jit(solution)/shard_map/ppermute | solution.py:20
  39.4 6.4 %collective-permute-start.17 = (f32[256,128]{1,0:T(8,128)S(1)}, f32[256,128]{1,0:T(8,128)S(1)}, u32[]{:S(2)}, u32[]{:S(2)}) collective-permute-start(f32[256,128]{1,0:T(8,128)S(1)} %shard_map.84.refs_0_), channel_id=1, source_target_pairs={{0,24},{8,16},{16,8},{24,0},{1,25},{9,17},{17,9},{25,1},{2,26},{10... | collective-permute-start | bytes 393224 | tf_op jit(solution)/shard_map/ppermute | solution.py:20
  48.1 6.9 %collective-permute-start.20 = (f32[128,128]{1,0:T(8,128)S(1)}, f32[128,128]{1,0:T(8,128)S(1)}, u32[]{:S(2)}, u32[]{:S(2)}) collective-permute-start(f32[128,128]{1,0:T(8,128)S(1)} %get-tuple-element.91), channel_id=1, source_target_pairs={{0,6},{1,7},{2,4},{3,5},{4,2},{5,3},{6,0},{7,1},{8,14},{9,15},{10,... | collective-permute-start | bytes 196616 | tf_op jit(solution)/shard_map/ppermute | solution.py:20
  49.9 6.8 %collective-permute-start.21 = (f32[128,128]{1,0:T(8,128)S(1)}, f32[128,128]{1,0:T(8,128)S(1)}, u32[]{:S(2)}, u32[]{:S(2)}) collective-permute-start(f32[128,128]{1,0:T(8,128)S(1)} %get-tuple-element.92), channel_id=1, source_target_pairs={{0,4},{1,5},{2,6},{3,7},{4,0},{5,1},{6,2},{7,3},{8,12},{9,13},{10,... | collective-permute-start | bytes 196616 | tf_op jit(solution)/shard_map/ppermute | solution.py:20
  49.9 6.8 %collective-permute-start.22 = (f32[128,128]{1,0:T(8,128)S(1)}, f32[128,128]{1,0:T(8,128)S(1)}, u32[]{:S(2)}, u32[]{:S(2)}) collective-permute-start(f32[128,128]{1,0:T(8,128)S(1)} %get-tuple-element.93), channel_id=1, source_target_pairs={{0,2},{1,3},{2,0},{3,1},{4,6},{5,7},{6,4},{7,5},{8,10},{9,11},{10,... | collective-permute-start | bytes 196616 | tf_op jit(solution)/shard_map/ppermute | solution.py:20
  69.7 6.9 %collective-permute-start.25 = (f32[128,128]{1,0:T(8,128)S(1)}, f32[128,128]{1,0:T(8,128)S(1)}, u32[]{:S(2)}, u32[]{:S(2)}) collective-permute-start(f32[128,128]{1,0:T(8,128)S(1)} %get-tuple-element.100), channel_id=1, source_target_pairs={{0,6},{1,7},{2,4},{3,5},{4,2},{5,3},{6,0},{7,1},{8,14},{9,15},{10,... | collective-permute-start | bytes 196616 | tf_op jit(solution)/shard_map/ppermute | solution.py:20
  70.4 7.9 %collective-permute-start.26 = (f32[128,128]{1,0:T(8,128)S(1)}, f32[128,128]{1,0:T(8,128)S(1)}, u32[]{:S(2)}, u32[]{:S(2)}) collective-permute-start(f32[128,128]{1,0:T(8,128)S(1)} %get-tuple-element.101), channel_id=1, source_target_pairs={{0,4},{1,5},{2,6},{3,7},{4,0},{5,1},{6,2},{7,3},{8,12},{9,13},{10,... | collective-permute-start | bytes 196616 | tf_op jit(solution)/shard_map/ppermute | solution.py:20
  79.7 6.9 %collective-permute-start.30 = (f32[128,128]{1,0:T(8,128)S(1)}, f32[128,128]{1,0:T(8,128)S(1)}, u32[]{:S(2)}, u32[]{:S(2)}) collective-permute-start(f32[128,128]{1,0:T(8,128)S(1)} %shard_map.95.refs_7_), channel_id=1, source_target_pairs={{0,4},{1,5},{2,6},{3,7},{4,0},{5,1},{6,2},{7,3},{8,12},{9,13},{10,... | collective-permute-start | bytes 196616 | tf_op jit(solution)/shard_map/ppermute | solution.py:20
  80.1 6.6 %collective-permute-start.32 = (f32[128,128]{1,0:T(8,128)S(1)}, f32[128,128]{1,0:T(8,128)S(1)}, u32[]{:S(2)}, u32[]{:S(2)}) collective-permute-start(f32[128,128]{1,0:T(8,128)S(1)} %shard_map.95.refs_7_), channel_id=1, source_target_pairs={{0,3},{1,2},{2,1},{3,0},{4,7},{5,6},{6,5},{7,4},{8,11},{9,10},{10,... | collective-permute-start | bytes 196616 | tf_op jit(solution)/shard_map/ppermute | solution.py:20
  81.2 6.7 %collective-permute-start.33 = (f32[128,128]{1,0:T(8,128)S(1)}, f32[128,128]{1,0:T(8,128)S(1)}, u32[]{:S(2)}, u32[]{:S(2)}) collective-permute-start(f32[128,128]{1,0:T(8,128)S(1)} %shard_map.95.refs_7_), channel_id=1, source_target_pairs={{0,2},{1,3},{2,0},{3,1},{4,6},{5,7},{6,4},{7,5},{8,10},{9,11},{10,... | collective-permute-start | bytes 196616 | tf_op jit(solution)/shard_map/ppermute | solution.py:20
  89.8 8.0 %collective-permute-start.36 = (f32[256,128]{1,0:T(8,128)S(1)}, f32[256,128]{1,0:T(8,128)S(1)}, u32[]{:S(2)}, u32[]{:S(2)}) collective-permute-start(f32[256,128]{1,0:T(8,128)S(1)} %get-tuple-element.105), channel_id=1, source_target_pairs={{0,16},{8,24},{16,0},{24,8},{1,17},{9,25},{17,1},{25,9},{2,18},{10... | collective-permute-start | bytes 393224 | tf_op jit(solution)/shard_map/ppermute | solution.py:20
  90.4 7.4 %collective-permute-start.37 = (f32[256,128]{1,0:T(8,128)S(1)}, f32[256,128]{1,0:T(8,128)S(1)}, u32[]{:S(2)}, u32[]{:S(2)}) collective-permute-start(f32[256,128]{1,0:T(8,128)S(1)} %get-tuple-element.106), channel_id=1, source_target_pairs={{0,24},{8,16},{16,8},{24,0},{1,25},{9,17},{17,9},{25,1},{2,26},{10... | collective-permute-start | bytes 393224 | tf_op jit(solution)/shard_map/ppermute | solution.py:20
  99.3 7.2 %collective-permute-start.39 = (f32[256,128]{1,0:T(8,128)S(1)}, f32[256,128]{1,0:T(8,128)S(1)}, u32[]{:S(2)}, u32[]{:S(2)}) collective-permute-start(f32[256,128]{1,0:T(8,128)S(1)} %shard_map.98.refs_0_), channel_id=1, source_target_pairs={{0,16},{8,24},{16,0},{24,8},{1,17},{9,25},{17,1},{25,9},{2,18},{10... | collective-permute-start | bytes 393224 | tf_op jit(solution)/shard_map/ppermute | solution.py:20
  100.0 6.5 %collective-permute-start.40 = (f32[256,128]{1,0:T(8,128)S(1)}, f32[256,128]{1,0:T(8,128)S(1)}, u32[]{:S(2)}, u32[]{:S(2)}) collective-permute-start(f32[256,128]{1,0:T(8,128)S(1)} %shard_map.98.refs_0_), channel_id=1, source_target_pairs={{0,24},{8,16},{16,8},{24,0},{1,25},{9,17},{17,9},{25,1},{2,26},{10... | collective-permute-start | bytes 393224 | tf_op jit(solution)/shard_map/ppermute | solution.py:20
  108.8 6.9 %collective-permute-start.43 = (f32[128,128]{1,0:T(8,128)S(1)}, f32[128,128]{1,0:T(8,128)S(1)}, u32[]{:S(2)}, u32[]{:S(2)}) collective-permute-start(f32[128,128]{1,0:T(8,128)S(1)} %get-tuple-element.113), channel_id=1, source_target_pairs={{0,6},{1,7},{2,4},{3,5},{4,2},{5,3},{6,0},{7,1},{8,14},{9,15},{10,... | collective-permute-start | bytes 196616 | tf_op jit(solution)/shard_map/ppermute | solution.py:20
  110.6 6.9 %collective-permute-start.44 = (f32[128,128]{1,0:T(8,128)S(1)}, f32[128,128]{1,0:T(8,128)S(1)}, u32[]{:S(2)}, u32[]{:S(2)}) collective-permute-start(f32[128,128]{1,0:T(8,128)S(1)} %get-tuple-element.114), channel_id=1, source_target_pairs={{0,4},{1,5},{2,6},{3,7},{4,0},{5,1},{6,2},{7,3},{8,12},{9,13},{10,... | collective-permute-start | bytes 196616 | tf_op jit(solution)/shard_map/ppermute | solution.py:20
  110.6 6.8 %collective-permute-start.45 = (f32[128,128]{1,0:T(8,128)S(1)}, f32[128,128]{1,0:T(8,128)S(1)}, u32[]{:S(2)}, u32[]{:S(2)}) collective-permute-start(f32[128,128]{1,0:T(8,128)S(1)} %get-tuple-element.115), channel_id=1, source_target_pairs={{0,2},{1,3},{2,0},{3,1},{4,6},{5,7},{6,4},{7,5},{8,10},{9,11},{10,... | collective-permute-start | bytes 196616 | tf_op jit(solution)/shard_map/ppermute | solution.py:20
  130.2 7.1 %collective-permute-start.48 = (f32[128,128]{1,0:T(8,128)S(1)}, f32[128,128]{1,0:T(8,128)S(1)}, u32[]{:S(2)}, u32[]{:S(2)}) collective-permute-start(f32[128,128]{1,0:T(8,128)S(1)} %get-tuple-element.121), channel_id=1, source_target_pairs={{0,6},{1,7},{2,4},{3,5},{4,2},{5,3},{6,0},{7,1},{8,14},{9,15},{10,... | collective-permute-start | bytes 196616 | tf_op jit(solution)/shard_map/ppermute | solution.py:20
  130.8 7.9 %collective-permute-start.49 = (f32[128,128]{1,0:T(8,128)S(1)}, f32[128,128]{1,0:T(8,128)S(1)}, u32[]{:S(2)}, u32[]{:S(2)}) collective-permute-start(f32[128,128]{1,0:T(8,128)S(1)} %get-tuple-element.122), channel_id=1, source_target_pairs={{0,4},{1,5},{2,6},{3,7},{4,0},{5,1},{6,2},{7,3},{8,12},{9,13},{10,... | collective-permute-start | bytes 196616 | tf_op jit(solution)/shard_map/ppermute | solution.py:20
  140.2 6.9 %collective-permute-start.53 = (f32[128,128]{1,0:T(8,128)S(1)}, f32[128,128]{1,0:T(8,128)S(1)}, u32[]{:S(2)}, u32[]{:S(2)}) collective-permute-start(f32[128,128]{1,0:T(8,128)S(1)} %shard_map.109.refs_7_), channel_id=1, source_target_pairs={{0,4},{1,5},{2,6},{3,7},{4,0},{5,1},{6,2},{7,3},{8,12},{9,13},{10,... | collective-permute-start | bytes 196616 | tf_op jit(solution)/shard_map/ppermute | solution.py:20
  140.5 6.6 %collective-permute-start.55 = (f32[128,128]{1,0:T(8,128)S(1)}, f32[128,128]{1,0:T(8,128)S(1)}, u32[]{:S(2)}, u32[]{:S(2)}) collective-permute-start(f32[128,128]{1,0:T(8,128)S(1)} %shard_map.109.refs_7_), channel_id=1, source_target_pairs={{0,3},{1,2},{2,1},{3,0},{4,7},{5,6},{6,5},{7,4},{8,11},{9,10},{10,... | collective-permute-start | bytes 196616 | tf_op jit(solution)/shard_map/ppermute | solution.py:20
  141.7 6.7 %collective-permute-start.56 = (f32[128,128]{1,0:T(8,128)S(1)}, f32[128,128]{1,0:T(8,128)S(1)}, u32[]{:S(2)}, u32[]{:S(2)}) collective-permute-start(f32[128,128]{1,0:T(8,128)S(1)} %shard_map.109.refs_7_), channel_id=1, source_target_pairs={{0,2},{1,3},{2,0},{3,1},{4,6},{5,7},{6,4},{7,5},{8,10},{9,11},{10,... | collective-permute-start | bytes 196616 | tf_op jit(solution)/shard_map/ppermute | solution.py:20
  149.3 6.5 %collective-permute-start.58 = (f32[264,128]{1,0:T(8,128)S(1)}, f32[264,128]{1,0:T(8,128)S(1)}, u32[]{:S(2)}, u32[]{:S(2)}) collective-permute-start(f32[264,128]{1,0:T(8,128)S(1)} %get-tuple-element.130), channel_id=1, source_target_pairs={{0,8},{8,0},{16,24},{24,16},{1,9},{9,1},{17,25},{25,17},{2,10},{10... | collective-permute-start | bytes 405512 | tf_op jit(solution)/shard_map/ppermute | solution.py:20
  150.0 8.2 %collective-permute-start.59 = (f32[264,128]{1,0:T(8,128)S(1)}, f32[264,128]{1,0:T(8,128)S(1)}, u32[]{:S(2)}, u32[]{:S(2)}) collective-permute-start(f32[264,128]{1,0:T(8,128)S(1)} %get-tuple-element.131), channel_id=1, source_target_pairs={{0,16},{8,24},{16,0},{24,8},{1,17},{9,25},{17,1},{25,9},{2,18},{10... | collective-permute-start | bytes 405512 | tf_op jit(solution)/shard_map/ppermute | solution.py:20
  150.6 7.6 %collective-permute-start.60 = (f32[264,128]{1,0:T(8,128)S(1)}, f32[264,128]{1,0:T(8,128)S(1)}, u32[]{:S(2)}, u32[]{:S(2)}) collective-permute-start(f32[264,128]{1,0:T(8,128)S(1)} %get-tuple-element.132), channel_id=1, source_target_pairs={{0,24},{8,16},{16,8},{24,0},{1,25},{9,17},{17,9},{25,1},{2,26},{10... | collective-permute-start | bytes 405512 | tf_op jit(solution)/shard_map/ppermute | solution.py:20
  159.9 7.3 %collective-permute-start.62 = (f32[256,128]{1,0:T(8,128)S(1)}, f32[256,128]{1,0:T(8,128)S(1)}, u32[]{:S(2)}, u32[]{:S(2)}) collective-permute-start(f32[256,128]{1,0:T(8,128)S(1)} %shard_map.112.refs_0_), channel_id=1, source_target_pairs={{0,16},{8,24},{16,0},{24,8},{1,17},{9,25},{17,1},{25,9},{2,18},{10... | collective-permute-start | bytes 393224 | tf_op jit(solution)/shard_map/ppermute | solution.py:20
  160.6 6.6 %collective-permute-start.63 = (f32[256,128]{1,0:T(8,128)S(1)}, f32[256,128]{1,0:T(8,128)S(1)}, u32[]{:S(2)}, u32[]{:S(2)}) collective-permute-start(f32[256,128]{1,0:T(8,128)S(1)} %shard_map.112.refs_0_), channel_id=1, source_target_pairs={{0,24},{8,16},{16,8},{24,0},{1,25},{9,17},{17,9},{25,1},{2,26},{10... | collective-permute-start | bytes 393224 | tf_op jit(solution)/shard_map/ppermute | solution.py:20
  (37 other events, 194.3 us)

commit v10 on v9

--- a/solution.py
+++ b/solution.py
@@ -173,15 +173,23 @@
         start = ((bits % 2) * (count // 2) + bits // 2) * block
         rows_ref[start : start + block] = pack(piece[...])
     packed_ref[...] = rows_ref[...].T
-    for partner, out in zip(partners, outs):
-        out[...] = grad_dot(packed_ref, parts, samp ^ partner, out.shape[0])
+    for place, partner in enumerate(partners):
+        first, second = outs[2 * place : 2 * place + 2]
+        rows = first.shape[0]
+        total = grad_dot(packed_ref, parts, samp ^ partner, 2 * rows)
+        first[...] = total[:rows]
+        second[...] = total[rows:]
 
 
 def grad_near_kernel(partners, *refs):
     packed_ref, parts, outs = refs[0], refs[1:5], refs[5:]
     samp = lax.axis_index("samp")
-    for partner, out in zip(partners, outs):
-        out[...] = grad_dot(packed_ref, parts, samp ^ partner, out.shape[0])
+    for place, partner in enumerate(partners):
+        first, second = outs[2 * place : 2 * place + 2]
+        rows = first.shape[0]
+        total = grad_dot(packed_ref, parts, samp ^ partner, 2 * rows)
+        first[...] = total[:rows]
+        second[...] = total[rows:]
 
 
 def image_kernel(count, *refs):
@@ -190,8 +198,9 @@
     grad_ref, packed_ref, far_ref = refs[-3:]
     samp = lax.axis_index("samp")
     block = pieces[0].shape[0]
-    for bits, piece in enumerate(pieces):
-        rows = pl.ds(pl.multiple_of((samp ^ bits) * block, block), block)
+    for place, piece in enumerate(pieces):
+        bits, second = place % (count // 2), place // (count // 2)
+        rows = pl.ds(pl.multiple_of(((samp ^ bits) * 2 + second) * block, block), block)
         value = piece[...]
         grad_ref[rows] = value
         packed_ref[rows] = pack(value)
@@ -199,12 +208,11 @@
 
 
 def norm_kernel(count, *refs):
-    grad_ref, pieces, out = refs[0], refs[1 : count + 1], refs[-1]
+    grad_refs, pieces, out = refs[:2], refs[2 : count + 2], refs[-1]
     total = pieces[0][...]
     for piece in pieces[1:]:
         total = total + piece[...]
-    grad = grad_ref[...]
-    grad_sq = jnp.sum(grad * grad, axis=0, keepdims=True)
+    grad_sq = sum(jnp.sum(ref[...] * ref[...], axis=0, keepdims=True) for ref in grad_refs)
     image_sq = jnp.sum(total * total, axis=0, keepdims=True)
     sums = jnp.concatenate([grad_sq, image_sq])
     for place in range(out.shape[0]):
@@ -386,7 +394,7 @@
     packed_cols = shape((cols, 2 * n_traits), jnp.bfloat16)
     packed_rows = shape((2 * n_traits, rows), jnp.bfloat16)
     rows_buffer = [pltpu.VMEM((rows, 2 * n_traits), jnp.bfloat16)]
-    grad_block = shape((width, n_traits))
+    grad_block = shape((width // 2, n_traits))
     score_block = shape((test_width + STATS, n_traits))
     coef_out = shape((cols, n_traits))
     group_rows = groups.reshape(cols // 128, 128)
@@ -426,25 +434,27 @@
         pieces = chrom_gather(own_residual(summands))
         packed, *far_out = call(
             functools.partial(grad_far_kernel, n_chrom, others),
-            [packed_rows] + [grad_block] * len(others),
+            [packed_rows] + [grad_block] * (2 * len(others)),
             [whole()] * (n_chrom + 4),
             rows_buffer,
             flops,
             moved,
         )(*pieces, *parts)
         near_out = call(
-            functools.partial(grad_near_kernel, own), [grad_block] * len(own), [whole()] * 5, (), flops, moved
+            functools.partial(grad_near_kernel, own), [grad_block] * (2 * len(own)), [whole()] * 5, (), flops, moved
         )(packed, *parts)
-        received = [swap(piece, "samp", partner) for partner, piece in zip(order, far_out)]
-        own_grad = call(functools.partial(mean_kernel, total_rows), grad_block, [whole()] * n_samp)(
-            near_out[-1], *received[::-1]
-        )
-        pieces = samp_gather(own_grad)
+        received = [
+            [swap(piece, "samp", partner) for partner, piece in zip(order, far_out[second::2])][::-1]
+            for second in range(2)
+        ]
+        mean = call(functools.partial(mean_kernel, total_rows), grad_block, [whole()] * n_samp)
+        own_grad = [mean(near_out[second], *received[second]) for second in range(2)]
+        pieces = samp_gather(own_grad[0]) + samp_gather(own_grad[1])
         after = (tested_sq,) if iteration == 0 else ()
         gradient, packed, far_give = call(
-            functools.partial(image_kernel, n_samp),
+            functools.partial(image_kernel, 2 * n_samp),
             [coef_out, packed_cols, give_outs[1]],
-            [whole()] * (n_samp + 2) + [anywhere()] * len(after),
+            [whole()] * (2 * n_samp + 2) + [anywhere()] * len(after),
             (),
             flops,
             moved,
@@ -453,8 +463,8 @@
         summands = chrom_scatter([near_give, far_give], keep)
         size = n_samp * n_chrom
         sums = call(
-            functools.partial(norm_kernel, half), shape((size, 2, n_traits)), [whole()] * (half + 1)
-        )(own_grad, *summands)
+            functools.partial(norm_kernel, half), shape((size, 2, n_traits)), [whole()] * (half + 2)
+        )(*own_grad, *summands)
         sums = lax.all_to_all(sums, ("samp", "chrom"), 0, 0)
         coefficients, packed, far_give = call(
             functools.partial(prox_kernel, total_rows),

time: 168 us -> 171 us (1.018)
  starting transfers between devices: 62.2 us -> 76.4 us
  waiting for transfers between devices: 64.5 us -> 53 us
    ppermute x64 -> x76, starting transfers between devices: 62.2 us -> 76.4 us  [swap(): return lax.ppermute(value, axis, [(i, i ^ bits) for i in range(size)])]
    ppermute x64 -> x76, waiting for transfers between devices: 64.5 us -> 53 us  [swap(): return lax.ppermute(value, axis, [(i, i ^ bits) for i in range(size)])]
  transfers between devices with their start and end apart: 64 -> 76, of which waited for: 31 -> 33; matrix products, arithmetic and copies ran while one was open for 0% -> 0% of each run, Pallas kernels for 6% -> 6%
where the time goes in v10:
time: 171 us
  starting transfers between devices  76.4 us (45%)
  waiting for transfers between devices  53 us (31%)
  blocking collectives  20.5 us (12%)
  Pallas kernels  20.2 us (12%)
    ppermute x76, starting transfers between devices, swap(): return lax.ppermute(value, axis, [(i, i ^ bits) for i in range(size)])  76.4 us
    ppermute x76, waiting for transfers between devices, swap(): return lax.ppermute(value, axis, [(i, i ^ bits) for i in range(size)])  53 us
    all_to_all x2, blocking collectives, body(): sums = lax.all_to_all(sums, ('samp', 'chrom'), 0, 0)  20.5 us
    pallas_call x4, Pallas kernels, near(): call(near_kernel, [give_outs[0], half_out], [whole()] * 5, (), 2 * flops,...  3.95 us
  transfers between devices with their start and end apart: 76, of which 33 were waited for; matrix products, arithmetic and copies ran while one was open for 0% of the time, Pallas kernels for 6%

profile of v10, /device:TPU:0, one launch (start us, length us, event | category | flops | bytes accessed | tf_op | source)
XLA Modules:
  0.0 171.2 jit_solution(12618254104989126300)
XLA Ops:
  0.6 3.0 %shard_map.77 = (bf16[512,1024]{1,0:T(8,128)(2,1)S(1)}, bf16[512,1024]{1,0:T(8,128)(2,1)S(1)}, f32[2,128,128]{2,1,0:T(8,128)S(1)}, f32[2,128,128]{2,1,0:T(8,128)...) custom-call(f32[4,2,128,1024]{3,2,1,0:T(8,128)} %bitcast.7, f32[1024,128]{1,0:T(8,128)} %coef_ref.3), custom_call_target="tpu_custom_call" | custom-call | flops 536870912 | bytes 8388608 | tf_op jit(solution)/shard_map/pallas_call | solution.py:417
  5.2 5.1 %collective-permute-start.2 = (f32[128,128]{1,0:T(8,128)S(1)}, f32[128,128]{1,0:T(8,128)S(1)}, u32[]{:S(2)}, u32[]{:S(2)}) collective-permute-start(f32[128,128]{1,0:T(8,128)S(1)} %get-tuple-element.88), channel_id=1, source_target_pairs={{0,6},{1,7},{2,4},{3,5},{4,2},{5,3},{6,0},{7,1},{8,14},{9,15},{10,... | collective-permute-start | bytes 196616 | tf_op jit(solution)/shard_map/ppermute | solution.py:20
  11.0 1.8 %collective-permute-done.2.refs_1_ = f32[128,128]{1,0:T(8,128)S(1)} collective-permute-done((f32[128,128]{1,0:T(8,128)S(1)}, f32[128,128]{1,0:T(8,128)S(1)}, u32[]{:S(2)}, u32[]{:S(2)}) %collective-permute-start.2) | collective-permute-done | bytes 65568 | tf_op jit(solution)/shard_map/ppermute | solution.py:20
  12.8 3.3 %collective-permute-done.3.refs_2_ = f32[128,128]{1,0:T(8,128)S(1)} collective-permute-done((f32[128,128]{1,0:T(8,128)S(1)}, f32[128,128]{1,0:T(8,128)S(1)}, u32[]{:S(2)}, u32[]{:S(2)}) %collective-permute-start.3) | collective-permute-done | bytes 65568 | tf_op jit(solution)/shard_map/ppermute | solution.py:20
  16.1 2.6 %collective-permute-start.5 = (f32[128,128]{1,0:T(8,128)S(1)}, f32[128,128]{1,0:T(8,128)S(1)}, u32[]{:S(2)}, u32[]{:S(2)}) collective-permute-start(f32[128,128]{1,0:T(8,128)S(1)} %shard_map.81.refs_7_), channel_id=1, source_target_pairs={{0,6},{1,7},{2,4},{3,5},{4,2},{5,3},{6,0},{7,1},{8,14},{9,15},{10,... | collective-permute-start | bytes 196616 | tf_op jit(solution)/shard_map/ppermute | solution.py:20
  18.7 1.8 %collective-permute-start.10 = (f32[128,128]{1,0:T(8,128)S(1)}, f32[128,128]{1,0:T(8,128)S(1)}, u32[]{:S(2)}, u32[]{:S(2)}) collective-permute-start(f32[128,128]{1,0:T(8,128)S(1)} %shard_map.81.refs_7_), channel_id=1, source_target_pairs={{0,2},{1,3},{2,0},{3,1},{4,6},{5,7},{6,4},{7,5},{8,10},{9,11},{10,... | collective-permute-start | bytes 196616 | tf_op jit(solution)/shard_map/ppermute | solution.py:20
  22.5 2.8 %collective-permute-done.7.refs_3_ = f32[128,128]{1,0:T(8,128)S(1)} collective-permute-done((f32[128,128]{1,0:T(8,128)S(1)}, f32[128,128]{1,0:T(8,128)S(1)}, u32[]{:S(2)}, u32[]{:S(2)}) %collective-permute-start.7) | collective-permute-done | bytes 65568 | tf_op jit(solution)/shard_map/ppermute | solution.py:20
  45.0 2.1 %collective-permute-done.17.refs_3_ = f32[128,128]{1,0:T(8,128)S(1)} collective-permute-done((f32[128,128]{1,0:T(8,128)S(1)}, f32[128,128]{1,0:T(8,128)S(1)}, u32[]{:S(2)}, u32[]{:S(2)}) %collective-permute-start.17) | collective-permute-done | bytes 65568 | tf_op jit(solution)/shard_map/ppermute | solution.py:20
  49.3 1.9 %collective-permute-start.26 = (f32[128,128]{1,0:T(8,128)S(1)}, f32[128,128]{1,0:T(8,128)S(1)}, u32[]{:S(2)}, u32[]{:S(2)}) collective-permute-start(f32[128,128]{1,0:T(8,128)S(1)} %get-tuple-element.106), channel_id=1, source_target_pairs={{0,6},{1,7},{2,4},{3,5},{4,2},{5,3},{6,0},{7,1},{8,14},{9,15},{10,... | collective-permute-start | bytes 196616 | tf_op jit(solution)/shard_map/ppermute | solution.py:20
  51.2 2.7 %collective-permute-start.28 = (f32[128,128]{1,0:T(8,128)S(1)}, f32[128,128]{1,0:T(8,128)S(1)}, u32[]{:S(2)}, u32[]{:S(2)}) collective-permute-start(f32[128,128]{1,0:T(8,128)S(1)} %get-tuple-element.108), channel_id=1, source_target_pairs={{0,2},{1,3},{2,0},{3,1},{4,6},{5,7},{6,4},{7,5},{8,10},{9,11},{10,... | collective-permute-start | bytes 196616 | tf_op jit(solution)/shard_map/ppermute | solution.py:20
  53.9 2.3 %collective-permute-done.26.refs_3_ = f32[128,128]{1,0:T(8,128)S(1)} collective-permute-done((f32[128,128]{1,0:T(8,128)S(1)}, f32[128,128]{1,0:T(8,128)S(1)}, u32[]{:S(2)}, u32[]{:S(2)}) %collective-permute-start.26) | collective-permute-done | bytes 65568 | tf_op jit(solution)/shard_map/ppermute | solution.py:20
  56.2 1.8 %collective-permute-done.27.refs_4_ = f32[128,128]{1,0:T(8,128)S(1)} collective-permute-done((f32[128,128]{1,0:T(8,128)S(1)}, f32[128,128]{1,0:T(8,128)S(1)}, u32[]{:S(2)}, u32[]{:S(2)}) %collective-permute-start.27) | collective-permute-done | bytes 65568 | tf_op jit(solution)/shard_map/ppermute | solution.py:20
  58.1 10.4 %all_to_all.10.sums_ref = f32[32,2,128]{2,1,0:T(2,128)S(1)} all-to-all(f32[32,2,128]{2,1,0:T(2,128)S(1)} %shard_map.91), channel_id=1, replica_groups=mesh['samp'=4,'chrom'=8] {'samp','chrom'}, dimensions={0} | all-to-all | bytes 65536 | tf_op jit(solution)/shard_map/all_to_all | solution.py:468
  73.3 2.5 %collective-permute-start.33 = (f32[128,128]{1,0:T(8,128)S(1)}, f32[128,128]{1,0:T(8,128)S(1)}, u32[]{:S(2)}, u32[]{:S(2)}) collective-permute-start(f32[128,128]{1,0:T(8,128)S(1)} %get-tuple-element.117), channel_id=1, source_target_pairs={{0,2},{1,3},{2,0},{3,1},{4,6},{5,7},{6,4},{7,5},{8,10},{9,11},{10,... | collective-permute-start | bytes 196616 | tf_op jit(solution)/shard_map/ppermute | solution.py:20
  75.7 2.3 %collective-permute-done.31.refs_1_ = f32[128,128]{1,0:T(8,128)S(1)} collective-permute-done((f32[128,128]{1,0:T(8,128)S(1)}, f32[128,128]{1,0:T(8,128)S(1)}, u32[]{:S(2)}, u32[]{:S(2)}) %collective-permute-start.31) | collective-permute-done | bytes 65568 | tf_op jit(solution)/shard_map/ppermute | solution.py:20
  86.0 2.2 %collective-permute-done.36.refs_3_ = f32[128,128]{1,0:T(8,128)S(1)} collective-permute-done((f32[128,128]{1,0:T(8,128)S(1)}, f32[128,128]{1,0:T(8,128)S(1)}, u32[]{:S(2)}, u32[]{:S(2)}) %collective-permute-start.36) | collective-permute-done | bytes 65568 | tf_op jit(solution)/shard_map/ppermute | solution.py:20
  91.9 2.2 %collective-permute-start.49 = (f32[128,128]{1,0:T(8,128)S(1)}, f32[128,128]{1,0:T(8,128)S(1)}, u32[]{:S(2)}, u32[]{:S(2)}) collective-permute-start(f32[128,128]{1,0:T(8,128)S(1)} %get-tuple-element.126), channel_id=1, source_target_pairs={{0,24},{8,16},{16,8},{24,0},{1,25},{9,17},{17,9},{25,1},{2,26},{10... | collective-permute-start | bytes 196616 | tf_op jit(solution)/shard_map/ppermute | solution.py:20
  96.0 2.2 %collective-permute-start.43 = (f32[128,128]{1,0:T(8,128)S(1)}, f32[128,128]{1,0:T(8,128)S(1)}, u32[]{:S(2)}, u32[]{:S(2)}) collective-permute-start(f32[128,128]{1,0:T(8,128)S(1)} %get-tuple-element.122), channel_id=1, source_target_pairs={{0,24},{8,16},{16,8},{24,0},{1,25},{9,17},{17,9},{25,1},{2,26},{10... | collective-permute-start | bytes 196616 | tf_op jit(solution)/shard_map/ppermute | solution.py:20
  107.2 2.2 %collective-permute-done.46.refs_3_ = f32[128,128]{1,0:T(8,128)S(1)} collective-permute-done((f32[128,128]{1,0:T(8,128)S(1)}, f32[128,128]{1,0:T(8,128)S(1)}, u32[]{:S(2)}, u32[]{:S(2)}) %collective-permute-start.46) | collective-permute-done | bytes 65568 | tf_op jit(solution)/shard_map/ppermute | solution.py:20
  111.6 2.3 %collective-permute-start.55 = (f32[128,128]{1,0:T(8,128)S(1)}, f32[128,128]{1,0:T(8,128)S(1)}, u32[]{:S(2)}, u32[]{:S(2)}) collective-permute-start(f32[128,128]{1,0:T(8,128)S(1)} %get-tuple-element.133), channel_id=1, source_target_pairs={{0,6},{1,7},{2,4},{3,5},{4,2},{5,3},{6,0},{7,1},{8,14},{9,15},{10,... | collective-permute-start | bytes 196616 | tf_op jit(solution)/shard_map/ppermute | solution.py:20
  113.9 2.2 %collective-permute-start.57 = (f32[128,128]{1,0:T(8,128)S(1)}, f32[128,128]{1,0:T(8,128)S(1)}, u32[]{:S(2)}, u32[]{:S(2)}) collective-permute-start(f32[128,128]{1,0:T(8,128)S(1)} %get-tuple-element.135), channel_id=1, source_target_pairs={{0,2},{1,3},{2,0},{3,1},{4,6},{5,7},{6,4},{7,5},{8,10},{9,11},{10,... | collective-permute-start | bytes 196616 | tf_op jit(solution)/shard_map/ppermute | solution.py:20
  116.2 2.2 %collective-permute-done.55.refs_3_ = f32[128,128]{1,0:T(8,128)S(1)} collective-permute-done((f32[128,128]{1,0:T(8,128)S(1)}, f32[128,128]{1,0:T(8,128)S(1)}, u32[]{:S(2)}, u32[]{:S(2)}) %collective-permute-start.55) | collective-permute-done | bytes 65568 | tf_op jit(solution)/shard_map/ppermute | solution.py:20
  118.3 2.0 %collective-permute-done.56.refs_4_ = f32[128,128]{1,0:T(8,128)S(1)} collective-permute-done((f32[128,128]{1,0:T(8,128)S(1)}, f32[128,128]{1,0:T(8,128)S(1)}, u32[]{:S(2)}, u32[]{:S(2)}) %collective-permute-start.56) | collective-permute-done | bytes 65568 | tf_op jit(solution)/shard_map/ppermute | solution.py:20
  120.4 10.1 %all_to_all.11.sums_ref = f32[32,2,128]{2,1,0:T(2,128)S(1)} all-to-all(f32[32,2,128]{2,1,0:T(2,128)S(1)} %shard_map.105), channel_id=1, replica_groups=mesh['samp'=4,'chrom'=8] {'samp','chrom'}, dimensions={0} | all-to-all | bytes 65536 | tf_op jit(solution)/shard_map/all_to_all | solution.py:468
  135.2 2.5 %collective-permute-start.62 = (f32[128,128]{1,0:T(8,128)S(1)}, f32[128,128]{1,0:T(8,128)S(1)}, u32[]{:S(2)}, u32[]{:S(2)}) collective-permute-start(f32[128,128]{1,0:T(8,128)S(1)} %get-tuple-element.143), channel_id=1, source_target_pairs={{0,2},{1,3},{2,0},{3,1},{4,6},{5,7},{6,4},{7,5},{8,10},{9,11},{10,... | collective-permute-start | bytes 196616 | tf_op jit(solution)/shard_map/ppermute | solution.py:20
  137.7 2.6 %shard_map.110 = (f32[1024,128]{1,0:T(8,128)S(1)}, f32[1024,128]{1,0:T(8,128)S(1)}) custom-call(f32[1024,128]{1,0:T(8,128)S(1)} %get-tuple-element.144.coef_ref, s32[8,128]{1,0:T(8,128)S(1)} %bitcast.6, bf16[512,1024]{1,0:T(8,128)(2,1)S(1)} %get-tuple-element.82.refs_8_.refs_1_.high0_ref.refs_0_, ...), custom_call_target="tpu_custom_call" | custom-call | flops 2147483648 | bytes 8388608 | tf_op jit(solution)/shard_map/pallas_call | solution.py:480
  147.9 2.1 %collective-permute-done.65.refs_3_ = f32[128,128]{1,0:T(8,128)S(1)} collective-permute-done((f32[128,128]{1,0:T(8,128)S(1)}, f32[128,128]{1,0:T(8,128)S(1)}, u32[]{:S(2)}, u32[]{:S(2)}) %collective-permute-start.65) | collective-permute-done | bytes 65568 | tf_op jit(solution)/shard_map/ppermute | solution.py:20
  153.6 2.1 %collective-permute-start.72 = (f32[264,128]{1,0:T(8,128)S(1)}, f32[264,128]{1,0:T(8,128)S(1)}, u32[]{:S(2)}, u32[]{:S(2)}) collective-permute-start(f32[264,128]{1,0:T(8,128)S(1)} %get-tuple-element.152), channel_id=1, source_target_pairs={{0,24},{8,16},{16,8},{24,0},{1,25},{9,17},{17,9},{25,1},{2,26},{10... | collective-permute-start | bytes 405512 | tf_op jit(solution)/shard_map/ppermute | solution.py:20
  156.7 1.9 %collective-permute-done.70.refs_1_ = f32[264,128]{1,0:T(8,128)S(1)} collective-permute-done((f32[264,128]{1,0:T(8,128)S(1)}, f32[264,128]{1,0:T(8,128)S(1)}, u32[]{:S(2)}, u32[]{:S(2)}) %collective-permute-start.70) | collective-permute-done | bytes 135200 | tf_op jit(solution)/shard_map/ppermute | solution.py:20
  158.7 2.5 %collective-permute-done.71.refs_2_ = f32[264,128]{1,0:T(8,128)S(1)} collective-permute-done((f32[264,128]{1,0:T(8,128)S(1)}, f32[264,128]{1,0:T(8,128)S(1)}, u32[]{:S(2)}, u32[]{:S(2)}) %collective-permute-start.71) | collective-permute-done | bytes 135200 | tf_op jit(solution)/shard_map/ppermute | solution.py:20
  165.0 2.5 %collective-permute-done.73.refs_1_ = f32[256,128]{1,0:T(8,128)S(1)} collective-permute-done((f32[256,128]{1,0:T(8,128)S(1)}, f32[256,128]{1,0:T(8,128)S(1)}, u32[]{:S(2)}, u32[]{:S(2)}) %collective-permute-start.73) | collective-permute-done | bytes 131104 | tf_op jit(solution)/shard_map/ppermute | solution.py:20
  167.5 2.8 %collective-permute-done.74.refs_2_ = f32[256,128]{1,0:T(8,128)S(1)} collective-permute-done((f32[256,128]{1,0:T(8,128)S(1)}, f32[256,128]{1,0:T(8,128)S(1)}, u32[]{:S(2)}, u32[]{:S(2)}) %collective-permute-start.74) | collective-permute-done | bytes 131104 | tf_op jit(solution)/shard_map/ppermute | solution.py:20
  (171 shorter events, 77.4 us)
Async XLA Ops:
  5.2 7.6 %collective-permute-start.2 = (f32[128,128]{1,0:T(8,128)S(1)}, f32[128,128]{1,0:T(8,128)S(1)}, u32[]{:S(2)}, u32[]{:S(2)}) collective-permute-start(f32[128,128]{1,0:T(8,128)S(1)} %get-tuple-element.88), channel_id=1, source_target_pairs={{0,6},{1,7},{2,4},{3,5},{4,2},{5,3},{6,0},{7,1},{8,14},{9,15},{10,... | collective-permute-start | bytes 196616 | tf_op jit(solution)/shard_map/ppermute | solution.py:20
  18.7 6.5 %collective-permute-start.7 = (f32[128,128]{1,0:T(8,128)S(1)}, f32[128,128]{1,0:T(8,128)S(1)}, u32[]{:S(2)}, u32[]{:S(2)}) collective-permute-start(f32[128,128]{1,0:T(8,128)S(1)} %shard_map.81.refs_7_), channel_id=1, source_target_pairs={{0,4},{1,5},{2,6},{3,7},{4,0},{5,1},{6,2},{7,3},{8,12},{9,13},{10,... | collective-permute-start | bytes 196616 | tf_op jit(solution)/shard_map/ppermute | solution.py:20
  18.7 6.5 %collective-permute-start.10 = (f32[128,128]{1,0:T(8,128)S(1)}, f32[128,128]{1,0:T(8,128)S(1)}, u32[]{:S(2)}, u32[]{:S(2)}) collective-permute-start(f32[128,128]{1,0:T(8,128)S(1)} %shard_map.81.refs_7_), channel_id=1, source_target_pairs={{0,2},{1,3},{2,0},{3,1},{4,6},{5,7},{6,4},{7,5},{8,10},{9,11},{10,... | collective-permute-start | bytes 196616 | tf_op jit(solution)/shard_map/ppermute | solution.py:20
  27.6 7.2 %collective-permute-start.18 = (f32[128,128]{1,0:T(8,128)S(1)}, f32[128,128]{1,0:T(8,128)S(1)}, u32[]{:S(2)}, u32[]{:S(2)}) collective-permute-start(f32[128,128]{1,0:T(8,128)S(1)} %get-tuple-element.97), channel_id=1, source_target_pairs={{0,8},{8,0},{16,24},{24,16},{1,9},{9,1},{17,25},{25,17},{2,10},{10... | collective-permute-start | bytes 196616 | tf_op jit(solution)/shard_map/ppermute | solution.py:20
  31.1 7.2 %collective-permute-start.12 = (f32[128,128]{1,0:T(8,128)S(1)}, f32[128,128]{1,0:T(8,128)S(1)}, u32[]{:S(2)}, u32[]{:S(2)}) collective-permute-start(f32[128,128]{1,0:T(8,128)S(1)} %get-tuple-element.93), channel_id=1, source_target_pairs={{0,8},{8,0},{16,24},{24,16},{1,9},{9,1},{17,25},{25,17},{2,10},{10... | collective-permute-start | bytes 196616 | tf_op jit(solution)/shard_map/ppermute | solution.py:20
  33.2 6.4 %collective-permute-start.13 = (f32[128,128]{1,0:T(8,128)S(1)}, f32[128,128]{1,0:T(8,128)S(1)}, u32[]{:S(2)}, u32[]{:S(2)}) collective-permute-start(f32[128,128]{1,0:T(8,128)S(1)} %get-tuple-element.94), channel_id=1, source_target_pairs={{0,16},{8,24},{16,0},{24,8},{1,17},{9,25},{17,1},{25,9},{2,18},{10... | collective-permute-start | bytes 196616 | tf_op jit(solution)/shard_map/ppermute | solution.py:20
  37.0 6.9 %collective-permute-start.22 = (f32[128,128]{1,0:T(8,128)S(1)}, f32[128,128]{1,0:T(8,128)S(1)}, u32[]{:S(2)}, u32[]{:S(2)}) collective-permute-start(f32[128,128]{1,0:T(8,128)S(1)} %shard_map.85.refs_4_.refs_1_), channel_id=1, source_target_pairs={{0,16},{8,24},{16,0},{24,8},{1,17},{9,25},{17,1},{25,9},{2,18},{10... | collective-permute-start | bytes 196616 | tf_op jit(solution)/shard_map/ppermute | solution.py:20
  49.3 6.9 %collective-permute-start.26 = (f32[128,128]{1,0:T(8,128)S(1)}, f32[128,128]{1,0:T(8,128)S(1)}, u32[]{:S(2)}, u32[]{:S(2)}) collective-permute-start(f32[128,128]{1,0:T(8,128)S(1)} %get-tuple-element.106), channel_id=1, source_target_pairs={{0,6},{1,7},{2,4},{3,5},{4,2},{5,3},{6,0},{7,1},{8,14},{9,15},{10,... | collective-permute-start | bytes 196616 | tf_op jit(solution)/shard_map/ppermute | solution.py:20
  51.2 6.8 %collective-permute-start.27 = (f32[128,128]{1,0:T(8,128)S(1)}, f32[128,128]{1,0:T(8,128)S(1)}, u32[]{:S(2)}, u32[]{:S(2)}) collective-permute-start(f32[128,128]{1,0:T(8,128)S(1)} %get-tuple-element.107), channel_id=1, source_target_pairs={{0,4},{1,5},{2,6},{3,7},{4,0},{5,1},{6,2},{7,3},{8,12},{9,13},{10,... | collective-permute-start | bytes 196616 | tf_op jit(solution)/shard_map/ppermute | solution.py:20
  51.2 6.8 %collective-permute-start.28 = (f32[128,128]{1,0:T(8,128)S(1)}, f32[128,128]{1,0:T(8,128)S(1)}, u32[]{:S(2)}, u32[]{:S(2)}) collective-permute-start(f32[128,128]{1,0:T(8,128)S(1)} %get-tuple-element.108), channel_id=1, source_target_pairs={{0,2},{1,3},{2,0},{3,1},{4,6},{5,7},{6,4},{7,5},{8,10},{9,11},{10,... | collective-permute-start | bytes 196616 | tf_op jit(solution)/shard_map/ppermute | solution.py:20
  71.2 6.9 %collective-permute-start.31 = (f32[128,128]{1,0:T(8,128)S(1)}, f32[128,128]{1,0:T(8,128)S(1)}, u32[]{:S(2)}, u32[]{:S(2)}) collective-permute-start(f32[128,128]{1,0:T(8,128)S(1)} %get-tuple-element.115), channel_id=1, source_target_pairs={{0,6},{1,7},{2,4},{3,5},{4,2},{5,3},{6,0},{7,1},{8,14},{9,15},{10,... | collective-permute-start | bytes 196616 | tf_op jit(solution)/shard_map/ppermute | solution.py:20
  71.8 7.9 %collective-permute-start.32 = (f32[128,128]{1,0:T(8,128)S(1)}, f32[128,128]{1,0:T(8,128)S(1)}, u32[]{:S(2)}, u32[]{:S(2)}) collective-permute-start(f32[128,128]{1,0:T(8,128)S(1)} %get-tuple-element.116), channel_id=1, source_target_pairs={{0,4},{1,5},{2,6},{3,7},{4,0},{5,1},{6,2},{7,3},{8,12},{9,13},{10,... | collective-permute-start | bytes 196616 | tf_op jit(solution)/shard_map/ppermute | solution.py:20
  73.3 6.4 %collective-permute-start.33 = (f32[128,128]{1,0:T(8,128)S(1)}, f32[128,128]{1,0:T(8,128)S(1)}, u32[]{:S(2)}, u32[]{:S(2)}) collective-permute-start(f32[128,128]{1,0:T(8,128)S(1)} %get-tuple-element.117), channel_id=1, source_target_pairs={{0,2},{1,3},{2,0},{3,1},{4,6},{5,7},{6,4},{7,5},{8,10},{9,11},{10,... | collective-permute-start | bytes 196616 | tf_op jit(solution)/shard_map/ppermute | solution.py:20
  81.2 6.9 %collective-permute-start.36 = (f32[128,128]{1,0:T(8,128)S(1)}, f32[128,128]{1,0:T(8,128)S(1)}, u32[]{:S(2)}, u32[]{:S(2)}) collective-permute-start(f32[128,128]{1,0:T(8,128)S(1)} %shard_map.96.refs_7_), channel_id=1, source_target_pairs={{0,4},{1,5},{2,6},{3,7},{4,0},{5,1},{6,2},{7,3},{8,12},{9,13},{10,... | collective-permute-start | bytes 196616 | tf_op jit(solution)/shard_map/ppermute | solution.py:20
  81.6 6.6 %collective-permute-start.38 = (f32[128,128]{1,0:T(8,128)S(1)}, f32[128,128]{1,0:T(8,128)S(1)}, u32[]{:S(2)}, u32[]{:S(2)}) collective-permute-start(f32[128,128]{1,0:T(8,128)S(1)} %shard_map.96.refs_7_), channel_id=1, source_target_pairs={{0,3},{1,2},{2,1},{3,0},{4,7},{5,6},{6,5},{7,4},{8,11},{9,10},{10,... | collective-permute-start | bytes 196616 | tf_op jit(solution)/shard_map/ppermute | solution.py:20
  82.7 6.7 %collective-permute-start.39 = (f32[128,128]{1,0:T(8,128)S(1)}, f32[128,128]{1,0:T(8,128)S(1)}, u32[]{:S(2)}, u32[]{:S(2)}) collective-permute-start(f32[128,128]{1,0:T(8,128)S(1)} %shard_map.96.refs_7_), channel_id=1, source_target_pairs={{0,2},{1,3},{2,0},{3,1},{4,6},{5,7},{6,4},{7,5},{8,10},{9,11},{10,... | collective-permute-start | bytes 196616 | tf_op jit(solution)/shard_map/ppermute | solution.py:20
  91.3 6.9 %collective-permute-start.48 = (f32[128,128]{1,0:T(8,128)S(1)}, f32[128,128]{1,0:T(8,128)S(1)}, u32[]{:S(2)}, u32[]{:S(2)}) collective-permute-start(f32[128,128]{1,0:T(8,128)S(1)} %get-tuple-element.125), channel_id=1, source_target_pairs={{0,16},{8,24},{16,0},{24,8},{1,17},{9,25},{17,1},{25,9},{2,18},{10... | collective-permute-start | bytes 196616 | tf_op jit(solution)/shard_map/ppermute | solution.py:20
  95.3 6.4 %collective-permute-start.42 = (f32[128,128]{1,0:T(8,128)S(1)}, f32[128,128]{1,0:T(8,128)S(1)}, u32[]{:S(2)}, u32[]{:S(2)}) collective-permute-start(f32[128,128]{1,0:T(8,128)S(1)} %get-tuple-element.121), channel_id=1, source_target_pairs={{0,16},{8,24},{16,0},{24,8},{1,17},{9,25},{17,1},{25,9},{2,18},{10... | collective-permute-start | bytes 196616 | tf_op jit(solution)/shard_map/ppermute | solution.py:20
  111.6 6.7 %collective-permute-start.55 = (f32[128,128]{1,0:T(8,128)S(1)}, f32[128,128]{1,0:T(8,128)S(1)}, u32[]{:S(2)}, u32[]{:S(2)}) collective-permute-start(f32[128,128]{1,0:T(8,128)S(1)} %get-tuple-element.133), channel_id=1, source_target_pairs={{0,6},{1,7},{2,4},{3,5},{4,2},{5,3},{6,0},{7,1},{8,14},{9,15},{10,... | collective-permute-start | bytes 196616 | tf_op jit(solution)/shard_map/ppermute | solution.py:20
  113.9 6.4 %collective-permute-start.56 = (f32[128,128]{1,0:T(8,128)S(1)}, f32[128,128]{1,0:T(8,128)S(1)}, u32[]{:S(2)}, u32[]{:S(2)}) collective-permute-start(f32[128,128]{1,0:T(8,128)S(1)} %get-tuple-element.134), channel_id=1, source_target_pairs={{0,4},{1,5},{2,6},{3,7},{4,0},{5,1},{6,2},{7,3},{8,12},{9,13},{10,... | collective-permute-start | bytes 196616 | tf_op jit(solution)/shard_map/ppermute | solution.py:20
  113.9 6.4 %collective-permute-start.57 = (f32[128,128]{1,0:T(8,128)S(1)}, f32[128,128]{1,0:T(8,128)S(1)}, u32[]{:S(2)}, u32[]{:S(2)}) collective-permute-start(f32[128,128]{1,0:T(8,128)S(1)} %get-tuple-element.135), channel_id=1, source_target_pairs={{0,2},{1,3},{2,0},{3,1},{4,6},{5,7},{6,4},{7,5},{8,10},{9,11},{10,... | collective-permute-start | bytes 196616 | tf_op jit(solution)/shard_map/ppermute | solution.py:20
  133.1 7.1 %collective-permute-start.60 = (f32[128,128]{1,0:T(8,128)S(1)}, f32[128,128]{1,0:T(8,128)S(1)}, u32[]{:S(2)}, u32[]{:S(2)}) collective-permute-start(f32[128,128]{1,0:T(8,128)S(1)} %get-tuple-element.141), channel_id=1, source_target_pairs={{0,6},{1,7},{2,4},{3,5},{4,2},{5,3},{6,0},{7,1},{8,14},{9,15},{10,... | collective-permute-start | bytes 196616 | tf_op jit(solution)/shard_map/ppermute | solution.py:20
  133.8 7.9 %collective-permute-start.61 = (f32[128,128]{1,0:T(8,128)S(1)}, f32[128,128]{1,0:T(8,128)S(1)}, u32[]{:S(2)}, u32[]{:S(2)}) collective-permute-start(f32[128,128]{1,0:T(8,128)S(1)} %get-tuple-element.142), channel_id=1, source_target_pairs={{0,4},{1,5},{2,6},{3,7},{4,0},{5,1},{6,2},{7,3},{8,12},{9,13},{10,... | collective-permute-start | bytes 196616 | tf_op jit(solution)/shard_map/ppermute | solution.py:20
  135.2 6.4 %collective-permute-start.62 = (f32[128,128]{1,0:T(8,128)S(1)}, f32[128,128]{1,0:T(8,128)S(1)}, u32[]{:S(2)}, u32[]{:S(2)}) collective-permute-start(f32[128,128]{1,0:T(8,128)S(1)} %get-tuple-element.143), channel_id=1, source_target_pairs={{0,2},{1,3},{2,0},{3,1},{4,6},{5,7},{6,4},{7,5},{8,10},{9,11},{10,... | collective-permute-start | bytes 196616 | tf_op jit(solution)/shard_map/ppermute | solution.py:20
  143.1 6.9 %collective-permute-start.65 = (f32[128,128]{1,0:T(8,128)S(1)}, f32[128,128]{1,0:T(8,128)S(1)}, u32[]{:S(2)}, u32[]{:S(2)}) collective-permute-start(f32[128,128]{1,0:T(8,128)S(1)} %shard_map.111.refs_7_), channel_id=1, source_target_pairs={{0,4},{1,5},{2,6},{3,7},{4,0},{5,1},{6,2},{7,3},{8,12},{9,13},{10,... | collective-permute-start | bytes 196616 | tf_op jit(solution)/shard_map/ppermute | solution.py:20
  143.5 6.6 %collective-permute-start.67 = (f32[128,128]{1,0:T(8,128)S(1)}, f32[128,128]{1,0:T(8,128)S(1)}, u32[]{:S(2)}, u32[]{:S(2)}) collective-permute-start(f32[128,128]{1,0:T(8,128)S(1)} %shard_map.111.refs_7_), channel_id=1, source_target_pairs={{0,3},{1,2},{2,1},{3,0},{4,7},{5,6},{6,5},{7,4},{8,11},{9,10},{10,... | collective-permute-start | bytes 196616 | tf_op jit(solution)/shard_map/ppermute | solution.py:20
  144.7 6.6 %collective-permute-start.68 = (f32[128,128]{1,0:T(8,128)S(1)}, f32[128,128]{1,0:T(8,128)S(1)}, u32[]{:S(2)}, u32[]{:S(2)}) collective-permute-start(f32[128,128]{1,0:T(8,128)S(1)} %shard_map.111.refs_7_), channel_id=1, source_target_pairs={{0,2},{1,3},{2,0},{3,1},{4,6},{5,7},{6,4},{7,5},{8,10},{9,11},{10,... | collective-permute-start | bytes 196616 | tf_op jit(solution)/shard_map/ppermute | solution.py:20
  152.2 6.5 %collective-permute-start.70 = (f32[264,128]{1,0:T(8,128)S(1)}, f32[264,128]{1,0:T(8,128)S(1)}, u32[]{:S(2)}, u32[]{:S(2)}) collective-permute-start(f32[264,128]{1,0:T(8,128)S(1)} %get-tuple-element.150), channel_id=1, source_target_pairs={{0,8},{8,0},{16,24},{24,16},{1,9},{9,1},{17,25},{25,17},{2,10},{10... | collective-permute-start | bytes 405512 | tf_op jit(solution)/shard_map/ppermute | solution.py:20
  153.0 8.2 %collective-permute-start.71 = (f32[264,128]{1,0:T(8,128)S(1)}, f32[264,128]{1,0:T(8,128)S(1)}, u32[]{:S(2)}, u32[]{:S(2)}) collective-permute-start(f32[264,128]{1,0:T(8,128)S(1)} %get-tuple-element.151), channel_id=1, source_target_pairs={{0,16},{8,24},{16,0},{24,8},{1,17},{9,25},{17,1},{25,9},{2,18},{10... | collective-permute-start | bytes 405512 | tf_op jit(solution)/shard_map/ppermute | solution.py:20
  153.6 7.6 %collective-permute-start.72 = (f32[264,128]{1,0:T(8,128)S(1)}, f32[264,128]{1,0:T(8,128)S(1)}, u32[]{:S(2)}, u32[]{:S(2)}) collective-permute-start(f32[264,128]{1,0:T(8,128)S(1)} %get-tuple-element.152), channel_id=1, source_target_pairs={{0,24},{8,16},{16,8},{24,0},{1,25},{9,17},{17,9},{25,1},{2,26},{10... | collective-permute-start | bytes 405512 | tf_op jit(solution)/shard_map/ppermute | solution.py:20
  162.9 7.4 %collective-permute-start.74 = (f32[256,128]{1,0:T(8,128)S(1)}, f32[256,128]{1,0:T(8,128)S(1)}, u32[]{:S(2)}, u32[]{:S(2)}) collective-permute-start(f32[256,128]{1,0:T(8,128)S(1)} %shard_map.114.refs_0_), channel_id=1, source_target_pairs={{0,16},{8,24},{16,0},{24,8},{1,17},{9,25},{17,1},{25,9},{2,18},{10... | collective-permute-start | bytes 393224 | tf_op jit(solution)/shard_map/ppermute | solution.py:20
  163.5 6.7 %collective-permute-start.75 = (f32[256,128]{1,0:T(8,128)S(1)}, f32[256,128]{1,0:T(8,128)S(1)}, u32[]{:S(2)}, u32[]{:S(2)}) collective-permute-start(f32[256,128]{1,0:T(8,128)S(1)} %shard_map.114.refs_0_), channel_id=1, source_target_pairs={{0,24},{8,16},{16,8},{24,0},{1,25},{9,17},{17,9},{25,1},{2,26},{10... | collective-permute-start | bytes 393224 | tf_op jit(solution)/shard_map/ppermute | solution.py:20
  (49 other events, 256.4 us)

commit v11 on v9

--- a/solution.py
+++ b/solution.py
@@ -346,11 +346,16 @@
         first -= count
         kernel = functools.partial(chip_kernel, first)
         sums = list(call(kernel, [shape(keep.shape[1:])] * count, [whole()] * 2)(keep, swap(part, "chrom", 1))) + sums
-    return [sums[0]] + [swap(sums[k], "chrom", 2 * k) for k in reversed(range(1, len(sums)))]
+    return [sums[0]] + [swap(sums[k], "chrom", 2 * k) for k in chip_order(len(sums))[:-1]]
+
+
+def chip_order(count):
+    order = list(reversed(range(count)))
+    return order[1::-1] + order[2:] if count > 2 else order
 
 
 def chrom_order(size):
-    return list(reversed(range(size)))
+    return [2 * k + bits for k in chip_order(size // 2) for bits in (range(2) if k > 1 else (1, 0))]
 
 
 def chrom_gather(own):

time: 168 us -> 170 us (1.012)
  waiting for transfers between devices: 64.5 us -> 66.5 us
    ppermute x64, waiting for transfers between devices: 64.5 us -> 66.5 us  [swap(): return lax.ppermute(value, axis, [(i, i ^ bits) for i in range(size)])]
  transfers between devices with their start and end apart: 64 -> 64, of which waited for: 31 -> 34; matrix products, arithmetic and copies ran while one was open for 0% -> 0% of each run, Pallas kernels for 6% -> 6%
where the time goes in v11:
time: 170 us
  waiting for transfers between devices  66.5 us (39%)
  starting transfers between devices  61.5 us (36%)
  blocking collectives  20.8 us (12%)
  Pallas kernels  20.3 us (12%)
    ppermute x64, waiting for transfers between devices, swap(): return lax.ppermute(value, axis, [(i, i ^ bits) for i in range(size)])  66.5 us
    ppermute x64, starting transfers between devices, swap(): return lax.ppermute(value, axis, [(i, i ^ bits) for i in range(size)])  61.5 us
    all_to_all x2, blocking collectives, body(): sums = lax.all_to_all(sums, ('samp', 'chrom'), 0, 0)  20.8 us
    pallas_call x4, Pallas kernels, near(): call(near_kernel, [give_outs[0], half_out], [whole()] * 5, (), 2 * flops,...  3.94 us
  transfers between devices with their start and end apart: 64, of which 34 were waited for; matrix products, arithmetic and copies ran while one was open for 0% of the time, Pallas kernels for 6%

profile of v11, /device:TPU:0, one launch (start us, length us, event | category | flops | bytes accessed | tf_op | source)
XLA Modules:
  0.0 170.2 jit_solution(1319748029358129197)
XLA Ops:
  0.6 3.0 %shard_map.77 = (bf16[512,1024]{1,0:T(8,128)(2,1)S(1)}, bf16[512,1024]{1,0:T(8,128)(2,1)S(1)}, f32[2,128,128]{2,1,0:T(8,128)S(1)}, f32[2,128,128]{2,1,0:T(8,128)...) custom-call(f32[4,2,128,1024]{3,2,1,0:T(8,128)} %bitcast.7, f32[1024,128]{1,0:T(8,128)} %coef_ref.3), custom_call_target="tpu_custom_call" | custom-call | flops 536870912 | bytes 8388608 | tf_op jit(solution)/shard_map/pallas_call | solution.py:414
  5.2 4.0 %collective-permute-start.2 = (f32[128,128]{1,0:T(8,128)S(1)}, f32[128,128]{1,0:T(8,128)S(1)}, u32[]{:S(2)}, u32[]{:S(2)}) collective-permute-start(f32[128,128]{1,0:T(8,128)S(1)} %get-tuple-element.78), channel_id=1, source_target_pairs={{0,4},{1,5},{2,6},{3,7},{4,0},{5,1},{6,2},{7,3},{8,12},{9,13},{10,... | collective-permute-start | bytes 196616 | tf_op jit(solution)/shard_map/ppermute | solution.py:20
  10.9 2.2 %collective-permute-done.2.refs_1_ = f32[128,128]{1,0:T(8,128)S(1)} collective-permute-done((f32[128,128]{1,0:T(8,128)S(1)}, f32[128,128]{1,0:T(8,128)S(1)}, u32[]{:S(2)}, u32[]{:S(2)}) %collective-permute-start.2) | collective-permute-done | bytes 65568 | tf_op jit(solution)/shard_map/ppermute | solution.py:20
  13.1 2.5 %collective-permute-done.3.refs_2_ = f32[128,128]{1,0:T(8,128)S(1)} collective-permute-done((f32[128,128]{1,0:T(8,128)S(1)}, f32[128,128]{1,0:T(8,128)S(1)}, u32[]{:S(2)}, u32[]{:S(2)}) %collective-permute-start.3) | collective-permute-done | bytes 65568 | tf_op jit(solution)/shard_map/ppermute | solution.py:20
  15.8 2.8 %collective-permute-start.5 = (f32[128,128]{1,0:T(8,128)S(1)}, f32[128,128]{1,0:T(8,128)S(1)}, u32[]{:S(2)}, u32[]{:S(2)}) collective-permute-start(f32[128,128]{1,0:T(8,128)S(1)} %shard_map.81.refs_7_), channel_id=1, source_target_pairs={{0,4},{1,5},{2,6},{3,7},{4,0},{5,1},{6,2},{7,3},{8,12},{9,13},{10,... | collective-permute-start | bytes 196616 | tf_op jit(solution)/shard_map/ppermute | solution.py:20
  22.7 2.2 %collective-permute-done.7.refs_2_ = f32[128,128]{1,0:T(8,128)S(1)} collective-permute-done((f32[128,128]{1,0:T(8,128)S(1)}, f32[128,128]{1,0:T(8,128)S(1)}, u32[]{:S(2)}, u32[]{:S(2)}) %collective-permute-start.7) | collective-permute-done | bytes 65568 | tf_op jit(solution)/shard_map/ppermute | solution.py:20
  33.2 3.7 %collective-permute-done.13.refs_2_ = f32[256,128]{1,0:T(8,128)S(1)} collective-permute-done((f32[256,128]{1,0:T(8,128)S(1)}, f32[256,128]{1,0:T(8,128)S(1)}, u32[]{:S(2)}, u32[]{:S(2)}) %collective-permute-start.13) | collective-permute-done | bytes 131104 | tf_op jit(solution)/shard_map/ppermute | solution.py:20
  40.6 2.4 %collective-permute-done.15.refs_1_ = f32[256,128]{1,0:T(8,128)S(1)} collective-permute-done((f32[256,128]{1,0:T(8,128)S(1)}, f32[256,128]{1,0:T(8,128)S(1)}, u32[]{:S(2)}, u32[]{:S(2)}) %collective-permute-start.15) | collective-permute-done | bytes 131104 | tf_op jit(solution)/shard_map/ppermute | solution.py:20
  43.0 2.5 %collective-permute-done.16.refs_2_ = f32[256,128]{1,0:T(8,128)S(1)} collective-permute-done((f32[256,128]{1,0:T(8,128)S(1)}, f32[256,128]{1,0:T(8,128)S(1)}, u32[]{:S(2)}, u32[]{:S(2)}) %collective-permute-start.16) | collective-permute-done | bytes 131104 | tf_op jit(solution)/shard_map/ppermute | solution.py:20
  47.7 2.3 %collective-permute-start.20 = (f32[128,128]{1,0:T(8,128)S(1)}, f32[128,128]{1,0:T(8,128)S(1)}, u32[]{:S(2)}, u32[]{:S(2)}) collective-permute-start(f32[128,128]{1,0:T(8,128)S(1)} %get-tuple-element.91), channel_id=1, source_target_pairs={{0,4},{1,5},{2,6},{3,7},{4,0},{5,1},{6,2},{7,3},{8,12},{9,13},{10,... | collective-permute-start | bytes 196616 | tf_op jit(solution)/shard_map/ppermute | solution.py:20
  51.4 3.8 %collective-permute-done.20.refs_2_ = f32[128,128]{1,0:T(8,128)S(1)} collective-permute-done((f32[128,128]{1,0:T(8,128)S(1)}, f32[128,128]{1,0:T(8,128)S(1)}, u32[]{:S(2)}, u32[]{:S(2)}) %collective-permute-start.20) | collective-permute-done | bytes 65568 | tf_op jit(solution)/shard_map/ppermute | solution.py:20
  57.0 10.9 %all_to_all.10.sums_ref = f32[32,2,128]{2,1,0:T(2,128)S(1)} all-to-all(f32[32,2,128]{2,1,0:T(2,128)S(1)} %shard_map.90), channel_id=1, replica_groups=mesh['samp'=4,'chrom'=8] {'samp','chrom'}, dimensions={0} | all-to-all | bytes 65536 | tf_op jit(solution)/shard_map/all_to_all | solution.py:463
  71.2 2.4 %collective-permute-start.26 = (f32[128,128]{1,0:T(8,128)S(1)}, f32[128,128]{1,0:T(8,128)S(1)}, u32[]{:S(2)}, u32[]{:S(2)}) collective-permute-start(f32[128,128]{1,0:T(8,128)S(1)} %get-tuple-element.101), channel_id=1, source_target_pairs={{0,6},{1,7},{2,4},{3,5},{4,2},{5,3},{6,0},{7,1},{8,14},{9,15},{10,... | collective-permute-start | bytes 196616 | tf_op jit(solution)/shard_map/ppermute | solution.py:20
  74.3 4.4 %collective-permute-done.25.refs_1_ = f32[128,128]{1,0:T(8,128)S(1)} collective-permute-done((f32[128,128]{1,0:T(8,128)S(1)}, f32[128,128]{1,0:T(8,128)S(1)}, u32[]{:S(2)}, u32[]{:S(2)}) %collective-permute-start.25) | collective-permute-done | bytes 65568 | tf_op jit(solution)/shard_map/ppermute | solution.py:20
  79.8 3.2 %collective-permute-start.30 = (f32[128,128]{1,0:T(8,128)S(1)}, f32[128,128]{1,0:T(8,128)S(1)}, u32[]{:S(2)}, u32[]{:S(2)}) collective-permute-start(f32[128,128]{1,0:T(8,128)S(1)} %shard_map.95.refs_7_), channel_id=1, source_target_pairs={{0,6},{1,7},{2,4},{3,5},{4,2},{5,3},{6,0},{7,1},{8,14},{9,15},{10,... | collective-permute-start | bytes 196616 | tf_op jit(solution)/shard_map/ppermute | solution.py:20
  84.8 3.0 %collective-permute-done.28.refs_0_ = f32[128,128]{1,0:T(8,128)S(1)} collective-permute-done((f32[128,128]{1,0:T(8,128)S(1)}, f32[128,128]{1,0:T(8,128)S(1)}, u32[]{:S(2)}, u32[]{:S(2)}) %collective-permute-start.28) | collective-permute-done | bytes 65568 | tf_op jit(solution)/shard_map/ppermute | solution.py:20
  91.7 2.6 %collective-permute-start.37 = (f32[256,128]{1,0:T(8,128)S(1)}, f32[256,128]{1,0:T(8,128)S(1)}, u32[]{:S(2)}, u32[]{:S(2)}) collective-permute-start(f32[256,128]{1,0:T(8,128)S(1)} %get-tuple-element.106), channel_id=1, source_target_pairs={{0,24},{8,16},{16,8},{24,0},{1,25},{9,17},{17,9},{25,1},{2,26},{10... | collective-permute-start | bytes 393224 | tf_op jit(solution)/shard_map/ppermute | solution.py:20
  94.8 2.3 %collective-permute-done.35.refs_1_ = f32[256,128]{1,0:T(8,128)S(1)} collective-permute-done((f32[256,128]{1,0:T(8,128)S(1)}, f32[256,128]{1,0:T(8,128)S(1)}, u32[]{:S(2)}, u32[]{:S(2)}) %collective-permute-start.35) | collective-permute-done | bytes 131104 | tf_op jit(solution)/shard_map/ppermute | solution.py:20
  97.1 2.2 %collective-permute-done.36.refs_2_ = f32[256,128]{1,0:T(8,128)S(1)} collective-permute-done((f32[256,128]{1,0:T(8,128)S(1)}, f32[256,128]{1,0:T(8,128)S(1)}, u32[]{:S(2)}, u32[]{:S(2)}) %collective-permute-start.36) | collective-permute-done | bytes 131104 | tf_op jit(solution)/shard_map/ppermute | solution.py:20
  103.0 2.6 %collective-permute-done.38.refs_1_ = f32[256,128]{1,0:T(8,128)S(1)} collective-permute-done((f32[256,128]{1,0:T(8,128)S(1)}, f32[256,128]{1,0:T(8,128)S(1)}, u32[]{:S(2)}, u32[]{:S(2)}) %collective-permute-start.38) | collective-permute-done | bytes 131104 | tf_op jit(solution)/shard_map/ppermute | solution.py:20
  105.5 2.5 %collective-permute-done.39.refs_2_ = f32[256,128]{1,0:T(8,128)S(1)} collective-permute-done((f32[256,128]{1,0:T(8,128)S(1)}, f32[256,128]{1,0:T(8,128)S(1)}, u32[]{:S(2)}, u32[]{:S(2)}) %collective-permute-start.39) | collective-permute-done | bytes 131104 | tf_op jit(solution)/shard_map/ppermute | solution.py:20
  110.3 3.3 %collective-permute-start.44 = (f32[128,128]{1,0:T(8,128)S(1)}, f32[128,128]{1,0:T(8,128)S(1)}, u32[]{:S(2)}, u32[]{:S(2)}) collective-permute-start(f32[128,128]{1,0:T(8,128)S(1)} %get-tuple-element.114), channel_id=1, source_target_pairs={{0,6},{1,7},{2,4},{3,5},{4,2},{5,3},{6,0},{7,1},{8,14},{9,15},{10,... | collective-permute-start | bytes 196616 | tf_op jit(solution)/shard_map/ppermute | solution.py:20
  113.9 4.6 %collective-permute-done.43.refs_2_ = f32[128,128]{1,0:T(8,128)S(1)} collective-permute-done((f32[128,128]{1,0:T(8,128)S(1)}, f32[128,128]{1,0:T(8,128)S(1)}, u32[]{:S(2)}, u32[]{:S(2)}) %collective-permute-start.43) | collective-permute-done | bytes 65568 | tf_op jit(solution)/shard_map/ppermute | solution.py:20
  119.1 9.9 %all_to_all.11.sums_ref = f32[32,2,128]{2,1,0:T(2,128)S(1)} all-to-all(f32[32,2,128]{2,1,0:T(2,128)S(1)} %shard_map.103), channel_id=1, replica_groups=mesh['samp'=4,'chrom'=8] {'samp','chrom'}, dimensions={0} | all-to-all | bytes 65536 | tf_op jit(solution)/shard_map/all_to_all | solution.py:463
  132.1 2.4 %collective-permute-start.49 = (f32[128,128]{1,0:T(8,128)S(1)}, f32[128,128]{1,0:T(8,128)S(1)}, u32[]{:S(2)}, u32[]{:S(2)}) collective-permute-start(f32[128,128]{1,0:T(8,128)S(1)} %get-tuple-element.122), channel_id=1, source_target_pairs={{0,6},{1,7},{2,4},{3,5},{4,2},{5,3},{6,0},{7,1},{8,14},{9,15},{10,... | collective-permute-start | bytes 196616 | tf_op jit(solution)/shard_map/ppermute | solution.py:20
  135.3 2.6 %shard_map.108 = (f32[1024,128]{1,0:T(8,128)S(1)}, f32[1024,128]{1,0:T(8,128)S(1)}) custom-call(f32[1024,128]{1,0:T(8,128)S(1)} %get-tuple-element.124.coef_ref, s32[8,128]{1,0:T(8,128)S(1)} %bitcast.6, bf16[512,1024]{1,0:T(8,128)(2,1)S(1)} %get-tuple-element.72.refs_8_.refs_1_.high0_ref.refs_0_, ...), custom_call_target="tpu_custom_call" | custom-call | flops 2147483648 | bytes 8388608 | tf_op jit(solution)/shard_map/pallas_call | solution.py:475
  140.7 3.2 %collective-permute-start.53 = (f32[128,128]{1,0:T(8,128)S(1)}, f32[128,128]{1,0:T(8,128)S(1)}, u32[]{:S(2)}, u32[]{:S(2)}) collective-permute-start(f32[128,128]{1,0:T(8,128)S(1)} %shard_map.109.refs_7_), channel_id=1, source_target_pairs={{0,6},{1,7},{2,4},{3,5},{4,2},{5,3},{6,0},{7,1},{8,14},{9,15},{10,... | collective-permute-start | bytes 196616 | tf_op jit(solution)/shard_map/ppermute | solution.py:20
  145.8 3.0 %collective-permute-done.51.refs_0_ = f32[128,128]{1,0:T(8,128)S(1)} collective-permute-done((f32[128,128]{1,0:T(8,128)S(1)}, f32[128,128]{1,0:T(8,128)S(1)}, u32[]{:S(2)}, u32[]{:S(2)}) %collective-permute-start.51) | collective-permute-done | bytes 65568 | tf_op jit(solution)/shard_map/ppermute | solution.py:20
  152.4 2.7 %collective-permute-start.60 = (f32[264,128]{1,0:T(8,128)S(1)}, f32[264,128]{1,0:T(8,128)S(1)}, u32[]{:S(2)}, u32[]{:S(2)}) collective-permute-start(f32[264,128]{1,0:T(8,128)S(1)} %get-tuple-element.132), channel_id=1, source_target_pairs={{0,24},{8,16},{16,8},{24,0},{1,25},{9,17},{17,9},{25,1},{2,26},{10... | collective-permute-start | bytes 405512 | tf_op jit(solution)/shard_map/ppermute | solution.py:20
  158.0 2.3 %collective-permute-done.59.refs_2_ = f32[264,128]{1,0:T(8,128)S(1)} collective-permute-done((f32[264,128]{1,0:T(8,128)S(1)}, f32[264,128]{1,0:T(8,128)S(1)}, u32[]{:S(2)}, u32[]{:S(2)}) %collective-permute-start.59) | collective-permute-done | bytes 135200 | tf_op jit(solution)/shard_map/ppermute | solution.py:20
  164.2 2.6 %collective-permute-done.61.refs_1_ = f32[256,128]{1,0:T(8,128)S(1)} collective-permute-done((f32[256,128]{1,0:T(8,128)S(1)}, f32[256,128]{1,0:T(8,128)S(1)}, u32[]{:S(2)}, u32[]{:S(2)}) %collective-permute-start.61) | collective-permute-done | bytes 131104 | tf_op jit(solution)/shard_map/ppermute | solution.py:20
  166.8 2.4 %collective-permute-done.62.refs_2_ = f32[256,128]{1,0:T(8,128)S(1)} collective-permute-done((f32[256,128]{1,0:T(8,128)S(1)}, f32[256,128]{1,0:T(8,128)S(1)}, u32[]{:S(2)}, u32[]{:S(2)}) %collective-permute-start.62) | collective-permute-done | bytes 131104 | tf_op jit(solution)/shard_map/ppermute | solution.py:20
  (145 shorter events, 62.7 us)
Async XLA Ops:
  4.2 6.4 %collective-permute-start = (f32[2,128,128]{2,1,0:T(8,128)S(1)}, f32[2,128,128]{2,1,0:T(8,128)S(1)}, u32[]{:S(2)}, u32[]{:S(2)}) collective-permute-start(f32[2,128,128]{2,1,0:T(8,128)S(1)} %get-tuple-element.75), channel_id=1, source_target_pairs={{0,1},{1,0},{2,3},{3,2},{4,5},{5,4},{6,7},{7,6},{8,9},{9,8},{10,11... | collective-permute-start | bytes 393224 | tf_op jit(solution)/shard_map/ppermute | solution.py:20
  5.2 7.9 %collective-permute-start.2 = (f32[128,128]{1,0:T(8,128)S(1)}, f32[128,128]{1,0:T(8,128)S(1)}, u32[]{:S(2)}, u32[]{:S(2)}) collective-permute-start(f32[128,128]{1,0:T(8,128)S(1)} %get-tuple-element.78), channel_id=1, source_target_pairs={{0,4},{1,5},{2,6},{3,7},{4,0},{5,1},{6,2},{7,3},{8,12},{9,13},{10,... | collective-permute-start | bytes 196616 | tf_op jit(solution)/shard_map/ppermute | solution.py:20
  9.2 6.4 %collective-permute-start.3 = (f32[128,128]{1,0:T(8,128)S(1)}, f32[128,128]{1,0:T(8,128)S(1)}, u32[]{:S(2)}, u32[]{:S(2)}) collective-permute-start(f32[128,128]{1,0:T(8,128)S(1)} %get-tuple-element.79), channel_id=1, source_target_pairs={{0,6},{1,7},{2,4},{3,5},{4,2},{5,3},{6,0},{7,1},{8,14},{9,15},{10,... | collective-permute-start | bytes 196616 | tf_op jit(solution)/shard_map/ppermute | solution.py:20
  15.8 6.9 %collective-permute-start.5 = (f32[128,128]{1,0:T(8,128)S(1)}, f32[128,128]{1,0:T(8,128)S(1)}, u32[]{:S(2)}, u32[]{:S(2)}) collective-permute-start(f32[128,128]{1,0:T(8,128)S(1)} %shard_map.81.refs_7_), channel_id=1, source_target_pairs={{0,4},{1,5},{2,6},{3,7},{4,0},{5,1},{6,2},{7,3},{8,12},{9,13},{10,... | collective-permute-start | bytes 196616 | tf_op jit(solution)/shard_map/ppermute | solution.py:20
  28.8 8.1 %collective-permute-start.13 = (f32[256,128]{1,0:T(8,128)S(1)}, f32[256,128]{1,0:T(8,128)S(1)}, u32[]{:S(2)}, u32[]{:S(2)}) collective-permute-start(f32[256,128]{1,0:T(8,128)S(1)} %get-tuple-element.83), channel_id=1, source_target_pairs={{0,16},{8,24},{16,0},{24,8},{1,17},{9,25},{17,1},{25,9},{2,18},{10... | collective-permute-start | bytes 393224 | tf_op jit(solution)/shard_map/ppermute | solution.py:20
  30.4 6.6 %collective-permute-start.14 = (f32[256,128]{1,0:T(8,128)S(1)}, f32[256,128]{1,0:T(8,128)S(1)}, u32[]{:S(2)}, u32[]{:S(2)}) collective-permute-start(f32[256,128]{1,0:T(8,128)S(1)} %get-tuple-element.84), channel_id=1, source_target_pairs={{0,24},{8,16},{16,8},{24,0},{1,25},{9,17},{17,9},{25,1},{2,26},{10... | collective-permute-start | bytes 393224 | tf_op jit(solution)/shard_map/ppermute | solution.py:20
  38.3 7.3 %collective-permute-start.16 = (f32[256,128]{1,0:T(8,128)S(1)}, f32[256,128]{1,0:T(8,128)S(1)}, u32[]{:S(2)}, u32[]{:S(2)}) collective-permute-start(f32[256,128]{1,0:T(8,128)S(1)} %shard_map.84.refs_0_), channel_id=1, source_target_pairs={{0,16},{8,24},{16,0},{24,8},{1,17},{9,25},{17,1},{25,9},{2,18},{10... | collective-permute-start | bytes 393224 | tf_op jit(solution)/shard_map/ppermute | solution.py:20
  39.1 6.4 %collective-permute-start.17 = (f32[256,128]{1,0:T(8,128)S(1)}, f32[256,128]{1,0:T(8,128)S(1)}, u32[]{:S(2)}, u32[]{:S(2)}) collective-permute-start(f32[256,128]{1,0:T(8,128)S(1)} %shard_map.84.refs_0_), channel_id=1, source_target_pairs={{0,24},{8,16},{16,8},{24,0},{1,25},{9,17},{17,9},{25,1},{2,26},{10... | collective-permute-start | bytes 393224 | tf_op jit(solution)/shard_map/ppermute | solution.py:20
  47.7 7.5 %collective-permute-start.20 = (f32[128,128]{1,0:T(8,128)S(1)}, f32[128,128]{1,0:T(8,128)S(1)}, u32[]{:S(2)}, u32[]{:S(2)}) collective-permute-start(f32[128,128]{1,0:T(8,128)S(1)} %get-tuple-element.91), channel_id=1, source_target_pairs={{0,4},{1,5},{2,6},{3,7},{4,0},{5,1},{6,2},{7,3},{8,12},{9,13},{10,... | collective-permute-start | bytes 196616 | tf_op jit(solution)/shard_map/ppermute | solution.py:20
  50.1 6.4 %collective-permute-start.21 = (f32[128,128]{1,0:T(8,128)S(1)}, f32[128,128]{1,0:T(8,128)S(1)}, u32[]{:S(2)}, u32[]{:S(2)}) collective-permute-start(f32[128,128]{1,0:T(8,128)S(1)} %get-tuple-element.92), channel_id=1, source_target_pairs={{0,6},{1,7},{2,4},{3,5},{4,2},{5,3},{6,0},{7,1},{8,14},{9,15},{10,... | collective-permute-start | bytes 196616 | tf_op jit(solution)/shard_map/ppermute | solution.py:20
  70.6 8.0 %collective-permute-start.25 = (f32[128,128]{1,0:T(8,128)S(1)}, f32[128,128]{1,0:T(8,128)S(1)}, u32[]{:S(2)}, u32[]{:S(2)}) collective-permute-start(f32[128,128]{1,0:T(8,128)S(1)} %get-tuple-element.100), channel_id=1, source_target_pairs={{0,4},{1,5},{2,6},{3,7},{4,0},{5,1},{6,2},{7,3},{8,12},{9,13},{10,... | collective-permute-start | bytes 196616 | tf_op jit(solution)/shard_map/ppermute | solution.py:20
  71.2 7.5 %collective-permute-start.26 = (f32[128,128]{1,0:T(8,128)S(1)}, f32[128,128]{1,0:T(8,128)S(1)}, u32[]{:S(2)}, u32[]{:S(2)}) collective-permute-start(f32[128,128]{1,0:T(8,128)S(1)} %get-tuple-element.101), channel_id=1, source_target_pairs={{0,6},{1,7},{2,4},{3,5},{4,2},{5,3},{6,0},{7,1},{8,14},{9,15},{10,... | collective-permute-start | bytes 196616 | tf_op jit(solution)/shard_map/ppermute | solution.py:20
  79.7 8.1 %collective-permute-start.28 = (f32[128,128]{1,0:T(8,128)S(1)}, f32[128,128]{1,0:T(8,128)S(1)}, u32[]{:S(2)}, u32[]{:S(2)}) collective-permute-start(f32[128,128]{1,0:T(8,128)S(1)} %shard_map.95.refs_7_), channel_id=1, source_target_pairs={{0,4},{1,5},{2,6},{3,7},{4,0},{5,1},{6,2},{7,3},{8,12},{9,13},{10,... | collective-permute-start | bytes 196616 | tf_op jit(solution)/shard_map/ppermute | solution.py:20
  79.8 8.0 %collective-permute-start.30 = (f32[128,128]{1,0:T(8,128)S(1)}, f32[128,128]{1,0:T(8,128)S(1)}, u32[]{:S(2)}, u32[]{:S(2)}) collective-permute-start(f32[128,128]{1,0:T(8,128)S(1)} %shard_map.95.refs_7_), channel_id=1, source_target_pairs={{0,6},{1,7},{2,4},{3,5},{4,2},{5,3},{6,0},{7,1},{8,14},{9,15},{10,... | collective-permute-start | bytes 196616 | tf_op jit(solution)/shard_map/ppermute | solution.py:20
  82.9 6.7 %collective-permute-start.33 = (f32[128,128]{1,0:T(8,128)S(1)}, f32[128,128]{1,0:T(8,128)S(1)}, u32[]{:S(2)}, u32[]{:S(2)}) collective-permute-start(f32[128,128]{1,0:T(8,128)S(1)} %shard_map.95.refs_7_), channel_id=1, source_target_pairs={{0,2},{1,3},{2,0},{3,1},{4,6},{5,7},{6,4},{7,5},{8,10},{9,11},{10,... | collective-permute-start | bytes 196616 | tf_op jit(solution)/shard_map/ppermute | solution.py:20
  90.7 6.4 %collective-permute-start.35 = (f32[256,128]{1,0:T(8,128)S(1)}, f32[256,128]{1,0:T(8,128)S(1)}, u32[]{:S(2)}, u32[]{:S(2)}) collective-permute-start(f32[256,128]{1,0:T(8,128)S(1)} %get-tuple-element.104), channel_id=1, source_target_pairs={{0,8},{8,0},{16,24},{24,16},{1,9},{9,1},{17,25},{25,17},{2,10},{10... | collective-permute-start | bytes 393224 | tf_op jit(solution)/shard_map/ppermute | solution.py:20
  91.3 8.0 %collective-permute-start.36 = (f32[256,128]{1,0:T(8,128)S(1)}, f32[256,128]{1,0:T(8,128)S(1)}, u32[]{:S(2)}, u32[]{:S(2)}) collective-permute-start(f32[256,128]{1,0:T(8,128)S(1)} %get-tuple-element.105), channel_id=1, source_target_pairs={{0,16},{8,24},{16,0},{24,8},{1,17},{9,25},{17,1},{25,9},{2,18},{10... | collective-permute-start | bytes 393224 | tf_op jit(solution)/shard_map/ppermute | solution.py:20
  91.7 7.7 %collective-permute-start.37 = (f32[256,128]{1,0:T(8,128)S(1)}, f32[256,128]{1,0:T(8,128)S(1)}, u32[]{:S(2)}, u32[]{:S(2)}) collective-permute-start(f32[256,128]{1,0:T(8,128)S(1)} %get-tuple-element.106), channel_id=1, source_target_pairs={{0,24},{8,16},{16,8},{24,0},{1,25},{9,17},{17,9},{25,1},{2,26},{10... | collective-permute-start | bytes 393224 | tf_op jit(solution)/shard_map/ppermute | solution.py:20
  101.0 7.0 %collective-permute-start.39 = (f32[256,128]{1,0:T(8,128)S(1)}, f32[256,128]{1,0:T(8,128)S(1)}, u32[]{:S(2)}, u32[]{:S(2)}) collective-permute-start(f32[256,128]{1,0:T(8,128)S(1)} %shard_map.98.refs_0_), channel_id=1, source_target_pairs={{0,16},{8,24},{16,0},{24,8},{1,17},{9,25},{17,1},{25,9},{2,18},{10... | collective-permute-start | bytes 393224 | tf_op jit(solution)/shard_map/ppermute | solution.py:20
  101.6 6.5 %collective-permute-start.40 = (f32[256,128]{1,0:T(8,128)S(1)}, f32[256,128]{1,0:T(8,128)S(1)}, u32[]{:S(2)}, u32[]{:S(2)}) collective-permute-start(f32[256,128]{1,0:T(8,128)S(1)} %shard_map.98.refs_0_), channel_id=1, source_target_pairs={{0,24},{8,16},{16,8},{24,0},{1,25},{9,17},{17,9},{25,1},{2,26},{10... | collective-permute-start | bytes 393224 | tf_op jit(solution)/shard_map/ppermute | solution.py:20
  110.2 8.2 %collective-permute-start.43 = (f32[128,128]{1,0:T(8,128)S(1)}, f32[128,128]{1,0:T(8,128)S(1)}, u32[]{:S(2)}, u32[]{:S(2)}) collective-permute-start(f32[128,128]{1,0:T(8,128)S(1)} %get-tuple-element.113), channel_id=1, source_target_pairs={{0,4},{1,5},{2,6},{3,7},{4,0},{5,1},{6,2},{7,3},{8,12},{9,13},{10,... | collective-permute-start | bytes 196616 | tf_op jit(solution)/shard_map/ppermute | solution.py:20
  110.3 8.2 %collective-permute-start.44 = (f32[128,128]{1,0:T(8,128)S(1)}, f32[128,128]{1,0:T(8,128)S(1)}, u32[]{:S(2)}, u32[]{:S(2)}) collective-permute-start(f32[128,128]{1,0:T(8,128)S(1)} %get-tuple-element.114), channel_id=1, source_target_pairs={{0,6},{1,7},{2,4},{3,5},{4,2},{5,3},{6,0},{7,1},{8,14},{9,15},{10,... | collective-permute-start | bytes 196616 | tf_op jit(solution)/shard_map/ppermute | solution.py:20
  131.6 8.0 %collective-permute-start.48 = (f32[128,128]{1,0:T(8,128)S(1)}, f32[128,128]{1,0:T(8,128)S(1)}, u32[]{:S(2)}, u32[]{:S(2)}) collective-permute-start(f32[128,128]{1,0:T(8,128)S(1)} %get-tuple-element.121), channel_id=1, source_target_pairs={{0,4},{1,5},{2,6},{3,7},{4,0},{5,1},{6,2},{7,3},{8,12},{9,13},{10,... | collective-permute-start | bytes 196616 | tf_op jit(solution)/shard_map/ppermute | solution.py:20
  132.1 7.5 %collective-permute-start.49 = (f32[128,128]{1,0:T(8,128)S(1)}, f32[128,128]{1,0:T(8,128)S(1)}, u32[]{:S(2)}, u32[]{:S(2)}) collective-permute-start(f32[128,128]{1,0:T(8,128)S(1)} %get-tuple-element.122), channel_id=1, source_target_pairs={{0,6},{1,7},{2,4},{3,5},{4,2},{5,3},{6,0},{7,1},{8,14},{9,15},{10,... | collective-permute-start | bytes 196616 | tf_op jit(solution)/shard_map/ppermute | solution.py:20
  140.7 8.1 %collective-permute-start.51 = (f32[128,128]{1,0:T(8,128)S(1)}, f32[128,128]{1,0:T(8,128)S(1)}, u32[]{:S(2)}, u32[]{:S(2)}) collective-permute-start(f32[128,128]{1,0:T(8,128)S(1)} %shard_map.109.refs_7_), channel_id=1, source_target_pairs={{0,4},{1,5},{2,6},{3,7},{4,0},{5,1},{6,2},{7,3},{8,12},{9,13},{10,... | collective-permute-start | bytes 196616 | tf_op jit(solution)/shard_map/ppermute | solution.py:20
  140.7 8.0 %collective-permute-start.53 = (f32[128,128]{1,0:T(8,128)S(1)}, f32[128,128]{1,0:T(8,128)S(1)}, u32[]{:S(2)}, u32[]{:S(2)}) collective-permute-start(f32[128,128]{1,0:T(8,128)S(1)} %shard_map.109.refs_7_), channel_id=1, source_target_pairs={{0,6},{1,7},{2,4},{3,5},{4,2},{5,3},{6,0},{7,1},{8,14},{9,15},{10,... | collective-permute-start | bytes 196616 | tf_op jit(solution)/shard_map/ppermute | solution.py:20
  143.9 6.7 %collective-permute-start.56 = (f32[128,128]{1,0:T(8,128)S(1)}, f32[128,128]{1,0:T(8,128)S(1)}, u32[]{:S(2)}, u32[]{:S(2)}) collective-permute-start(f32[128,128]{1,0:T(8,128)S(1)} %shard_map.109.refs_7_), channel_id=1, source_target_pairs={{0,2},{1,3},{2,0},{3,1},{4,6},{5,7},{6,4},{7,5},{8,10},{9,11},{10,... | collective-permute-start | bytes 196616 | tf_op jit(solution)/shard_map/ppermute | solution.py:20
  151.5 6.5 %collective-permute-start.58 = (f32[264,128]{1,0:T(8,128)S(1)}, f32[264,128]{1,0:T(8,128)S(1)}, u32[]{:S(2)}, u32[]{:S(2)}) collective-permute-start(f32[264,128]{1,0:T(8,128)S(1)} %get-tuple-element.130), channel_id=1, source_target_pairs={{0,8},{8,0},{16,24},{24,16},{1,9},{9,1},{17,25},{25,17},{2,10},{10... | collective-permute-start | bytes 405512 | tf_op jit(solution)/shard_map/ppermute | solution.py:20
  152.1 8.2 %collective-permute-start.59 = (f32[264,128]{1,0:T(8,128)S(1)}, f32[264,128]{1,0:T(8,128)S(1)}, u32[]{:S(2)}, u32[]{:S(2)}) collective-permute-start(f32[264,128]{1,0:T(8,128)S(1)} %get-tuple-element.131), channel_id=1, source_target_pairs={{0,16},{8,24},{16,0},{24,8},{1,17},{9,25},{17,1},{25,9},{2,18},{10... | collective-permute-start | bytes 405512 | tf_op jit(solution)/shard_map/ppermute | solution.py:20
  152.4 8.0 %collective-permute-start.60 = (f32[264,128]{1,0:T(8,128)S(1)}, f32[264,128]{1,0:T(8,128)S(1)}, u32[]{:S(2)}, u32[]{:S(2)}) collective-permute-start(f32[264,128]{1,0:T(8,128)S(1)} %get-tuple-element.132), channel_id=1, source_target_pairs={{0,24},{8,16},{16,8},{24,0},{1,25},{9,17},{17,9},{25,1},{2,26},{10... | collective-permute-start | bytes 405512 | tf_op jit(solution)/shard_map/ppermute | solution.py:20
  162.2 7.0 %collective-permute-start.62 = (f32[256,128]{1,0:T(8,128)S(1)}, f32[256,128]{1,0:T(8,128)S(1)}, u32[]{:S(2)}, u32[]{:S(2)}) collective-permute-start(f32[256,128]{1,0:T(8,128)S(1)} %shard_map.112.refs_0_), channel_id=1, source_target_pairs={{0,16},{8,24},{16,0},{24,8},{1,17},{9,25},{17,1},{25,9},{2,18},{10... | collective-permute-start | bytes 393224 | tf_op jit(solution)/shard_map/ppermute | solution.py:20
  162.8 6.4 %collective-permute-start.63 = (f32[256,128]{1,0:T(8,128)S(1)}, f32[256,128]{1,0:T(8,128)S(1)}, u32[]{:S(2)}, u32[]{:S(2)}) collective-permute-start(f32[256,128]{1,0:T(8,128)S(1)} %shard_map.112.refs_0_), channel_id=1, source_target_pairs={{0,24},{8,16},{16,8},{24,0},{1,25},{9,17},{17,9},{25,1},{2,26},{10... | collective-permute-start | bytes 393224 | tf_op jit(solution)/shard_map/ppermute | solution.py:20
  (37 other events, 198.4 us)

commit v12 on v11

--- a/solution.py
+++ b/solution.py
@@ -346,7 +346,7 @@
         first -= count
         kernel = functools.partial(chip_kernel, first)
         sums = list(call(kernel, [shape(keep.shape[1:])] * count, [whole()] * 2)(keep, swap(part, "chrom", 1))) + sums
-    return [sums[0]] + [swap(sums[k], "chrom", 2 * k) for k in chip_order(len(sums))[:-1]]
+    return [sums[0]] + [swap(sums[k], "chrom", 2 * k) for k in reversed(range(1, len(sums)))]
 
 
 def chip_order(count):

time: 170 us -> 167 us (0.982)
  waiting for transfers between devices: 66.5 us -> 61.6 us
  starting transfers between devices: 61.5 us -> 63.8 us
    ppermute x64, waiting for transfers between devices: 66.5 us -> 61.6 us  [swap(): return lax.ppermute(value, axis, [(i, i ^ bits) for i in range(size)])]
    ppermute x64, starting transfers between devices: 61.5 us -> 63.8 us  [swap(): return lax.ppermute(value, axis, [(i, i ^ bits) for i in range(size)])]
  transfers between devices with their start and end apart: 64 -> 64, of which waited for: 34 -> 32; matrix products, arithmetic and copies ran while one was open for 0% -> 0% of each run, Pallas kernels for 6% -> 6%
where the time goes in v12:
time: 167 us
  starting transfers between devices  63.8 us (38%)
  waiting for transfers between devices  61.6 us (37%)
  blocking collectives  20.3 us (12%)
  Pallas kernels  20.2 us (12%)
    ppermute x64, starting transfers between devices, swap(): return lax.ppermute(value, axis, [(i, i ^ bits) for i in range(size)])  63.8 us
    ppermute x64, waiting for transfers between devices, swap(): return lax.ppermute(value, axis, [(i, i ^ bits) for i in range(size)])  61.6 us
    all_to_all x2, blocking collectives, body(): sums = lax.all_to_all(sums, ('samp', 'chrom'), 0, 0)  20.3 us
    pallas_call x4, Pallas kernels, near(): call(near_kernel, [give_outs[0], half_out], [whole()] * 5, (), 2 * flops,...  3.94 us
  transfers between devices with their start and end apart: 64, of which 32 were waited for; matrix products, arithmetic and copies ran while one was open for 0% of the time, Pallas kernels for 6%

profile of v12, /device:TPU:0, one launch (start us, length us, event | category | flops | bytes accessed | tf_op | source)
XLA Modules:
  0.0 167.0 jit_solution(5886179752804729005)
XLA Ops:
  0.6 3.0 %shard_map.77 = (bf16[512,1024]{1,0:T(8,128)(2,1)S(1)}, bf16[512,1024]{1,0:T(8,128)(2,1)S(1)}, f32[2,128,128]{2,1,0:T(8,128)S(1)}, f32[2,128,128]{2,1,0:T(8,128)...) custom-call(f32[4,2,128,1024]{3,2,1,0:T(8,128)} %bitcast.7, f32[1024,128]{1,0:T(8,128)} %coef_ref.3), custom_call_target="tpu_custom_call" | custom-call | flops 536870912 | bytes 8388608 | tf_op jit(solution)/shard_map/pallas_call | solution.py:414
  5.2 5.1 %collective-permute-start.2 = (f32[128,128]{1,0:T(8,128)S(1)}, f32[128,128]{1,0:T(8,128)S(1)}, u32[]{:S(2)}, u32[]{:S(2)}) collective-permute-start(f32[128,128]{1,0:T(8,128)S(1)} %get-tuple-element.78), channel_id=1, source_target_pairs={{0,6},{1,7},{2,4},{3,5},{4,2},{5,3},{6,0},{7,1},{8,14},{9,15},{10,... | collective-permute-start | bytes 196616 | tf_op jit(solution)/shard_map/ppermute | solution.py:20
  12.8 3.3 %collective-permute-done.3.refs_2_ = f32[128,128]{1,0:T(8,128)S(1)} collective-permute-done((f32[128,128]{1,0:T(8,128)S(1)}, f32[128,128]{1,0:T(8,128)S(1)}, u32[]{:S(2)}, u32[]{:S(2)}) %collective-permute-start.3) | collective-permute-done | bytes 65568 | tf_op jit(solution)/shard_map/ppermute | solution.py:20
  17.6 2.0 %collective-permute-start.7 = (f32[128,128]{1,0:T(8,128)S(1)}, f32[128,128]{1,0:T(8,128)S(1)}, u32[]{:S(2)}, u32[]{:S(2)}) collective-permute-start(f32[128,128]{1,0:T(8,128)S(1)} %shard_map.81.refs_7_), channel_id=1, source_target_pairs={{0,6},{1,7},{2,4},{3,5},{4,2},{5,3},{6,0},{7,1},{8,14},{9,15},{10,... | collective-permute-start | bytes 196616 | tf_op jit(solution)/shard_map/ppermute | solution.py:20
  19.7 2.1 %collective-permute-start.9 = (f32[128,128]{1,0:T(8,128)S(1)}, f32[128,128]{1,0:T(8,128)S(1)}, u32[]{:S(2)}, u32[]{:S(2)}) collective-permute-start(f32[128,128]{1,0:T(8,128)S(1)} %shard_map.81.refs_7_), channel_id=1, source_target_pairs={{0,3},{1,2},{2,1},{3,0},{4,7},{5,6},{6,5},{7,4},{8,11},{9,10},{10,... | collective-permute-start | bytes 196616 | tf_op jit(solution)/shard_map/ppermute | solution.py:20
  21.8 2.1 %collective-permute-done.5.refs_0_ = f32[128,128]{1,0:T(8,128)S(1)} collective-permute-done((f32[128,128]{1,0:T(8,128)S(1)}, f32[128,128]{1,0:T(8,128)S(1)}, u32[]{:S(2)}, u32[]{:S(2)}) %collective-permute-start.5) | collective-permute-done | bytes 65568 | tf_op jit(solution)/shard_map/ppermute | solution.py:20
  30.5 2.2 %collective-permute-done.12.refs_1_ = f32[256,128]{1,0:T(8,128)S(1)} collective-permute-done((f32[256,128]{1,0:T(8,128)S(1)}, f32[256,128]{1,0:T(8,128)S(1)}, u32[]{:S(2)}, u32[]{:S(2)}) %collective-permute-start.12) | collective-permute-done | bytes 131104 | tf_op jit(solution)/shard_map/ppermute | solution.py:20
  32.7 3.7 %collective-permute-done.13.refs_2_ = f32[256,128]{1,0:T(8,128)S(1)} collective-permute-done((f32[256,128]{1,0:T(8,128)S(1)}, f32[256,128]{1,0:T(8,128)S(1)}, u32[]{:S(2)}, u32[]{:S(2)}) %collective-permute-start.13) | collective-permute-done | bytes 131104 | tf_op jit(solution)/shard_map/ppermute | solution.py:20
  42.0 3.3 %collective-permute-done.16.refs_2_ = f32[256,128]{1,0:T(8,128)S(1)} collective-permute-done((f32[256,128]{1,0:T(8,128)S(1)}, f32[256,128]{1,0:T(8,128)S(1)}, u32[]{:S(2)}, u32[]{:S(2)}) %collective-permute-start.16) | collective-permute-done | bytes 131104 | tf_op jit(solution)/shard_map/ppermute | solution.py:20
  47.5 2.0 %collective-permute-start.20 = (f32[128,128]{1,0:T(8,128)S(1)}, f32[128,128]{1,0:T(8,128)S(1)}, u32[]{:S(2)}, u32[]{:S(2)}) collective-permute-start(f32[128,128]{1,0:T(8,128)S(1)} %get-tuple-element.91), channel_id=1, source_target_pairs={{0,6},{1,7},{2,4},{3,5},{4,2},{5,3},{6,0},{7,1},{8,14},{9,15},{10,... | collective-permute-start | bytes 196616 | tf_op jit(solution)/shard_map/ppermute | solution.py:20
  49.8 2.3 %collective-permute-start.22 = (f32[128,128]{1,0:T(8,128)S(1)}, f32[128,128]{1,0:T(8,128)S(1)}, u32[]{:S(2)}, u32[]{:S(2)}) collective-permute-start(f32[128,128]{1,0:T(8,128)S(1)} %get-tuple-element.93), channel_id=1, source_target_pairs={{0,2},{1,3},{2,0},{3,1},{4,6},{5,7},{6,4},{7,5},{8,10},{9,11},{10,... | collective-permute-start | bytes 196616 | tf_op jit(solution)/shard_map/ppermute | solution.py:20
  52.1 2.2 %collective-permute-done.20.refs_2_ = f32[128,128]{1,0:T(8,128)S(1)} collective-permute-done((f32[128,128]{1,0:T(8,128)S(1)}, f32[128,128]{1,0:T(8,128)S(1)}, u32[]{:S(2)}, u32[]{:S(2)}) %collective-permute-start.20) | collective-permute-done | bytes 65568 | tf_op jit(solution)/shard_map/ppermute | solution.py:20
  54.2 2.0 %collective-permute-done.21.refs_3_ = f32[128,128]{1,0:T(8,128)S(1)} collective-permute-done((f32[128,128]{1,0:T(8,128)S(1)}, f32[128,128]{1,0:T(8,128)S(1)}, u32[]{:S(2)}, u32[]{:S(2)}) %collective-permute-start.21) | collective-permute-done | bytes 65568 | tf_op jit(solution)/shard_map/ppermute | solution.py:20
  56.3 10.4 %all_to_all.10.sums_ref = f32[32,2,128]{2,1,0:T(2,128)S(1)} all-to-all(f32[32,2,128]{2,1,0:T(2,128)S(1)} %shard_map.90), channel_id=1, replica_groups=mesh['samp'=4,'chrom'=8] {'samp','chrom'}, dimensions={0} | all-to-all | bytes 65536 | tf_op jit(solution)/shard_map/all_to_all | solution.py:463
  71.4 2.5 %collective-permute-start.27 = (f32[128,128]{1,0:T(8,128)S(1)}, f32[128,128]{1,0:T(8,128)S(1)}, u32[]{:S(2)}, u32[]{:S(2)}) collective-permute-start(f32[128,128]{1,0:T(8,128)S(1)} %get-tuple-element.102), channel_id=1, source_target_pairs={{0,2},{1,3},{2,0},{3,1},{4,6},{5,7},{6,4},{7,5},{8,10},{9,11},{10,... | collective-permute-start | bytes 196616 | tf_op jit(solution)/shard_map/ppermute | solution.py:20
  73.9 2.3 %collective-permute-done.25.refs_1_ = f32[128,128]{1,0:T(8,128)S(1)} collective-permute-done((f32[128,128]{1,0:T(8,128)S(1)}, f32[128,128]{1,0:T(8,128)S(1)}, u32[]{:S(2)}, u32[]{:S(2)}) %collective-permute-start.25) | collective-permute-done | bytes 65568 | tf_op jit(solution)/shard_map/ppermute | solution.py:20
  82.4 2.3 %collective-permute-done.28.refs_0_ = f32[128,128]{1,0:T(8,128)S(1)} collective-permute-done((f32[128,128]{1,0:T(8,128)S(1)}, f32[128,128]{1,0:T(8,128)S(1)}, u32[]{:S(2)}, u32[]{:S(2)}) %collective-permute-start.28) | collective-permute-done | bytes 65568 | tf_op jit(solution)/shard_map/ppermute | solution.py:20
  89.5 2.0 %collective-permute-start.37 = (f32[256,128]{1,0:T(8,128)S(1)}, f32[256,128]{1,0:T(8,128)S(1)}, u32[]{:S(2)}, u32[]{:S(2)}) collective-permute-start(f32[256,128]{1,0:T(8,128)S(1)} %get-tuple-element.106), channel_id=1, source_target_pairs={{0,24},{8,16},{16,8},{24,0},{1,25},{9,17},{17,9},{25,1},{2,26},{10... | collective-permute-start | bytes 393224 | tf_op jit(solution)/shard_map/ppermute | solution.py:20
  92.1 2.3 %collective-permute-done.35.refs_1_ = f32[256,128]{1,0:T(8,128)S(1)} collective-permute-done((f32[256,128]{1,0:T(8,128)S(1)}, f32[256,128]{1,0:T(8,128)S(1)}, u32[]{:S(2)}, u32[]{:S(2)}) %collective-permute-start.35) | collective-permute-done | bytes 131104 | tf_op jit(solution)/shard_map/ppermute | solution.py:20
  94.4 2.6 %collective-permute-done.36.refs_2_ = f32[256,128]{1,0:T(8,128)S(1)} collective-permute-done((f32[256,128]{1,0:T(8,128)S(1)}, f32[256,128]{1,0:T(8,128)S(1)}, u32[]{:S(2)}, u32[]{:S(2)}) %collective-permute-start.36) | collective-permute-done | bytes 131104 | tf_op jit(solution)/shard_map/ppermute | solution.py:20
  100.6 2.4 %collective-permute-done.38.refs_1_ = f32[256,128]{1,0:T(8,128)S(1)} collective-permute-done((f32[256,128]{1,0:T(8,128)S(1)}, f32[256,128]{1,0:T(8,128)S(1)}, u32[]{:S(2)}, u32[]{:S(2)}) %collective-permute-start.38) | collective-permute-done | bytes 131104 | tf_op jit(solution)/shard_map/ppermute | solution.py:20
  103.0 2.8 %collective-permute-done.39.refs_2_ = f32[256,128]{1,0:T(8,128)S(1)} collective-permute-done((f32[256,128]{1,0:T(8,128)S(1)}, f32[256,128]{1,0:T(8,128)S(1)}, u32[]{:S(2)}, u32[]{:S(2)}) %collective-permute-start.39) | collective-permute-done | bytes 131104 | tf_op jit(solution)/shard_map/ppermute | solution.py:20
  110.2 2.4 %collective-permute-start.45 = (f32[128,128]{1,0:T(8,128)S(1)}, f32[128,128]{1,0:T(8,128)S(1)}, u32[]{:S(2)}, u32[]{:S(2)}) collective-permute-start(f32[128,128]{1,0:T(8,128)S(1)} %get-tuple-element.115), channel_id=1, source_target_pairs={{0,2},{1,3},{2,0},{3,1},{4,6},{5,7},{6,4},{7,5},{8,10},{9,11},{10,... | collective-permute-start | bytes 196616 | tf_op jit(solution)/shard_map/ppermute | solution.py:20
  112.5 2.3 %collective-permute-done.43.refs_2_ = f32[128,128]{1,0:T(8,128)S(1)} collective-permute-done((f32[128,128]{1,0:T(8,128)S(1)}, f32[128,128]{1,0:T(8,128)S(1)}, u32[]{:S(2)}, u32[]{:S(2)}) %collective-permute-start.43) | collective-permute-done | bytes 65568 | tf_op jit(solution)/shard_map/ppermute | solution.py:20
  116.8 9.9 %all_to_all.11.sums_ref = f32[32,2,128]{2,1,0:T(2,128)S(1)} all-to-all(f32[32,2,128]{2,1,0:T(2,128)S(1)} %shard_map.103), channel_id=1, replica_groups=mesh['samp'=4,'chrom'=8] {'samp','chrom'}, dimensions={0} | all-to-all | bytes 65536 | tf_op jit(solution)/shard_map/all_to_all | solution.py:463
  131.4 2.5 %collective-permute-start.50 = (f32[128,128]{1,0:T(8,128)S(1)}, f32[128,128]{1,0:T(8,128)S(1)}, u32[]{:S(2)}, u32[]{:S(2)}) collective-permute-start(f32[128,128]{1,0:T(8,128)S(1)} %get-tuple-element.123), channel_id=1, source_target_pairs={{0,2},{1,3},{2,0},{3,1},{4,6},{5,7},{6,4},{7,5},{8,10},{9,11},{10,... | collective-permute-start | bytes 196616 | tf_op jit(solution)/shard_map/ppermute | solution.py:20
  133.9 2.6 %shard_map.108 = (f32[1024,128]{1,0:T(8,128)S(1)}, f32[1024,128]{1,0:T(8,128)S(1)}) custom-call(f32[1024,128]{1,0:T(8,128)S(1)} %get-tuple-element.124.coef_ref, s32[8,128]{1,0:T(8,128)S(1)} %bitcast.6, bf16[512,1024]{1,0:T(8,128)(2,1)S(1)} %get-tuple-element.72.refs_8_.refs_1_.high0_ref.refs_0_, ...), custom_call_target="tpu_custom_call" | custom-call | flops 2147483648 | bytes 8388608 | tf_op jit(solution)/shard_map/pallas_call | solution.py:475
  142.5 2.3 %collective-permute-done.51.refs_0_ = f32[128,128]{1,0:T(8,128)S(1)} collective-permute-done((f32[128,128]{1,0:T(8,128)S(1)}, f32[128,128]{1,0:T(8,128)S(1)}, u32[]{:S(2)}, u32[]{:S(2)}) %collective-permute-start.51) | collective-permute-done | bytes 65568 | tf_op jit(solution)/shard_map/ppermute | solution.py:20
  149.4 2.0 %collective-permute-start.60 = (f32[264,128]{1,0:T(8,128)S(1)}, f32[264,128]{1,0:T(8,128)S(1)}, u32[]{:S(2)}, u32[]{:S(2)}) collective-permute-start(f32[264,128]{1,0:T(8,128)S(1)} %get-tuple-element.132), channel_id=1, source_target_pairs={{0,24},{8,16},{16,8},{24,0},{1,25},{9,17},{17,9},{25,1},{2,26},{10... | collective-permute-start | bytes 405512 | tf_op jit(solution)/shard_map/ppermute | solution.py:20
  154.3 2.7 %collective-permute-done.59.refs_2_ = f32[264,128]{1,0:T(8,128)S(1)} collective-permute-done((f32[264,128]{1,0:T(8,128)S(1)}, f32[264,128]{1,0:T(8,128)S(1)}, u32[]{:S(2)}, u32[]{:S(2)}) %collective-permute-start.59) | collective-permute-done | bytes 135200 | tf_op jit(solution)/shard_map/ppermute | solution.py:20
  160.9 2.4 %collective-permute-done.61.refs_1_ = f32[256,128]{1,0:T(8,128)S(1)} collective-permute-done((f32[256,128]{1,0:T(8,128)S(1)}, f32[256,128]{1,0:T(8,128)S(1)}, u32[]{:S(2)}, u32[]{:S(2)}) %collective-permute-start.61) | collective-permute-done | bytes 131104 | tf_op jit(solution)/shard_map/ppermute | solution.py:20
  163.3 2.8 %collective-permute-done.62.refs_2_ = f32[256,128]{1,0:T(8,128)S(1)} collective-permute-done((f32[256,128]{1,0:T(8,128)S(1)}, f32[256,128]{1,0:T(8,128)S(1)}, u32[]{:S(2)}, u32[]{:S(2)}) %collective-permute-start.62) | collective-permute-done | bytes 131104 | tf_op jit(solution)/shard_map/ppermute | solution.py:20
  (145 shorter events, 69.3 us)
Async XLA Ops:
  5.2 7.6 %collective-permute-start.2 = (f32[128,128]{1,0:T(8,128)S(1)}, f32[128,128]{1,0:T(8,128)S(1)}, u32[]{:S(2)}, u32[]{:S(2)}) collective-permute-start(f32[128,128]{1,0:T(8,128)S(1)} %get-tuple-element.78), channel_id=1, source_target_pairs={{0,6},{1,7},{2,4},{3,5},{4,2},{5,3},{6,0},{7,1},{8,14},{9,15},{10,... | collective-permute-start | bytes 196616 | tf_op jit(solution)/shard_map/ppermute | solution.py:20
  16.1 7.8 %collective-permute-start.5 = (f32[128,128]{1,0:T(8,128)S(1)}, f32[128,128]{1,0:T(8,128)S(1)}, u32[]{:S(2)}, u32[]{:S(2)}) collective-permute-start(f32[128,128]{1,0:T(8,128)S(1)} %shard_map.81.refs_7_), channel_id=1, source_target_pairs={{0,4},{1,5},{2,6},{3,7},{4,0},{5,1},{6,2},{7,3},{8,12},{9,13},{10,... | collective-permute-start | bytes 196616 | tf_op jit(solution)/shard_map/ppermute | solution.py:20
  28.0 8.4 %collective-permute-start.13 = (f32[256,128]{1,0:T(8,128)S(1)}, f32[256,128]{1,0:T(8,128)S(1)}, u32[]{:S(2)}, u32[]{:S(2)}) collective-permute-start(f32[256,128]{1,0:T(8,128)S(1)} %get-tuple-element.83), channel_id=1, source_target_pairs={{0,16},{8,24},{16,0},{24,8},{1,17},{9,25},{17,1},{25,9},{2,18},{10... | collective-permute-start | bytes 393224 | tf_op jit(solution)/shard_map/ppermute | solution.py:20
  29.5 6.9 %collective-permute-start.14 = (f32[256,128]{1,0:T(8,128)S(1)}, f32[256,128]{1,0:T(8,128)S(1)}, u32[]{:S(2)}, u32[]{:S(2)}) collective-permute-start(f32[256,128]{1,0:T(8,128)S(1)} %get-tuple-element.84), channel_id=1, source_target_pairs={{0,24},{8,16},{16,8},{24,0},{1,25},{9,17},{17,9},{25,1},{2,26},{10... | collective-permute-start | bytes 393224 | tf_op jit(solution)/shard_map/ppermute | solution.py:20
  37.7 7.6 %collective-permute-start.16 = (f32[256,128]{1,0:T(8,128)S(1)}, f32[256,128]{1,0:T(8,128)S(1)}, u32[]{:S(2)}, u32[]{:S(2)}) collective-permute-start(f32[256,128]{1,0:T(8,128)S(1)} %shard_map.84.refs_0_), channel_id=1, source_target_pairs={{0,16},{8,24},{16,0},{24,8},{1,17},{9,25},{17,1},{25,9},{2,18},{10... | collective-permute-start | bytes 393224 | tf_op jit(solution)/shard_map/ppermute | solution.py:20
  38.5 6.8 %collective-permute-start.17 = (f32[256,128]{1,0:T(8,128)S(1)}, f32[256,128]{1,0:T(8,128)S(1)}, u32[]{:S(2)}, u32[]{:S(2)}) collective-permute-start(f32[256,128]{1,0:T(8,128)S(1)} %shard_map.84.refs_0_), channel_id=1, source_target_pairs={{0,24},{8,16},{16,8},{24,0},{1,25},{9,17},{17,9},{25,1},{2,26},{10... | collective-permute-start | bytes 393224 | tf_op jit(solution)/shard_map/ppermute | solution.py:20
  47.5 6.7 %collective-permute-start.20 = (f32[128,128]{1,0:T(8,128)S(1)}, f32[128,128]{1,0:T(8,128)S(1)}, u32[]{:S(2)}, u32[]{:S(2)}) collective-permute-start(f32[128,128]{1,0:T(8,128)S(1)} %get-tuple-element.91), channel_id=1, source_target_pairs={{0,6},{1,7},{2,4},{3,5},{4,2},{5,3},{6,0},{7,1},{8,14},{9,15},{10,... | collective-permute-start | bytes 196616 | tf_op jit(solution)/shard_map/ppermute | solution.py:20
  49.5 6.7 %collective-permute-start.21 = (f32[128,128]{1,0:T(8,128)S(1)}, f32[128,128]{1,0:T(8,128)S(1)}, u32[]{:S(2)}, u32[]{:S(2)}) collective-permute-start(f32[128,128]{1,0:T(8,128)S(1)} %get-tuple-element.92), channel_id=1, source_target_pairs={{0,4},{1,5},{2,6},{3,7},{4,0},{5,1},{6,2},{7,3},{8,12},{9,13},{10,... | collective-permute-start | bytes 196616 | tf_op jit(solution)/shard_map/ppermute | solution.py:20
  49.8 6.5 %collective-permute-start.22 = (f32[128,128]{1,0:T(8,128)S(1)}, f32[128,128]{1,0:T(8,128)S(1)}, u32[]{:S(2)}, u32[]{:S(2)}) collective-permute-start(f32[128,128]{1,0:T(8,128)S(1)} %get-tuple-element.93), channel_id=1, source_target_pairs={{0,2},{1,3},{2,0},{3,1},{4,6},{5,7},{6,4},{7,5},{8,10},{9,11},{10,... | collective-permute-start | bytes 196616 | tf_op jit(solution)/shard_map/ppermute | solution.py:20
  69.3 6.9 %collective-permute-start.25 = (f32[128,128]{1,0:T(8,128)S(1)}, f32[128,128]{1,0:T(8,128)S(1)}, u32[]{:S(2)}, u32[]{:S(2)}) collective-permute-start(f32[128,128]{1,0:T(8,128)S(1)} %get-tuple-element.100), channel_id=1, source_target_pairs={{0,6},{1,7},{2,4},{3,5},{4,2},{5,3},{6,0},{7,1},{8,14},{9,15},{10,... | collective-permute-start | bytes 196616 | tf_op jit(solution)/shard_map/ppermute | solution.py:20
  70.0 7.9 %collective-permute-start.26 = (f32[128,128]{1,0:T(8,128)S(1)}, f32[128,128]{1,0:T(8,128)S(1)}, u32[]{:S(2)}, u32[]{:S(2)}) collective-permute-start(f32[128,128]{1,0:T(8,128)S(1)} %get-tuple-element.101), channel_id=1, source_target_pairs={{0,4},{1,5},{2,6},{3,7},{4,0},{5,1},{6,2},{7,3},{8,12},{9,13},{10,... | collective-permute-start | bytes 196616 | tf_op jit(solution)/shard_map/ppermute | solution.py:20
  71.4 6.4 %collective-permute-start.27 = (f32[128,128]{1,0:T(8,128)S(1)}, f32[128,128]{1,0:T(8,128)S(1)}, u32[]{:S(2)}, u32[]{:S(2)}) collective-permute-start(f32[128,128]{1,0:T(8,128)S(1)} %get-tuple-element.102), channel_id=1, source_target_pairs={{0,2},{1,3},{2,0},{3,1},{4,6},{5,7},{6,4},{7,5},{8,10},{9,11},{10,... | collective-permute-start | bytes 196616 | tf_op jit(solution)/shard_map/ppermute | solution.py:20
  77.8 6.9 %collective-permute-start.28 = (f32[128,128]{1,0:T(8,128)S(1)}, f32[128,128]{1,0:T(8,128)S(1)}, u32[]{:S(2)}, u32[]{:S(2)}) collective-permute-start(f32[128,128]{1,0:T(8,128)S(1)} %shard_map.95.refs_7_), channel_id=1, source_target_pairs={{0,4},{1,5},{2,6},{3,7},{4,0},{5,1},{6,2},{7,3},{8,12},{9,13},{10,... | collective-permute-start | bytes 196616 | tf_op jit(solution)/shard_map/ppermute | solution.py:20
  78.8 6.4 %collective-permute-start.30 = (f32[128,128]{1,0:T(8,128)S(1)}, f32[128,128]{1,0:T(8,128)S(1)}, u32[]{:S(2)}, u32[]{:S(2)}) collective-permute-start(f32[128,128]{1,0:T(8,128)S(1)} %shard_map.95.refs_7_), channel_id=1, source_target_pairs={{0,6},{1,7},{2,4},{3,5},{4,2},{5,3},{6,0},{7,1},{8,14},{9,15},{10,... | collective-permute-start | bytes 196616 | tf_op jit(solution)/shard_map/ppermute | solution.py:20
  88.0 6.4 %collective-permute-start.35 = (f32[256,128]{1,0:T(8,128)S(1)}, f32[256,128]{1,0:T(8,128)S(1)}, u32[]{:S(2)}, u32[]{:S(2)}) collective-permute-start(f32[256,128]{1,0:T(8,128)S(1)} %get-tuple-element.104), channel_id=1, source_target_pairs={{0,8},{8,0},{16,24},{24,16},{1,9},{9,1},{17,25},{25,17},{2,10},{10... | collective-permute-start | bytes 393224 | tf_op jit(solution)/shard_map/ppermute | solution.py:20
  88.9 8.1 %collective-permute-start.36 = (f32[256,128]{1,0:T(8,128)S(1)}, f32[256,128]{1,0:T(8,128)S(1)}, u32[]{:S(2)}, u32[]{:S(2)}) collective-permute-start(f32[256,128]{1,0:T(8,128)S(1)} %get-tuple-element.105), channel_id=1, source_target_pairs={{0,16},{8,24},{16,0},{24,8},{1,17},{9,25},{17,1},{25,9},{2,18},{10... | collective-permute-start | bytes 393224 | tf_op jit(solution)/shard_map/ppermute | solution.py:20
  89.5 7.5 %collective-permute-start.37 = (f32[256,128]{1,0:T(8,128)S(1)}, f32[256,128]{1,0:T(8,128)S(1)}, u32[]{:S(2)}, u32[]{:S(2)}) collective-permute-start(f32[256,128]{1,0:T(8,128)S(1)} %get-tuple-element.106), channel_id=1, source_target_pairs={{0,24},{8,16},{16,8},{24,0},{1,25},{9,17},{17,9},{25,1},{2,26},{10... | collective-permute-start | bytes 393224 | tf_op jit(solution)/shard_map/ppermute | solution.py:20
  98.3 7.4 %collective-permute-start.39 = (f32[256,128]{1,0:T(8,128)S(1)}, f32[256,128]{1,0:T(8,128)S(1)}, u32[]{:S(2)}, u32[]{:S(2)}) collective-permute-start(f32[256,128]{1,0:T(8,128)S(1)} %shard_map.98.refs_0_), channel_id=1, source_target_pairs={{0,16},{8,24},{16,0},{24,8},{1,17},{9,25},{17,1},{25,9},{2,18},{10... | collective-permute-start | bytes 393224 | tf_op jit(solution)/shard_map/ppermute | solution.py:20
  99.1 6.7 %collective-permute-start.40 = (f32[256,128]{1,0:T(8,128)S(1)}, f32[256,128]{1,0:T(8,128)S(1)}, u32[]{:S(2)}, u32[]{:S(2)}) collective-permute-start(f32[256,128]{1,0:T(8,128)S(1)} %shard_map.98.refs_0_), channel_id=1, source_target_pairs={{0,24},{8,16},{16,8},{24,0},{1,25},{9,17},{17,9},{25,1},{2,26},{10... | collective-permute-start | bytes 393224 | tf_op jit(solution)/shard_map/ppermute | solution.py:20
  108.0 6.9 %collective-permute-start.43 = (f32[128,128]{1,0:T(8,128)S(1)}, f32[128,128]{1,0:T(8,128)S(1)}, u32[]{:S(2)}, u32[]{:S(2)}) collective-permute-start(f32[128,128]{1,0:T(8,128)S(1)} %get-tuple-element.113), channel_id=1, source_target_pairs={{0,6},{1,7},{2,4},{3,5},{4,2},{5,3},{6,0},{7,1},{8,14},{9,15},{10,... | collective-permute-start | bytes 196616 | tf_op jit(solution)/shard_map/ppermute | solution.py:20
  109.8 6.9 %collective-permute-start.44 = (f32[128,128]{1,0:T(8,128)S(1)}, f32[128,128]{1,0:T(8,128)S(1)}, u32[]{:S(2)}, u32[]{:S(2)}) collective-permute-start(f32[128,128]{1,0:T(8,128)S(1)} %get-tuple-element.114), channel_id=1, source_target_pairs={{0,4},{1,5},{2,6},{3,7},{4,0},{5,1},{6,2},{7,3},{8,12},{9,13},{10,... | collective-permute-start | bytes 196616 | tf_op jit(solution)/shard_map/ppermute | solution.py:20
  110.2 6.5 %collective-permute-start.45 = (f32[128,128]{1,0:T(8,128)S(1)}, f32[128,128]{1,0:T(8,128)S(1)}, u32[]{:S(2)}, u32[]{:S(2)}) collective-permute-start(f32[128,128]{1,0:T(8,128)S(1)} %get-tuple-element.115), channel_id=1, source_target_pairs={{0,2},{1,3},{2,0},{3,1},{4,6},{5,7},{6,4},{7,5},{8,10},{9,11},{10,... | collective-permute-start | bytes 196616 | tf_op jit(solution)/shard_map/ppermute | solution.py:20
  129.4 7.1 %collective-permute-start.48 = (f32[128,128]{1,0:T(8,128)S(1)}, f32[128,128]{1,0:T(8,128)S(1)}, u32[]{:S(2)}, u32[]{:S(2)}) collective-permute-start(f32[128,128]{1,0:T(8,128)S(1)} %get-tuple-element.121), channel_id=1, source_target_pairs={{0,6},{1,7},{2,4},{3,5},{4,2},{5,3},{6,0},{7,1},{8,14},{9,15},{10,... | collective-permute-start | bytes 196616 | tf_op jit(solution)/shard_map/ppermute | solution.py:20
  130.0 7.9 %collective-permute-start.49 = (f32[128,128]{1,0:T(8,128)S(1)}, f32[128,128]{1,0:T(8,128)S(1)}, u32[]{:S(2)}, u32[]{:S(2)}) collective-permute-start(f32[128,128]{1,0:T(8,128)S(1)} %get-tuple-element.122), channel_id=1, source_target_pairs={{0,4},{1,5},{2,6},{3,7},{4,0},{5,1},{6,2},{7,3},{8,12},{9,13},{10,... | collective-permute-start | bytes 196616 | tf_op jit(solution)/shard_map/ppermute | solution.py:20
  131.4 6.4 %collective-permute-start.50 = (f32[128,128]{1,0:T(8,128)S(1)}, f32[128,128]{1,0:T(8,128)S(1)}, u32[]{:S(2)}, u32[]{:S(2)}) collective-permute-start(f32[128,128]{1,0:T(8,128)S(1)} %get-tuple-element.123), channel_id=1, source_target_pairs={{0,2},{1,3},{2,0},{3,1},{4,6},{5,7},{6,4},{7,5},{8,10},{9,11},{10,... | collective-permute-start | bytes 196616 | tf_op jit(solution)/shard_map/ppermute | solution.py:20
  137.9 6.9 %collective-permute-start.51 = (f32[128,128]{1,0:T(8,128)S(1)}, f32[128,128]{1,0:T(8,128)S(1)}, u32[]{:S(2)}, u32[]{:S(2)}) collective-permute-start(f32[128,128]{1,0:T(8,128)S(1)} %shard_map.109.refs_7_), channel_id=1, source_target_pairs={{0,4},{1,5},{2,6},{3,7},{4,0},{5,1},{6,2},{7,3},{8,12},{9,13},{10,... | collective-permute-start | bytes 196616 | tf_op jit(solution)/shard_map/ppermute | solution.py:20
  138.9 6.4 %collective-permute-start.53 = (f32[128,128]{1,0:T(8,128)S(1)}, f32[128,128]{1,0:T(8,128)S(1)}, u32[]{:S(2)}, u32[]{:S(2)}) collective-permute-start(f32[128,128]{1,0:T(8,128)S(1)} %shard_map.109.refs_7_), channel_id=1, source_target_pairs={{0,6},{1,7},{2,4},{3,5},{4,2},{5,3},{6,0},{7,1},{8,14},{9,15},{10,... | collective-permute-start | bytes 196616 | tf_op jit(solution)/shard_map/ppermute | solution.py:20
  147.8 6.5 %collective-permute-start.58 = (f32[264,128]{1,0:T(8,128)S(1)}, f32[264,128]{1,0:T(8,128)S(1)}, u32[]{:S(2)}, u32[]{:S(2)}) collective-permute-start(f32[264,128]{1,0:T(8,128)S(1)} %get-tuple-element.130), channel_id=1, source_target_pairs={{0,8},{8,0},{16,24},{24,16},{1,9},{9,1},{17,25},{25,17},{2,10},{10... | collective-permute-start | bytes 405512 | tf_op jit(solution)/shard_map/ppermute | solution.py:20
  148.8 8.3 %collective-permute-start.59 = (f32[264,128]{1,0:T(8,128)S(1)}, f32[264,128]{1,0:T(8,128)S(1)}, u32[]{:S(2)}, u32[]{:S(2)}) collective-permute-start(f32[264,128]{1,0:T(8,128)S(1)} %get-tuple-element.131), channel_id=1, source_target_pairs={{0,16},{8,24},{16,0},{24,8},{1,17},{9,25},{17,1},{25,9},{2,18},{10... | collective-permute-start | bytes 405512 | tf_op jit(solution)/shard_map/ppermute | solution.py:20
  149.4 7.7 %collective-permute-start.60 = (f32[264,128]{1,0:T(8,128)S(1)}, f32[264,128]{1,0:T(8,128)S(1)}, u32[]{:S(2)}, u32[]{:S(2)}) collective-permute-start(f32[264,128]{1,0:T(8,128)S(1)} %get-tuple-element.132), channel_id=1, source_target_pairs={{0,24},{8,16},{16,8},{24,0},{1,25},{9,17},{17,9},{25,1},{2,26},{10... | collective-permute-start | bytes 405512 | tf_op jit(solution)/shard_map/ppermute | solution.py:20
  158.6 7.4 %collective-permute-start.62 = (f32[256,128]{1,0:T(8,128)S(1)}, f32[256,128]{1,0:T(8,128)S(1)}, u32[]{:S(2)}, u32[]{:S(2)}) collective-permute-start(f32[256,128]{1,0:T(8,128)S(1)} %shard_map.112.refs_0_), channel_id=1, source_target_pairs={{0,16},{8,24},{16,0},{24,8},{1,17},{9,25},{17,1},{25,9},{2,18},{10... | collective-permute-start | bytes 393224 | tf_op jit(solution)/shard_map/ppermute | solution.py:20
  159.4 6.6 %collective-permute-start.63 = (f32[256,128]{1,0:T(8,128)S(1)}, f32[256,128]{1,0:T(8,128)S(1)}, u32[]{:S(2)}, u32[]{:S(2)}) collective-permute-start(f32[256,128]{1,0:T(8,128)S(1)} %shard_map.112.refs_0_), channel_id=1, source_target_pairs={{0,24},{8,16},{16,8},{24,0},{1,25},{9,17},{17,9},{25,1},{2,26},{10... | collective-permute-start | bytes 393224 | tf_op jit(solution)/shard_map/ppermute | solution.py:20
  (37 other events, 190.3 us)
